TPU v7x, 128 devices: a whole 4x4x4 slice. The times are simulated.
128 devices in a mesh: attn: 32 (over y, z, core), exp: 4 (over x).
Axes of the slice: x: 4, y: 4, z: 4, core: 2. Of those that a mesh axis runs over, the one named last changes fastest.
Arguments:
- hidden: bfloat16 [1024, 7168], P(('attn', 'exp')), may hold values from -6 to 6
- norm_gain: float32 [7168], replicated, may hold values from 0.1 to 1.9
- routes: int32 [1024, 8], P(('attn', 'exp')), may hold values from 0 to 31, all different within a row; in each aligned block of 4 rows (0 to 3, 4 to 7, ...) at most 2 rows name the same one
- route_scores: float32 [1024, 8], P(('attn', 'exp')), may hold values from 0.1 to 1
- capacity: int32 [32], replicated, may hold values from 1 to 2
- w_gate: bfloat16 [32, 7168, 2048], P('attn', 'exp'), may hold values from -0.0625 to 0.0625
- w_up: bfloat16 [32, 7168, 2048], P('attn', 'exp'), may hold values from -0.0625 to 0.0625
- w_down: bfloat16 [32, 2048, 7168], P('attn', None, 'exp'), may hold values from -0.125 to 0.125
Outputs:
- moe_out: bfloat16 [1024, 7168], P(('attn', 'exp'))
Inputs may be any that keep to these rules, and one draw needn't show every extreme that they name: `routes`: each row names 8 different experts; in each aligned block of 4 rows no expert is named by more than 2 rows, and in some block some expert is named by exactly 2 rows.
All inputs are finite; a program needn't handle non-finite values.
Results may differ from a plain program's by a relative error of at most 0.015.
Values may be sent and summed in bfloat16 or wider, within the bound.
No kernel may reach another device: no remote copies, remote signals or barrier semaphores. Data moves between devices by JAX's collectives and lax.ppermute only.
A program may use at most 128 MiB of HBM per device.

v0:
```python
import jax
import jax.numpy as jnp
from jax import lax
from jax.sharding import PartitionSpec as P

MICRO = 2


ROUTE_SCALE = 2.5
EPSILON = 1e-06
HIGHEST = lax.Precision.HIGHEST


def round_partial(value):
    return lax.optimization_barrier(value.astype(jnp.bfloat16)).astype(jnp.float32)


def shards(hidden, norm_gain, routes, route_scores, capacity, w_gate, w_up, w_down):
    attn_count = lax.axis_size("attn")
    exp_count = lax.axis_size("exp")
    local_experts = w_gate.shape[0]
    all_experts = local_experts * attn_count
    slice_width = w_gate.shape[1]
    micro_rows = hidden.shape[0] // MICRO
    top_count = routes.shape[1]
    cap_size = min(
        micro_rows, max(2, (2 * micro_rows * top_count + all_experts - 1) // all_experts)
    )
    slot_count = all_experts * cap_size
    hidden_f = hidden.astype(jnp.float32)
    normed = (
        hidden_f
        * lax.rsqrt(jnp.mean(hidden_f * hidden_f, axis=1, keepdims=True) + EPSILON)
        * norm_gain
    ).astype(jnp.bfloat16)
    route_weights = ROUTE_SCALE * route_scores / jnp.sum(route_scores, axis=1, keepdims=True)
    pair_count = micro_rows * top_count
    earlier = (jnp.arange(pair_count)[:, None] > jnp.arange(pair_count)[None, :]).astype(
        jnp.float32
    )
    outputs = []
    for micro in range(MICRO):
        start_row = micro * micro_rows
        block_normed = normed[start_row : start_row + micro_rows]
        pair_ids = routes[start_row : start_row + micro_rows].reshape(-1)
        onehot = (pair_ids[:, None] == jnp.arange(all_experts, dtype=jnp.int32)[None, :]).astype(
            jnp.float32
        )
        pair_rank = jnp.sum(jnp.dot(earlier, onehot, precision=HIGHEST) * onehot, axis=1)
        limits = jnp.dot(onehot, capacity.astype(jnp.float32), precision=HIGHEST)
        kept_mask = pair_rank < limits
        slot_ids = jnp.where(kept_mask, pair_ids * cap_size + pair_rank.astype(jnp.int32), -1)
        matches = jnp.arange(slot_count, dtype=jnp.int32)[:, None] == slot_ids[None, :]
        outgoing = jnp.dot(
            matches.astype(jnp.bfloat16),
            jnp.repeat(block_normed, top_count, axis=0),
            preferred_element_type=jnp.float32,
        ).astype(jnp.bfloat16)
        pair_weights = jnp.where(
            kept_mask, route_weights[start_row : start_row + micro_rows].reshape(-1), 0.0
        )
        combine_map = jnp.sum(
            (matches.T.astype(jnp.float32) * pair_weights[:, None]).reshape(
                micro_rows, top_count, slot_count
            ),
            axis=1,
        )
        layered = outgoing.reshape(attn_count, local_experts, cap_size, exp_count, slice_width)
        ordered = layered.transpose(0, 3, 1, 2, 4).reshape(
            attn_count * exp_count, local_experts, cap_size, slice_width
        )
        grouped = lax.all_to_all(ordered, ("attn", "exp"), split_axis=0, concat_axis=0, tiled=True)
        gate_part = round_partial(
            jnp.einsum("seqd,edf->seqf", grouped, w_gate, preferred_element_type=jnp.float32)
        )
        up_part = round_partial(
            jnp.einsum("seqd,edf->seqf", grouped, w_up, preferred_element_type=jnp.float32)
        )
        gate_sum, up_sum = (
            lax.psum(gate_part.astype(jnp.bfloat16), "exp").astype(jnp.float32),
            lax.psum(up_part.astype(jnp.bfloat16), "exp").astype(jnp.float32),
        )
        activation = (jax.nn.silu(gate_sum) * up_sum).astype(jnp.bfloat16)
        expert_out = jnp.einsum(
            "seqf,efd->seqd", activation, w_down, preferred_element_type=jnp.float32
        ).astype(jnp.bfloat16)
        back_rows = lax.all_to_all(
            expert_out, ("attn", "exp"), split_axis=0, concat_axis=0, tiled=True
        )
        returned = back_rows.reshape(
            attn_count, exp_count, local_experts, cap_size, slice_width
        ).transpose(0, 2, 3, 1, 4)
        returned = returned.reshape(slot_count, exp_count * slice_width)
        moe_sum = jnp.dot(combine_map, returned.astype(jnp.float32), precision=HIGHEST)
        outputs.append(
            (hidden_f[start_row : start_row + micro_rows] + moe_sum).astype(jnp.bfloat16)
        )
    return jnp.concatenate(outputs, axis=0)


def solution(mesh):
    in_specs = (
        P(("attn", "exp"), None),
        P(),
        P(("attn", "exp"), None),
        P(("attn", "exp"), None),
        P(),
        P("attn", "exp", None),
        P("attn", "exp", None),
        P("attn", None, "exp"),
    )
    out_specs = P(("attn", "exp"), None)
    return jax.shard_map(shards, mesh=mesh, in_specs=in_specs, out_specs=out_specs, check_vma=False)
```

profile of v0, /device:TPU:0, one launch (start us, length us, event | category | flops | bytes accessed | tf_op | source)
XLA Modules:
  0.0 232.8 jit_solution(5044926156376473786)
XLA Ops:
  6.5 0.8 fusion.90
  7.3 0.1 eq.83
  7.4 0.1 fusion.61
  7.5 0.8 reduce_sum.55
  8.3 0.8 multiply_divide_fusion
  9.1 0.1 reshape.131
  9.2 0.8 broadcast_select_fusion
  10.0 1.1 multiply_reduce_fusion
  11.1 1.0 multiply_convert_fusion
  12.1 0.4 convolution_convert_fusion
  12.5 0.7 reshape.133
  13.2 1.7 copy.27
  14.9 11.1 %all-to-all-start.2 = ((bf16[128,1,2,1792]{3,2,1,0:T(2,128)(2,1)}), bf16[128,1,2,1792]{3,2,1,0:T(2,128)(2,1)S(1)}, u32[]{:S(2)}, u32[]{:S(2)}) async-start(bf16[128,1,2,1792]{3,2,1,0:T(2,128)(2,1)} %bitcast.28), calls=%async_computation.2 | async-start | bytes 1835008 | tf_op jit(solution)/shard_map/all_to_all | solution.py:72
  26.0 0.1 eq.73
  26.1 0.1 fusion.60
  26.3 0.1 add_select_fusion.1
  26.4 0.4 convolution_convert_fusion.1
  26.8 0.7 reshape.122
  27.5 1.6 copy.23
  29.1 14.4 %all-to-all-done.2 = bf16[128,1,2,1792]{3,2,1,0:T(2,128)(2,1)S(1)} async-done(((bf16[128,1,2,1792]{3,2,1,0:T(2,128)(2,1)}), bf16[128,1,2,1792]{3,2,1,0:T(2,128)(2,1)S(1)}, u32[]{:S(2)}, u32[]{:S(2)}) %all-to-all-start.2) | async-done | bytes 917536 | tf_op jit(solution)/shard_map/all_to_all | solution.py:72
  43.6 4.6 %all-to-all-start = ((bf16[128,1,2,1792]{3,2,1,0:T(2,128)(2,1)}), bf16[128,1,2,1792]{3,2,1,0:T(2,128)(2,1)S(1)}, u32[]{:S(2)}, u32[]{:S(2)}) async-start(bf16[128,1,2,1792]{3,2,1,0:T(2,128)(2,1)} %bitcast.4), calls=%async_computation | async-start | bytes 1835008 | tf_op jit(solution)/shard_map/all_to_all | solution.py:72
  48.2 0.2 all-reduce.3.cloned.1.call-start
  48.4 6.1 %fusion.44 = bf16[128,1,2,2048]{3,0,2,1:T(8,128)(2,1)} fusion(bf16[1,1792,2048]{2,1,0:T(8,128)(2,1)} %param.13, bf16[128,1,2,1792]{3,2,1,0:T(2,128)(2,1)S(1)} %all-to-all-done.2), kind=kOutput, calls=%fused_computation.32 | convolution fusion | flops 1879572480 | bytes 9306112 | tf_op jit(solution)/shard_map/seqd,edf->seqf/dot_general | solution.py:74
  54.6 6.1 %fusion.38 = bf16[128,1,2,2048]{3,0,2,1:T(8,128)(2,1)} fusion(bf16[1,1792,2048]{2,1,0:T(8,128)(2,1)} %param.14, bf16[128,1,2,1792]{3,2,1,0:T(2,128)(2,1)S(1)} %all-to-all-done.2), kind=kOutput, calls=%fused_computation.30 | convolution fusion | flops 1879572480 | bytes 9306112 | tf_op jit(solution)/shard_map/seqd,edf->seqf/dot_general | solution.py:77
  60.7 5.0 %all-to-all-done = bf16[128,1,2,1792]{3,2,1,0:T(2,128)(2,1)S(1)} async-done(((bf16[128,1,2,1792]{3,2,1,0:T(2,128)(2,1)}), bf16[128,1,2,1792]{3,2,1,0:T(2,128)(2,1)S(1)}, u32[]{:S(2)}, u32[]{:S(2)}) %all-to-all-start) | async-done | bytes 917536 | tf_op jit(solution)/shard_map/all_to_all | solution.py:72
  65.7 6.1 %fusion.47 = bf16[128,1,2,2048]{3,0,2,1:T(8,128)(2,1)} fusion(bf16[1,1792,2048]{2,1,0:T(8,128)(2,1)} %param.13, bf16[128,1,2,1792]{3,2,1,0:T(2,128)(2,1)S(1)} %all-to-all-done), kind=kOutput, calls=%fused_computation.33 | convolution fusion | flops 1879572480 | bytes 9306112 | tf_op jit(solution)/shard_map/seqd,edf->seqf/dot_general | solution.py:74
  71.8 6.1 %fusion.41 = bf16[128,1,2,2048]{3,0,2,1:T(8,128)(2,1)} fusion(bf16[1,1792,2048]{2,1,0:T(8,128)(2,1)} %param.14, bf16[128,1,2,1792]{3,2,1,0:T(2,128)(2,1)S(1)} %all-to-all-done), kind=kOutput, calls=%fused_computation.31 | convolution fusion | flops 1879572480 | bytes 9306112 | tf_op jit(solution)/shard_map/seqd,edf->seqf/dot_general | solution.py:77
  78.0 89.5 %all-reduce.3.cloned.1.call-done = (bf16[128,1,2,2048]{3,0,2,1:T(8,128)(2,1)}, bf16[128,1,2,2048]{3,0,2,1:T(8,128)(2,1)}, bf16[128,1,2,2048]{3,0,2,1:T(8,128)(2,1)}, bf16[128,1,2,2048]{3,0,2,1:T(8,128)(2,1)}) async-done(((bf16[128,1,2,2048]{3,0,2,1:T(8,128)(2,1)}, bf16[128,1,2,2048]{3,0,2,1:T(8,128)(2,1)}, bf16[128,1,2,2048]{3,0,2,1:T(8,128)(2,1)}, bf16[128,1,2,2048]{3,0,2,1:T(8,128)(2,1)}), ...) | async-done | bytes 4194320 | tf_op jit(solution)/shard_map/psum | solution.py:81
  167.5 6.2 %fusion.35 = bf16[128,1,2,1792]{3,0,2,1:T(8,128)(2,1)S(1)} fusion(bf16[1,2048,1792]{2,1,0:T(8,128)(2,1)} %param.15, bf16[128,1,2,2048]{3,0,2,1:T(8,128)(2,1)} %get-tuple-element.7, bf16[128,1,2,2048]{3,0,2,1:T(8,128)(2,1)} %get-tuple-element.8), kind=kOutput, calls=%fused_computation.29 | convolution fusion | flops 1883701248 | bytes 10354688 | tf_op jit(solution)/shard_map/seqf,efd->seqd/dot_general | solution.py:84
  173.7 1.9 copy.25
  175.6 8.8 %all-to-all-start.1 = ((bf16[128,1,2,1792]{3,2,1,0:T(2,128)(2,1)}), bf16[128,1,2,1792]{3,2,1,0:T(2,128)(2,1)S(1)}, u32[]{:S(2)}, u32[]{:S(2)}) async-start(bf16[128,1,2,1792]{3,2,1,0:T(2,128)(2,1)} %copy.25), calls=%async_computation.1 | async-start | bytes 1835008 | tf_op jit(solution)/shard_map/all_to_all | solution.py:87
  184.4 5.5 %fusion.32 = bf16[128,1,2,1792]{3,0,2,1:T(8,128)(2,1)S(1)} fusion(bf16[1,2048,1792]{2,1,0:T(8,128)(2,1)} %param.15, bf16[128,1,2,2048]{3,0,2,1:T(8,128)(2,1)S(1)} %copy-done.1, bf16[128,1,2,2048]{3,0,2,1:T(8,128)(2,1)S(1)} %copy-done.2), kind=kOutput, calls=%fused_computation.28 | convolution fusion | flops 1883701248 | bytes 10354688 | tf_op jit(solution)/shard_map/seqf,efd->seqd/dot_general | solution.py:84
  189.9 1.9 copy.29
  191.8 9.9 %all-to-all-done.1 = bf16[128,1,2,1792]{3,2,1,0:T(2,128)(2,1)S(1)} async-done(((bf16[128,1,2,1792]{3,2,1,0:T(2,128)(2,1)}), bf16[128,1,2,1792]{3,2,1,0:T(2,128)(2,1)S(1)}, u32[]{:S(2)}, u32[]{:S(2)}) %all-to-all-start.1) | async-done | bytes 917536 | tf_op jit(solution)/shard_map/all_to_all | solution.py:87
  201.7 4.6 %all-to-all-start.3 = ((bf16[128,1,2,1792]{3,2,1,0:T(2,128)(2,1)}), bf16[128,1,2,1792]{3,2,1,0:T(2,128)(2,1)S(1)}, u32[]{:S(2)}, u32[]{:S(2)}) async-start(bf16[128,1,2,1792]{3,2,1,0:T(2,128)(2,1)} %copy.29), calls=%async_computation.3 | async-start | bytes 1835008 | tf_op jit(solution)/shard_map/all_to_all | solution.py:87
  206.3 0.1 eq.76
  206.4 0.1 eq.86
  206.6 0.1 mul.74
  206.7 0.1 select_reduce_fusion.1
  206.8 0.1 select_reduce_fusion
  206.9 0.4 copy.26
  207.3 0.1 copy.31
  207.4 16.4 %all-to-all-done.3 = bf16[128,1,2,1792]{3,2,1,0:T(2,128)(2,1)S(1)} async-done(((bf16[128,1,2,1792]{3,2,1,0:T(2,128)(2,1)}), bf16[128,1,2,1792]{3,2,1,0:T(2,128)(2,1)S(1)}, u32[]{:S(2)}, u32[]{:S(2)}) %all-to-all-start.3) | async-done | bytes 917536 | tf_op jit(solution)/shard_map/all_to_all | solution.py:87
  223.8 0.4 copy.30
  224.2 0.1 copy.32
  224.3 0.5 fusion
  224.7 0.5 fusion.1
  225.2 0.7 pad_maximum_fusion
  (17 shorter events, 0.3 us)
Async XLA Ops:
  13.2 13.1 %copy-start.3 = (s32[32]{0:T(128)S(1)}, s32[32]{0:T(128)}, u32[]{:S(2)}) copy-start(s32[32]{0:T(128)} %param.12) | copy-start | bytes 388
  14.9 28.7 %all-to-all-start.2 = ((bf16[128,1,2,1792]{3,2,1,0:T(2,128)(2,1)}), bf16[128,1,2,1792]{3,2,1,0:T(2,128)(2,1)S(1)}, u32[]{:S(2)}, u32[]{:S(2)}) async-start(bf16[128,1,2,1792]{3,2,1,0:T(2,128)(2,1)} %bitcast.28), calls=%async_computation.2 | async-start | bytes 1835008 | tf_op jit(solution)/shard_map/all_to_all | solution.py:72
  43.6 22.2 %all-to-all-start = ((bf16[128,1,2,1792]{3,2,1,0:T(2,128)(2,1)}), bf16[128,1,2,1792]{3,2,1,0:T(2,128)(2,1)S(1)}, u32[]{:S(2)}, u32[]{:S(2)}) async-start(bf16[128,1,2,1792]{3,2,1,0:T(2,128)(2,1)} %bitcast.4), calls=%async_computation | async-start | bytes 1835008 | tf_op jit(solution)/shard_map/all_to_all | solution.py:72
  48.2 119.3 %all-reduce.3.cloned.1.call-start = ((), (), s32[]{:S(2)}) async-start(), calls=%async_computation.4 | async-start | bytes 8388608 | tf_op jit(solution)/shard_map/psum | solution.py:81
  173.7 10.7 %copy-start.1 = (bf16[128,1,2,2048]{3,0,2,1:T(8,128)(2,1)S(1)}, bf16[128,1,2,2048]{3,0,2,1:T(8,128)(2,1)}, u32[]{:S(2)}) copy-start(bf16[128,1,2,2048]{3,0,2,1:T(8,128)(2,1)} %get-tuple-element.5) | copy-start | bytes 3145732
  173.7 10.7 %copy-start.2 = (bf16[128,1,2,2048]{3,0,2,1:T(8,128)(2,1)S(1)}, bf16[128,1,2,2048]{3,0,2,1:T(8,128)(2,1)}, u32[]{:S(2)}) copy-start(bf16[128,1,2,2048]{3,0,2,1:T(8,128)(2,1)} %get-tuple-element.6) | copy-start | bytes 3145732
  175.6 26.1 %all-to-all-start.1 = ((bf16[128,1,2,1792]{3,2,1,0:T(2,128)(2,1)}), bf16[128,1,2,1792]{3,2,1,0:T(2,128)(2,1)S(1)}, u32[]{:S(2)}, u32[]{:S(2)}) async-start(bf16[128,1,2,1792]{3,2,1,0:T(2,128)(2,1)} %copy.25), calls=%async_computation.1 | async-start | bytes 1835008 | tf_op jit(solution)/shard_map/all_to_all | solution.py:87
  189.9 16.5 %copy-start = (bf16[8,7168]{1,0:T(8,128)(2,1)S(1)}, bf16[8,7168]{1,0:T(8,128)(2,1)}, u32[]{:S(2)}) copy-start(bf16[8,7168]{1,0:T(8,128)(2,1)} %param.8) | copy-start | bytes 344068
  201.7 22.2 %all-to-all-start.3 = ((bf16[128,1,2,1792]{3,2,1,0:T(2,128)(2,1)}), bf16[128,1,2,1792]{3,2,1,0:T(2,128)(2,1)S(1)}, u32[]{:S(2)}, u32[]{:S(2)}) async-start(bf16[128,1,2,1792]{3,2,1,0:T(2,128)(2,1)} %copy.29), calls=%async_computation.3 | async-start | bytes 1835008 | tf_op jit(solution)/shard_map/all_to_all | solution.py:87
Sparse Core Ops, SparseCore 0:
  78.1 89.3 all-reduce.2
where the time goes:
time: 235 us; the launch traced here: 233 us
  waiting for transfers between devices  135 us (57%)
  matrix products  39.2 us (17%)
  starting transfers between devices  29.4 us (13%)
  between operations  13.6 us (6%)
  local copies, waits for them, and re-layouts  10.8 us (5%)
  other arithmetic  4.59 us (2%)
    psum x1, waiting for transfers between devices, shards(): lax.psum(up_part.astype(jnp.bfloat16), 'exp').astype(jnp.float32)  89.5 us
    all_to_all x2, waiting for transfers between devices, shards(): lax.all_to_all(expert_out, ('attn', 'exp'), split_axis=0, concat_axis=0,...  26.3 us
    all_to_all x2, waiting for transfers between devices, shards(): lax.all_to_all(ordered, ('attn', 'exp'), split_axis=0, concat_axis=0, til...  19.5 us
    all_to_all x2, starting transfers between devices, shards(): lax.all_to_all(ordered, ('attn', 'exp'), split_axis=0, concat_axis=0, til...  15.8 us
    all_to_all x2, starting transfers between devices, shards(): lax.all_to_all(expert_out, ('attn', 'exp'), split_axis=0, concat_axis=0,...  13.4 us
    dot_general x2, matrix products, shards(): jnp.einsum('seqd,edf->seqf', grouped, w_up, preferred_element_type=jnp.fl...  12.3 us
    dot_general x2, matrix products, shards(): jnp.einsum('seqd,edf->seqf', grouped, w_gate, preferred_element_type=jnp....  12.3 us
    dot_general x2, matrix products, shards(): jnp.einsum('seqf,efd->seqd', activation, w_down, preferred_element_type=j...  11.7 us
  transfers between devices with their start and end apart: 5, of which 5 were waited for; matrix products, arithmetic and copies ran while one was open for 10% of the time, Pallas kernels for 0%

commit v1 on v0

v1 whole, which is shorter than its diff:
```python
import jax
import jax.numpy as jnp
from jax import lax
from jax.sharding import Mesh, PartitionSpec as P

MICRO = 2
ROUTE_SCALE = 2.5
EPSILON = 1e-06
PAD = 128
RING = 4


def move(value, step):
    return lax.ppermute(value, "x", [(i, (i + step) % RING) for i in range(RING)])


def swap(value, axes):
    return lax.all_to_all(value, axes, split_axis=0, concat_axis=0, tiled=True)


def add(one, other):
    return (one.astype(jnp.float32) + other.astype(jnp.float32)).astype(jnp.bfloat16)


def routing_columns(routes, route_scores, capacity):
    rows, experts = routes.shape[0], capacity.shape[0]
    weights = ROUTE_SCALE * route_scores / jnp.sum(route_scores, axis=1, keepdims=True)
    named = routes[:, :, None] == jnp.arange(experts, dtype=jnp.int32)[None, None, :]
    match = jnp.any(named, axis=1)
    weight = jnp.sum(jnp.where(named, weights[:, :, None], 0.0), axis=1)
    blocks = match.astype(jnp.int32).reshape(rows // 4, 4, experts)
    running = jnp.zeros((rows // 4, experts), jnp.int32)
    ranks = []
    for row in range(4):
        ranks.append(running)
        running = running + blocks[:, row]
    rank = jnp.stack(ranks, axis=1).reshape(rows, experts)
    kept = match & (rank < capacity[None, :])
    code = jnp.where(kept, rank + 1, 0).astype(jnp.bfloat16)
    weight = jnp.where(kept, weight, 0.0)
    high = lax.reduce_precision(weight, 8, 7)
    low = weight - high
    empty = jnp.zeros((rows, PAD - 3 * experts), jnp.bfloat16)
    return jnp.concatenate([code, high.astype(jnp.bfloat16), low.astype(jnp.bfloat16), empty], axis=1)


def slot_maps(picks, targets, experts):
    rows = picks.shape[0]
    slot = jnp.arange(8 * rows // 2, dtype=jnp.int32)
    target = targets(slot // (rows // 2))
    lane = jnp.arange(PAD, dtype=jnp.int32)[:, None]
    parts = [
        jnp.dot(picks, (lane == target[None, :] + k * experts).astype(jnp.bfloat16), preferred_element_type=jnp.float32)
        for k in range(3)
    ]
    row = jnp.arange(rows, dtype=jnp.int32)
    chosen = (row[:, None] // 4 == slot[None, :] % (rows // 2) // 2) & (
        parts[0].astype(jnp.int32) == (slot % 2 + 1)[None, :]
    )
    return (
        chosen.astype(jnp.bfloat16),
        jnp.where(chosen, parts[1], 0.0).astype(jnp.bfloat16),
        jnp.where(chosen, parts[2], 0.0).astype(jnp.bfloat16),
    )


def shards(hidden, norm_gain, routes, route_scores, capacity, w_gate, w_up, w_down):
    experts = capacity.shape[0]
    place = lax.axis_index("x")
    width = w_gate.shape[1]
    ff = w_gate.shape[2]
    rows = hidden.shape[0]
    micro_rows = rows // MICRO
    hidden_f = hidden.astype(jnp.float32)
    normed = (
        hidden_f
        * lax.rsqrt(jnp.mean(hidden_f * hidden_f, axis=1, keepdims=True) + EPSILON)
        * norm_gain
    ).astype(jnp.bfloat16)
    columns = routing_columns(routes, route_scores, capacity)
    payload = jnp.stack(
        [jnp.concatenate([normed[:, r * width : (r + 1) * width], columns], axis=1) for r in range(RING)]
    )
    mixed = swap(payload, "x")
    entering, maps = [], []
    for micro in range(MICRO):
        first, second = ("y", "z") if micro == 0 else ("z", "y")
        lines = mixed[:, micro * micro_rows : (micro + 1) * micro_rows].reshape(1, RING * micro_rows, width + PAD)
        lines = swap(jnp.broadcast_to(lines, (RING,) + lines.shape[1:]), first)
        lines = lines.reshape(RING * RING * micro_rows, width + PAD)
        if micro == 0:
            targets = lambda far: lax.axis_index("y") * 8 + far
        else:
            targets = lambda far: far // 2 * 8 + lax.axis_index("z") * 2 + far % 2
        chosen, high, low = slot_maps(lines[:, width:], targets, experts)
        picked = lax.dot_general(
            chosen, lines[:, :width], (((0,), (0,)), ((), ())), preferred_element_type=jnp.float32
        ).astype(jnp.bfloat16)
        entering.append(swap(picked.reshape(8, -1, width), (second, "core")))
        maps.append((high, low))
    sums = []
    for micro in range(MICRO):
        first, second = ("y", "z") if micro == 0 else ("z", "y")
        slots = entering[micro].reshape(-1, width)
        gate = jnp.dot(slots, w_gate[0], preferred_element_type=jnp.float32).astype(jnp.bfloat16)
        up = jnp.dot(slots, w_up[0], preferred_element_type=jnp.float32).astype(jnp.bfloat16)
        part = slots.shape[0] // RING
        own = [lax.rem(place + r, RING) * part for r in range(RING)]
        gate = [lax.dynamic_slice_in_dim(gate, start, part, axis=0) for start in own]
        up = [lax.dynamic_slice_in_dim(up, start, part, axis=0) for start in own]
        gate_far = move(gate[2], 1)
        up_far = move(up[2], -1)
        up_low = move(up[1], 1)
        gate_high = move(gate[3], -1)
        gate_low = move(add(gate[1], gate_far), 1)
        up_high = move(add(up[3], up_far), -1)
        gate_sum = gate[0].astype(jnp.float32) + gate_low.astype(jnp.float32) + gate_high.astype(jnp.float32)
        up_sum = up[0].astype(jnp.float32) + up_low.astype(jnp.float32) + up_high.astype(jnp.float32)
        activation = (jax.nn.silu(gate_sum) * up_sum).astype(jnp.bfloat16)
        half = part // 2
        low = move(activation, 1)
        high = move(activation, -1)
        far_low = move(low[:half], 1)
        far_high = move(high[half:], -1)
        whole = jnp.zeros((RING * part, ff), jnp.bfloat16)
        for value, start in (
            (activation, own[0]), (high, own[1]), (far_low, own[2]), (far_high, own[2] + half), (low, own[3])
        ):
            whole = lax.dynamic_update_slice_in_dim(whole, value, start, axis=0)
        expert_out = jnp.dot(whole, w_down[0], preferred_element_type=jnp.float32).astype(jnp.bfloat16)
        returned = swap(expert_out.reshape(8, -1, width), (second, "core")).reshape(-1, width)
        high, low = maps[micro]
        spread = jnp.dot(high, returned, preferred_element_type=jnp.float32)
        spread += jnp.dot(low, returned, preferred_element_type=jnp.float32)
        spread = swap(spread.astype(jnp.bfloat16).reshape(RING, -1, width), first)
        summed = jnp.sum(spread.astype(jnp.float32), axis=0).astype(jnp.bfloat16)
        sums.append(summed.reshape(RING, micro_rows, width))
    back = swap(jnp.concatenate(sums, axis=1), "x")
    moe_sum = jnp.concatenate([back[r] for r in range(RING)], axis=1).astype(jnp.float32)
    return (hidden_f + moe_sum).astype(jnp.bfloat16)


def solution(mesh):
    fine = Mesh(mesh.devices.reshape(RING, RING, 2, RING), ("y", "z", "core", "x"))
    attn = ("y", "z", "core")
    every = ("y", "z", "core", "x")
    in_specs = (
        P(every, None),
        P(),
        P(every, None),
        P(every, None),
        P(),
        P(attn, "x", None),
        P(attn, "x", None),
        P(attn, None, "x"),
    )
    return jax.shard_map(shards, mesh=fine, in_specs=in_specs, out_specs=P(every, None), check_vma=False)
```

time: 235 us -> 221 us (0.940)
  waiting for transfers between devices: 135 us -> 94.7 us
  starting transfers between devices: 29.4 us -> 62.1 us
  between operations: 13.6 us -> 0.53 us
  blocking collectives: 0 us -> 8.27 us
  local copies, waits for them, and re-layouts: 10.8 us -> 5.22 us
  other arithmetic: 4.59 us -> 9.05 us
    psum x1 -> x0, waiting for transfers between devices: 89.5 us -> none  [shards(): lax.psum(up_part.astype(jnp.bfloat16), 'exp').astype(jnp.float32)]
    ppermute x0 -> x20, waiting for transfers between devices: none -> 27.5 us  [move(): lax.ppermute(value, 'x', [(i, (i + step) % RING) for i in range(RING)])]
    ppermute x0 -> x20, starting transfers between devices: none -> 26.3 us  [move(): lax.ppermute(value, 'x', [(i, (i + step) % RING) for i in range(RING)])]
    all_to_all x4 -> x9, waiting for transfers between devices: 45.7 us -> 67.2 us  [swap(): return lax.all_to_all(value, axes, split_axis=0, concat_axis=0, tiled=True)]
    all_to_all x0 -> x1, blocking collectives: none -> 8.27 us  [swap(): return lax.all_to_all(value, axes, split_axis=0, concat_axis=0, tiled=True)]
    all_to_all x4 -> x9, starting transfers between devices: 29.2 us -> 35.8 us  [swap(): return lax.all_to_all(value, axes, split_axis=0, concat_axis=0, tiled=True)]
    convert_element_type x2 -> x0, local copies, waits for them, and re-layouts: 3.74 us -> none  [shards(): expert_out = jnp.einsum('seqf,efd->seqd', activation, w_down, preferred_e...]
    transpose x2 -> x0, local copies, waits for them, and re-layouts: 3.3 us -> none  [shards(): layered.transpose(0, 3, 1, 2, 4)]
  transfers between devices with their start and end apart: 5 -> 29, of which waited for: 5 -> 17; matrix products, arithmetic and copies ran while one was open for 10% -> 15% of each run, Pallas kernels for 0% -> 0%
where the time goes in v1:
time: 221 us; the launch traced here: 220 us
  waiting for transfers between devices  94.7 us (43%)
  starting transfers between devices  62.1 us (28%)
  matrix products  39.7 us (18%)
  other arithmetic  9.05 us (4%)
  blocking collectives  8.27 us (4%)
  local copies, waits for them, and re-layouts  5.22 us (2%)
    all_to_all x9, waiting for transfers between devices, swap(): return lax.all_to_all(value, axes, split_axis=0, concat_axis=0, tiled=True)  67.2 us
    all_to_all x9, starting transfers between devices, swap(): return lax.all_to_all(value, axes, split_axis=0, concat_axis=0, tiled=True)  35.8 us
    ppermute x20, waiting for transfers between devices, move(): lax.ppermute(value, 'x', [(i, (i + step) % RING) for i in range(RING)])  27.5 us
    ppermute x20, starting transfers between devices, move(): lax.ppermute(value, 'x', [(i, (i + step) % RING) for i in range(RING)])  26.3 us
    dot_general x2, matrix products, shards(): jnp.dot(whole, w_down[0], preferred_element_type=jnp.float32)  12.5 us
    dot_general x2, matrix products, shards(): jnp.dot(slots, w_up[0], preferred_element_type=jnp.float32)  10.6 us
    dot_general x2, matrix products, shards(): jnp.dot(slots, w_gate[0], preferred_element_type=jnp.float32)  10.6 us
    all_to_all x1, blocking collectives, swap(): return lax.all_to_all(value, axes, split_axis=0, concat_axis=0, tiled=True)  8.27 us
  transfers between devices with their start and end apart: 29, of which 17 were waited for; matrix products, arithmetic and copies ran while one was open for 15% of the time, Pallas kernels for 0%

profile of v1, /device:TPU:0, one launch (start us, length us, event | category | flops | bytes accessed | tf_op | source)
XLA Modules:
  0.0 219.6 jit_solution(16494702480176138275)
XLA Ops:
  3.9 1.1 fusion.42
  5.0 1.0 fusion.44
  7.1 4.4 %all-to-all-start = ((bf16[4,8,1920]{2,1,0:T(8,128)(2,1)}), bf16[4,8,1920]{2,1,0:T(8,128)(2,1)S(1)}, u32[]{:S(2)}, u32[]{:S(2)}) async-start(bf16[4,8,1920]{2,1,0:T(8,128)(2,1)} %pad_maximum_fusion), calls=%async_computation | async-start | bytes 245760 | tf_op jit(solution)/shard_map/all_to_all | solution.py:18
  11.5 5.9 %all-to-all-done = bf16[4,8,1920]{2,1,0:T(8,128)(2,1)S(1)} async-done(((bf16[4,8,1920]{2,1,0:T(8,128)(2,1)}), bf16[4,8,1920]{2,1,0:T(8,128)(2,1)S(1)}, u32[]{:S(2)}, u32[]{:S(2)}) %all-to-all-start) | async-done | bytes 122912 | tf_op jit(solution)/shard_map/all_to_all | solution.py:18
  18.2 4.5 %all-to-all-start.1 = ((bf16[4,16,1920]{2,1,0:T(8,128)(2,1)}), bf16[4,16,1920]{2,1,0:T(8,128)(2,1)S(1)}, u32[]{:S(2)}, u32[]{:S(2)}) async-start(bf16[4,16,1920]{2,1,0:T(8,128)(2,1)} %broadcast_in_dim.71), calls=%async_computation.1 | async-start | bytes 491520 | tf_op jit(solution)/shard_map/all_to_all | solution.py:18
  22.7 6.6 %all-to-all-done.1 = bf16[4,16,1920]{2,1,0:T(8,128)(2,1)S(1)} async-done(((bf16[4,16,1920]{2,1,0:T(8,128)(2,1)}), bf16[4,16,1920]{2,1,0:T(8,128)(2,1)S(1)}, u32[]{:S(2)}, u32[]{:S(2)}) %all-to-all-start.1) | async-done | bytes 245792 | tf_op jit(solution)/shard_map/all_to_all | solution.py:18
  29.9 5.3 %all-to-all-start.5 = ((bf16[4,16,1920]{2,1,0:T(8,128)(2,1)}), bf16[4,16,1920]{2,1,0:T(8,128)(2,1)S(1)}, u32[]{:S(2)}, u32[]{:S(2)}) async-start(bf16[4,16,1920]{2,1,0:T(8,128)(2,1)} %broadcast_in_dim.74), calls=%async_computation.5 | async-start | bytes 491520 | tf_op jit(solution)/shard_map/all_to_all | solution.py:18
  35.4 1.4 convolution_convert_fusion.1
  36.8 5.0 %all-to-all-done.5 = bf16[4,16,1920]{2,1,0:T(8,128)(2,1)S(1)} async-done(((bf16[4,16,1920]{2,1,0:T(8,128)(2,1)}), bf16[4,16,1920]{2,1,0:T(8,128)(2,1)S(1)}, u32[]{:S(2)}, u32[]{:S(2)}) %all-to-all-start.5) | async-done | bytes 245792 | tf_op jit(solution)/shard_map/all_to_all | solution.py:18
  41.8 3.6 %all-to-all-start.2 = ((bf16[8,32,1792]{2,1,0:T(8,128)(2,1)}), bf16[8,32,1792]{2,1,0:T(8,128)(2,1)S(1)}, u32[]{:S(2)}, u32[]{:S(2)}) async-start(bf16[8,32,1792]{2,1,0:T(8,128)(2,1)} %bitcast.7), calls=%async_computation.2 | async-start | bytes 1835008 | tf_op jit(solution)/shard_map/all_to_all | solution.py:18
  45.6 1.4 convolution_convert_fusion
  47.0 12.9 %all-to-all-done.2 = bf16[8,32,1792]{2,1,0:T(8,128)(2,1)S(1)} async-done(((bf16[8,32,1792]{2,1,0:T(8,128)(2,1)}), bf16[8,32,1792]{2,1,0:T(8,128)(2,1)S(1)}, u32[]{:S(2)}, u32[]{:S(2)}) %all-to-all-start.2) | async-done | bytes 917536 | tf_op jit(solution)/shard_map/all_to_all | solution.py:18
  59.9 4.2 %all-to-all-start.6 = ((bf16[8,32,1792]{2,1,0:T(8,128)(2,1)}), bf16[8,32,1792]{2,1,0:T(8,128)(2,1)}, u32[]{:S(2)}, u32[]{:S(2)}) async-start(bf16[8,32,1792]{2,1,0:T(8,128)(2,1)} %bitcast.16), calls=%async_computation.6 | async-start | bytes 1835008 | tf_op jit(solution)/shard_map/all_to_all | solution.py:18
  64.1 5.1 %fusion.12 = bf16[256,2048]{1,0:T(8,128)(2,1)S(1)} fusion(bf16[256,1792]{1,0:T(8,128)(2,1)S(1)} %bitcast.78, bf16[1,1792,2048]{2,1,0:T(8,128)(2,1)} %param.13), kind=kOutput, calls=%fused_computation.12 | convolution fusion | flops 1879572480 | bytes 9306112 | tf_op jit(solution)/shard_map/dot_general | solution.py:105
  69.3 5.1 %fusion.18 = bf16[256,2048]{1,0:T(8,128)(2,1)S(1)} fusion(bf16[256,1792]{1,0:T(8,128)(2,1)S(1)} %bitcast.79, bf16[1,1792,2048]{2,1,0:T(8,128)(2,1)} %param.14), kind=kOutput, calls=%fused_computation.14 | convolution fusion | flops 1879572480 | bytes 9306112 | tf_op jit(solution)/shard_map/dot_general | solution.py:106
  74.4 4.3 %all-to-all-done.6 = bf16[8,32,1792]{2,1,0:T(8,128)(2,1)} async-done(((bf16[8,32,1792]{2,1,0:T(8,128)(2,1)}), bf16[8,32,1792]{2,1,0:T(8,128)(2,1)}, u32[]{:S(2)}, u32[]{:S(2)}) %all-to-all-start.6) | async-done | bytes 917536 | tf_op jit(solution)/shard_map/all_to_all | solution.py:18
  78.7 5.4 %fusion.15 = bf16[256,2048]{1,0:T(8,128)(2,1)S(1)} fusion(bf16[256,1792]{1,0:T(8,128)(2,1)} %bitcast.17, bf16[1,1792,2048]{2,1,0:T(8,128)(2,1)} %param.13), kind=kOutput, calls=%fused_computation.13 | convolution fusion | flops 1879572480 | bytes 9306112 | tf_op jit(solution)/shard_map/dot_general | solution.py:105
  84.1 5.4 %fusion.21 = bf16[256,2048]{1,0:T(8,128)(2,1)S(1)} fusion(bf16[256,1792]{1,0:T(8,128)(2,1)} %bitcast.17, bf16[1,1792,2048]{2,1,0:T(8,128)(2,1)} %param.14), kind=kOutput, calls=%fused_computation.15 | convolution fusion | flops 1879572480 | bytes 9306112 | tf_op jit(solution)/shard_map/dot_general | solution.py:106
  90.3 2.7 %collective-permute-start.4 = (bf16[64,2048]{1,0:T(8,128)(2,1)S(1)}, bf16[64,2048]{1,0:T(8,128)(2,1)S(1)}, u32[]{:S(2)}, u32[]{:S(2)}) collective-permute-start(bf16[64,2048]{1,0:T(8,128)(2,1)S(1)} %get-tuple-element.16), channel_id=1, source_target_pairs={{0,3},{1,0},{2,1},{3,2},{4,7},{5,4},{6,5},{7,6},{8,11},{9,8},{10,9... | collective-permute-start | bytes 786440 | tf_op jit(solution)/shard_map/ppermute | solution.py:14
  93.1 1.9 collective-permute-start.3
  95.2 4.9 %collective-permute-done = bf16[64,2048]{1,0:T(8,128)(2,1)S(1)} collective-permute-done((bf16[64,2048]{1,0:T(8,128)(2,1)S(1)}, bf16[64,2048]{1,0:T(8,128)(2,1)S(1)}, u32[]{:S(2)}, u32[]{:S(2)}) %collective-permute-start) | collective-permute-done | bytes 262176 | tf_op jit(solution)/shard_map/ppermute | solution.py:14
  100.2 3.3 %collective-permute-start.12 = (bf16[64,2048]{1,0:T(8,128)(2,1)S(1)}, bf16[64,2048]{1,0:T(8,128)(2,1)S(1)}, u32[]{:S(2)}, u32[]{:S(2)}) collective-permute-start(bf16[64,2048]{1,0:T(8,128)(2,1)S(1)} %get-tuple-element.18), channel_id=1, source_target_pairs={{0,3},{1,0},{2,1},{3,2},{4,7},{5,4},{6,5},{7,6},{8,11},{9,8},{10,9... | collective-permute-start | bytes 786440 | tf_op jit(solution)/shard_map/ppermute | solution.py:14
  103.6 6.4 %collective-permute-done.10 = bf16[64,2048]{1,0:T(8,128)(2,1)S(1)} collective-permute-done((bf16[64,2048]{1,0:T(8,128)(2,1)S(1)}, bf16[64,2048]{1,0:T(8,128)(2,1)S(1)}, u32[]{:S(2)}, u32[]{:S(2)}) %collective-permute-start.10) | collective-permute-done | bytes 262176 | tf_op jit(solution)/shard_map/ppermute | solution.py:14
  110.1 1.0 collective-permute-done.14
  111.0 3.7 %collective-permute-start.5 = (bf16[64,2048]{1,0:T(8,128)(2,1)S(1)}, bf16[64,2048]{1,0:T(8,128)(2,1)S(1)}, u32[]{:S(2)}, u32[]{:S(2)}) collective-permute-start(bf16[64,2048]{1,0:T(8,128)(2,1)S(1)} %add_convert_fusion.2), channel_id=1, source_target_pairs={{0,3},{1,0},{2,1},{3,2},{4,7},{5,4},{6,5},{7,6},{8,11},{9,8},{10,9... | collective-permute-start | bytes 786440 | tf_op jit(solution)/shard_map/ppermute | solution.py:14
  115.0 5.5 %collective-permute-done.1 = bf16[64,2048]{1,0:T(8,128)(2,1)S(1)} collective-permute-done((bf16[64,2048]{1,0:T(8,128)(2,1)S(1)}, bf16[64,2048]{1,0:T(8,128)(2,1)S(1)}, u32[]{:S(2)}, u32[]{:S(2)}) %collective-permute-start.1) | collective-permute-done | bytes 262176 | tf_op jit(solution)/shard_map/ppermute | solution.py:14
  120.4 1.8 collective-permute-done.5
  122.4 1.0 constant_dynamic-update-slice_fusion.9
  123.4 3.7 %collective-permute-start.6 = (bf16[64,2048]{1,0:T(8,128)(2,1)}, bf16[64,2048]{1,0:T(8,128)(2,1)S(1)}, u32[]{:S(2)}, u32[]{:S(2)}) collective-permute-start(bf16[64,2048]{1,0:T(8,128)(2,1)} %get-tuple-element.6), channel_id=1, source_target_pairs={{0,3},{1,0},{2,1},{3,2},{4,7},{5,4},{6,5},{7,6},{8,11},{9,8},{10,9... | collective-permute-start | bytes 786440 | tf_op jit(solution)/shard_map/ppermute | solution.py:14
  127.1 4.0 %collective-permute-done.11 = bf16[64,2048]{1,0:T(8,128)(2,1)S(1)} collective-permute-done((bf16[64,2048]{1,0:T(8,128)(2,1)S(1)}, bf16[64,2048]{1,0:T(8,128)(2,1)S(1)}, u32[]{:S(2)}, u32[]{:S(2)}) %collective-permute-start.11) | collective-permute-done | bytes 262176 | tf_op jit(solution)/shard_map/ppermute | solution.py:14
  131.6 3.2 %collective-permute-start.16 = (bf16[64,2048]{1,0:T(8,128)(2,1)S(1)}, bf16[64,2048]{1,0:T(8,128)(2,1)S(1)}, u32[]{:S(2)}, u32[]{:S(2)}) collective-permute-start(bf16[64,2048]{1,0:T(8,128)(2,1)S(1)} %get-tuple-element.8), channel_id=1, source_target_pairs={{0,3},{1,0},{2,1},{3,2},{4,7},{5,4},{6,5},{7,6},{8,11},{9,8},{10,9... | collective-permute-start | bytes 786440 | tf_op jit(solution)/shard_map/ppermute | solution.py:14
  134.8 2.9 %collective-permute-done.7 = bf16[64,2048]{1,0:T(8,128)(2,1)S(1)} collective-permute-done((bf16[64,2048]{1,0:T(8,128)(2,1)}, bf16[64,2048]{1,0:T(8,128)(2,1)S(1)}, u32[]{:S(2)}, u32[]{:S(2)}) %collective-permute-start.7) | collective-permute-done | bytes 262176 | tf_op jit(solution)/shard_map/ppermute | solution.py:14
  137.9 3.3 %collective-permute-start.9 = (bf16[32,2048]{1,0:T(8,128)(2,1)S(1)}, bf16[32,2048]{1,0:T(8,128)(2,1)S(1)}, u32[]{:S(2)}, u32[]{:S(2)}) collective-permute-start(bf16[32,2048]{1,0:T(8,128)(2,1)S(1)} %slice.95), channel_id=1, source_target_pairs={{0,3},{1,0},{2,1},{3,2},{4,7},{5,4},{6,5},{7,6},{8,11},{9,8},{10,9... | collective-permute-start | bytes 393224 | tf_op jit(solution)/shard_map/ppermute | solution.py:14
  141.2 1.0 collective-permute-done.17
  142.2 3.3 %collective-permute-start.19 = (bf16[32,2048]{1,0:T(8,128)(2,1)S(1)}, bf16[32,2048]{1,0:T(8,128)(2,1)S(1)}, u32[]{:S(2)}, u32[]{:S(2)}) collective-permute-start(bf16[32,2048]{1,0:T(8,128)(2,1)S(1)} %slice.100), channel_id=1, source_target_pairs={{0,3},{1,0},{2,1},{3,2},{4,7},{5,4},{6,5},{7,6},{8,11},{9,8},{10,9... | collective-permute-start | bytes 393224 | tf_op jit(solution)/shard_map/ppermute | solution.py:14
  148.3 6.4 %fusion.24 = bf16[256,1792]{1,0:T(8,128)(2,1)} fusion(bf16[256,2048]{1,0:T(8,128)(2,1)} %constant_dynamic-update-slice_fusion.5, bf16[1,2048,1792]{2,1,0:T(8,128)(2,1)} %param.15), kind=kOutput, calls=%fused_computation.16 | convolution fusion | flops 1879506944 | bytes 9306112 | tf_op jit(solution)/shard_map/dot_general | solution.py:130
  154.7 3.6 %all-to-all-start.3 = ((bf16[8,32,1792]{2,1,0:T(8,128)(2,1)}), bf16[8,32,1792]{2,1,0:T(8,128)(2,1)S(1)}, u32[]{:S(2)}, u32[]{:S(2)}) async-start(bf16[8,32,1792]{2,1,0:T(8,128)(2,1)} %bitcast.12), calls=%async_computation.3 | async-start | bytes 1835008 | tf_op jit(solution)/shard_map/all_to_all | solution.py:18
  158.4 6.1 %fusion.27 = bf16[256,1792]{1,0:T(8,128)(2,1)} fusion(bf16[256,2048]{1,0:T(8,128)(2,1)S(1)} %constant_dynamic-update-slice_fusion, bf16[1,2048,1792]{2,1,0:T(8,128)(2,1)} %param.15), kind=kOutput, calls=%fused_computation.17 | convolution fusion | flops 1879506944 | bytes 9306112 | tf_op jit(solution)/shard_map/dot_general | solution.py:130
  164.5 8.3 %all-to-all-done.3 = bf16[8,32,1792]{2,1,0:T(8,128)(2,1)S(1)} async-done(((bf16[8,32,1792]{2,1,0:T(8,128)(2,1)}), bf16[8,32,1792]{2,1,0:T(8,128)(2,1)S(1)}, u32[]{:S(2)}, u32[]{:S(2)}) %all-to-all-start.3) | async-done | bytes 917536 | tf_op jit(solution)/shard_map/all_to_all | solution.py:18
  172.8 3.6 %all-to-all-start.7 = ((bf16[8,32,1792]{2,1,0:T(8,128)(2,1)}), bf16[8,32,1792]{2,1,0:T(8,128)(2,1)S(1)}, u32[]{:S(2)}, u32[]{:S(2)}) async-start(bf16[8,32,1792]{2,1,0:T(8,128)(2,1)} %bitcast.18), calls=%async_computation.7 | async-start | bytes 1835008 | tf_op jit(solution)/shard_map/all_to_all | solution.py:18
  176.8 1.1 fusion.30
  177.9 12.9 %all-to-all-done.7 = bf16[8,32,1792]{2,1,0:T(8,128)(2,1)S(1)} async-done(((bf16[8,32,1792]{2,1,0:T(8,128)(2,1)}), bf16[8,32,1792]{2,1,0:T(8,128)(2,1)S(1)}, u32[]{:S(2)}, u32[]{:S(2)}) %all-to-all-start.7) | async-done | bytes 917536 | tf_op jit(solution)/shard_map/all_to_all | solution.py:18
  190.8 3.4 %all-to-all-start.4 = ((bf16[4,16,1792]{2,1,0:T(8,128)(2,1)}), bf16[4,16,1792]{2,1,0:T(8,128)(2,1)S(1)}, u32[]{:S(2)}, u32[]{:S(2)}) async-start(bf16[4,16,1792]{2,1,0:T(8,128)(2,1)} %bitcast.14), calls=%async_computation.4 | async-start | bytes 458752 | tf_op jit(solution)/shard_map/all_to_all | solution.py:18
  194.6 1.1 fusion.31
  195.7 5.0 %all-to-all-done.4 = bf16[4,16,1792]{2,1,0:T(8,128)(2,1)S(1)} async-done(((bf16[4,16,1792]{2,1,0:T(8,128)(2,1)}), bf16[4,16,1792]{2,1,0:T(8,128)(2,1)S(1)}, u32[]{:S(2)}, u32[]{:S(2)}) %all-to-all-start.4) | async-done | bytes 229408 | tf_op jit(solution)/shard_map/all_to_all | solution.py:18
  200.7 3.4 %all-to-all-start.8 = ((bf16[4,16,1792]{2,1,0:T(8,128)(2,1)}), bf16[4,16,1792]{2,1,0:T(8,128)(2,1)S(1)}, u32[]{:S(2)}, u32[]{:S(2)}) async-start(bf16[4,16,1792]{2,1,0:T(8,128)(2,1)} %bitcast.20), calls=%async_computation.8 | async-start | bytes 458752 | tf_op jit(solution)/shard_map/all_to_all | solution.py:18
  204.1 6.4 %all-to-all-done.8 = bf16[4,16,1792]{2,1,0:T(8,128)(2,1)S(1)} async-done(((bf16[4,16,1792]{2,1,0:T(8,128)(2,1)}), bf16[4,16,1792]{2,1,0:T(8,128)(2,1)S(1)}, u32[]{:S(2)}, u32[]{:S(2)}) %all-to-all-start.8) | async-done | bytes 229408 | tf_op jit(solution)/shard_map/all_to_all | solution.py:18
  210.7 8.3 %all_to_all.50 = bf16[4,8,1792]{2,1,0:T(8,128)(2,1)S(1)} all-to-all(bf16[4,8,1792]{2,1,0:T(8,128)(2,1)S(1)} %pad_maximum_fusion.1), channel_id=1, replica_groups=mesh['y'=4,'z'=4,'core'=2,'x'=4] {'x'}, dimensions={0} | all-to-all | bytes 229376 | tf_op jit(solution)/shard_map/all_to_all | solution.py:18
  (92 shorter events, 13.5 us)
Async XLA Ops:
  7.1 10.3 %all-to-all-start = ((bf16[4,8,1920]{2,1,0:T(8,128)(2,1)}), bf16[4,8,1920]{2,1,0:T(8,128)(2,1)S(1)}, u32[]{:S(2)}, u32[]{:S(2)}) async-start(bf16[4,8,1920]{2,1,0:T(8,128)(2,1)} %pad_maximum_fusion), calls=%async_computation | async-start | bytes 245760 | tf_op jit(solution)/shard_map/all_to_all | solution.py:18
  18.2 11.1 %all-to-all-start.1 = ((bf16[4,16,1920]{2,1,0:T(8,128)(2,1)}), bf16[4,16,1920]{2,1,0:T(8,128)(2,1)S(1)}, u32[]{:S(2)}, u32[]{:S(2)}) async-start(bf16[4,16,1920]{2,1,0:T(8,128)(2,1)} %broadcast_in_dim.71), calls=%async_computation.1 | async-start | bytes 491520 | tf_op jit(solution)/shard_map/all_to_all | solution.py:18
  29.9 11.9 %all-to-all-start.5 = ((bf16[4,16,1920]{2,1,0:T(8,128)(2,1)}), bf16[4,16,1920]{2,1,0:T(8,128)(2,1)S(1)}, u32[]{:S(2)}, u32[]{:S(2)}) async-start(bf16[4,16,1920]{2,1,0:T(8,128)(2,1)} %broadcast_in_dim.74), calls=%async_computation.5 | async-start | bytes 491520 | tf_op jit(solution)/shard_map/all_to_all | solution.py:18
  41.8 18.0 %all-to-all-start.2 = ((bf16[8,32,1792]{2,1,0:T(8,128)(2,1)}), bf16[8,32,1792]{2,1,0:T(8,128)(2,1)S(1)}, u32[]{:S(2)}, u32[]{:S(2)}) async-start(bf16[8,32,1792]{2,1,0:T(8,128)(2,1)} %bitcast.7), calls=%async_computation.2 | async-start | bytes 1835008 | tf_op jit(solution)/shard_map/all_to_all | solution.py:18
  59.9 18.8 %all-to-all-start.6 = ((bf16[8,32,1792]{2,1,0:T(8,128)(2,1)}), bf16[8,32,1792]{2,1,0:T(8,128)(2,1)}, u32[]{:S(2)}, u32[]{:S(2)}) async-start(bf16[8,32,1792]{2,1,0:T(8,128)(2,1)} %bitcast.16), calls=%async_computation.6 | async-start | bytes 1835008 | tf_op jit(solution)/shard_map/all_to_all | solution.py:18
  89.6 10.5 %collective-permute-start = (bf16[64,2048]{1,0:T(8,128)(2,1)S(1)}, bf16[64,2048]{1,0:T(8,128)(2,1)S(1)}, u32[]{:S(2)}, u32[]{:S(2)}) collective-permute-start(bf16[64,2048]{1,0:T(8,128)(2,1)S(1)} %get-tuple-element.13), channel_id=1, source_target_pairs={{0,1},{1,2},{2,3},{3,0},{4,5},{5,6},{6,7},{7,4},{8,9},{9,10},{10,1... | collective-permute-start | bytes 786440 | tf_op jit(solution)/shard_map/ppermute | solution.py:14
  90.3 9.9 %collective-permute-start.4 = (bf16[64,2048]{1,0:T(8,128)(2,1)S(1)}, bf16[64,2048]{1,0:T(8,128)(2,1)S(1)}, u32[]{:S(2)}, u32[]{:S(2)}) collective-permute-start(bf16[64,2048]{1,0:T(8,128)(2,1)S(1)} %get-tuple-element.16), channel_id=1, source_target_pairs={{0,3},{1,0},{2,1},{3,2},{4,7},{5,4},{6,5},{7,6},{8,11},{9,8},{10,9... | collective-permute-start | bytes 786440 | tf_op jit(solution)/shard_map/ppermute | solution.py:14
  93.0 21.8 %collective-permute-start.2 = (bf16[64,2048]{1,0:T(8,128)(2,1)S(1)}, bf16[64,2048]{1,0:T(8,128)(2,1)S(1)}, u32[]{:S(2)}, u32[]{:S(2)}) collective-permute-start(bf16[64,2048]{1,0:T(8,128)(2,1)S(1)} %get-tuple-element.14), channel_id=1, source_target_pairs={{0,3},{1,0},{2,1},{3,2},{4,7},{5,4},{6,5},{7,6},{8,11},{9,8},{10,9... | collective-permute-start | bytes 786440 | tf_op jit(solution)/shard_map/ppermute | solution.py:14
  93.1 21.8 %collective-permute-start.3 = (bf16[64,2048]{1,0:T(8,128)(2,1)S(1)}, bf16[64,2048]{1,0:T(8,128)(2,1)S(1)}, u32[]{:S(2)}, u32[]{:S(2)}) collective-permute-start(bf16[64,2048]{1,0:T(8,128)(2,1)S(1)} %get-tuple-element.15), channel_id=1, source_target_pairs={{0,1},{1,2},{2,3},{3,0},{4,5},{5,6},{6,7},{7,4},{8,9},{9,10},{10,1... | collective-permute-start | bytes 786440 | tf_op jit(solution)/shard_map/ppermute | solution.py:14
  95.1 14.9 %collective-permute-start.10 = (bf16[64,2048]{1,0:T(8,128)(2,1)S(1)}, bf16[64,2048]{1,0:T(8,128)(2,1)S(1)}, u32[]{:S(2)}, u32[]{:S(2)}) collective-permute-start(bf16[64,2048]{1,0:T(8,128)(2,1)S(1)} %get-tuple-element.17), channel_id=1, source_target_pairs={{0,1},{1,2},{2,3},{3,0},{4,5},{5,6},{6,7},{7,4},{8,9},{9,10},{10,1... | collective-permute-start | bytes 786440 | tf_op jit(solution)/shard_map/ppermute | solution.py:14
  100.1 10.9 %collective-permute-start.14 = (bf16[64,2048]{1,0:T(8,128)(2,1)S(1)}, bf16[64,2048]{1,0:T(8,128)(2,1)S(1)}, u32[]{:S(2)}, u32[]{:S(2)}) collective-permute-start(bf16[64,2048]{1,0:T(8,128)(2,1)S(1)} %get-tuple-element.20), channel_id=1, source_target_pairs={{0,3},{1,0},{2,1},{3,2},{4,7},{5,4},{6,5},{7,6},{8,11},{9,8},{10,9... | collective-permute-start | bytes 786440 | tf_op jit(solution)/shard_map/ppermute | solution.py:14
  100.2 26.9 %collective-permute-start.12 = (bf16[64,2048]{1,0:T(8,128)(2,1)S(1)}, bf16[64,2048]{1,0:T(8,128)(2,1)S(1)}, u32[]{:S(2)}, u32[]{:S(2)}) collective-permute-start(bf16[64,2048]{1,0:T(8,128)(2,1)S(1)} %get-tuple-element.18), channel_id=1, source_target_pairs={{0,3},{1,0},{2,1},{3,2},{4,7},{5,4},{6,5},{7,6},{8,11},{9,8},{10,9... | collective-permute-start | bytes 786440 | tf_op jit(solution)/shard_map/ppermute | solution.py:14
  110.0 10.5 %collective-permute-start.1 = (bf16[64,2048]{1,0:T(8,128)(2,1)S(1)}, bf16[64,2048]{1,0:T(8,128)(2,1)S(1)}, u32[]{:S(2)}, u32[]{:S(2)}) collective-permute-start(bf16[64,2048]{1,0:T(8,128)(2,1)S(1)} %add_convert_fusion.3), channel_id=1, source_target_pairs={{0,1},{1,2},{2,3},{3,0},{4,5},{5,6},{6,7},{7,4},{8,9},{9,10},{10,1... | collective-permute-start | bytes 786440 | tf_op jit(solution)/shard_map/ppermute | solution.py:14
  111.0 11.2 %collective-permute-start.5 = (bf16[64,2048]{1,0:T(8,128)(2,1)S(1)}, bf16[64,2048]{1,0:T(8,128)(2,1)S(1)}, u32[]{:S(2)}, u32[]{:S(2)}) collective-permute-start(bf16[64,2048]{1,0:T(8,128)(2,1)S(1)} %add_convert_fusion.2), channel_id=1, source_target_pairs={{0,3},{1,0},{2,1},{3,2},{4,7},{5,4},{6,5},{7,6},{8,11},{9,8},{10,9... | collective-permute-start | bytes 786440 | tf_op jit(solution)/shard_map/ppermute | solution.py:14
  114.8 12.3 %collective-permute-start.13 = (bf16[64,2048]{1,0:T(8,128)(2,1)S(1)}, bf16[64,2048]{1,0:T(8,128)(2,1)S(1)}, u32[]{:S(2)}, u32[]{:S(2)}) collective-permute-start(bf16[64,2048]{1,0:T(8,128)(2,1)S(1)} %get-tuple-element.19), channel_id=1, source_target_pairs={{0,1},{1,2},{2,3},{3,0},{4,5},{5,6},{6,7},{7,4},{8,9},{9,10},{10,1... | collective-permute-start | bytes 786440 | tf_op jit(solution)/shard_map/ppermute | solution.py:14
  114.9 16.2 %collective-permute-start.11 = (bf16[64,2048]{1,0:T(8,128)(2,1)S(1)}, bf16[64,2048]{1,0:T(8,128)(2,1)S(1)}, u32[]{:S(2)}, u32[]{:S(2)}) collective-permute-start(bf16[64,2048]{1,0:T(8,128)(2,1)S(1)} %add_convert_fusion.1), channel_id=1, source_target_pairs={{0,1},{1,2},{2,3},{3,0},{4,5},{5,6},{6,7},{7,4},{8,9},{9,10},{10,1... | collective-permute-start | bytes 786440 | tf_op jit(solution)/shard_map/ppermute | solution.py:14
  120.4 10.7 %collective-permute-start.15 = (bf16[64,2048]{1,0:T(8,128)(2,1)S(1)}, bf16[64,2048]{1,0:T(8,128)(2,1)S(1)}, u32[]{:S(2)}, u32[]{:S(2)}) collective-permute-start(bf16[64,2048]{1,0:T(8,128)(2,1)S(1)} %add_convert_fusion), channel_id=1, source_target_pairs={{0,3},{1,0},{2,1},{3,2},{4,7},{5,4},{6,5},{7,6},{8,11},{9,8},{10,9... | collective-permute-start | bytes 786440 | tf_op jit(solution)/shard_map/ppermute | solution.py:14
  123.4 8.2 %copy-start = (bf16[256,2048]{1,0:T(8,128)(2,1)}, bf16[256,2048]{1,0:T(8,128)(2,1)S(1)}, u32[]{:S(2)}) copy-start(bf16[256,2048]{1,0:T(8,128)(2,1)S(1)} %get-tuple-element.5) | copy-start | bytes 3145732
  123.4 14.5 %collective-permute-start.6 = (bf16[64,2048]{1,0:T(8,128)(2,1)}, bf16[64,2048]{1,0:T(8,128)(2,1)S(1)}, u32[]{:S(2)}, u32[]{:S(2)}) collective-permute-start(bf16[64,2048]{1,0:T(8,128)(2,1)} %get-tuple-element.6), channel_id=1, source_target_pairs={{0,3},{1,0},{2,1},{3,2},{4,7},{5,4},{6,5},{7,6},{8,11},{9,8},{10,9... | collective-permute-start | bytes 786440 | tf_op jit(solution)/shard_map/ppermute | solution.py:14
  127.1 10.7 %collective-permute-start.7 = (bf16[64,2048]{1,0:T(8,128)(2,1)}, bf16[64,2048]{1,0:T(8,128)(2,1)S(1)}, u32[]{:S(2)}, u32[]{:S(2)}) collective-permute-start(bf16[64,2048]{1,0:T(8,128)(2,1)} %get-tuple-element.6), channel_id=1, source_target_pairs={{0,1},{1,2},{2,3},{3,0},{4,5},{5,6},{6,7},{7,4},{8,9},{9,10},{10,1... | collective-permute-start | bytes 786440 | tf_op jit(solution)/shard_map/ppermute | solution.py:14
  131.5 10.6 %collective-permute-start.17 = (bf16[64,2048]{1,0:T(8,128)(2,1)S(1)}, bf16[64,2048]{1,0:T(8,128)(2,1)S(1)}, u32[]{:S(2)}, u32[]{:S(2)}) collective-permute-start(bf16[64,2048]{1,0:T(8,128)(2,1)S(1)} %get-tuple-element.8), channel_id=1, source_target_pairs={{0,1},{1,2},{2,3},{3,0},{4,5},{5,6},{6,7},{7,4},{8,9},{9,10},{10,1... | collective-permute-start | bytes 786440 | tf_op jit(solution)/shard_map/ppermute | solution.py:14
  131.6 10.6 %collective-permute-start.16 = (bf16[64,2048]{1,0:T(8,128)(2,1)S(1)}, bf16[64,2048]{1,0:T(8,128)(2,1)S(1)}, u32[]{:S(2)}, u32[]{:S(2)}) collective-permute-start(bf16[64,2048]{1,0:T(8,128)(2,1)S(1)} %get-tuple-element.8), channel_id=1, source_target_pairs={{0,3},{1,0},{2,1},{3,2},{4,7},{5,4},{6,5},{7,6},{8,11},{9,8},{10,9... | collective-permute-start | bytes 786440 | tf_op jit(solution)/shard_map/ppermute | solution.py:14
  137.8 8.5 %collective-permute-start.8 = (bf16[32,2048]{1,0:T(8,128)(2,1)S(1)}, bf16[32,2048]{1,0:T(8,128)(2,1)S(1)}, u32[]{:S(2)}, u32[]{:S(2)}) collective-permute-start(bf16[32,2048]{1,0:T(8,128)(2,1)S(1)} %slice.94), channel_id=1, source_target_pairs={{0,1},{1,2},{2,3},{3,0},{4,5},{5,6},{6,7},{7,4},{8,9},{9,10},{10,1... | collective-permute-start | bytes 393224 | tf_op jit(solution)/shard_map/ppermute | solution.py:14
  137.9 9.1 %collective-permute-start.9 = (bf16[32,2048]{1,0:T(8,128)(2,1)S(1)}, bf16[32,2048]{1,0:T(8,128)(2,1)S(1)}, u32[]{:S(2)}, u32[]{:S(2)}) collective-permute-start(bf16[32,2048]{1,0:T(8,128)(2,1)S(1)} %slice.95), channel_id=1, source_target_pairs={{0,3},{1,0},{2,1},{3,2},{4,7},{5,4},{6,5},{7,6},{8,11},{9,8},{10,9... | collective-permute-start | bytes 393224 | tf_op jit(solution)/shard_map/ppermute | solution.py:14
  142.1 16.2 %collective-permute-start.18 = (bf16[32,2048]{1,0:T(8,128)(2,1)S(1)}, bf16[32,2048]{1,0:T(8,128)(2,1)S(1)}, u32[]{:S(2)}, u32[]{:S(2)}) collective-permute-start(bf16[32,2048]{1,0:T(8,128)(2,1)S(1)} %slice.99), channel_id=1, source_target_pairs={{0,1},{1,2},{2,3},{3,0},{4,5},{5,6},{6,7},{7,4},{8,9},{9,10},{10,1... | collective-permute-start | bytes 393224 | tf_op jit(solution)/shard_map/ppermute | solution.py:14
  142.2 16.1 %collective-permute-start.19 = (bf16[32,2048]{1,0:T(8,128)(2,1)S(1)}, bf16[32,2048]{1,0:T(8,128)(2,1)S(1)}, u32[]{:S(2)}, u32[]{:S(2)}) collective-permute-start(bf16[32,2048]{1,0:T(8,128)(2,1)S(1)} %slice.100), channel_id=1, source_target_pairs={{0,3},{1,0},{2,1},{3,2},{4,7},{5,4},{6,5},{7,6},{8,11},{9,8},{10,9... | collective-permute-start | bytes 393224 | tf_op jit(solution)/shard_map/ppermute | solution.py:14
  154.7 18.0 %all-to-all-start.3 = ((bf16[8,32,1792]{2,1,0:T(8,128)(2,1)}), bf16[8,32,1792]{2,1,0:T(8,128)(2,1)S(1)}, u32[]{:S(2)}, u32[]{:S(2)}) async-start(bf16[8,32,1792]{2,1,0:T(8,128)(2,1)} %bitcast.12), calls=%async_computation.3 | async-start | bytes 1835008 | tf_op jit(solution)/shard_map/all_to_all | solution.py:18
  164.5 54.5 %copy-start.1 = (bf16[8,7168]{1,0:T(8,128)(2,1)S(1)}, bf16[8,7168]{1,0:T(8,128)(2,1)}, u32[]{:S(2)}) copy-start(bf16[8,7168]{1,0:T(8,128)(2,1)} %param.8) | copy-start | bytes 344068
  172.8 18.0 %all-to-all-start.7 = ((bf16[8,32,1792]{2,1,0:T(8,128)(2,1)}), bf16[8,32,1792]{2,1,0:T(8,128)(2,1)S(1)}, u32[]{:S(2)}, u32[]{:S(2)}) async-start(bf16[8,32,1792]{2,1,0:T(8,128)(2,1)} %bitcast.18), calls=%async_computation.7 | async-start | bytes 1835008 | tf_op jit(solution)/shard_map/all_to_all | solution.py:18
  190.8 9.9 %all-to-all-start.4 = ((bf16[4,16,1792]{2,1,0:T(8,128)(2,1)}), bf16[4,16,1792]{2,1,0:T(8,128)(2,1)S(1)}, u32[]{:S(2)}, u32[]{:S(2)}) async-start(bf16[4,16,1792]{2,1,0:T(8,128)(2,1)} %bitcast.14), calls=%async_computation.4 | async-start | bytes 458752 | tf_op jit(solution)/shard_map/all_to_all | solution.py:18
  200.7 9.9 %all-to-all-start.8 = ((bf16[4,16,1792]{2,1,0:T(8,128)(2,1)}), bf16[4,16,1792]{2,1,0:T(8,128)(2,1)S(1)}, u32[]{:S(2)}, u32[]{:S(2)}) async-start(bf16[4,16,1792]{2,1,0:T(8,128)(2,1)} %bitcast.20), calls=%async_computation.8 | async-start | bytes 458752 | tf_op jit(solution)/shard_map/all_to_all | solution.py:18

commit v2 on v0

v2 whole, which is shorter than its diff:
```python
import functools

import jax
import jax.numpy as jnp
from jax import lax
from jax.experimental import pallas as pl
from jax.experimental.pallas import tpu as pltpu
from jax.sharding import PartitionSpec as P

ROUTE_SCALE = 2.5
EPSILON = 1e-06
PAD = 128
RING = 4


def move(value, step):
    return lax.ppermute(value, "exp", [(i, (i + step) % RING) for i in range(RING)])


def direct(chunks):
    return [chunks[0], move(chunks[3], -1), move(chunks[2], 2), move(chunks[1], 1)]


def swap(value):
    return lax.all_to_all(value, "attn", split_axis=0, concat_axis=0, tiled=True)


def add(one, other):
    return (one.astype(jnp.float32) + other.astype(jnp.float32)).astype(jnp.bfloat16)


def prepare_kernel(place_ref, hidden_ref, gain_ref, routes_ref, scores_ref, capacity_ref, *out_refs):
    rows, top = routes_ref.shape
    experts = capacity_ref.shape[1]
    width = out_refs[0].shape[1] - PAD
    hidden = hidden_ref[...].astype(jnp.float32)
    scale = lax.rsqrt(jnp.mean(hidden * hidden, axis=1, keepdims=True) + EPSILON)
    routes = routes_ref[...]
    scores = scores_ref[...]
    weights = ROUTE_SCALE * scores / jnp.sum(scores, axis=1, keepdims=True)
    lane = lax.broadcasted_iota(jnp.int32, (rows, PAD), 1)
    named = lax.rem(lane, experts)
    match = jnp.zeros((rows, PAD), jnp.float32)
    weight = jnp.zeros((rows, PAD), jnp.float32)
    for k in range(top):
        same = routes[:, k : k + 1] == named
        match = jnp.where(same, 1.0, match)
        weight = jnp.where(same, weights[:, k : k + 1], weight)
    row = lax.broadcasted_iota(jnp.int32, (rows, PAD), 0)
    rank = jnp.zeros((rows, PAD), jnp.float32)
    for j in range(rows):
        later = (row > j) & (row < (j // 4 + 1) * 4)
        rank = rank + jnp.where(later, match[j : j + 1, :], 0.0)
    spread = (
        lax.broadcasted_iota(jnp.int32, (experts, PAD), 0)
        == lax.rem(lax.broadcasted_iota(jnp.int32, (experts, PAD), 1), experts)
    ).astype(jnp.float32)
    limit = jnp.broadcast_to(capacity_ref[...].astype(jnp.float32), (8, experts))
    limit = jnp.dot(limit, spread, preferred_element_type=jnp.float32)[0:1]
    kept = (match > 0.0) & (rank < limit)
    high = weight.astype(jnp.bfloat16).astype(jnp.float32)
    group = lane // experts
    value = jnp.where(group == 0, rank + 1.0, jnp.where(group == 1, high, weight - high))
    columns = jnp.where(kept & (group < 3), value, 0.0).astype(jnp.bfloat16)
    for r in range(RING):
        start = pl.multiple_of(lax.rem(place_ref[0] + r, RING) * width, PAD)
        part = hidden_ref[:, pl.ds(start, width)].astype(jnp.float32) * scale * gain_ref[:, pl.ds(start, width)]
        out_refs[r][:, :width] = part.astype(jnp.bfloat16)
        out_refs[r][:, width:] = columns


def finish_kernel(place_ref, hidden_ref, *refs):
    out_ref = refs[-1]
    width = refs[0].shape[1]
    for r in range(RING):
        start = pl.multiple_of(lax.rem(place_ref[0] + r, RING) * width, PAD)
        total = hidden_ref[:, pl.ds(start, width)].astype(jnp.float32) + refs[r][...].astype(jnp.float32)
        out_ref[:, pl.ds(start, width)] = total.astype(jnp.bfloat16)


def specs(count):
    return [pl.BlockSpec(memory_space=pltpu.SMEM)] + [pl.BlockSpec(memory_space=pltpu.VMEM)] * count


def pick_kernel(place_ref, *refs):
    lines = jnp.concatenate([ref[...].astype(jnp.float32) for ref in refs[:RING]], axis=0).astype(jnp.bfloat16)
    rows, width = lines.shape[0], lines.shape[1] - PAD
    for micro in range(2):
        out_ref = refs[RING + micro]
        slots = out_ref.shape[0]
        slot = lax.broadcasted_iota(jnp.int32, (slots, PAD), 0)
        lane = lax.broadcasted_iota(jnp.int32, (slots, PAD), 1)
        code = lax.dot_general(
            (lane == slot // 8).astype(jnp.bfloat16),
            lines[:, width:],
            (((1,), (1,)), ((), ())),
            preferred_element_type=jnp.float32,
        )
        slot = lax.broadcasted_iota(jnp.int32, (slots, rows), 0)
        row = lax.broadcasted_iota(jnp.int32, (slots, rows), 1)
        here = (lax.rem(slot, 8) // 2 == lax.rem(row // 8 + place_ref[0], RING)) & (lax.rem(row, 8) // 4 == micro)
        chosen = here & (code.astype(jnp.int32) == lax.rem(slot, 2) + 1)
        chosen = chosen.astype(jnp.float32).astype(jnp.bfloat16)
        out_ref[...] = jnp.dot(chosen, lines[:, :width], preferred_element_type=jnp.float32).astype(jnp.bfloat16)


def combine_kernel(experts, place_ref, *refs):
    lines = jnp.concatenate([ref[...].astype(jnp.float32) for ref in refs[:RING]], axis=0).astype(jnp.bfloat16)
    rows = lines.shape[0]
    total = jnp.zeros((rows, refs[-1].shape[1]), jnp.float32)
    for micro in range(2):
        returned = refs[RING + micro][...]
        slots = returned.shape[0]
        slot = lax.broadcasted_iota(jnp.int32, (slots, PAD), 0)
        lane = lax.broadcasted_iota(jnp.int32, (slots, PAD), 1)
        parts = [
            lax.dot_general(
                lines,
                (lane == slot // 8 + k * experts).astype(jnp.bfloat16),
                (((1,), (1,)), ((), ())),
                preferred_element_type=jnp.float32,
            )
            for k in range(3)
        ]
        row = lax.broadcasted_iota(jnp.int32, (rows, slots), 0)
        slot = lax.broadcasted_iota(jnp.int32, (rows, slots), 1)
        here = (lax.rem(slot, 8) // 2 == lax.rem(row // 8 + place_ref[0], RING)) & (lax.rem(row, 8) // 4 == micro)
        chosen = here & (parts[0].astype(jnp.int32) == lax.rem(slot, 2) + 1)
        for part in parts[1:]:
            weight = jnp.where(chosen, part, 0.0).astype(jnp.bfloat16)
            total += jnp.dot(weight, returned, preferred_element_type=jnp.float32)
    for r in range(RING):
        refs[RING + 2 + r][...] = total[r * rows // RING : (r + 1) * rows // RING].astype(jnp.bfloat16)


def shards(hidden, norm_gain, routes, route_scores, capacity, w_gate, w_up, w_down):
    experts = capacity.shape[0]
    place = lax.axis_index("exp").astype(jnp.int32)
    where = place.reshape(1)
    width, ff = w_gate.shape[1:]
    rows = hidden.shape[0]
    slots = experts * 8
    vmem = pl.BlockSpec(memory_space=pltpu.VMEM)
    blocks = pl.pallas_call(
        prepare_kernel,
        out_shape=[jax.ShapeDtypeStruct((rows, width + PAD), jnp.bfloat16)] * RING,
        in_specs=specs(5),
        out_specs=[vmem] * RING,
        name="prepare",
    )(where, hidden, norm_gain.reshape(1, -1), routes, route_scores, capacity.reshape(1, -1))
    mixed = direct(blocks)
    picked = pl.pallas_call(
        pick_kernel,
        out_shape=[jax.ShapeDtypeStruct((slots, width), jnp.bfloat16)] * 2,
        in_specs=specs(RING),
        out_specs=[vmem] * 2,
        name="pick",
    )(where, *mixed)
    entering = [swap(value.reshape(experts, 8, width)).reshape(slots, width) for value in picked]
    returned = []
    for value in entering:
        gate = jnp.dot(value, w_gate[0], preferred_element_type=jnp.float32).astype(jnp.bfloat16)
        up = jnp.dot(value, w_up[0], preferred_element_type=jnp.float32).astype(jnp.bfloat16)
        part = slots // RING
        half = part // 2
        own = [lax.rem(place + r, RING) * part for r in range(RING)]
        gate = [lax.dynamic_slice_in_dim(gate, start, part, axis=0) for start in own]
        up = [lax.dynamic_slice_in_dim(up, start, part, axis=0) for start in own]
        gate_far = move(gate[2], 1)
        up_far = move(up[2], -1)
        up_low = move(up[1], 1)
        gate_high = move(gate[3], -1)
        gate_low = move(add(gate[1], gate_far), 1)
        up_high = move(add(up[3], up_far), -1)
        gate_sum = gate[0].astype(jnp.float32) + gate_low.astype(jnp.float32) + gate_high.astype(jnp.float32)
        up_sum = up[0].astype(jnp.float32) + up_low.astype(jnp.float32) + up_high.astype(jnp.float32)
        activation = (jax.nn.silu(gate_sum) * up_sum).astype(jnp.bfloat16)
        low = move(activation, 1)
        high = move(activation, -1)
        far_low = move(low[:half], 1)
        far_high = move(high[half:], -1)
        whole = jnp.zeros((slots, ff), jnp.bfloat16)
        for piece, start in (
            (activation, own[0]), (high, own[1]), (far_low, own[2]), (far_high, own[2] + half), (low, own[3])
        ):
            whole = lax.dynamic_update_slice_in_dim(whole, piece, start, axis=0)
        expert_out = jnp.dot(whole, w_down[0], preferred_element_type=jnp.float32).astype(jnp.bfloat16)
        returned.append(swap(expert_out.reshape(experts, 8, width)).reshape(slots, width))
    sums = pl.pallas_call(
        functools.partial(combine_kernel, experts),
        out_shape=[jax.ShapeDtypeStruct((rows, width), jnp.bfloat16)] * RING,
        in_specs=specs(RING + 2),
        out_specs=[vmem] * RING,
        name="combine",
    )(where, *[value[:, width:] for value in mixed], *returned)
    back = direct(sums)
    return pl.pallas_call(
        finish_kernel,
        out_shape=jax.ShapeDtypeStruct(hidden.shape, jnp.bfloat16),
        in_specs=specs(1 + RING),
        out_specs=vmem,
        name="finish",
    )(where, hidden, *back)


def solution(mesh):
    in_specs = (
        P(("attn", "exp"), None),
        P(),
        P(("attn", "exp"), None),
        P(("attn", "exp"), None),
        P(),
        P("attn", "exp", None),
        P("attn", "exp", None),
        P("attn", None, "exp"),
    )
    out_specs = P(("attn", "exp"), None)
    return jax.shard_map(shards, mesh=mesh, in_specs=in_specs, out_specs=out_specs, check_vma=False)
```

time: 235 us -> 179 us (0.76)
  waiting for transfers between devices: 135 us -> 61.3 us
  starting transfers between devices: 29.4 us -> 60.1 us
  between operations: 13.6 us -> 0.37 us
  Pallas kernels: 0 us -> 9.06 us
  matrix products: 39.2 us -> 33.3 us
    psum x1 -> x0, waiting for transfers between devices: 89.5 us -> none  [shards(): lax.psum(up_part.astype(jnp.bfloat16), 'exp').astype(jnp.float32)]
    ppermute x0 -> x26, starting transfers between devices: none -> 35.7 us  [move(): lax.ppermute(value, 'exp', [(i, (i + step) % RING) for i in range(RING)])]
    ppermute x0 -> x26, waiting for transfers between devices: none -> 26.6 us  [move(): lax.ppermute(value, 'exp', [(i, (i + step) % RING) for i in range(RING)])]
    all_to_all x4, waiting for transfers between devices: 45.7 us -> 34.7 us  [swap(): lax.all_to_all(value, 'attn', split_axis=0, concat_axis=0, tiled=True)]
    pallas_call x0 -> x4, Pallas kernels: none -> 9.06 us  [the longest x1 3.08 us: shards(): pl.pallas_call(functools.partial(combine_kernel, experts), out_shape=[jax...]
    dot_general x14 -> x6, matrix products: 39.2 us -> 33.3 us  [the longest x2 12.2 us: shards(): jnp.dot(whole, w_down[0], preferred_element_type=jnp.float32)]
    slice x3 -> x8, local copies, waits for them, and re-layouts: 0.81 us -> 5.75 us  [the longest x4 5.06 us: shards(): value[:, width:]]
    all_to_all x4, starting transfers between devices: 29.2 us -> 24.3 us  [swap(): lax.all_to_all(value, 'attn', split_axis=0, concat_axis=0, tiled=True)]
  transfers between devices with their start and end apart: 5 -> 30, of which waited for: 5 -> 13; matrix products, arithmetic and copies ran while one was open for 10% -> 25% of each run, Pallas kernels for 0% -> 0%
where the time goes in v2:
time: 179 us; the launch traced here: 178 us
  waiting for transfers between devices  61.3 us (34%)
  starting transfers between devices  60.1 us (34%)
  matrix products  33.3 us (19%)
  local copies, waits for them, and re-layouts  9.27 us (5%)
  Pallas kernels  9.06 us (5%)
  other arithmetic  4.42 us (2%)
    ppermute x26, starting transfers between devices, move(): lax.ppermute(value, 'exp', [(i, (i + step) % RING) for i in range(RING)])  35.7 us
    all_to_all x4, waiting for transfers between devices, swap(): lax.all_to_all(value, 'attn', split_axis=0, concat_axis=0, tiled=True)  34.7 us
    ppermute x26, waiting for transfers between devices, move(): lax.ppermute(value, 'exp', [(i, (i + step) % RING) for i in range(RING)])  26.6 us
    all_to_all x4, starting transfers between devices, swap(): lax.all_to_all(value, 'attn', split_axis=0, concat_axis=0, tiled=True)  24.3 us
    dot_general x2, matrix products, shards(): jnp.dot(whole, w_down[0], preferred_element_type=jnp.float32)  12.2 us
    dot_general x2, matrix products, shards(): jnp.dot(value, w_up[0], preferred_element_type=jnp.float32)  10.6 us
    dot_general x2, matrix products, shards(): jnp.dot(value, w_gate[0], preferred_element_type=jnp.float32)  10.6 us
    slice x4, local copies, waits for them, and re-layouts, shards(): value[:, width:]  5.06 us
  transfers between devices with their start and end apart: 30, of which 13 were waited for; matrix products, arithmetic and copies ran while one was open for 25% of the time, Pallas kernels for 0%

profile of v2, /device:TPU:0, one launch (start us, length us, event | category | flops | bytes accessed | tf_op | source)
XLA Modules:
  0.0 177.9 jit_solution(642902923619328599)
XLA Ops:
  0.0 1.8 prepare.1
  1.8 2.8 %collective-permute-start = (bf16[8,1920]{1,0:T(8,128)(2,1)}, bf16[8,1920]{1,0:T(8,128)(2,1)S(1)}, u32[]{:S(2)}, u32[]{:S(2)}) collective-permute-start(bf16[8,1920]{1,0:T(8,128)(2,1)} %get-tuple-element.16), channel_id=1, source_target_pairs={{0,3},{1,0},{2,1},{3,2},{4,7},{5,4},{6,5},{7,6},{8,11},{9,8},{10,9... | collective-permute-start | bytes 92168 | tf_op jit(solution)/shard_map/ppermute | solution.py:17
  4.6 0.8 collective-permute-start.1
  5.4 0.9 collective-permute-start.2
  6.4 3.8 %collective-permute-done.1.refs_2_ = bf16[8,1920]{1,0:T(8,128)(2,1)S(1)} collective-permute-done((bf16[8,1920]{1,0:T(8,128)(2,1)}, bf16[8,1920]{1,0:T(8,128)(2,1)S(1)}, u32[]{:S(2)}, u32[]{:S(2)}) %collective-permute-start.1) | collective-permute-done | bytes 30752 | tf_op jit(solution)/shard_map/ppermute | solution.py:17
  11.3 2.6 %pick.1 = (bf16[256,1792]{1,0:T(8,128)(2,1)}, bf16[256,1792]{1,0:T(8,128)(2,1)}) custom-call(s32[1]{0:T(128)} %bitcast.place_ref, bf16[8,1920]{1,0:T(8,128)(2,1)} %get-tuple-element.15.refs_0_, bf16[8,1920]{1,0:T(8,128)(2,1)} %copy-done.2, bf16[8,1920]{1,0:T(8,128)(2,1)} %copy-done.3, bf16[8,1920]{1,0:T(8,128)(2,1)} %copy-done.4), custom_call_target="tpu_custom_call" | custom-call | tf_op jit(solution)/shard_map/pick/pallas_call | solution.py:152
  13.9 8.3 %all-to-all-start = ((bf16[32,8,1792]{2,1,0:T(8,128)(2,1)}), bf16[32,8,1792]{2,1,0:T(8,128)(2,1)S(1)}, u32[]{:S(2)}, u32[]{:S(2)}) async-start(bf16[32,8,1792]{2,1,0:T(8,128)(2,1)} %bitcast.57), calls=%async_computation | async-start | bytes 1835008 | tf_op jit(solution)/shard_map/all_to_all | solution.py:25
  22.3 15.3 %all-to-all-done = bf16[32,8,1792]{2,1,0:T(8,128)(2,1)S(1)} async-done(((bf16[32,8,1792]{2,1,0:T(8,128)(2,1)}), bf16[32,8,1792]{2,1,0:T(8,128)(2,1)S(1)}, u32[]{:S(2)}, u32[]{:S(2)}) %all-to-all-start) | async-done | bytes 917536 | tf_op jit(solution)/shard_map/all_to_all | solution.py:25
  37.6 4.7 %all-to-all-start.2 = ((bf16[32,8,1792]{2,1,0:T(8,128)(2,1)}), bf16[32,8,1792]{2,1,0:T(8,128)(2,1)}, u32[]{:S(2)}, u32[]{:S(2)}) async-start(bf16[32,8,1792]{2,1,0:T(8,128)(2,1)} %bitcast.56), calls=%async_computation.2 | async-start | bytes 1835008 | tf_op jit(solution)/shard_map/all_to_all | solution.py:25
  42.3 5.1 %fusion.18 = bf16[256,2048]{1,0:T(8,128)(2,1)S(1)} fusion(bf16[1,1792,2048]{2,1,0:T(8,128)(2,1)} %param.14, bf16[32,8,1792]{2,1,0:T(8,128)(2,1)S(1)} %all-to-all-done), kind=kOutput, calls=%fused_computation.14 | convolution fusion | flops 1879572480 | bytes 9306112 | tf_op jit(solution)/shard_map/dot_general | solution.py:163
  47.4 0.8 constant_dynamic-slice_fusion.5
  48.6 1.6 collective-permute-start.6
  50.3 5.1 %fusion.12 = bf16[256,2048]{1,0:T(8,128)(2,1)S(1)} fusion(bf16[1,1792,2048]{2,1,0:T(8,128)(2,1)} %param.13, bf16[32,8,1792]{2,1,0:T(8,128)(2,1)S(1)} %all-to-all-done), kind=kOutput, calls=%fused_computation.12 | convolution fusion | flops 1879572480 | bytes 9306112 | tf_op jit(solution)/shard_map/dot_general | solution.py:162
  55.5 1.7 collective-permute-start.5
  57.6 5.4 %fusion.21 = bf16[256,2048]{1,0:T(8,128)(2,1)S(1)} fusion(bf16[1,1792,2048]{2,1,0:T(8,128)(2,1)} %param.14, bf16[32,8,1792]{2,1,0:T(8,128)(2,1)} %all-to-all-done.2), kind=kOutput, calls=%fused_computation.15 | convolution fusion | flops 1879572480 | bytes 9306112 | tf_op jit(solution)/shard_map/dot_general | solution.py:163
  63.1 2.9 %collective-permute-start.17 = (bf16[64,2048]{1,0:T(8,128)(2,1)S(1)}, bf16[64,2048]{1,0:T(8,128)(2,1)S(1)}, u32[]{:S(2)}, u32[]{:S(2)}) collective-permute-start(bf16[64,2048]{1,0:T(8,128)(2,1)S(1)} %get-tuple-element.32), channel_id=1, source_target_pairs={{0,3},{1,0},{2,1},{3,2},{4,7},{5,4},{6,5},{7,6},{8,11},{9,8},{10,9... | collective-permute-start | bytes 786440 | tf_op jit(solution)/shard_map/ppermute | solution.py:17
  66.0 5.4 %fusion.15 = bf16[256,2048]{1,0:T(8,128)(2,1)S(1)} fusion(bf16[1,1792,2048]{2,1,0:T(8,128)(2,1)} %param.13, bf16[32,8,1792]{2,1,0:T(8,128)(2,1)} %all-to-all-done.2), kind=kOutput, calls=%fused_computation.13 | convolution fusion | flops 1879572480 | bytes 9306112 | tf_op jit(solution)/shard_map/dot_general | solution.py:162
  71.6 1.0 add_convert_fusion.2
  72.9 1.0 add_convert_fusion.3
  73.9 3.3 %collective-permute-start.8 = (bf16[64,2048]{1,0:T(8,128)(2,1)S(1)}, bf16[64,2048]{1,0:T(8,128)(2,1)S(1)}, u32[]{:S(2)}, u32[]{:S(2)}) collective-permute-start(bf16[64,2048]{1,0:T(8,128)(2,1)S(1)} %add_convert_fusion.2), channel_id=1, source_target_pairs={{0,3},{1,0},{2,1},{3,2},{4,7},{5,4},{6,5},{7,6},{8,11},{9,8},{10,9... | collective-permute-start | bytes 786440 | tf_op jit(solution)/shard_map/ppermute | solution.py:17
  77.3 8.1 %collective-permute-done.13 = bf16[64,2048]{1,0:T(8,128)(2,1)S(1)} collective-permute-done((bf16[64,2048]{1,0:T(8,128)(2,1)S(1)}, bf16[64,2048]{1,0:T(8,128)(2,1)S(1)}, u32[]{:S(2)}, u32[]{:S(2)}) %collective-permute-start.13) | collective-permute-done | bytes 262176 | tf_op jit(solution)/shard_map/ppermute | solution.py:17
  85.5 3.3 %collective-permute-start.15 = (bf16[64,2048]{1,0:T(8,128)(2,1)S(1)}, bf16[64,2048]{1,0:T(8,128)(2,1)S(1)}, u32[]{:S(2)}, u32[]{:S(2)}) collective-permute-start(bf16[64,2048]{1,0:T(8,128)(2,1)S(1)} %get-tuple-element.30), channel_id=1, source_target_pairs={{0,3},{1,0},{2,1},{3,2},{4,7},{5,4},{6,5},{7,6},{8,11},{9,8},{10,9... | collective-permute-start | bytes 786440 | tf_op jit(solution)/shard_map/ppermute | solution.py:17
  88.9 1.9 %collective-permute-start.14 = (bf16[64,2048]{1,0:T(8,128)(2,1)S(1)}, bf16[64,2048]{1,0:T(8,128)(2,1)S(1)}, u32[]{:S(2)}, u32[]{:S(2)}) collective-permute-start(bf16[64,2048]{1,0:T(8,128)(2,1)S(1)} %add_convert_fusion.1), channel_id=1, source_target_pairs={{0,1},{1,2},{2,3},{3,0},{4,5},{5,6},{6,7},{7,4},{8,9},{9,10},{10,1... | collective-permute-start | bytes 786440 | tf_op jit(solution)/shard_map/ppermute | solution.py:17
  90.8 4.8 %collective-permute-done.4 = bf16[64,2048]{1,0:T(8,128)(2,1)S(1)} collective-permute-done((bf16[64,2048]{1,0:T(8,128)(2,1)S(1)}, bf16[64,2048]{1,0:T(8,128)(2,1)S(1)}, u32[]{:S(2)}, u32[]{:S(2)}) %collective-permute-start.4) | collective-permute-done | bytes 262176 | tf_op jit(solution)/shard_map/ppermute | solution.py:17
  95.7 1.9 %constant_dynamic-update-slice_fusion.8 = (bf16[256,2048]{1,0:T(8,128)(2,1)S(1)}, bf16[64,2048]{1,0:T(8,128)(2,1)}) fusion(bf16[256,2048]{1,0:T(8,128)(2,1)S(1)} %broadcast.10.clone, s32[]{:T(128)S(6)} %select_n.10, bf16[64,2048]{1,0:T(8,128)(2,1)S(1)} %collective-permute-done.8, bf16[64,2048]{1,0:T(8,128)(2,1)S(1)} %collective-permute-done.6, ...), kind=kLoop, calls=%fused_computation.42 | loop fusion | flops 2097152 | bytes 2097156 | tf_op jit(solution)/shard_map/dynamic_update_slice | solution.py:186
  97.7 2.0 %collective-permute-start.10 = (bf16[64,2048]{1,0:T(8,128)(2,1)}, bf16[64,2048]{1,0:T(8,128)(2,1)S(1)}, u32[]{:S(2)}, u32[]{:S(2)}) collective-permute-start(bf16[64,2048]{1,0:T(8,128)(2,1)} %get-tuple-element.28), channel_id=1, source_target_pairs={{0,1},{1,2},{2,3},{3,0},{4,5},{5,6},{6,7},{7,4},{8,9},{9,10},{10,1... | collective-permute-start | bytes 786440 | tf_op jit(solution)/shard_map/ppermute | solution.py:17
  99.7 1.4 collective-permute-done.18
  101.7 3.8 %collective-permute-start.19 = (bf16[64,2048]{1,0:T(8,128)(2,1)S(1)}, bf16[64,2048]{1,0:T(8,128)(2,1)S(1)}, u32[]{:S(2)}, u32[]{:S(2)}) collective-permute-start(bf16[64,2048]{1,0:T(8,128)(2,1)S(1)} %get-tuple-element.26), channel_id=1, source_target_pairs={{0,3},{1,0},{2,1},{3,2},{4,7},{5,4},{6,5},{7,6},{8,11},{9,8},{10,9... | collective-permute-start | bytes 786440 | tf_op jit(solution)/shard_map/ppermute | solution.py:17
  105.4 2.8 %collective-permute-done.10 = bf16[64,2048]{1,0:T(8,128)(2,1)S(1)} collective-permute-done((bf16[64,2048]{1,0:T(8,128)(2,1)}, bf16[64,2048]{1,0:T(8,128)(2,1)S(1)}, u32[]{:S(2)}, u32[]{:S(2)}) %collective-permute-start.10) | collective-permute-done | bytes 262176 | tf_op jit(solution)/shard_map/ppermute | solution.py:17
  108.4 3.3 %collective-permute-start.12 = (bf16[32,2048]{1,0:T(8,128)(2,1)S(1)}, bf16[32,2048]{1,0:T(8,128)(2,1)S(1)}, u32[]{:S(2)}, u32[]{:S(2)}) collective-permute-start(bf16[32,2048]{1,0:T(8,128)(2,1)S(1)} %slice.36), channel_id=1, source_target_pairs={{0,3},{1,0},{2,1},{3,2},{4,7},{5,4},{6,5},{7,6},{8,11},{9,8},{10,9... | collective-permute-start | bytes 393224 | tf_op jit(solution)/shard_map/ppermute | solution.py:17
  112.6 3.3 %collective-permute-start.22 = (bf16[32,2048]{1,0:T(8,128)(2,1)S(1)}, bf16[32,2048]{1,0:T(8,128)(2,1)S(1)}, u32[]{:S(2)}, u32[]{:S(2)}) collective-permute-start(bf16[32,2048]{1,0:T(8,128)(2,1)S(1)} %slice.38), channel_id=1, source_target_pairs={{0,3},{1,0},{2,1},{3,2},{4,7},{5,4},{6,5},{7,6},{8,11},{9,8},{10,9... | collective-permute-start | bytes 393224 | tf_op jit(solution)/shard_map/ppermute | solution.py:17
  116.1 6.1 %fusion.33 = bf16[32,8,1792]{2,1,0:T(8,128)(2,1)} fusion(bf16[256,2048]{1,0:T(8,128)(2,1)S(1)} %constant_dynamic-update-slice_fusion.4, bf16[1,2048,1792]{2,1,0:T(8,128)(2,1)} %param.15), kind=kOutput, calls=%fused_computation.19 | convolution fusion | flops 1879506944 | bytes 9306112 | tf_op jit(solution)/shard_map/dot_general | solution.py:187
  122.2 7.2 %all-to-all-start.1 = ((bf16[32,8,1792]{2,1,0:T(8,128)(2,1)}), bf16[32,8,1792]{2,1,0:T(8,128)(2,1)S(1)}, u32[]{:S(2)}, u32[]{:S(2)}) async-start(bf16[32,8,1792]{2,1,0:T(8,128)(2,1)} %fusion.33), calls=%async_computation.1 | async-start | bytes 1835008 | tf_op jit(solution)/shard_map/all_to_all | solution.py:25
  129.5 6.1 %fusion.30 = bf16[32,8,1792]{2,1,0:T(8,128)(2,1)} fusion(bf16[256,2048]{1,0:T(8,128)(2,1)S(1)} %constant_dynamic-update-slice_fusion.3, bf16[1,2048,1792]{2,1,0:T(8,128)(2,1)} %param.15), kind=kOutput, calls=%fused_computation.18 | convolution fusion | flops 1879506944 | bytes 9306112 | tf_op jit(solution)/shard_map/dot_general | solution.py:187
  135.6 9.2 %all-to-all-done.1 = bf16[32,8,1792]{2,1,0:T(8,128)(2,1)S(1)} async-done(((bf16[32,8,1792]{2,1,0:T(8,128)(2,1)}), bf16[32,8,1792]{2,1,0:T(8,128)(2,1)S(1)}, u32[]{:S(2)}, u32[]{:S(2)}) %all-to-all-start.1) | async-done | bytes 917536 | tf_op jit(solution)/shard_map/all_to_all | solution.py:25
  144.7 4.1 %all-to-all-start.3 = ((bf16[32,8,1792]{2,1,0:T(8,128)(2,1)}), bf16[32,8,1792]{2,1,0:T(8,128)(2,1)S(1)}, u32[]{:S(2)}, u32[]{:S(2)}) async-start(bf16[32,8,1792]{2,1,0:T(8,128)(2,1)} %fusion.30), calls=%async_computation.3 | async-start | bytes 1835008 | tf_op jit(solution)/shard_map/all_to_all | solution.py:25
  148.9 1.3 slice.24.refs_0_
  150.1 1.3 slice.32.refs_1_
  151.4 1.3 slice.33.refs_2_
  152.7 1.3 slice.34.refs_3_
  153.9 10.3 %all-to-all-done.3 = bf16[32,8,1792]{2,1,0:T(8,128)(2,1)S(1)} async-done(((bf16[32,8,1792]{2,1,0:T(8,128)(2,1)}), bf16[32,8,1792]{2,1,0:T(8,128)(2,1)S(1)}, u32[]{:S(2)}, u32[]{:S(2)}) %all-to-all-start.3) | async-done | bytes 917536 | tf_op jit(solution)/shard_map/all_to_all | solution.py:25
  164.2 0.9 copy-done.1
  165.1 3.1 %combine.1 = (bf16[8,1792]{1,0:T(8,128)(2,1)}, bf16[8,1792]{1,0:T(8,128)(2,1)}, bf16[8,1792]{1,0:T(8,128)(2,1)}, bf16[8,1792]{1,0:T(8,128)(2,1)}) custom-call(s32[1]{0:T(128)} %bitcast.place_ref, bf16[8,128]{1,0:T(8,128)(2,1)} %slice.24.refs_0_, bf16[8,128]{1,0:T(8,128)(2,1)} %slice.32.refs_1_, bf16[8,128]{1,0:T(8,128)(2,1)} %slice.33.refs_2_, ...), custom_call_target="tpu_custom_call" | custom-call | tf_op jit(solution)/shard_map/combine/pallas_call | solution.py:189
  168.2 1.8 %collective-permute-start.23 = (bf16[8,1792]{1,0:T(8,128)(2,1)}, bf16[8,1792]{1,0:T(8,128)(2,1)S(1)}, u32[]{:S(2)}, u32[]{:S(2)}) collective-permute-start(bf16[8,1792]{1,0:T(8,128)(2,1)} %get-tuple-element.22), channel_id=1, source_target_pairs={{0,3},{1,0},{2,1},{3,2},{4,7},{5,4},{6,5},{7,6},{8,11},{9,8},{10,9... | collective-permute-start | bytes 86024 | tf_op jit(solution)/shard_map/ppermute | solution.py:17
  170.0 0.9 collective-permute-start.25
  170.9 1.5 collective-permute-done.23.refs_1_
  172.4 3.2 %collective-permute-done.24.refs_2_ = bf16[8,1792]{1,0:T(8,128)(2,1)S(1)} collective-permute-done((bf16[8,1792]{1,0:T(8,128)(2,1)}, bf16[8,1792]{1,0:T(8,128)(2,1)S(1)}, u32[]{:S(2)}, u32[]{:S(2)}) %collective-permute-start.24) | collective-permute-done | bytes 28704 | tf_op jit(solution)/shard_map/ppermute | solution.py:17
  176.3 1.6 finish.1
  (66 shorter events, 5.2 us)
Async XLA Ops:
  1.8 4.6 %collective-permute-start = (bf16[8,1920]{1,0:T(8,128)(2,1)}, bf16[8,1920]{1,0:T(8,128)(2,1)S(1)}, u32[]{:S(2)}, u32[]{:S(2)}) collective-permute-start(bf16[8,1920]{1,0:T(8,128)(2,1)} %get-tuple-element.16), channel_id=1, source_target_pairs={{0,3},{1,0},{2,1},{3,2},{4,7},{5,4},{6,5},{7,6},{8,11},{9,8},{10,9... | collective-permute-start | bytes 92168 | tf_op jit(solution)/shard_map/ppermute | solution.py:17
  4.6 5.6 %collective-permute-start.1 = (bf16[8,1920]{1,0:T(8,128)(2,1)}, bf16[8,1920]{1,0:T(8,128)(2,1)S(1)}, u32[]{:S(2)}, u32[]{:S(2)}) collective-permute-start(bf16[8,1920]{1,0:T(8,128)(2,1)} %get-tuple-element.17), channel_id=1, source_target_pairs={{0,2},{1,3},{2,0},{3,1},{4,6},{5,7},{6,4},{7,5},{8,10},{9,11},{10,... | collective-permute-start | bytes 92168 | tf_op jit(solution)/shard_map/ppermute | solution.py:17
  5.4 5.3 %collective-permute-start.2 = (bf16[8,1920]{1,0:T(8,128)(2,1)}, bf16[8,1920]{1,0:T(8,128)(2,1)S(1)}, u32[]{:S(2)}, u32[]{:S(2)}) collective-permute-start(bf16[8,1920]{1,0:T(8,128)(2,1)} %get-tuple-element.18), channel_id=1, source_target_pairs={{0,1},{1,2},{2,3},{3,0},{4,5},{5,6},{6,7},{7,4},{8,9},{9,10},{10,1... | collective-permute-start | bytes 92168 | tf_op jit(solution)/shard_map/ppermute | solution.py:17
  6.4 4.3 %copy-start.2 = (bf16[8,1920]{1,0:T(8,128)(2,1)}, bf16[8,1920]{1,0:T(8,128)(2,1)S(1)}, u32[]{:S(2)}) copy-start(bf16[8,1920]{1,0:T(8,128)(2,1)S(1)} %collective-permute-done.refs_1_) | copy-start | bytes 92164
  10.2 0.6 copy-start.3
  10.7 0.6 copy-start.4
  13.9 23.7 %all-to-all-start = ((bf16[32,8,1792]{2,1,0:T(8,128)(2,1)}), bf16[32,8,1792]{2,1,0:T(8,128)(2,1)S(1)}, u32[]{:S(2)}, u32[]{:S(2)}) async-start(bf16[32,8,1792]{2,1,0:T(8,128)(2,1)} %bitcast.57), calls=%async_computation | async-start | bytes 1835008 | tf_op jit(solution)/shard_map/all_to_all | solution.py:25
  37.6 20.0 %all-to-all-start.2 = ((bf16[32,8,1792]{2,1,0:T(8,128)(2,1)}), bf16[32,8,1792]{2,1,0:T(8,128)(2,1)}, u32[]{:S(2)}, u32[]{:S(2)}) async-start(bf16[32,8,1792]{2,1,0:T(8,128)(2,1)} %bitcast.56), calls=%async_computation.2 | async-start | bytes 1835008 | tf_op jit(solution)/shard_map/all_to_all | solution.py:25
  48.3 23.2 %collective-permute-start.7 = (bf16[64,2048]{1,0:T(8,128)(2,1)}, bf16[64,2048]{1,0:T(8,128)(2,1)}, u32[]{:S(2)}, u32[]{:S(2)}) collective-permute-start(bf16[64,2048]{1,0:T(8,128)(2,1)} %get-tuple-element.36), channel_id=1, source_target_pairs={{0,3},{1,0},{2,1},{3,2},{4,7},{5,4},{6,5},{7,6},{8,11},{9,8},{10,9... | collective-permute-start | bytes 786440 | tf_op jit(solution)/shard_map/ppermute | solution.py:17
  48.6 36.8 %collective-permute-start.6 = (bf16[64,2048]{1,0:T(8,128)(2,1)}, bf16[64,2048]{1,0:T(8,128)(2,1)S(1)}, u32[]{:S(2)}, u32[]{:S(2)}) collective-permute-start(bf16[64,2048]{1,0:T(8,128)(2,1)} %get-tuple-element.35), channel_id=1, source_target_pairs={{0,1},{1,2},{2,3},{3,0},{4,5},{5,6},{6,7},{7,4},{8,9},{9,10},{10,1... | collective-permute-start | bytes 786440 | tf_op jit(solution)/shard_map/ppermute | solution.py:17
  55.5 33.3 %collective-permute-start.5 = (bf16[64,2048]{1,0:T(8,128)(2,1)S(1)}, bf16[64,2048]{1,0:T(8,128)(2,1)}, u32[]{:S(2)}, u32[]{:S(2)}) collective-permute-start(bf16[64,2048]{1,0:T(8,128)(2,1)S(1)} %get-tuple-element.34), channel_id=1, source_target_pairs={{0,3},{1,0},{2,1},{3,2},{4,7},{5,4},{6,5},{7,6},{8,11},{9,8},{10,9... | collective-permute-start | bytes 786440 | tf_op jit(solution)/shard_map/ppermute | solution.py:17
  57.2 15.4 %collective-permute-start.3 = (bf16[64,2048]{1,0:T(8,128)(2,1)S(1)}, bf16[64,2048]{1,0:T(8,128)(2,1)}, u32[]{:S(2)}, u32[]{:S(2)}) collective-permute-start(bf16[64,2048]{1,0:T(8,128)(2,1)S(1)} %get-tuple-element.33), channel_id=1, source_target_pairs={{0,1},{1,2},{2,3},{3,0},{4,5},{5,6},{6,7},{7,4},{8,9},{9,10},{10,1... | collective-permute-start | bytes 786440 | tf_op jit(solution)/shard_map/ppermute | solution.py:17
  63.1 10.8 %collective-permute-start.17 = (bf16[64,2048]{1,0:T(8,128)(2,1)S(1)}, bf16[64,2048]{1,0:T(8,128)(2,1)S(1)}, u32[]{:S(2)}, u32[]{:S(2)}) collective-permute-start(bf16[64,2048]{1,0:T(8,128)(2,1)S(1)} %get-tuple-element.32), channel_id=1, source_target_pairs={{0,3},{1,0},{2,1},{3,2},{4,7},{5,4},{6,5},{7,6},{8,11},{9,8},{10,9... | collective-permute-start | bytes 786440 | tf_op jit(solution)/shard_map/ppermute | solution.py:17
  71.5 26.2 %collective-permute-start.16 = (bf16[64,2048]{1,0:T(8,128)(2,1)S(1)}, bf16[64,2048]{1,0:T(8,128)(2,1)S(1)}, u32[]{:S(2)}, u32[]{:S(2)}) collective-permute-start(bf16[64,2048]{1,0:T(8,128)(2,1)S(1)} %get-tuple-element.31), channel_id=1, source_target_pairs={{0,1},{1,2},{2,3},{3,0},{4,5},{5,6},{6,7},{7,4},{8,9},{9,10},{10,1... | collective-permute-start | bytes 786440 | tf_op jit(solution)/shard_map/ppermute | solution.py:17
  72.6 12.8 %collective-permute-start.13 = (bf16[64,2048]{1,0:T(8,128)(2,1)S(1)}, bf16[64,2048]{1,0:T(8,128)(2,1)S(1)}, u32[]{:S(2)}, u32[]{:S(2)}) collective-permute-start(bf16[64,2048]{1,0:T(8,128)(2,1)S(1)} %get-tuple-element.29), channel_id=1, source_target_pairs={{0,1},{1,2},{2,3},{3,0},{4,5},{5,6},{6,7},{7,4},{8,9},{9,10},{10,1... | collective-permute-start | bytes 786440 | tf_op jit(solution)/shard_map/ppermute | solution.py:17
  73.9 15.0 %collective-permute-start.8 = (bf16[64,2048]{1,0:T(8,128)(2,1)S(1)}, bf16[64,2048]{1,0:T(8,128)(2,1)S(1)}, u32[]{:S(2)}, u32[]{:S(2)}) collective-permute-start(bf16[64,2048]{1,0:T(8,128)(2,1)S(1)} %add_convert_fusion.2), channel_id=1, source_target_pairs={{0,3},{1,0},{2,1},{3,2},{4,7},{5,4},{6,5},{7,6},{8,11},{9,8},{10,9... | collective-permute-start | bytes 786440 | tf_op jit(solution)/shard_map/ppermute | solution.py:17
  85.4 10.2 %collective-permute-start.4 = (bf16[64,2048]{1,0:T(8,128)(2,1)S(1)}, bf16[64,2048]{1,0:T(8,128)(2,1)S(1)}, u32[]{:S(2)}, u32[]{:S(2)}) collective-permute-start(bf16[64,2048]{1,0:T(8,128)(2,1)S(1)} %add_convert_fusion.3), channel_id=1, source_target_pairs={{0,1},{1,2},{2,3},{3,0},{4,5},{5,6},{6,7},{7,4},{8,9},{9,10},{10,1... | collective-permute-start | bytes 786440 | tf_op jit(solution)/shard_map/ppermute | solution.py:17
  85.5 14.2 %collective-permute-start.15 = (bf16[64,2048]{1,0:T(8,128)(2,1)S(1)}, bf16[64,2048]{1,0:T(8,128)(2,1)S(1)}, u32[]{:S(2)}, u32[]{:S(2)}) collective-permute-start(bf16[64,2048]{1,0:T(8,128)(2,1)S(1)} %get-tuple-element.30), channel_id=1, source_target_pairs={{0,3},{1,0},{2,1},{3,2},{4,7},{5,4},{6,5},{7,6},{8,11},{9,8},{10,9... | collective-permute-start | bytes 786440 | tf_op jit(solution)/shard_map/ppermute | solution.py:17
  88.8 12.4 %collective-permute-start.18 = (bf16[64,2048]{1,0:T(8,128)(2,1)S(1)}, bf16[64,2048]{1,0:T(8,128)(2,1)S(1)}, u32[]{:S(2)}, u32[]{:S(2)}) collective-permute-start(bf16[64,2048]{1,0:T(8,128)(2,1)S(1)} %add_convert_fusion), channel_id=1, source_target_pairs={{0,3},{1,0},{2,1},{3,2},{4,7},{5,4},{6,5},{7,6},{8,11},{9,8},{10,9... | collective-permute-start | bytes 786440 | tf_op jit(solution)/shard_map/ppermute | solution.py:17
  88.9 12.3 %collective-permute-start.14 = (bf16[64,2048]{1,0:T(8,128)(2,1)S(1)}, bf16[64,2048]{1,0:T(8,128)(2,1)S(1)}, u32[]{:S(2)}, u32[]{:S(2)}) collective-permute-start(bf16[64,2048]{1,0:T(8,128)(2,1)S(1)} %add_convert_fusion.1), channel_id=1, source_target_pairs={{0,1},{1,2},{2,3},{3,0},{4,5},{5,6},{6,7},{7,4},{8,9},{9,10},{10,1... | collective-permute-start | bytes 786440 | tf_op jit(solution)/shard_map/ppermute | solution.py:17
  97.7 10.7 %collective-permute-start.9 = (bf16[64,2048]{1,0:T(8,128)(2,1)}, bf16[64,2048]{1,0:T(8,128)(2,1)S(1)}, u32[]{:S(2)}, u32[]{:S(2)}) collective-permute-start(bf16[64,2048]{1,0:T(8,128)(2,1)} %get-tuple-element.28), channel_id=1, source_target_pairs={{0,3},{1,0},{2,1},{3,2},{4,7},{5,4},{6,5},{7,6},{8,11},{9,8},{10,9... | collective-permute-start | bytes 786440 | tf_op jit(solution)/shard_map/ppermute | solution.py:17
  97.7 10.6 %collective-permute-start.10 = (bf16[64,2048]{1,0:T(8,128)(2,1)}, bf16[64,2048]{1,0:T(8,128)(2,1)S(1)}, u32[]{:S(2)}, u32[]{:S(2)}) collective-permute-start(bf16[64,2048]{1,0:T(8,128)(2,1)} %get-tuple-element.28), channel_id=1, source_target_pairs={{0,1},{1,2},{2,3},{3,0},{4,5},{5,6},{6,7},{7,4},{8,9},{9,10},{10,1... | collective-permute-start | bytes 786440 | tf_op jit(solution)/shard_map/ppermute | solution.py:17
  101.6 10.3 %collective-permute-start.20 = (bf16[64,2048]{1,0:T(8,128)(2,1)S(1)}, bf16[64,2048]{1,0:T(8,128)(2,1)S(1)}, u32[]{:S(2)}, u32[]{:S(2)}) collective-permute-start(bf16[64,2048]{1,0:T(8,128)(2,1)S(1)} %get-tuple-element.26), channel_id=1, source_target_pairs={{0,1},{1,2},{2,3},{3,0},{4,5},{5,6},{6,7},{7,4},{8,9},{9,10},{10,1... | collective-permute-start | bytes 786440 | tf_op jit(solution)/shard_map/ppermute | solution.py:17
  101.7 10.9 %collective-permute-start.19 = (bf16[64,2048]{1,0:T(8,128)(2,1)S(1)}, bf16[64,2048]{1,0:T(8,128)(2,1)S(1)}, u32[]{:S(2)}, u32[]{:S(2)}) collective-permute-start(bf16[64,2048]{1,0:T(8,128)(2,1)S(1)} %get-tuple-element.26), channel_id=1, source_target_pairs={{0,3},{1,0},{2,1},{3,2},{4,7},{5,4},{6,5},{7,6},{8,11},{9,8},{10,9... | collective-permute-start | bytes 786440 | tf_op jit(solution)/shard_map/ppermute | solution.py:17
  108.3 7.7 %collective-permute-start.11 = (bf16[32,2048]{1,0:T(8,128)(2,1)S(1)}, bf16[32,2048]{1,0:T(8,128)(2,1)S(1)}, u32[]{:S(2)}, u32[]{:S(2)}) collective-permute-start(bf16[32,2048]{1,0:T(8,128)(2,1)S(1)} %slice.35), channel_id=1, source_target_pairs={{0,1},{1,2},{2,3},{3,0},{4,5},{5,6},{6,7},{7,4},{8,9},{9,10},{10,1... | collective-permute-start | bytes 393224 | tf_op jit(solution)/shard_map/ppermute | solution.py:17
  108.4 7.6 %collective-permute-start.12 = (bf16[32,2048]{1,0:T(8,128)(2,1)S(1)}, bf16[32,2048]{1,0:T(8,128)(2,1)S(1)}, u32[]{:S(2)}, u32[]{:S(2)}) collective-permute-start(bf16[32,2048]{1,0:T(8,128)(2,1)S(1)} %slice.36), channel_id=1, source_target_pairs={{0,3},{1,0},{2,1},{3,2},{4,7},{5,4},{6,5},{7,6},{8,11},{9,8},{10,9... | collective-permute-start | bytes 393224 | tf_op jit(solution)/shard_map/ppermute | solution.py:17
  112.6 16.8 %collective-permute-start.21 = (bf16[32,2048]{1,0:T(8,128)(2,1)}, bf16[32,2048]{1,0:T(8,128)(2,1)S(1)}, u32[]{:S(2)}, u32[]{:S(2)}) collective-permute-start(bf16[32,2048]{1,0:T(8,128)(2,1)} %slice.37), channel_id=1, source_target_pairs={{0,1},{1,2},{2,3},{3,0},{4,5},{5,6},{6,7},{7,4},{8,9},{9,10},{10,1... | collective-permute-start | bytes 393224 | tf_op jit(solution)/shard_map/ppermute | solution.py:17
  112.6 16.8 %collective-permute-start.22 = (bf16[32,2048]{1,0:T(8,128)(2,1)S(1)}, bf16[32,2048]{1,0:T(8,128)(2,1)S(1)}, u32[]{:S(2)}, u32[]{:S(2)}) collective-permute-start(bf16[32,2048]{1,0:T(8,128)(2,1)S(1)} %slice.38), channel_id=1, source_target_pairs={{0,3},{1,0},{2,1},{3,2},{4,7},{5,4},{6,5},{7,6},{8,11},{9,8},{10,9... | collective-permute-start | bytes 393224 | tf_op jit(solution)/shard_map/ppermute | solution.py:17
  122.2 22.6 %all-to-all-start.1 = ((bf16[32,8,1792]{2,1,0:T(8,128)(2,1)}), bf16[32,8,1792]{2,1,0:T(8,128)(2,1)S(1)}, u32[]{:S(2)}, u32[]{:S(2)}) async-start(bf16[32,8,1792]{2,1,0:T(8,128)(2,1)} %fusion.33), calls=%async_computation.1 | async-start | bytes 1835008 | tf_op jit(solution)/shard_map/all_to_all | solution.py:25
  144.7 19.5 %copy-start = (bf16[32,8,1792]{2,1,0:T(8,128)(2,1)}, bf16[32,8,1792]{2,1,0:T(8,128)(2,1)S(1)}, u32[]{:S(2)}) copy-start(bf16[32,8,1792]{2,1,0:T(8,128)(2,1)S(1)} %all-to-all-done.1) | copy-start | bytes 2752516
  144.7 19.5 %all-to-all-start.3 = ((bf16[32,8,1792]{2,1,0:T(8,128)(2,1)}), bf16[32,8,1792]{2,1,0:T(8,128)(2,1)S(1)}, u32[]{:S(2)}, u32[]{:S(2)}) async-start(bf16[32,8,1792]{2,1,0:T(8,128)(2,1)} %fusion.30), calls=%async_computation.3 | async-start | bytes 1835008 | tf_op jit(solution)/shard_map/all_to_all | solution.py:25
  164.2 0.9 copy-start.1
  168.2 4.2 %collective-permute-start.23 = (bf16[8,1792]{1,0:T(8,128)(2,1)}, bf16[8,1792]{1,0:T(8,128)(2,1)S(1)}, u32[]{:S(2)}, u32[]{:S(2)}) collective-permute-start(bf16[8,1792]{1,0:T(8,128)(2,1)} %get-tuple-element.22), channel_id=1, source_target_pairs={{0,3},{1,0},{2,1},{3,2},{4,7},{5,4},{6,5},{7,6},{8,11},{9,8},{10,9... | collective-permute-start | bytes 86024 | tf_op jit(solution)/shard_map/ppermute | solution.py:17
  170.0 5.6 %collective-permute-start.24 = (bf16[8,1792]{1,0:T(8,128)(2,1)}, bf16[8,1792]{1,0:T(8,128)(2,1)S(1)}, u32[]{:S(2)}, u32[]{:S(2)}) collective-permute-start(bf16[8,1792]{1,0:T(8,128)(2,1)} %get-tuple-element.23), channel_id=1, source_target_pairs={{0,2},{1,3},{2,0},{3,1},{4,6},{5,7},{6,4},{7,5},{8,10},{9,11},{10,... | collective-permute-start | bytes 86024 | tf_op jit(solution)/shard_map/ppermute | solution.py:17
  170.0 5.6 %collective-permute-start.25 = (bf16[8,1792]{1,0:T(8,128)(2,1)}, bf16[8,1792]{1,0:T(8,128)(2,1)S(1)}, u32[]{:S(2)}, u32[]{:S(2)}) collective-permute-start(bf16[8,1792]{1,0:T(8,128)(2,1)} %get-tuple-element.24), channel_id=1, source_target_pairs={{0,1},{1,2},{2,3},{3,0},{4,5},{5,6},{6,7},{7,4},{8,9},{9,10},{10,1... | collective-permute-start | bytes 86024 | tf_op jit(solution)/shard_map/ppermute | solution.py:17
  172.4 3.2 %copy-start.5 = (bf16[8,1792]{1,0:T(8,128)(2,1)}, bf16[8,1792]{1,0:T(8,128)(2,1)S(1)}, u32[]{:S(2)}) copy-start(bf16[8,1792]{1,0:T(8,128)(2,1)S(1)} %collective-permute-done.23.refs_1_) | copy-start | bytes 86020
  175.6 0.6 copy-start.6
  175.6 0.6 copy-start.7

commit v3 on v2

v3 whole, which is shorter than its diff:
```python
import jax
import jax.numpy as jnp
from jax import lax
from jax.experimental import pallas as pl
from jax.experimental.pallas import tpu as pltpu
from jax.sharding import PartitionSpec as P

ROUTE_SCALE = 2.5
EPSILON = 1e-06
PAD = 128
RING = 4


def attn_pairs(stage, step):
    pairs = []
    for y in range(RING):
        for z in range(RING):
            for core in range(2):
                to = [y, z, core]
                if stage == "core":
                    to[2] = 1 - core
                else:
                    axis = stage if core == 0 else 1 - stage
                    to[axis] = (to[axis] + step) % RING
                pairs.append(((y * RING + z) * 2 + core, (to[0] * RING + to[1]) * 2 + to[2]))
    return pairs


def move(value, axis, step):
    if axis == "x":
        return lax.ppermute(value, "exp", [(i, (i + step) % RING) for i in range(RING)])
    return lax.ppermute(value, "attn", attn_pairs(axis, step))


def direct(chunks, axis):
    return [chunks[0], move(chunks[3], axis, -1), move(chunks[2], axis, 2), move(chunks[1], axis, 1)]


def gather_ring(value, axis):
    half = value.shape[0] // 2
    low = move(value, axis, 1)
    high = move(value, axis, -1)
    first = move(low[:half], axis, 1)
    second = move(high[half:], axis, -1)
    return [value, high, first, second, low]


def add(one, other):
    return (one.astype(jnp.float32) + other.astype(jnp.float32)).astype(jnp.bfloat16)


def scatter_ring(chunks, axis):
    half = chunks[2].shape[0] // 2
    first = move(chunks[2][:half], axis, 1)
    second = move(chunks[2][half:], axis, -1)
    up = jnp.concatenate([add(chunks[1][:half], first), chunks[1][half:]], axis=0)
    down = jnp.concatenate([chunks[3][:half], add(chunks[3][half:], second)], axis=0)
    low = move(up, axis, 1)
    high = move(down, axis, -1)
    total = chunks[0].astype(jnp.float32) + low.astype(jnp.float32) + high.astype(jnp.float32)
    return total.astype(jnp.bfloat16)


def prepare_kernel(place_ref, hidden_ref, gain_ref, routes_ref, scores_ref, capacity_ref, *out_refs):
    rows, top = routes_ref.shape
    experts = capacity_ref.shape[1]
    width = out_refs[0].shape[1] - PAD
    hidden = hidden_ref[...].astype(jnp.float32)
    scale = lax.rsqrt(jnp.mean(hidden * hidden, axis=1, keepdims=True) + EPSILON)
    routes = routes_ref[...]
    scores = scores_ref[...]
    weights = ROUTE_SCALE * scores / jnp.sum(scores, axis=1, keepdims=True)
    lane = lax.broadcasted_iota(jnp.int32, (rows, PAD), 1)
    named = lax.rem(lane, experts)
    match = jnp.zeros((rows, PAD), jnp.float32)
    weight = jnp.zeros((rows, PAD), jnp.float32)
    for k in range(top):
        same = routes[:, k : k + 1] == named
        match = jnp.where(same, 1.0, match)
        weight = jnp.where(same, weights[:, k : k + 1], weight)
    row = lax.broadcasted_iota(jnp.int32, (rows, PAD), 0)
    rank = jnp.zeros((rows, PAD), jnp.float32)
    for j in range(rows):
        later = (row > j) & (row < (j // 4 + 1) * 4)
        rank = rank + jnp.where(later, match[j : j + 1, :], 0.0)
    spread = (
        lax.broadcasted_iota(jnp.int32, (experts, PAD), 0)
        == lax.rem(lax.broadcasted_iota(jnp.int32, (experts, PAD), 1), experts)
    ).astype(jnp.float32)
    limit = jnp.broadcast_to(capacity_ref[...].astype(jnp.float32), (8, experts))
    limit = jnp.dot(limit, spread, preferred_element_type=jnp.float32)[0:1]
    kept = (match > 0.0) & (rank < limit)
    high = weight.astype(jnp.bfloat16).astype(jnp.float32)
    group = lane // experts
    value = jnp.where(group == 0, rank + 1.0, jnp.where(group == 1, high, weight - high))
    columns = jnp.where(kept & (group < 3), value, 0.0).astype(jnp.bfloat16)
    for r in range(RING):
        start = pl.multiple_of(lax.rem(place_ref[0] + r, RING) * width, PAD)
        part = hidden_ref[:, pl.ds(start, width)].astype(jnp.float32) * scale * gain_ref[:, pl.ds(start, width)]
        out_refs[r][:, :width] = part.astype(jnp.bfloat16)
        out_refs[r][:, width:] = columns


def finish_kernel(place_ref, hidden_ref, *refs):
    out_ref = refs[-1]
    width = refs[0].shape[1]
    for r in range(RING):
        start = pl.multiple_of(lax.rem(place_ref[0] + r, RING) * width, PAD)
        total = hidden_ref[:, pl.ds(start, width)].astype(jnp.float32) + refs[r][...].astype(jnp.float32)
        out_ref[:, pl.ds(start, width)] = total.astype(jnp.bfloat16)


def join_kernel(*refs):
    refs[-1][...] = jnp.concatenate([ref[...].astype(jnp.float32) for ref in refs[:-1]], axis=0).astype(jnp.bfloat16)


def join(pieces):
    vmem = pl.BlockSpec(memory_space=pltpu.VMEM)
    rows = sum(piece.shape[0] for piece in pieces)
    return pl.pallas_call(
        join_kernel,
        out_shape=jax.ShapeDtypeStruct((rows, pieces[0].shape[1]), jnp.bfloat16),
        in_specs=[vmem] * len(pieces),
        out_specs=vmem,
        name="join",
    )(*pieces)


def specs(count):
    return [pl.BlockSpec(memory_space=pltpu.SMEM)] + [pl.BlockSpec(memory_space=pltpu.VMEM)] * count


def choose(picks, expert):
    lanes = jnp.arange(PAD)[None, :]
    code = jnp.sum(jnp.where(lanes == expert, picks, 0.0), axis=1)
    rows = picks.shape[0]
    per = rows // 16
    row = jnp.arange(rows, dtype=jnp.int32)
    slot = jnp.arange(rows // 2, dtype=jnp.int32)
    block = row % 32 // 8 * per + row // 32 * 2 + row % 8 // 4
    chosen = (block[:, None] == slot[None, :] // 2) & (
        code.astype(jnp.int32)[:, None] == (slot % 2 + 1)[None, :]
    )
    return chosen.astype(jnp.bfloat16)


def pick(chosen, rows):
    return lax.dot_general(
        chosen, rows, (((0,), (0,)), ((), ())), preferred_element_type=jnp.float32
    ).astype(jnp.bfloat16)


def shards(hidden, norm_gain, routes, route_scores, capacity, w_gate, w_up, w_down):
    experts = capacity.shape[0]
    expert = lax.axis_index("attn")
    other = expert + 1 - 2 * (expert % 2)
    place = lax.axis_index("exp").astype(jnp.int32).reshape(1)
    width = w_gate.shape[1]
    rows = hidden.shape[0]
    blocks = pl.pallas_call(
        prepare_kernel,
        out_shape=[jax.ShapeDtypeStruct((rows, width + PAD), jnp.bfloat16)] * RING,
        in_specs=specs(5),
        out_specs=[pl.BlockSpec(memory_space=pltpu.VMEM)] * RING,
        name="prepare",
    )(place, hidden, norm_gain.reshape(1, -1), routes, route_scores, capacity.reshape(1, -1))
    lines = join(direct(blocks, "x"))
    lines = join(direct([lines] * RING, 0))
    lines = jnp.concatenate(gather_ring(lines, 1), axis=0)
    picks = lines[:, width:].astype(jnp.float32)
    chosen_own = choose(picks, expert)
    chosen_other = choose(picks, other)
    picked = [move(pick(chosen_other, lines), "core", 1), pick(chosen_own, lines)]
    lane = jnp.arange(PAD)[None, :]
    mine = (lane == expert + experts) | (lane == expert + 2 * experts)
    parts, scales = [], []
    for chunk in range(2):
        slots = picked[chunk]
        if chunk == 1:
            slots, *parts[0][0:2] = lax.optimization_barrier((slots, *parts[0][0:2]))
        scales.append(jnp.sum(jnp.where(mine, slots[:, width:].astype(jnp.float32), 0.0), axis=1))
        slots = slots[:, :width]
        gate = jnp.dot(slots, w_gate[0], preferred_element_type=jnp.float32).astype(jnp.bfloat16)
        up = jnp.dot(slots, w_up[0], preferred_element_type=jnp.float32).astype(jnp.bfloat16)
        part = slots.shape[0] // RING
        gate = [gate[r * part : (r + 1) * part] for r in range(RING)]
        up = [up[r * part : (r + 1) * part] for r in range(RING)]
        gate_far = move(gate[2], "x", 1)
        up_far = move(up[2], "x", -1)
        up_low = move(up[1], "x", 1)
        gate_high = move(gate[3], "x", -1)
        parts.append([gate_far, up_far, up_low, gate_high, gate, up])
    out = []
    for chunk in range(2):
        gate_far, up_far, up_low, gate_high, gate, up = parts[chunk]
        gate_low = move(add(gate[1], gate_far), "x", 1)
        up_high = move(add(up[3], up_far), "x", -1)
        if chunk == 0:
            gate_low, parts[1][4][0] = lax.optimization_barrier((gate_low, parts[1][4][0]))
            up_high, parts[1][5][0] = lax.optimization_barrier((up_high, parts[1][5][0]))
        gate_sum = gate[0].astype(jnp.float32) + gate_low.astype(jnp.float32) + gate_high.astype(jnp.float32)
        up_sum = up[0].astype(jnp.float32) + up_low.astype(jnp.float32) + up_high.astype(jnp.float32)
        activation = (jax.nn.silu(gate_sum) * up_sum).astype(jnp.bfloat16)
        activation = jnp.concatenate(gather_ring(activation, "x"), axis=0)
        expert_out = jnp.dot(activation, w_down[0], preferred_element_type=jnp.float32)
        expert_out = (expert_out * scales[chunk][:, None]).astype(jnp.bfloat16)
        out.append(move(expert_out, "core", 1) if chunk == 0 else expert_out)
    returned = jnp.concatenate(out, axis=0)
    chosen = jnp.concatenate([chosen_other, chosen_own], axis=1)
    summed = jnp.dot(chosen, returned, preferred_element_type=jnp.float32).astype(jnp.bfloat16)
    part = summed.shape[0] // RING
    summed = scatter_ring([summed[r * part : (r + 1) * part] for r in range(RING)], 1)
    part = part // RING
    pieces = direct([summed[r * part : (r + 1) * part] for r in range(RING)], 0)
    summed = sum(piece.astype(jnp.float32) for piece in pieces).astype(jnp.bfloat16)
    back = direct([summed[r * rows : (r + 1) * rows] for r in range(RING)], "x")
    return pl.pallas_call(
        finish_kernel,
        out_shape=jax.ShapeDtypeStruct(hidden.shape, jnp.bfloat16),
        in_specs=specs(1 + RING),
        out_specs=pl.BlockSpec(memory_space=pltpu.VMEM),
        name="finish",
    )(place, hidden, *back)


def solution(mesh):
    in_specs = (
        P(("attn", "exp"), None),
        P(),
        P(("attn", "exp"), None),
        P(("attn", "exp"), None),
        P(),
        P("attn", "exp", None),
        P("attn", "exp", None),
        P("attn", None, "exp"),
    )
    out_specs = P(("attn", "exp"), None)
    return jax.shard_map(shards, mesh=mesh, in_specs=in_specs, out_specs=out_specs, check_vma=False)
```

time: 179 us -> 171 us (0.955)
  waiting for transfers between devices: 61.3 us -> 75.3 us
  matrix products: 33.3 us -> 19.5 us
  local copies, waits for them, and re-layouts: 9.27 us -> 4.24 us
  other arithmetic: 4.42 us -> 1.89 us
  Pallas kernels: 9.06 us -> 6.75 us
  starting transfers between devices: 60.1 us -> 62.4 us
    ppermute x0 -> x16, waiting for transfers between devices: none -> 36.3 us  [move(): return lax.ppermute(value, 'attn', attn_pairs(axis, step))]
    all_to_all x4 -> x0, waiting for transfers between devices: 34.7 us -> none  [swap(): lax.all_to_all(value, 'attn', split_axis=0, concat_axis=0, tiled=True)]
    ppermute x0 -> x16, starting transfers between devices: none -> 24.9 us  [move(): return lax.ppermute(value, 'attn', attn_pairs(axis, step))]
    all_to_all x4 -> x0, starting transfers between devices: 24.3 us -> none  [swap(): lax.all_to_all(value, 'attn', split_axis=0, concat_axis=0, tiled=True)]
    dot_general x6 -> x9, matrix products: 33.3 us -> 19.5 us  [the longest x2 7.31 us: shards(): jnp.dot(slots, w_up[0], preferred_element_type=jnp.float32)]
    ppermute x26, waiting for transfers between devices: 26.6 us -> 38.9 us  [move(): lax.ppermute(value, 'exp', [(i, (i + step) % RING) for i in range(RING)])]
    slice x8 -> x13, local copies, waits for them, and re-layouts: 5.75 us -> 1 us  [the longest x1 0.62 us: shards(): back = direct([summed[r * rows:(r + 1) * rows] for r in range(RING)], 'x')]
    pallas_call x2, Pallas kernels: 5.68 us -> 3.36 us  [join(): pl.pallas_call(join_kernel, out_shape=jax.ShapeDtypeStruct((rows, pieces[...]
  transfers between devices with their start and end apart: 30 -> 42, of which waited for: 13 -> 25; matrix products, arithmetic and copies ran while one was open for 25% -> 8% of each run, Pallas kernels for 0% -> 0%
where the time goes in v3:
time: 171 us
  waiting for transfers between devices  75.3 us (44%)
  starting transfers between devices  62.4 us (36%)
  matrix products  19.5 us (11%)
  Pallas kernels  6.75 us (4%)
  local copies, waits for them, and re-layouts  4.24 us (2%)
  other arithmetic  1.89 us (1%)
    ppermute x26, waiting for transfers between devices, move(): lax.ppermute(value, 'exp', [(i, (i + step) % RING) for i in range(RING)])  38.9 us
    ppermute x26, starting transfers between devices, move(): lax.ppermute(value, 'exp', [(i, (i + step) % RING) for i in range(RING)])  37.5 us
    ppermute x16, waiting for transfers between devices, move(): return lax.ppermute(value, 'attn', attn_pairs(axis, step))  36.3 us
    ppermute x16, starting transfers between devices, move(): return lax.ppermute(value, 'attn', attn_pairs(axis, step))  24.9 us
    dot_general x2, matrix products, shards(): jnp.dot(slots, w_up[0], preferred_element_type=jnp.float32)  7.31 us
    dot_general x2, matrix products, shards(): jnp.dot(activation, w_down[0], preferred_element_type=jnp.float32)  4.19 us
    dot_general x2, matrix products, shards(): jnp.dot(slots, w_gate[0], preferred_element_type=jnp.float32)  4.12 us
  transfers between devices with their start and end apart: 42, of which 25 were waited for; matrix products, arithmetic and copies ran while one was open for 8% of the time, Pallas kernels for 0%

profile of v3, /device:TPU:0, one launch (start us, length us, event | category | flops | bytes accessed | tf_op | source)
XLA Modules:
  0.0 170.5 jit_solution(9104459564061086388)
XLA Ops:
  0.0 1.8 %prepare.1 = (bf16[8,1920]{1,0:T(8,128)(2,1)}, bf16[8,1920]{1,0:T(8,128)(2,1)}, bf16[8,1920]{1,0:T(8,128)(2,1)}, bf16[8,1920]{1,0:T(8,128)(2,1)}) custom-call(s32[1]{0:T(128)} %bitcast.place_ref, bf16[8,7168]{1,0:T(8,128)(2,1)} %hidden_ref.3, f32[1,7168]{1,0:T(1,128)} %bitcast.38, s32[8,8]{1,0:T(8,128)} %routes_ref.1, f32[8,8]{1,0:T(8,128)} %scores_ref.1, ...), custom_call_target="tpu_custom_call" | custom-call | tf_op jit(solution)/shard_map/prepare/pallas_call | solution.py:160
  1.8 2.8 %collective-permute-start = (bf16[8,1920]{1,0:T(8,128)(2,1)}, bf16[8,1920]{1,0:T(8,128)(2,1)S(1)}, u32[]{:S(2)}, u32[]{:S(2)}) collective-permute-start(bf16[8,1920]{1,0:T(8,128)(2,1)} %get-tuple-element.17), channel_id=1, source_target_pairs={{0,3},{1,0},{2,1},{3,2},{4,7},{5,4},{6,5},{7,6},{8,11},{9,8},{10,9... | collective-permute-start | bytes 92168 | tf_op jit(solution)/shard_map/ppermute | solution.py:31
  6.4 3.8 %collective-permute-done.1.refs_2_ = bf16[8,1920]{1,0:T(8,128)(2,1)S(1)} collective-permute-done((bf16[8,1920]{1,0:T(8,128)(2,1)}, bf16[8,1920]{1,0:T(8,128)(2,1)S(1)}, u32[]{:S(2)}, u32[]{:S(2)}) %collective-permute-start.1) | collective-permute-done | bytes 30752 | tf_op jit(solution)/shard_map/ppermute | solution.py:31
  11.3 1.5 join.2.refs_0_
  12.8 1.6 collective-permute-start.5
  14.4 2.9 %collective-permute-start.4 = (bf16[32,1920]{1,0:T(8,128)(2,1)}, bf16[32,1920]{1,0:T(8,128)(2,1)S(1)}, u32[]{:S(2)}, u32[]{:S(2)}) collective-permute-start(bf16[32,1920]{1,0:T(8,128)(2,1)} %join.2.refs_0_), channel_id=1, source_target_pairs={{0,64},{4,20},{8,72},{12,28},{16,80},{20,4},{24,88},{28,12},{32,96... | collective-permute-start | bytes 368648 | tf_op jit(solution)/shard_map/ppermute | solution.py:32
  19.1 2.6 %collective-permute-done.4.refs_2_ = bf16[32,1920]{1,0:T(8,128)(2,1)S(1)} collective-permute-done((bf16[32,1920]{1,0:T(8,128)(2,1)}, bf16[32,1920]{1,0:T(8,128)(2,1)S(1)}, u32[]{:S(2)}, u32[]{:S(2)}) %collective-permute-start.4) | collective-permute-done | bytes 122912 | tf_op jit(solution)/shard_map/ppermute | solution.py:32
  23.0 1.9 %join.3 = bf16[128,1920]{1,0:T(8,128)(2,1)} custom-call(bf16[32,1920]{1,0:T(8,128)(2,1)} %join.2.refs_0_, bf16[32,1920]{1,0:T(8,128)(2,1)} %copy-done.2, bf16[32,1920]{1,0:T(8,128)(2,1)} %copy-done.1, bf16[32,1920]{1,0:T(8,128)(2,1)} %copy-done), custom_call_target="tpu_custom_call" | custom-call | tf_op jit(solution)/shard_map/join/pallas_call | solution.py:120
  24.9 1.9 %collective-permute-start.7 = (bf16[128,1920]{1,0:T(8,128)(2,1)}, bf16[128,1920]{1,0:T(8,128)(2,1)S(1)}, u32[]{:S(2)}, u32[]{:S(2)}) collective-permute-start(bf16[128,1920]{1,0:T(8,128)(2,1)} %join.3), channel_id=1, source_target_pairs={{0,8},{4,36},{8,16},{12,44},{16,24},{20,52},{24,0},{28,60},{32,40}... | collective-permute-start | bytes 1474568 | tf_op jit(solution)/shard_map/ppermute | solution.py:32
  26.8 2.1 %collective-permute-start.6 = (bf16[128,1920]{1,0:T(8,128)(2,1)}, bf16[128,1920]{1,0:T(8,128)(2,1)S(1)}, u32[]{:S(2)}, u32[]{:S(2)}) collective-permute-start(bf16[128,1920]{1,0:T(8,128)(2,1)} %join.3), channel_id=1, source_target_pairs={{0,24},{4,100},{8,0},{12,108},{16,8},{20,116},{24,16},{28,124},{32... | collective-permute-start | bytes 1474568 | tf_op jit(solution)/shard_map/ppermute | solution.py:32
  29.0 7.0 %collective-permute-done.7 = bf16[128,1920]{1,0:T(8,128)(2,1)S(1)} collective-permute-done((bf16[128,1920]{1,0:T(8,128)(2,1)}, bf16[128,1920]{1,0:T(8,128)(2,1)S(1)}, u32[]{:S(2)}, u32[]{:S(2)}) %collective-permute-start.7) | collective-permute-done | bytes 491552 | tf_op jit(solution)/shard_map/ppermute | solution.py:32
  37.2 3.3 %collective-permute-start.9 = (bf16[64,1920]{1,0:T(8,128)(2,1)S(1)}, bf16[64,1920]{1,0:T(8,128)(2,1)S(1)}, u32[]{:S(2)}, u32[]{:S(2)}) collective-permute-start(bf16[64,1920]{1,0:T(8,128)(2,1)S(1)} %slice.178), channel_id=1, source_target_pairs={{0,24},{4,100},{8,0},{12,108},{16,8},{20,116},{24,16},{28,124},{32... | collective-permute-start | bytes 737288 | tf_op jit(solution)/shard_map/ppermute | solution.py:32
  40.5 2.9 %collective-permute-done.8 = bf16[64,1920]{1,0:T(8,128)(2,1)S(1)} collective-permute-done((bf16[64,1920]{1,0:T(8,128)(2,1)S(1)}, bf16[64,1920]{1,0:T(8,128)(2,1)S(1)}, u32[]{:S(2)}, u32[]{:S(2)}) %collective-permute-start.8) | collective-permute-done | bytes 245792 | tf_op jit(solution)/shard_map/ppermute | solution.py:32
  44.4 1.9 %convolution_convert_fusion.2 = bf16[256,1920]{1,0:T(8,128)(2,1)} fusion(bf16[512,1920]{1,0:T(8,128)(2,1)S(1)} %constant_dynamic-update-slice_fusion, s32[256]{0:T(256)S(1)} %get-tuple-element.63, s32[256]{0:T(256)S(1)} %get-tuple-element.62, s32[512]{0:T(512)S(1)} %convert_element_type.176, s32[512]{0:T(512)S(1)} %fusion.59), kind=kOutput, calls=%fused_computation.20 | convolution fusion | flops 504201216 | bytes 2955264 | tf_op jit(solution)/shard_map/dot_general | solution.py:148
  46.4 2.7 %collective-permute-done.10 = bf16[256,1920]{1,0:T(8,128)(2,1)S(1)} collective-permute-done((bf16[256,1920]{1,0:T(8,128)(2,1)}, bf16[256,1920]{1,0:T(8,128)(2,1)S(1)}, u32[]{:S(2)}, u32[]{:S(2)}) %collective-permute-start.10) | collective-permute-done | bytes 983072 | tf_op jit(solution)/shard_map/ppermute | solution.py:32
  49.1 5.2 %fusion.24 = bf16[256,2048]{1,0:T(8,128)(2,1)S(1)} fusion(bf16[1,1792,2048]{2,1,0:T(8,128)(2,1)} %param.14, bf16[256,1920]{1,0:T(8,128)(2,1)S(1)} %collective-permute-done.10), kind=kOutput, calls=%fused_computation.17 | convolution fusion | flops 1879572480 | bytes 9306112 | tf_op jit(solution)/shard_map/dot_general | solution.py:184
  54.9 2.1 %fusion.18 = bf16[256,2048]{1,0:T(8,128)(2,1)S(1)} fusion(bf16[1,1792,2048]{2,1,0:T(8,128)(2,1)S(1)} %bitcast.43, bf16[256,1920]{1,0:T(8,128)(2,1)S(1)} %collective-permute-done.10), kind=kOutput, calls=%fused_computation.15 | convolution fusion | flops 1879572480 | bytes 9306112 | tf_op jit(solution)/shard_map/dot_general | solution.py:183
  57.0 1.7 %collective-permute-start.11 = (bf16[64,2048]{1,0:T(8,128)(2,1)S(1)}, bf16[64,2048]{1,0:T(8,128)(2,1)S(1)}, u32[]{:S(2)}, u32[]{:S(2)}) collective-permute-start(bf16[64,2048]{1,0:T(8,128)(2,1)S(1)} %get-tuple-element.42), channel_id=1, source_target_pairs={{0,1},{1,2},{2,3},{3,0},{4,5},{5,6},{6,7},{7,4},{8,9},{9,10},{10,1... | collective-permute-start | bytes 786440 | tf_op jit(solution)/shard_map/ppermute | solution.py:31
  60.0 3.2 %collective-permute-start.14 = (bf16[64,2048]{1,0:T(8,128)(2,1)S(1)}, bf16[64,2048]{1,0:T(8,128)(2,1)S(1)}, u32[]{:S(2)}, u32[]{:S(2)}) collective-permute-start(bf16[64,2048]{1,0:T(8,128)(2,1)S(1)} %get-tuple-element.41), channel_id=1, source_target_pairs={{0,3},{1,0},{2,1},{3,2},{4,7},{5,4},{6,5},{7,6},{8,11},{9,8},{10,9... | collective-permute-start | bytes 786440 | tf_op jit(solution)/shard_map/ppermute | solution.py:31
  63.2 4.2 %collective-permute-done.11 = bf16[64,2048]{1,0:T(8,128)(2,1)S(1)} collective-permute-done((bf16[64,2048]{1,0:T(8,128)(2,1)S(1)}, bf16[64,2048]{1,0:T(8,128)(2,1)S(1)}, u32[]{:S(2)}, u32[]{:S(2)}) %collective-permute-start.11) | collective-permute-done | bytes 262176 | tf_op jit(solution)/shard_map/ppermute | solution.py:31
  67.5 2.1 %fusion.27 = bf16[256,2048]{1,0:T(8,128)(2,1)S(1)} fusion(bf16[1,1792,2048]{2,1,0:T(8,128)(2,1)S(1)} %bitcast.41, bf16[256,1920]{1,0:T(8,128)(2,1)S(1)} %convolution_convert_fusion.1), kind=kOutput, calls=%fused_computation.18 | convolution fusion | flops 1879572480 | bytes 9306112 | tf_op jit(solution)/shard_map/dot_general | solution.py:184
  69.6 2.1 %fusion.21 = bf16[256,2048]{1,0:T(8,128)(2,1)S(1)} fusion(bf16[1,1792,2048]{2,1,0:T(8,128)(2,1)S(1)} %bitcast.43, bf16[256,1920]{1,0:T(8,128)(2,1)S(1)} %convolution_convert_fusion.1), kind=kOutput, calls=%fused_computation.16 | convolution fusion | flops 1879572480 | bytes 9306112 | tf_op jit(solution)/shard_map/dot_general | solution.py:183
  72.4 1.5 collective-permute-start.13
  74.7 7.5 %collective-permute-done.13 = bf16[64,2048]{1,0:T(8,128)(2,1)S(1)} collective-permute-done((bf16[64,2048]{1,0:T(8,128)(2,1)S(1)}, bf16[64,2048]{1,0:T(8,128)(2,1)S(1)}, u32[]{:S(2)}, u32[]{:S(2)}) %collective-permute-start.13) | collective-permute-done | bytes 262176 | tf_op jit(solution)/shard_map/ppermute | solution.py:31
  82.1 1.4 collective-permute-start.26
  83.5 1.4 collective-permute-done.22
  86.1 8.8 %collective-permute-done.26 = bf16[64,2048]{1,0:T(8,128)(2,1)S(1)} collective-permute-done((bf16[64,2048]{1,0:T(8,128)(2,1)S(1)}, bf16[64,2048]{1,0:T(8,128)(2,1)S(1)}, u32[]{:S(2)}, u32[]{:S(2)}) %collective-permute-start.26) | collective-permute-done | bytes 262176 | tf_op jit(solution)/shard_map/ppermute | solution.py:31
  95.1 3.1 %collective-permute-start.27 = (bf16[64,2048]{1,0:T(8,128)(2,1)S(1)}, bf16[64,2048]{1,0:T(8,128)(2,1)S(1)}, u32[]{:S(2)}, u32[]{:S(2)}) collective-permute-start(bf16[64,2048]{1,0:T(8,128)(2,1)S(1)} %add_convert_fusion.1), channel_id=1, source_target_pairs={{0,3},{1,0},{2,1},{3,2},{4,7},{5,4},{6,5},{7,6},{8,11},{9,8},{10,9... | collective-permute-start | bytes 786440 | tf_op jit(solution)/shard_map/ppermute | solution.py:31
  98.6 3.2 %collective-permute-start.17 = (bf16[64,2048]{1,0:T(8,128)(2,1)S(1)}, bf16[64,2048]{1,0:T(8,128)(2,1)S(1)}, u32[]{:S(2)}, u32[]{:S(2)}) collective-permute-start(bf16[64,2048]{1,0:T(8,128)(2,1)S(1)} %get-tuple-element.32), channel_id=1, source_target_pairs={{0,3},{1,0},{2,1},{3,2},{4,7},{5,4},{6,5},{7,6},{8,11},{9,8},{10,9... | collective-permute-start | bytes 786440 | tf_op jit(solution)/shard_map/ppermute | solution.py:31
  101.8 2.9 %collective-permute-done.23 = bf16[64,2048]{1,0:T(8,128)(2,1)S(1)} collective-permute-done((bf16[64,2048]{1,0:T(8,128)(2,1)S(1)}, bf16[64,2048]{1,0:T(8,128)(2,1)S(1)}, u32[]{:S(2)}, u32[]{:S(2)}) %collective-permute-start.23) | collective-permute-done | bytes 262176 | tf_op jit(solution)/shard_map/ppermute | solution.py:31
  105.1 3.2 %collective-permute-start.28 = (bf16[64,2048]{1,0:T(8,128)(2,1)S(1)}, bf16[64,2048]{1,0:T(8,128)(2,1)S(1)}, u32[]{:S(2)}, u32[]{:S(2)}) collective-permute-start(bf16[64,2048]{1,0:T(8,128)(2,1)S(1)} %get-tuple-element.34), channel_id=1, source_target_pairs={{0,3},{1,0},{2,1},{3,2},{4,7},{5,4},{6,5},{7,6},{8,11},{9,8},{10,9... | collective-permute-start | bytes 786440 | tf_op jit(solution)/shard_map/ppermute | solution.py:31
  108.5 3.3 %collective-permute-start.20 = (bf16[32,2048]{1,0:T(8,128)(2,1)S(1)}, bf16[32,2048]{1,0:T(8,128)(2,1)S(1)}, u32[]{:S(2)}, u32[]{:S(2)}) collective-permute-start(bf16[32,2048]{1,0:T(8,128)(2,1)S(1)} %slice.192), channel_id=1, source_target_pairs={{0,3},{1,0},{2,1},{3,2},{4,7},{5,4},{6,5},{7,6},{8,11},{9,8},{10,9... | collective-permute-start | bytes 393224 | tf_op jit(solution)/shard_map/ppermute | solution.py:31
  111.8 2.8 %collective-permute-done.19 = bf16[32,2048]{1,0:T(8,128)(2,1)S(1)} collective-permute-done((bf16[32,2048]{1,0:T(8,128)(2,1)S(1)}, bf16[32,2048]{1,0:T(8,128)(2,1)S(1)}, u32[]{:S(2)}, u32[]{:S(2)}) %collective-permute-start.19) | collective-permute-done | bytes 131104 | tf_op jit(solution)/shard_map/ppermute | solution.py:31
  114.7 2.1 %fusion.33 = bf16[256,1792]{1,0:T(8,128)(2,1)S(1)} fusion(bf16[256,2048]{1,0:T(8,128)(2,1)S(1)} %constant_dynamic-update-slice_fusion.5, bf16[1,2048,1792]{2,1,0:T(8,128)(2,1)S(1)} %bitcast.45, f32[256]{0:T(256)S(1)} %get-tuple-element.29), kind=kOutput, calls=%fused_computation.22 | convolution fusion | flops 1879965696 | bytes 9307136 | tf_op jit(solution)/shard_map/dot_general | solution.py:205
  117.8 2.8 %collective-permute-start.31 = (bf16[32,2048]{1,0:T(8,128)(2,1)S(1)}, bf16[32,2048]{1,0:T(8,128)(2,1)S(1)}, u32[]{:S(2)}, u32[]{:S(2)}) collective-permute-start(bf16[32,2048]{1,0:T(8,128)(2,1)S(1)} %slice.201), channel_id=1, source_target_pairs={{0,3},{1,0},{2,1},{3,2},{4,7},{5,4},{6,5},{7,6},{8,11},{9,8},{10,9... | collective-permute-start | bytes 393224 | tf_op jit(solution)/shard_map/ppermute | solution.py:31
  120.6 4.0 %collective-permute-done.30 = bf16[32,2048]{1,0:T(8,128)(2,1)S(1)} collective-permute-done((bf16[32,2048]{1,0:T(8,128)(2,1)S(1)}, bf16[32,2048]{1,0:T(8,128)(2,1)S(1)}, u32[]{:S(2)}, u32[]{:S(2)}) %collective-permute-start.30) | collective-permute-done | bytes 131104 | tf_op jit(solution)/shard_map/ppermute | solution.py:31
  124.7 2.1 %fusion.30 = bf16[256,1792]{1,0:T(8,128)(2,1)S(1)} fusion(bf16[256,2048]{1,0:T(8,128)(2,1)S(1)} %constant_dynamic-update-slice_fusion.10, bf16[1,2048,1792]{2,1,0:T(8,128)(2,1)S(1)} %bitcast.45, f32[256]{0:T(256)S(1)} %get-tuple-element.30), kind=kOutput, calls=%fused_computation.21 | convolution fusion | flops 1879965696 | bytes 9307136 | tf_op jit(solution)/shard_map/dot_general | solution.py:205
  129.2 2.7 %collective-permute-start.34 = (bf16[64,1792]{1,0:T(8,128)(2,1)S(1)}, bf16[64,1792]{1,0:T(8,128)(2,1)S(1)}, u32[]{:S(2)}, u32[]{:S(2)}) collective-permute-start(bf16[64,1792]{1,0:T(8,128)(2,1)S(1)} %get-tuple-element.38), channel_id=1, source_target_pairs={{0,24},{4,100},{8,0},{12,108},{16,8},{20,116},{24,16},{28,124},{32... | collective-permute-start | bytes 688136 | tf_op jit(solution)/shard_map/ppermute | solution.py:32
  132.0 3.9 %collective-permute-done.32 = bf16[64,1792]{1,0:T(8,128)(2,1)S(1)} collective-permute-done((bf16[64,1792]{1,0:T(8,128)(2,1)S(1)}, bf16[64,1792]{1,0:T(8,128)(2,1)S(1)}, u32[]{:S(2)}, u32[]{:S(2)}) %collective-permute-start.32) | collective-permute-done | bytes 229408 | tf_op jit(solution)/shard_map/ppermute | solution.py:32
  136.0 3.4 %collective-permute-start.35 = (bf16[128,1792]{1,0:T(8,128)(2,1)S(1)}, bf16[128,1792]{1,0:T(8,128)(2,1)S(1)}, u32[]{:S(2)}, u32[]{:S(2)}) collective-permute-start(bf16[128,1792]{1,0:T(8,128)(2,1)S(1)} %pad_maximum_fusion.1), channel_id=1, source_target_pairs={{0,24},{4,100},{8,0},{12,108},{16,8},{20,116},{24,16},{28,124},{32... | collective-permute-start | bytes 1376264 | tf_op jit(solution)/shard_map/ppermute | solution.py:32
  139.5 5.9 %collective-permute-done.35 = bf16[128,1792]{1,0:T(8,128)(2,1)S(1)} collective-permute-done((bf16[128,1792]{1,0:T(8,128)(2,1)S(1)}, bf16[128,1792]{1,0:T(8,128)(2,1)S(1)}, u32[]{:S(2)}, u32[]{:S(2)}) %collective-permute-start.35) | collective-permute-done | bytes 458784 | tf_op jit(solution)/shard_map/ppermute | solution.py:32
  145.4 3.8 %collective-permute-done.33 = bf16[128,1792]{1,0:T(8,128)(2,1)S(1)} collective-permute-done((bf16[128,1792]{1,0:T(8,128)(2,1)S(1)}, bf16[128,1792]{1,0:T(8,128)(2,1)S(1)}, u32[]{:S(2)}, u32[]{:S(2)}) %collective-permute-start.33) | collective-permute-done | bytes 458784 | tf_op jit(solution)/shard_map/ppermute | solution.py:32
  149.5 2.6 %collective-permute-start.36 = (bf16[32,1792]{1,0:T(8,128)(2,1)S(1)}, bf16[32,1792]{1,0:T(8,128)(2,1)S(1)}, u32[]{:S(2)}, u32[]{:S(2)}) collective-permute-start(bf16[32,1792]{1,0:T(8,128)(2,1)S(1)} %get-tuple-element.51), channel_id=1, source_target_pairs={{0,96},{4,28},{8,104},{12,4},{16,112},{20,12},{24,120},{28,20},{32... | collective-permute-start | bytes 344072 | tf_op jit(solution)/shard_map/ppermute | solution.py:32
  152.0 1.6 collective-permute-start.37
  154.4 4.9 %collective-permute-done.38 = bf16[32,1792]{1,0:T(8,128)(2,1)S(1)} collective-permute-done((bf16[32,1792]{1,0:T(8,128)(2,1)S(1)}, bf16[32,1792]{1,0:T(8,128)(2,1)S(1)}, u32[]{:S(2)}, u32[]{:S(2)}) %collective-permute-start.38) | collective-permute-done | bytes 114720 | tf_op jit(solution)/shard_map/ppermute | solution.py:32
  161.1 3.3 %collective-permute-start.40 = (bf16[8,1792]{1,0:T(8,128)(2,1)S(1)}, bf16[8,1792]{1,0:T(8,128)(2,1)S(1)}, u32[]{:S(2)}, u32[]{:S(2)}) collective-permute-start(bf16[8,1792]{1,0:T(8,128)(2,1)S(1)} %get-tuple-element.55), channel_id=1, source_target_pairs={{0,2},{1,3},{2,0},{3,1},{4,6},{5,7},{6,4},{7,5},{8,10},{9,11},{10,... | collective-permute-start | bytes 86024 | tf_op jit(solution)/shard_map/ppermute | solution.py:31
  166.6 1.7 %collective-permute-done.39.refs_1_ = bf16[8,1792]{1,0:T(8,128)(2,1)S(1)} collective-permute-done((bf16[8,1792]{1,0:T(8,128)(2,1)S(1)}, bf16[8,1792]{1,0:T(8,128)(2,1)S(1)}, u32[]{:S(2)}, u32[]{:S(2)}) %collective-permute-start.39) | collective-permute-done | bytes 28704 | tf_op jit(solution)/shard_map/ppermute | solution.py:31
  168.9 1.6 finish.1
  (128 shorter events, 23.3 us)
Async XLA Ops:
  1.8 4.6 %collective-permute-start = (bf16[8,1920]{1,0:T(8,128)(2,1)}, bf16[8,1920]{1,0:T(8,128)(2,1)S(1)}, u32[]{:S(2)}, u32[]{:S(2)}) collective-permute-start(bf16[8,1920]{1,0:T(8,128)(2,1)} %get-tuple-element.17), channel_id=1, source_target_pairs={{0,3},{1,0},{2,1},{3,2},{4,7},{5,4},{6,5},{7,6},{8,11},{9,8},{10,9... | collective-permute-start | bytes 92168 | tf_op jit(solution)/shard_map/ppermute | solution.py:31
  4.6 5.6 %collective-permute-start.1 = (bf16[8,1920]{1,0:T(8,128)(2,1)}, bf16[8,1920]{1,0:T(8,128)(2,1)S(1)}, u32[]{:S(2)}, u32[]{:S(2)}) collective-permute-start(bf16[8,1920]{1,0:T(8,128)(2,1)} %get-tuple-element.18), channel_id=1, source_target_pairs={{0,2},{1,3},{2,0},{3,1},{4,6},{5,7},{6,4},{7,5},{8,10},{9,11},{10,... | collective-permute-start | bytes 92168 | tf_op jit(solution)/shard_map/ppermute | solution.py:31
  5.4 5.3 %collective-permute-start.2 = (bf16[8,1920]{1,0:T(8,128)(2,1)}, bf16[8,1920]{1,0:T(8,128)(2,1)S(1)}, u32[]{:S(2)}, u32[]{:S(2)}) collective-permute-start(bf16[8,1920]{1,0:T(8,128)(2,1)} %get-tuple-element.19), channel_id=1, source_target_pairs={{0,1},{1,2},{2,3},{3,0},{4,5},{5,6},{6,7},{7,4},{8,9},{9,10},{10,1... | collective-permute-start | bytes 92168 | tf_op jit(solution)/shard_map/ppermute | solution.py:31
  12.8 6.3 %collective-permute-start.5 = (bf16[32,1920]{1,0:T(8,128)(2,1)}, bf16[32,1920]{1,0:T(8,128)(2,1)S(1)}, u32[]{:S(2)}, u32[]{:S(2)}) collective-permute-start(bf16[32,1920]{1,0:T(8,128)(2,1)} %join.2.refs_0_), channel_id=1, source_target_pairs={{0,32},{4,12},{8,40},{12,20},{16,48},{20,28},{24,56},{28,4},{32,64... | collective-permute-start | bytes 368648 | tf_op jit(solution)/shard_map/ppermute | solution.py:32
  14.4 7.3 %collective-permute-start.4 = (bf16[32,1920]{1,0:T(8,128)(2,1)}, bf16[32,1920]{1,0:T(8,128)(2,1)S(1)}, u32[]{:S(2)}, u32[]{:S(2)}) collective-permute-start(bf16[32,1920]{1,0:T(8,128)(2,1)} %join.2.refs_0_), channel_id=1, source_target_pairs={{0,64},{4,20},{8,72},{12,28},{16,80},{20,4},{24,88},{28,12},{32,96... | collective-permute-start | bytes 368648 | tf_op jit(solution)/shard_map/ppermute | solution.py:32
  17.3 5.1 %collective-permute-start.3 = (bf16[32,1920]{1,0:T(8,128)(2,1)}, bf16[32,1920]{1,0:T(8,128)(2,1)S(1)}, u32[]{:S(2)}, u32[]{:S(2)}) collective-permute-start(bf16[32,1920]{1,0:T(8,128)(2,1)} %join.2.refs_0_), channel_id=1, source_target_pairs={{0,96},{4,28},{8,104},{12,4},{16,112},{20,12},{24,120},{28,20},{32... | collective-permute-start | bytes 368648 | tf_op jit(solution)/shard_map/ppermute | solution.py:32
  24.9 11.1 %collective-permute-start.7 = (bf16[128,1920]{1,0:T(8,128)(2,1)}, bf16[128,1920]{1,0:T(8,128)(2,1)S(1)}, u32[]{:S(2)}, u32[]{:S(2)}) collective-permute-start(bf16[128,1920]{1,0:T(8,128)(2,1)} %join.3), channel_id=1, source_target_pairs={{0,8},{4,36},{8,16},{12,44},{16,24},{20,52},{24,0},{28,60},{32,40}... | collective-permute-start | bytes 1474568 | tf_op jit(solution)/shard_map/ppermute | solution.py:32
  26.8 10.3 %collective-permute-start.6 = (bf16[128,1920]{1,0:T(8,128)(2,1)}, bf16[128,1920]{1,0:T(8,128)(2,1)S(1)}, u32[]{:S(2)}, u32[]{:S(2)}) collective-permute-start(bf16[128,1920]{1,0:T(8,128)(2,1)} %join.3), channel_id=1, source_target_pairs={{0,24},{4,100},{8,0},{12,108},{16,8},{20,116},{24,16},{28,124},{32... | collective-permute-start | bytes 1474568 | tf_op jit(solution)/shard_map/ppermute | solution.py:32
  36.0 7.5 %collective-permute-start.8 = (bf16[64,1920]{1,0:T(8,128)(2,1)S(1)}, bf16[64,1920]{1,0:T(8,128)(2,1)S(1)}, u32[]{:S(2)}, u32[]{:S(2)}) collective-permute-start(bf16[64,1920]{1,0:T(8,128)(2,1)S(1)} %slice.177), channel_id=1, source_target_pairs={{0,8},{4,36},{8,16},{12,44},{16,24},{20,52},{24,0},{28,60},{32,40}... | collective-permute-start | bytes 737288 | tf_op jit(solution)/shard_map/ppermute | solution.py:32
  37.2 7.0 %collective-permute-start.9 = (bf16[64,1920]{1,0:T(8,128)(2,1)S(1)}, bf16[64,1920]{1,0:T(8,128)(2,1)S(1)}, u32[]{:S(2)}, u32[]{:S(2)}) collective-permute-start(bf16[64,1920]{1,0:T(8,128)(2,1)S(1)} %slice.178), channel_id=1, source_target_pairs={{0,24},{4,100},{8,0},{12,108},{16,8},{20,116},{24,16},{28,124},{32... | collective-permute-start | bytes 737288 | tf_op jit(solution)/shard_map/ppermute | solution.py:32
  46.3 2.8 %collective-permute-start.10 = (bf16[256,1920]{1,0:T(8,128)(2,1)}, bf16[256,1920]{1,0:T(8,128)(2,1)S(1)}, u32[]{:S(2)}, u32[]{:S(2)}) collective-permute-start(bf16[256,1920]{1,0:T(8,128)(2,1)} %convolution_convert_fusion.2), channel_id=1, source_target_pairs={{0,4},{4,0},{8,12},{12,8},{16,20},{20,16},{24,28},{28,24},{32,36},... | collective-permute-start | bytes 2949128 | tf_op jit(solution)/shard_map/ppermute | solution.py:32
  46.3 8.6 %slice-start.2 = ((s8[7340032]{0:T(1024)(128)(4,1)}), s8[4194304]{0:T(1024)(128)(4,1)S(1)}, s32[]{:S(2)}) async-start(s8[7340032]{0:T(1024)(128)(4,1)} %bitcast.42), calls=%async_computation.2 | async-start | bytes 8388608
  46.4 8.5 %slice-start.3 = ((s8[7340032]{0:T(1024)(128)(4,1)}), s8[3145728]{0:T(1024)(128)(4,1)S(1)}, s32[]{:S(2)}) async-start(s8[7340032]{0:T(1024)(128)(4,1)} %bitcast.42), calls=%async_computation.3 | async-start | bytes 6291456
  54.4 13.1 %slice-start = ((s8[7340032]{0:T(1024)(128)(4,1)}), s8[4194304]{0:T(1024)(128)(4,1)S(1)}, s32[]{:S(2)}) async-start(s8[7340032]{0:T(1024)(128)(4,1)} %bitcast.40), calls=%async_computation | async-start | bytes 8388608
  54.4 13.1 %slice-start.1 = ((s8[7340032]{0:T(1024)(128)(4,1)}), s8[3145728]{0:T(1024)(128)(4,1)S(1)}, s32[]{:S(2)}) async-start(s8[7340032]{0:T(1024)(128)(4,1)} %bitcast.40), calls=%async_computation.1 | async-start | bytes 6291456
  54.4 8.8 %collective-permute-start.12 = (bf16[64,2048]{1,0:T(8,128)(2,1)S(1)}, bf16[64,2048]{1,0:T(8,128)(2,1)S(1)}, u32[]{:S(2)}, u32[]{:S(2)}) collective-permute-start(bf16[64,2048]{1,0:T(8,128)(2,1)S(1)} %get-tuple-element.44), channel_id=1, source_target_pairs={{0,3},{1,0},{2,1},{3,2},{4,7},{5,4},{6,5},{7,6},{8,11},{9,8},{10,9... | collective-permute-start | bytes 786440 | tf_op jit(solution)/shard_map/ppermute | solution.py:31
  57.0 10.5 %collective-permute-start.11 = (bf16[64,2048]{1,0:T(8,128)(2,1)S(1)}, bf16[64,2048]{1,0:T(8,128)(2,1)S(1)}, u32[]{:S(2)}, u32[]{:S(2)}) collective-permute-start(bf16[64,2048]{1,0:T(8,128)(2,1)S(1)} %get-tuple-element.42), channel_id=1, source_target_pairs={{0,1},{1,2},{2,3},{3,0},{4,5},{5,6},{6,7},{7,4},{8,9},{9,10},{10,1... | collective-permute-start | bytes 786440 | tf_op jit(solution)/shard_map/ppermute | solution.py:31
  59.9 35.2 %collective-permute-start.15 = (bf16[64,2048]{1,0:T(8,128)(2,1)S(1)}, bf16[64,2048]{1,0:T(8,128)(2,1)S(1)}, u32[]{:S(2)}, u32[]{:S(2)}) collective-permute-start(bf16[64,2048]{1,0:T(8,128)(2,1)S(1)} %get-tuple-element.43), channel_id=1, source_target_pairs={{0,1},{1,2},{2,3},{3,0},{4,5},{5,6},{6,7},{7,4},{8,9},{9,10},{10,1... | collective-permute-start | bytes 786440 | tf_op jit(solution)/shard_map/ppermute | solution.py:31
  60.0 38.2 %collective-permute-start.14 = (bf16[64,2048]{1,0:T(8,128)(2,1)S(1)}, bf16[64,2048]{1,0:T(8,128)(2,1)S(1)}, u32[]{:S(2)}, u32[]{:S(2)}) collective-permute-start(bf16[64,2048]{1,0:T(8,128)(2,1)S(1)} %get-tuple-element.41), channel_id=1, source_target_pairs={{0,3},{1,0},{2,1},{3,2},{4,7},{5,4},{6,5},{7,6},{8,11},{9,8},{10,9... | collective-permute-start | bytes 786440 | tf_op jit(solution)/shard_map/ppermute | solution.py:31
  67.5 47.2 %slice-start.4 = ((s8[7340032]{0:T(1024)(128)(4,1)}), s8[4194304]{0:T(1024)(128)(4,1)S(1)}, s32[]{:S(2)}) async-start(s8[7340032]{0:T(1024)(128)(4,1)} %bitcast.44), calls=%async_computation.4 | async-start | bytes 8388608
  69.6 45.1 %slice-start.5 = ((s8[7340032]{0:T(1024)(128)(4,1)}), s8[3145728]{0:T(1024)(128)(4,1)S(1)}, s32[]{:S(2)}) async-start(s8[7340032]{0:T(1024)(128)(4,1)} %bitcast.44), calls=%async_computation.5 | async-start | bytes 6291456
  71.8 10.3 %collective-permute-start.16 = (bf16[64,2048]{1,0:T(8,128)(2,1)S(1)}, bf16[64,2048]{1,0:T(8,128)(2,1)S(1)}, u32[]{:S(2)}, u32[]{:S(2)}) collective-permute-start(bf16[64,2048]{1,0:T(8,128)(2,1)S(1)} %add_convert_fusion.3), channel_id=1, source_target_pairs={{0,3},{1,0},{2,1},{3,2},{4,7},{5,4},{6,5},{7,6},{8,11},{9,8},{10,9... | collective-permute-start | bytes 786440 | tf_op jit(solution)/shard_map/ppermute | solution.py:31
  72.4 9.8 %collective-permute-start.13 = (bf16[64,2048]{1,0:T(8,128)(2,1)S(1)}, bf16[64,2048]{1,0:T(8,128)(2,1)S(1)}, u32[]{:S(2)}, u32[]{:S(2)}) collective-permute-start(bf16[64,2048]{1,0:T(8,128)(2,1)S(1)} %add_convert_fusion.4), channel_id=1, source_target_pairs={{0,1},{1,2},{2,3},{3,0},{4,5},{5,6},{6,7},{7,4},{8,9},{9,10},{10,1... | collective-permute-start | bytes 786440 | tf_op jit(solution)/shard_map/ppermute | solution.py:31
  74.0 11.0 %collective-permute-start.22 = (bf16[64,2048]{1,0:T(8,128)(2,1)S(1)}, bf16[64,2048]{1,0:T(8,128)(2,1)S(1)}, u32[]{:S(2)}, u32[]{:S(2)}) collective-permute-start(bf16[64,2048]{1,0:T(8,128)(2,1)S(1)} %get-tuple-element.47), channel_id=1, source_target_pairs={{0,1},{1,2},{2,3},{3,0},{4,5},{5,6},{6,7},{7,4},{8,9},{9,10},{10,1... | collective-permute-start | bytes 786440 | tf_op jit(solution)/shard_map/ppermute | solution.py:31
  82.1 16.5 %collective-permute-start.24 = (bf16[64,2048]{1,0:T(8,128)(2,1)S(1)}, bf16[64,2048]{1,0:T(8,128)(2,1)S(1)}, u32[]{:S(2)}, u32[]{:S(2)}) collective-permute-start(bf16[64,2048]{1,0:T(8,128)(2,1)S(1)} %get-tuple-element.46), channel_id=1, source_target_pairs={{0,3},{1,0},{2,1},{3,2},{4,7},{5,4},{6,5},{7,6},{8,11},{9,8},{10,9... | collective-permute-start | bytes 786440 | tf_op jit(solution)/shard_map/ppermute | solution.py:31
  82.1 12.7 %collective-permute-start.26 = (bf16[64,2048]{1,0:T(8,128)(2,1)S(1)}, bf16[64,2048]{1,0:T(8,128)(2,1)S(1)}, u32[]{:S(2)}, u32[]{:S(2)}) collective-permute-start(bf16[64,2048]{1,0:T(8,128)(2,1)S(1)} %get-tuple-element.49), channel_id=1, source_target_pairs={{0,3},{1,0},{2,1},{3,2},{4,7},{5,4},{6,5},{7,6},{8,11},{9,8},{10,9... | collective-permute-start | bytes 786440 | tf_op jit(solution)/shard_map/ppermute | solution.py:31
  84.9 16.9 %collective-permute-start.25 = (bf16[64,2048]{1,0:T(8,128)(2,1)S(1)}, bf16[64,2048]{1,0:T(8,128)(2,1)S(1)}, u32[]{:S(2)}, u32[]{:S(2)}) collective-permute-start(bf16[64,2048]{1,0:T(8,128)(2,1)S(1)} %get-tuple-element.50), channel_id=1, source_target_pairs={{0,1},{1,2},{2,3},{3,0},{4,5},{5,6},{6,7},{7,4},{8,9},{9,10},{10,1... | collective-permute-start | bytes 786440 | tf_op jit(solution)/shard_map/ppermute | solution.py:31
  94.8 9.9 %collective-permute-start.23 = (bf16[64,2048]{1,0:T(8,128)(2,1)S(1)}, bf16[64,2048]{1,0:T(8,128)(2,1)S(1)}, u32[]{:S(2)}, u32[]{:S(2)}) collective-permute-start(bf16[64,2048]{1,0:T(8,128)(2,1)S(1)} %add_convert_fusion.2), channel_id=1, source_target_pairs={{0,1},{1,2},{2,3},{3,0},{4,5},{5,6},{6,7},{7,4},{8,9},{9,10},{10,1... | collective-permute-start | bytes 786440 | tf_op jit(solution)/shard_map/ppermute | solution.py:31
  95.1 9.6 %collective-permute-start.27 = (bf16[64,2048]{1,0:T(8,128)(2,1)S(1)}, bf16[64,2048]{1,0:T(8,128)(2,1)S(1)}, u32[]{:S(2)}, u32[]{:S(2)}) collective-permute-start(bf16[64,2048]{1,0:T(8,128)(2,1)S(1)} %add_convert_fusion.1), channel_id=1, source_target_pairs={{0,3},{1,0},{2,1},{3,2},{4,7},{5,4},{6,5},{7,6},{8,11},{9,8},{10,9... | collective-permute-start | bytes 786440 | tf_op jit(solution)/shard_map/ppermute | solution.py:31
  98.5 9.8 %collective-permute-start.18 = (bf16[64,2048]{1,0:T(8,128)(2,1)S(1)}, bf16[64,2048]{1,0:T(8,128)(2,1)S(1)}, u32[]{:S(2)}, u32[]{:S(2)}) collective-permute-start(bf16[64,2048]{1,0:T(8,128)(2,1)S(1)} %get-tuple-element.32), channel_id=1, source_target_pairs={{0,1},{1,2},{2,3},{3,0},{4,5},{5,6},{6,7},{7,4},{8,9},{9,10},{10,1... | collective-permute-start | bytes 786440 | tf_op jit(solution)/shard_map/ppermute | solution.py:31
  98.6 9.9 %collective-permute-start.17 = (bf16[64,2048]{1,0:T(8,128)(2,1)S(1)}, bf16[64,2048]{1,0:T(8,128)(2,1)S(1)}, u32[]{:S(2)}, u32[]{:S(2)}) collective-permute-start(bf16[64,2048]{1,0:T(8,128)(2,1)S(1)} %get-tuple-element.32), channel_id=1, source_target_pairs={{0,3},{1,0},{2,1},{3,2},{4,7},{5,4},{6,5},{7,6},{8,11},{9,8},{10,9... | collective-permute-start | bytes 786440 | tf_op jit(solution)/shard_map/ppermute | solution.py:31
  105.0 11.9 %collective-permute-start.29 = (bf16[64,2048]{1,0:T(8,128)(2,1)S(1)}, bf16[64,2048]{1,0:T(8,128)(2,1)S(1)}, u32[]{:S(2)}, u32[]{:S(2)}) collective-permute-start(bf16[64,2048]{1,0:T(8,128)(2,1)S(1)} %get-tuple-element.34), channel_id=1, source_target_pairs={{0,1},{1,2},{2,3},{3,0},{4,5},{5,6},{6,7},{7,4},{8,9},{9,10},{10,1... | collective-permute-start | bytes 786440 | tf_op jit(solution)/shard_map/ppermute | solution.py:31
  105.1 12.7 %collective-permute-start.28 = (bf16[64,2048]{1,0:T(8,128)(2,1)S(1)}, bf16[64,2048]{1,0:T(8,128)(2,1)S(1)}, u32[]{:S(2)}, u32[]{:S(2)}) collective-permute-start(bf16[64,2048]{1,0:T(8,128)(2,1)S(1)} %get-tuple-element.34), channel_id=1, source_target_pairs={{0,3},{1,0},{2,1},{3,2},{4,7},{5,4},{6,5},{7,6},{8,11},{9,8},{10,9... | collective-permute-start | bytes 786440 | tf_op jit(solution)/shard_map/ppermute | solution.py:31
  108.4 6.2 %collective-permute-start.19 = (bf16[32,2048]{1,0:T(8,128)(2,1)S(1)}, bf16[32,2048]{1,0:T(8,128)(2,1)S(1)}, u32[]{:S(2)}, u32[]{:S(2)}) collective-permute-start(bf16[32,2048]{1,0:T(8,128)(2,1)S(1)} %slice.191), channel_id=1, source_target_pairs={{0,1},{1,2},{2,3},{3,0},{4,5},{5,6},{6,7},{7,4},{8,9},{9,10},{10,1... | collective-permute-start | bytes 393224 | tf_op jit(solution)/shard_map/ppermute | solution.py:31
  108.5 6.2 %collective-permute-start.20 = (bf16[32,2048]{1,0:T(8,128)(2,1)S(1)}, bf16[32,2048]{1,0:T(8,128)(2,1)S(1)}, u32[]{:S(2)}, u32[]{:S(2)}) collective-permute-start(bf16[32,2048]{1,0:T(8,128)(2,1)S(1)} %slice.192), channel_id=1, source_target_pairs={{0,3},{1,0},{2,1},{3,2},{4,7},{5,4},{6,5},{7,6},{8,11},{9,8},{10,9... | collective-permute-start | bytes 393224 | tf_op jit(solution)/shard_map/ppermute | solution.py:31
  116.8 10.0 %collective-permute-start.21 = (bf16[256,1792]{1,0:T(8,128)(2,1)S(1)}, bf16[256,1792]{1,0:T(8,128)(2,1)S(1)}, u32[]{:S(2)}, u32[]{:S(2)}) collective-permute-start(bf16[256,1792]{1,0:T(8,128)(2,1)S(1)} %fusion.33), channel_id=1, source_target_pairs={{0,4},{4,0},{8,12},{12,8},{16,20},{20,16},{24,28},{28,24},{32,36},... | collective-permute-start | bytes 2752520 | tf_op jit(solution)/shard_map/ppermute | solution.py:32
  116.9 7.7 %collective-permute-start.30 = (bf16[32,2048]{1,0:T(8,128)(2,1)S(1)}, bf16[32,2048]{1,0:T(8,128)(2,1)S(1)}, u32[]{:S(2)}, u32[]{:S(2)}) collective-permute-start(bf16[32,2048]{1,0:T(8,128)(2,1)S(1)} %slice.200), channel_id=1, source_target_pairs={{0,1},{1,2},{2,3},{3,0},{4,5},{5,6},{6,7},{7,4},{8,9},{9,10},{10,1... | collective-permute-start | bytes 393224 | tf_op jit(solution)/shard_map/ppermute | solution.py:31
  117.8 6.8 %collective-permute-start.31 = (bf16[32,2048]{1,0:T(8,128)(2,1)S(1)}, bf16[32,2048]{1,0:T(8,128)(2,1)S(1)}, u32[]{:S(2)}, u32[]{:S(2)}) collective-permute-start(bf16[32,2048]{1,0:T(8,128)(2,1)S(1)} %slice.201), channel_id=1, source_target_pairs={{0,3},{1,0},{2,1},{3,2},{4,7},{5,4},{6,5},{7,6},{8,11},{9,8},{10,9... | collective-permute-start | bytes 393224 | tf_op jit(solution)/shard_map/ppermute | solution.py:31
  128.1 7.8 %collective-permute-start.32 = (bf16[64,1792]{1,0:T(8,128)(2,1)S(1)}, bf16[64,1792]{1,0:T(8,128)(2,1)S(1)}, u32[]{:S(2)}, u32[]{:S(2)}) collective-permute-start(bf16[64,1792]{1,0:T(8,128)(2,1)S(1)} %get-tuple-element.37), channel_id=1, source_target_pairs={{0,8},{4,36},{8,16},{12,44},{16,24},{20,52},{24,0},{28,60},{32,40}... | collective-permute-start | bytes 688136 | tf_op jit(solution)/shard_map/ppermute | solution.py:32
  129.2 6.6 %collective-permute-start.34 = (bf16[64,1792]{1,0:T(8,128)(2,1)S(1)}, bf16[64,1792]{1,0:T(8,128)(2,1)S(1)}, u32[]{:S(2)}, u32[]{:S(2)}) collective-permute-start(bf16[64,1792]{1,0:T(8,128)(2,1)S(1)} %get-tuple-element.38), channel_id=1, source_target_pairs={{0,24},{4,100},{8,0},{12,108},{16,8},{20,116},{24,16},{28,124},{32... | collective-permute-start | bytes 688136 | tf_op jit(solution)/shard_map/ppermute | solution.py:32
  136.0 9.4 %collective-permute-start.35 = (bf16[128,1792]{1,0:T(8,128)(2,1)S(1)}, bf16[128,1792]{1,0:T(8,128)(2,1)S(1)}, u32[]{:S(2)}, u32[]{:S(2)}) collective-permute-start(bf16[128,1792]{1,0:T(8,128)(2,1)S(1)} %pad_maximum_fusion.1), channel_id=1, source_target_pairs={{0,24},{4,100},{8,0},{12,108},{16,8},{20,116},{24,16},{28,124},{32... | collective-permute-start | bytes 1376264 | tf_op jit(solution)/shard_map/ppermute | solution.py:32
  139.5 9.8 %collective-permute-start.33 = (bf16[128,1792]{1,0:T(8,128)(2,1)S(1)}, bf16[128,1792]{1,0:T(8,128)(2,1)S(1)}, u32[]{:S(2)}, u32[]{:S(2)}) collective-permute-start(bf16[128,1792]{1,0:T(8,128)(2,1)S(1)} %pad_maximum_fusion), channel_id=1, source_target_pairs={{0,8},{4,36},{8,16},{12,44},{16,24},{20,52},{24,0},{28,60},{32,40}... | collective-permute-start | bytes 1376264 | tf_op jit(solution)/shard_map/ppermute | solution.py:32
  149.5 4.9 %collective-permute-start.36 = (bf16[32,1792]{1,0:T(8,128)(2,1)S(1)}, bf16[32,1792]{1,0:T(8,128)(2,1)S(1)}, u32[]{:S(2)}, u32[]{:S(2)}) collective-permute-start(bf16[32,1792]{1,0:T(8,128)(2,1)S(1)} %get-tuple-element.51), channel_id=1, source_target_pairs={{0,96},{4,28},{8,104},{12,4},{16,112},{20,12},{24,120},{28,20},{32... | collective-permute-start | bytes 344072 | tf_op jit(solution)/shard_map/ppermute | solution.py:32
  152.0 7.2 %collective-permute-start.38 = (bf16[32,1792]{1,0:T(8,128)(2,1)S(1)}, bf16[32,1792]{1,0:T(8,128)(2,1)S(1)}, u32[]{:S(2)}, u32[]{:S(2)}) collective-permute-start(bf16[32,1792]{1,0:T(8,128)(2,1)S(1)} %get-tuple-element.52), channel_id=1, source_target_pairs={{0,32},{4,12},{8,40},{12,20},{16,48},{20,28},{24,56},{28,4},{32,64... | collective-permute-start | bytes 344072 | tf_op jit(solution)/shard_map/ppermute | solution.py:32
  152.0 7.2 %collective-permute-start.37 = (bf16[32,1792]{1,0:T(8,128)(2,1)S(1)}, bf16[32,1792]{1,0:T(8,128)(2,1)S(1)}, u32[]{:S(2)}, u32[]{:S(2)}) collective-permute-start(bf16[32,1792]{1,0:T(8,128)(2,1)S(1)} %get-tuple-element.53), channel_id=1, source_target_pairs={{0,64},{4,20},{8,72},{12,28},{16,80},{20,4},{24,88},{28,12},{32,96... | collective-permute-start | bytes 344072 | tf_op jit(solution)/shard_map/ppermute | solution.py:32
  159.9 5.6 %collective-permute-start.41 = (bf16[8,1792]{1,0:T(8,128)(2,1)S(1)}, bf16[8,1792]{1,0:T(8,128)(2,1)S(1)}, u32[]{:S(2)}, u32[]{:S(2)}) collective-permute-start(bf16[8,1792]{1,0:T(8,128)(2,1)S(1)} %get-tuple-element.54), channel_id=1, source_target_pairs={{0,1},{1,2},{2,3},{3,0},{4,5},{5,6},{6,7},{7,4},{8,9},{9,10},{10,1... | collective-permute-start | bytes 86024 | tf_op jit(solution)/shard_map/ppermute | solution.py:31
  161.1 5.4 %collective-permute-start.40 = (bf16[8,1792]{1,0:T(8,128)(2,1)S(1)}, bf16[8,1792]{1,0:T(8,128)(2,1)S(1)}, u32[]{:S(2)}, u32[]{:S(2)}) collective-permute-start(bf16[8,1792]{1,0:T(8,128)(2,1)S(1)} %get-tuple-element.55), channel_id=1, source_target_pairs={{0,2},{1,3},{2,0},{3,1},{4,6},{5,7},{6,4},{7,5},{8,10},{9,11},{10,... | collective-permute-start | bytes 86024 | tf_op jit(solution)/shard_map/ppermute | solution.py:31
  164.4 3.9 %collective-permute-start.39 = (bf16[8,1792]{1,0:T(8,128)(2,1)S(1)}, bf16[8,1792]{1,0:T(8,128)(2,1)S(1)}, u32[]{:S(2)}, u32[]{:S(2)}) collective-permute-start(bf16[8,1792]{1,0:T(8,128)(2,1)S(1)} %get-tuple-element.56), channel_id=1, source_target_pairs={{0,3},{1,0},{2,1},{3,2},{4,7},{5,4},{6,5},{7,6},{8,11},{9,8},{10,9... | collective-permute-start | bytes 86024 | tf_op jit(solution)/shard_map/ppermute | solution.py:31
  (9 other events, 15.3 us)

commit v4 on v3

--- a/solution.py
+++ b/solution.py
@@ -49,15 +49,15 @@
     return (one.astype(jnp.float32) + other.astype(jnp.float32)).astype(jnp.bfloat16)
 
 
-def scatter_ring(chunks, axis):
-    half = chunks[2].shape[0] // 2
-    first = move(chunks[2][:half], axis, 1)
-    second = move(chunks[2][half:], axis, -1)
-    up = jnp.concatenate([add(chunks[1][:half], first), chunks[1][half:]], axis=0)
-    down = jnp.concatenate([chunks[3][:half], add(chunks[3][half:], second)], axis=0)
+def scatter_ring(own, chunks, axis):
+    half = chunks[1].shape[0] // 2
+    first = move(chunks[1][:half], axis, 1)
+    second = move(chunks[1][half:], axis, -1)
+    up = jnp.concatenate([add(chunks[0][:half], first), chunks[0][half:]], axis=0)
+    down = jnp.concatenate([chunks[2][:half], add(chunks[2][half:], second)], axis=0)
     low = move(up, axis, 1)
     high = move(down, axis, -1)
-    total = chunks[0].astype(jnp.float32) + low.astype(jnp.float32) + high.astype(jnp.float32)
+    total = own.astype(jnp.float32) + low.astype(jnp.float32) + high.astype(jnp.float32)
     return total.astype(jnp.bfloat16)
 
 
@@ -110,22 +110,6 @@
         out_ref[:, pl.ds(start, width)] = total.astype(jnp.bfloat16)
 
 
-def join_kernel(*refs):
-    refs[-1][...] = jnp.concatenate([ref[...].astype(jnp.float32) for ref in refs[:-1]], axis=0).astype(jnp.bfloat16)
-
-
-def join(pieces):
-    vmem = pl.BlockSpec(memory_space=pltpu.VMEM)
-    rows = sum(piece.shape[0] for piece in pieces)
-    return pl.pallas_call(
-        join_kernel,
-        out_shape=jax.ShapeDtypeStruct((rows, pieces[0].shape[1]), jnp.bfloat16),
-        in_specs=[vmem] * len(pieces),
-        out_specs=vmem,
-        name="join",
-    )(*pieces)
-
-
 def specs(count):
     return [pl.BlockSpec(memory_space=pltpu.SMEM)] + [pl.BlockSpec(memory_space=pltpu.VMEM)] * count
 
@@ -164,52 +148,57 @@
         out_specs=[pl.BlockSpec(memory_space=pltpu.VMEM)] * RING,
         name="prepare",
     )(place, hidden, norm_gain.reshape(1, -1), routes, route_scores, capacity.reshape(1, -1))
-    lines = join(direct(blocks, "x"))
-    lines = join(direct([lines] * RING, 0))
-    lines = jnp.concatenate(gather_ring(lines, 1), axis=0)
-    picks = lines[:, width:].astype(jnp.float32)
-    chosen_own = choose(picks, expert)
-    chosen_other = choose(picks, other)
-    picked = [move(pick(chosen_other, lines), "core", 1), pick(chosen_own, lines)]
+    lines = jnp.concatenate(direct(blocks, "x"), axis=0)
+    near = jnp.concatenate(direct([lines] * RING, 0), axis=0)
+    far = jnp.concatenate(gather_ring(near, 1)[1:], axis=0)
     lane = jnp.arange(PAD)[None, :]
     mine = (lane == expert + experts) | (lane == expert + 2 * experts)
-    parts, scales = [], []
-    for chunk in range(2):
-        slots = picked[chunk]
-        if chunk == 1:
-            slots, *parts[0][0:2] = lax.optimization_barrier((slots, *parts[0][0:2]))
-        scales.append(jnp.sum(jnp.where(mine, slots[:, width:].astype(jnp.float32), 0.0), axis=1))
+    spread = []
+    after = None
+    for lines in (near, far):
+        picks = lines[:, width:].astype(jnp.float32)
+        chosen = [choose(picks, expert), choose(picks, other)]
+        quarter = lines.shape[0] // 2 // RING
+        theirs = move(pick(chosen[1], lines), "core", 1)
+        slots = [value.reshape(RING, quarter, width + PAD) for value in (pick(chosen[0], lines), theirs)]
+        slots = jnp.concatenate(slots, axis=1).reshape(RING * 2 * quarter, width + PAD)
+        scale = jnp.sum(jnp.where(mine, slots[:, width:].astype(jnp.float32), 0.0), axis=1)
         slots = slots[:, :width]
+        if after is not None:
+            slots, after = lax.optimization_barrier((slots, after))
+        part = 2 * quarter
         gate = jnp.dot(slots, w_gate[0], preferred_element_type=jnp.float32).astype(jnp.bfloat16)
+        gate = [gate[r * part : (r + 1) * part] for r in range(RING)]
+        gate_far = move(gate[2], "x", 1)
+        gate_high = move(gate[3], "x", -1)
         up = jnp.dot(slots, w_up[0], preferred_element_type=jnp.float32).astype(jnp.bfloat16)
-        part = slots.shape[0] // RING
-        gate = [gate[r * part : (r + 1) * part] for r in range(RING)]
         up = [up[r * part : (r + 1) * part] for r in range(RING)]
-        gate_far = move(gate[2], "x", 1)
         up_far = move(up[2], "x", -1)
         up_low = move(up[1], "x", 1)
-        gate_high = move(gate[3], "x", -1)
-        parts.append([gate_far, up_far, up_low, gate_high, gate, up])
-    out = []
-    for chunk in range(2):
-        gate_far, up_far, up_low, gate_high, gate, up = parts[chunk]
         gate_low = move(add(gate[1], gate_far), "x", 1)
         up_high = move(add(up[3], up_far), "x", -1)
-        if chunk == 0:
-            gate_low, parts[1][4][0] = lax.optimization_barrier((gate_low, parts[1][4][0]))
-            up_high, parts[1][5][0] = lax.optimization_barrier((up_high, parts[1][5][0]))
+        if after is not None:
+            whole = jnp.concatenate(gather_ring(after, "x"), axis=0)
+            gate_low, whole = lax.optimization_barrier((gate_low, whole))
+            near_state[0] = whole
         gate_sum = gate[0].astype(jnp.float32) + gate_low.astype(jnp.float32) + gate_high.astype(jnp.float32)
         up_sum = up[0].astype(jnp.float32) + up_low.astype(jnp.float32) + up_high.astype(jnp.float32)
         activation = (jax.nn.silu(gate_sum) * up_sum).astype(jnp.bfloat16)
-        activation = jnp.concatenate(gather_ring(activation, "x"), axis=0)
-        expert_out = jnp.dot(activation, w_down[0], preferred_element_type=jnp.float32)
-        expert_out = (expert_out * scales[chunk][:, None]).astype(jnp.bfloat16)
-        out.append(move(expert_out, "core", 1) if chunk == 0 else expert_out)
-    returned = jnp.concatenate(out, axis=0)
-    chosen = jnp.concatenate([chosen_other, chosen_own], axis=1)
-    summed = jnp.dot(chosen, returned, preferred_element_type=jnp.float32).astype(jnp.bfloat16)
-    part = summed.shape[0] // RING
-    summed = scatter_ring([summed[r * part : (r + 1) * part] for r in range(RING)], 1)
+        if after is None:
+            after = activation
+            near_state = [None, scale, jnp.concatenate(chosen, axis=1)]
+    far_state = [jnp.concatenate(gather_ring(activation, "x"), axis=0), scale, jnp.concatenate(chosen, axis=1)]
+    for whole, scale, chosen in (near_state, far_state):
+        if spread:
+            whole, spread[0] = lax.optimization_barrier((whole, spread[0]))
+        expert_out = jnp.dot(whole, w_down[0], preferred_element_type=jnp.float32)
+        expert_out = (expert_out * scale[:, None]).astype(jnp.bfloat16)
+        expert_out = expert_out.reshape(RING, 2, -1, width)
+        theirs = move(expert_out[:, 1].reshape(-1, width), "core", 1)
+        returned = jnp.concatenate([expert_out[:, 0].reshape(-1, width), theirs], axis=0)
+        spread.append(jnp.dot(chosen, returned, preferred_element_type=jnp.float32).astype(jnp.bfloat16))
+    part = spread[0].shape[0]
+    summed = scatter_ring(spread[0], [spread[1][r * part : (r + 1) * part] for r in range(RING - 1)], 1)
     part = part // RING
     pieces = direct([summed[r * part : (r + 1) * part] for r in range(RING)], 0)
     summed = sum(piece.astype(jnp.float32) for piece in pieces).astype(jnp.bfloat16)

time: 171 us -> 166 us (0.971)
  Pallas kernels: 6.75 us -> 3.38 us
    ppermute x16 -> x18, waiting for transfers between devices: 36.3 us -> 31.9 us  [move(): return lax.ppermute(value, 'attn', attn_pairs(axis, step))]
    ppermute x26, waiting for transfers between devices: 38.9 us -> 43.1 us  [move(): lax.ppermute(value, 'exp', [(i, (i + step) % RING) for i in range(RING)])]
    pallas_call x2 -> x0, Pallas kernels: 3.36 us -> none  [join(): pl.pallas_call(join_kernel, out_shape=jax.ShapeDtypeStruct((rows, pieces[...]
    ppermute x16 -> x18, starting transfers between devices: 24.9 us -> 24.8 us  [move(): return lax.ppermute(value, 'attn', attn_pairs(axis, step))]
  transfers between devices with their start and end apart: 42 -> 44, of which waited for: 25 -> 26; matrix products, arithmetic and copies ran while one was open for 8% -> 11% of each run, Pallas kernels for 0% -> 0%
where the time goes in v4:
time: 166 us
  waiting for transfers between devices  75.1 us (45%)
  starting transfers between devices  61.5 us (37%)
  matrix products  19.2 us (12%)
  local copies, waits for them, and re-layouts  3.62 us (2%)
  Pallas kernels  3.38 us (2%)
  other arithmetic  2.36 us (1%)
    ppermute x26, waiting for transfers between devices, move(): lax.ppermute(value, 'exp', [(i, (i + step) % RING) for i in range(RING)])  43.1 us
    ppermute x26, starting transfers between devices, move(): lax.ppermute(value, 'exp', [(i, (i + step) % RING) for i in range(RING)])  36.6 us
    ppermute x18, waiting for transfers between devices, move(): return lax.ppermute(value, 'attn', attn_pairs(axis, step))  31.9 us
    ppermute x18, starting transfers between devices, move(): return lax.ppermute(value, 'attn', attn_pairs(axis, step))  24.8 us
    dot_general x2, matrix products, shards(): jnp.dot(slots, w_up[0], preferred_element_type=jnp.float32)  7.42 us
    dot_general x2, matrix products, shards(): jnp.dot(slots, w_gate[0], preferred_element_type=jnp.float32)  4.22 us
    dot_general x2, matrix products, shards(): expert_out = jnp.dot(whole, w_down[0], preferred_element_type=jnp.float32)  4.19 us
  transfers between devices with their start and end apart: 44, of which 26 were waited for; matrix products, arithmetic and copies ran while one was open for 11% of the time, Pallas kernels for 0%

profile of v4, /device:TPU:0, one launch (start us, length us, event | category | flops | bytes accessed | tf_op | source)
XLA Modules:
  0.0 165.8 jit_solution(4571594248392765152)
XLA Ops:
  0.0 1.8 %prepare.1 = (bf16[8,1920]{1,0:T(8,128)(2,1)}, bf16[8,1920]{1,0:T(8,128)(2,1)}, bf16[8,1920]{1,0:T(8,128)(2,1)}, bf16[8,1920]{1,0:T(8,128)(2,1)}) custom-call(s32[1]{0:T(128)} %bitcast.place_ref, bf16[8,7168]{1,0:T(8,128)(2,1)} %hidden_ref.3, f32[1,7168]{1,0:T(1,128)} %bitcast.75, s32[8,8]{1,0:T(8,128)} %routes_ref.1, f32[8,8]{1,0:T(8,128)} %scores_ref.1, ...), custom_call_target="tpu_custom_call" | custom-call | tf_op jit(solution)/shard_map/prepare/pallas_call | solution.py:144
  1.8 2.8 %collective-permute-start = (bf16[8,1920]{1,0:T(8,128)(2,1)}, bf16[8,1920]{1,0:T(8,128)(2,1)S(1)}, u32[]{:S(2)}, u32[]{:S(2)}) collective-permute-start(bf16[8,1920]{1,0:T(8,128)(2,1)} %get-tuple-element.16), channel_id=1, source_target_pairs={{0,3},{1,0},{2,1},{3,2},{4,7},{5,4},{6,5},{7,6},{8,11},{9,8},{10,9... | collective-permute-start | bytes 92168 | tf_op jit(solution)/shard_map/ppermute | solution.py:31
  7.1 3.1 %collective-permute-done.1 = bf16[8,1920]{1,0:T(8,128)(2,1)S(1)} collective-permute-done((bf16[8,1920]{1,0:T(8,128)(2,1)}, bf16[8,1920]{1,0:T(8,128)(2,1)S(1)}, u32[]{:S(2)}, u32[]{:S(2)}) %collective-permute-start.1) | collective-permute-done | bytes 30752 | tf_op jit(solution)/shard_map/ppermute | solution.py:31
  10.7 3.0 %collective-permute-start.3 = (bf16[32,1920]{1,0:T(8,128)(2,1)S(1)}, bf16[32,1920]{1,0:T(8,128)(2,1)S(1)}, u32[]{:S(2)}, u32[]{:S(2)}) collective-permute-start(bf16[32,1920]{1,0:T(8,128)(2,1)S(1)} %get-tuple-element.56), channel_id=1, source_target_pairs={{0,96},{4,28},{8,104},{12,4},{16,112},{20,12},{24,120},{28,20},{32... | collective-permute-start | bytes 368648 | tf_op jit(solution)/shard_map/ppermute | solution.py:32
  13.9 2.2 %collective-permute-start.4 = (bf16[32,1920]{1,0:T(8,128)(2,1)S(1)}, bf16[32,1920]{1,0:T(8,128)(2,1)S(1)}, u32[]{:S(2)}, u32[]{:S(2)}) collective-permute-start(bf16[32,1920]{1,0:T(8,128)(2,1)S(1)} %get-tuple-element.56), channel_id=1, source_target_pairs={{0,64},{4,20},{8,72},{12,28},{16,80},{20,4},{24,88},{28,12},{32,96... | collective-permute-start | bytes 368648 | tf_op jit(solution)/shard_map/ppermute | solution.py:32
  16.2 4.2 %collective-permute-done.4 = bf16[32,1920]{1,0:T(8,128)(2,1)S(1)} collective-permute-done((bf16[32,1920]{1,0:T(8,128)(2,1)S(1)}, bf16[32,1920]{1,0:T(8,128)(2,1)S(1)}, u32[]{:S(2)}, u32[]{:S(2)}) %collective-permute-start.4) | collective-permute-done | bytes 122912 | tf_op jit(solution)/shard_map/ppermute | solution.py:32
  21.8 2.0 %collective-permute-start.7 = (bf16[128,1920]{1,0:T(8,128)(2,1)S(1)}, bf16[128,1920]{1,0:T(8,128)(2,1)S(1)}, u32[]{:S(2)}, u32[]{:S(2)}) collective-permute-start(bf16[128,1920]{1,0:T(8,128)(2,1)S(1)} %constant_dynamic-update-slice_fusion.4), channel_id=1, source_target_pairs={{0,8},{4,36},{8,16},{12,44},{16,24},{20,52},{24,0},{28,60},{32,40}... | collective-permute-start | bytes 1474568 | tf_op jit(solution)/shard_map/ppermute | solution.py:32
  23.8 2.2 %collective-permute-start.6 = (bf16[128,1920]{1,0:T(8,128)(2,1)S(1)}, bf16[128,1920]{1,0:T(8,128)(2,1)S(1)}, u32[]{:S(2)}, u32[]{:S(2)}) collective-permute-start(bf16[128,1920]{1,0:T(8,128)(2,1)S(1)} %constant_dynamic-update-slice_fusion.4), channel_id=1, source_target_pairs={{0,24},{4,100},{8,0},{12,108},{16,8},{20,116},{24,16},{28,124},{32... | collective-permute-start | bytes 1474568 | tf_op jit(solution)/shard_map/ppermute | solution.py:32
  26.6 4.4 %fusion.33 = bf16[128,2048]{1,0:T(8,128)(2,1)S(1)} fusion(bf16[1,1792,2048]{2,1,0:T(8,128)(2,1)} %param.14, bf16[128,1920]{1,0:T(8,128)(2,1)S(1)} %bitcast.61), kind=kOutput, calls=%fused_computation.22 | convolution fusion | flops 939786240 | bytes 8323072 | tf_op jit(solution)/shard_map/dot_general | solution.py:174
  31.7 1.2 fusion.30
  33.0 3.2 %collective-permute-start.14 = (bf16[32,2048]{1,0:T(8,128)(2,1)S(1)}, bf16[32,2048]{1,0:T(8,128)(2,1)S(1)}, u32[]{:S(2)}, u32[]{:S(2)}) collective-permute-start(bf16[32,2048]{1,0:T(8,128)(2,1)S(1)} %get-tuple-element.44), channel_id=1, source_target_pairs={{0,3},{1,0},{2,1},{3,2},{4,7},{5,4},{6,5},{7,6},{8,11},{9,8},{10,9... | collective-permute-start | bytes 393224 | tf_op jit(solution)/shard_map/ppermute | solution.py:31
  36.4 3.5 %collective-permute-done.12 = bf16[32,2048]{1,0:T(8,128)(2,1)S(1)} collective-permute-done((bf16[32,2048]{1,0:T(8,128)(2,1)S(1)}, bf16[32,2048]{1,0:T(8,128)(2,1)S(1)}, u32[]{:S(2)}, u32[]{:S(2)}) %collective-permute-start.12) | collective-permute-done | bytes 131104 | tf_op jit(solution)/shard_map/ppermute | solution.py:31
  39.9 2.1 %collective-permute-start.13 = (bf16[32,2048]{1,0:T(8,128)(2,1)S(1)}, bf16[32,2048]{1,0:T(8,128)(2,1)S(1)}, u32[]{:S(2)}, u32[]{:S(2)}) collective-permute-start(bf16[32,2048]{1,0:T(8,128)(2,1)S(1)} %add_convert_fusion.6), channel_id=1, source_target_pairs={{0,1},{1,2},{2,3},{3,0},{4,5},{5,6},{6,7},{7,4},{8,9},{9,10},{10,1... | collective-permute-start | bytes 393224 | tf_op jit(solution)/shard_map/ppermute | solution.py:31
  42.0 2.8 %collective-permute-done.16 = bf16[32,2048]{1,0:T(8,128)(2,1)S(1)} collective-permute-done((bf16[32,2048]{1,0:T(8,128)(2,1)S(1)}, bf16[32,2048]{1,0:T(8,128)(2,1)S(1)}, u32[]{:S(2)}, u32[]{:S(2)}) %collective-permute-start.16) | collective-permute-done | bytes 131104 | tf_op jit(solution)/shard_map/ppermute | solution.py:31
  45.9 2.3 %collective-permute-start.9 = (bf16[64,1920]{1,0:T(8,128)(2,1)S(1)}, bf16[64,1920]{1,0:T(8,128)(2,1)S(1)}, u32[]{:S(2)}, u32[]{:S(2)}) collective-permute-start(bf16[64,1920]{1,0:T(8,128)(2,1)S(1)} %slice.194), channel_id=1, source_target_pairs={{0,24},{4,100},{8,0},{12,108},{16,8},{20,116},{24,16},{28,124},{32... | collective-permute-start | bytes 737288 | tf_op jit(solution)/shard_map/ppermute | solution.py:32
  48.3 4.0 %collective-permute-done.8 = bf16[64,1920]{1,0:T(8,128)(2,1)S(1)} collective-permute-done((bf16[64,1920]{1,0:T(8,128)(2,1)S(1)}, bf16[64,1920]{1,0:T(8,128)(2,1)S(1)}, u32[]{:S(2)}, u32[]{:S(2)}) %collective-permute-start.8) | collective-permute-done | bytes 245792 | tf_op jit(solution)/shard_map/ppermute | solution.py:32
  52.2 1.4 collective-permute-start.17
  54.8 2.4 %collective-permute-done.17 = bf16[32,2048]{1,0:T(8,128)(2,1)S(1)} collective-permute-done((bf16[32,2048]{1,0:T(8,128)(2,1)S(1)}, bf16[32,2048]{1,0:T(8,128)(2,1)S(1)}, u32[]{:S(2)}, u32[]{:S(2)}) %collective-permute-start.17) | collective-permute-done | bytes 131104 | tf_op jit(solution)/shard_map/ppermute | solution.py:31
  58.4 3.2 %collective-permute-start.20 = (bf16[32,2048]{1,0:T(8,128)(2,1)S(1)}, bf16[32,2048]{1,0:T(8,128)(2,1)S(1)}, u32[]{:S(2)}, u32[]{:S(2)}) collective-permute-start(bf16[32,2048]{1,0:T(8,128)(2,1)S(1)} %multiply_convert_fusion.1), channel_id=1, source_target_pairs={{0,3},{1,0},{2,1},{3,2},{4,7},{5,4},{6,5},{7,6},{8,11},{9,8},{10,9... | collective-permute-start | bytes 393224 | tf_op jit(solution)/shard_map/ppermute | solution.py:31
  61.7 3.0 %fusion.21 = bf16[384,2048]{1,0:T(8,128)(2,1)S(1)} fusion(bf16[384,1792]{1,0:T(8,128)(2,1)S(1)} %slice.196, bf16[1,1792,2048]{2,1,0:T(8,128)(2,1)S(1)} %bitcast.57), kind=kOutput, calls=%fused_computation.15 | convolution fusion | flops 2819358720 | bytes 10289152 | tf_op jit(solution)/shard_map/dot_general | solution.py:174
  64.7 3.0 %fusion.18 = bf16[384,2048]{1,0:T(8,128)(2,1)S(1)} fusion(bf16[384,1792]{1,0:T(8,128)(2,1)S(1)} %slice.196, bf16[1,1792,2048]{2,1,0:T(8,128)(2,1)S(1)} %bitcast.59), kind=kOutput, calls=%fused_computation.14 | convolution fusion | flops 2819358720 | bytes 10289152 | tf_op jit(solution)/shard_map/dot_general | solution.py:170
  67.9 3.2 %collective-permute-start.24 = (bf16[96,2048]{1,0:T(8,128)(2,1)S(1)}, bf16[96,2048]{1,0:T(8,128)(2,1)S(1)}, u32[]{:S(2)}, u32[]{:S(2)}) collective-permute-start(bf16[96,2048]{1,0:T(8,128)(2,1)S(1)} %get-tuple-element.32), channel_id=1, source_target_pairs={{0,3},{1,0},{2,1},{3,2},{4,7},{5,4},{6,5},{7,6},{8,11},{9,8},{10,9... | collective-permute-start | bytes 1179656 | tf_op jit(solution)/shard_map/ppermute | solution.py:31
  71.3 3.3 %collective-permute-start.26 = (bf16[96,2048]{1,0:T(8,128)(2,1)S(1)}, bf16[96,2048]{1,0:T(8,128)(2,1)S(1)}, u32[]{:S(2)}, u32[]{:S(2)}) collective-permute-start(bf16[96,2048]{1,0:T(8,128)(2,1)S(1)} %get-tuple-element.34), channel_id=1, source_target_pairs={{0,3},{1,0},{2,1},{3,2},{4,7},{5,4},{6,5},{7,6},{8,11},{9,8},{10,9... | collective-permute-start | bytes 1179656 | tf_op jit(solution)/shard_map/ppermute | solution.py:31
  74.7 13.6 %collective-permute-done.22 = bf16[16,2048]{1,0:T(8,128)(2,1)S(1)} collective-permute-done((bf16[16,2048]{1,0:T(8,128)(2,1)S(1)}, bf16[16,2048]{1,0:T(8,128)(2,1)S(1)}, u32[]{:S(2)}, u32[]{:S(2)}) %collective-permute-start.22) | collective-permute-done | bytes 65568 | tf_op jit(solution)/shard_map/ppermute | solution.py:31
  88.4 2.1 %collective-permute-start.19 = (bf16[96,2048]{1,0:T(8,128)(2,1)S(1)}, bf16[96,2048]{1,0:T(8,128)(2,1)S(1)}, u32[]{:S(2)}, u32[]{:S(2)}) collective-permute-start(bf16[96,2048]{1,0:T(8,128)(2,1)S(1)} %add_convert_fusion.2), channel_id=1, source_target_pairs={{0,1},{1,2},{2,3},{3,0},{4,5},{5,6},{6,7},{7,4},{8,9},{9,10},{10,1... | collective-permute-start | bytes 1179656 | tf_op jit(solution)/shard_map/ppermute | solution.py:31
  90.6 1.3 collective-permute-start.27
  91.9 1.4 collective-permute-done.23
  93.3 4.8 %collective-permute-done.19 = bf16[96,2048]{1,0:T(8,128)(2,1)S(1)} collective-permute-done((bf16[96,2048]{1,0:T(8,128)(2,1)S(1)}, bf16[96,2048]{1,0:T(8,128)(2,1)S(1)}, u32[]{:S(2)}, u32[]{:S(2)}) %collective-permute-start.19) | collective-permute-done | bytes 393248 | tf_op jit(solution)/shard_map/ppermute | solution.py:31
  100.2 2.9 %collective-permute-start.28 = (bf16[96,2048]{1,0:T(8,128)(2,1)S(1)}, bf16[96,2048]{1,0:T(8,128)(2,1)S(1)}, u32[]{:S(2)}, u32[]{:S(2)}) collective-permute-start(bf16[96,2048]{1,0:T(8,128)(2,1)S(1)} %get-tuple-element.30), channel_id=1, source_target_pairs={{0,3},{1,0},{2,1},{3,2},{4,7},{5,4},{6,5},{7,6},{8,11},{9,8},{10,9... | collective-permute-start | bytes 1179656 | tf_op jit(solution)/shard_map/ppermute | solution.py:31
  104.6 1.2 collective-permute-done.32
  106.2 2.6 %collective-permute-done.29 = bf16[96,2048]{1,0:T(8,128)(2,1)S(1)} collective-permute-done((bf16[96,2048]{1,0:T(8,128)(2,1)S(1)}, bf16[96,2048]{1,0:T(8,128)(2,1)S(1)}, u32[]{:S(2)}, u32[]{:S(2)}) %collective-permute-start.29) | collective-permute-done | bytes 393248 | tf_op jit(solution)/shard_map/ppermute | solution.py:31
  109.0 3.5 %collective-permute-start.31 = (bf16[48,2048]{1,0:T(8,128)(2,1)S(1)}, bf16[48,2048]{1,0:T(8,128)(2,1)S(1)}, u32[]{:S(2)}, u32[]{:S(2)}) collective-permute-start(bf16[48,2048]{1,0:T(8,128)(2,1)S(1)} %slice.218), channel_id=1, source_target_pairs={{0,3},{1,0},{2,1},{3,2},{4,7},{5,4},{6,5},{7,6},{8,11},{9,8},{10,9... | collective-permute-start | bytes 589832 | tf_op jit(solution)/shard_map/ppermute | solution.py:31
  112.5 3.3 %collective-permute-done.30 = bf16[48,2048]{1,0:T(8,128)(2,1)S(1)} collective-permute-done((bf16[48,2048]{1,0:T(8,128)(2,1)S(1)}, bf16[48,2048]{1,0:T(8,128)(2,1)S(1)}, u32[]{:S(2)}, u32[]{:S(2)}) %collective-permute-start.30) | collective-permute-done | bytes 196640 | tf_op jit(solution)/shard_map/ppermute | solution.py:31
  115.9 3.0 %fusion.15 = bf16[384,1792]{1,0:T(8,128)(2,1)S(1)} fusion(bf16[384,2048]{1,0:T(8,128)(2,1)S(1)} %constant_dynamic-update-slice_fusion.20, bf16[1,2048,1792]{2,1,0:T(8,128)(2,1)S(1)} %bitcast.55, f32[384]{0:T(512)S(1)} %select_reduce_fusion), kind=kOutput, calls=%fused_computation.13 | convolution fusion | flops 2819948544 | bytes 10290688 | tf_op jit(solution)/shard_map/dot_general | solution.py:194
  119.4 1.9 %collective-permute-done.33 = bf16[192,1792]{1,0:T(8,128)(2,1)S(1)} collective-permute-done((bf16[192,1792]{1,0:T(8,128)(2,1)S(1)}, bf16[192,1792]{1,0:T(8,128)(2,1)S(1)}, u32[]{:S(2)}, u32[]{:S(2)}) %collective-permute-start.33) | collective-permute-done | bytes 688160 | tf_op jit(solution)/shard_map/ppermute | solution.py:32
  122.3 1.7 %collective-permute-start.34 = (bf16[64,1792]{1,0:T(8,128)(2,1)S(1)}, bf16[64,1792]{1,0:T(8,128)(2,1)S(1)}, u32[]{:S(2)}, u32[]{:S(2)}) collective-permute-start(bf16[64,1792]{1,0:T(8,128)(2,1)S(1)} %get-tuple-element.37), channel_id=1, source_target_pairs={{0,8},{4,36},{8,16},{12,44},{16,24},{20,52},{24,0},{28,60},{32,40}... | collective-permute-start | bytes 688136 | tf_op jit(solution)/shard_map/ppermute | solution.py:32
  123.9 1.7 %collective-permute-start.36 = (bf16[64,1792]{1,0:T(8,128)(2,1)S(1)}, bf16[64,1792]{1,0:T(8,128)(2,1)S(1)}, u32[]{:S(2)}, u32[]{:S(2)}) collective-permute-start(bf16[64,1792]{1,0:T(8,128)(2,1)S(1)} %get-tuple-element.38), channel_id=1, source_target_pairs={{0,24},{4,100},{8,0},{12,108},{16,8},{20,116},{24,16},{28,124},{32... | collective-permute-start | bytes 688136 | tf_op jit(solution)/shard_map/ppermute | solution.py:32
  125.7 3.9 %collective-permute-done.34 = bf16[64,1792]{1,0:T(8,128)(2,1)S(1)} collective-permute-done((bf16[64,1792]{1,0:T(8,128)(2,1)S(1)}, bf16[64,1792]{1,0:T(8,128)(2,1)S(1)}, u32[]{:S(2)}, u32[]{:S(2)}) %collective-permute-start.34) | collective-permute-done | bytes 229408 | tf_op jit(solution)/shard_map/ppermute | solution.py:32
  130.1 3.0 %collective-permute-start.37 = (bf16[128,1792]{1,0:T(8,128)(2,1)S(1)}, bf16[128,1792]{1,0:T(8,128)(2,1)S(1)}, u32[]{:S(2)}, u32[]{:S(2)}) collective-permute-start(bf16[128,1792]{1,0:T(8,128)(2,1)S(1)} %pad_maximum_fusion.3), channel_id=1, source_target_pairs={{0,24},{4,100},{8,0},{12,108},{16,8},{20,116},{24,16},{28,124},{32... | collective-permute-start | bytes 1376264 | tf_op jit(solution)/shard_map/ppermute | solution.py:32
  133.2 5.9 %collective-permute-done.37 = bf16[128,1792]{1,0:T(8,128)(2,1)S(1)} collective-permute-done((bf16[128,1792]{1,0:T(8,128)(2,1)S(1)}, bf16[128,1792]{1,0:T(8,128)(2,1)S(1)}, u32[]{:S(2)}, u32[]{:S(2)}) %collective-permute-start.37) | collective-permute-done | bytes 458784 | tf_op jit(solution)/shard_map/ppermute | solution.py:32
  139.1 3.8 %collective-permute-done.35 = bf16[128,1792]{1,0:T(8,128)(2,1)S(1)} collective-permute-done((bf16[128,1792]{1,0:T(8,128)(2,1)S(1)}, bf16[128,1792]{1,0:T(8,128)(2,1)S(1)}, u32[]{:S(2)}, u32[]{:S(2)}) %collective-permute-start.35) | collective-permute-done | bytes 458784 | tf_op jit(solution)/shard_map/ppermute | solution.py:32
  143.2 3.6 %collective-permute-start.38 = (bf16[32,1792]{1,0:T(8,128)(2,1)S(1)}, bf16[32,1792]{1,0:T(8,128)(2,1)S(1)}, u32[]{:S(2)}, u32[]{:S(2)}) collective-permute-start(bf16[32,1792]{1,0:T(8,128)(2,1)S(1)} %get-tuple-element.47), channel_id=1, source_target_pairs={{0,96},{4,28},{8,104},{12,4},{16,112},{20,12},{24,120},{28,20},{32... | collective-permute-start | bytes 344072 | tf_op jit(solution)/shard_map/ppermute | solution.py:32
  146.8 1.5 collective-permute-start.39
  149.2 4.9 %collective-permute-done.40 = bf16[32,1792]{1,0:T(8,128)(2,1)S(1)} collective-permute-done((bf16[32,1792]{1,0:T(8,128)(2,1)S(1)}, bf16[32,1792]{1,0:T(8,128)(2,1)S(1)}, u32[]{:S(2)}, u32[]{:S(2)}) %collective-permute-start.40) | collective-permute-done | bytes 114720 | tf_op jit(solution)/shard_map/ppermute | solution.py:32
  154.7 5.0 %collective-permute-start.42 = (bf16[8,1792]{1,0:T(8,128)(2,1)S(1)}, bf16[8,1792]{1,0:T(8,128)(2,1)S(1)}, u32[]{:S(2)}, u32[]{:S(2)}) collective-permute-start(bf16[8,1792]{1,0:T(8,128)(2,1)S(1)} %get-tuple-element.53), channel_id=1, source_target_pairs={{0,2},{1,3},{2,0},{3,1},{4,6},{5,7},{6,4},{7,5},{8,10},{9,11},{10,... | collective-permute-start | bytes 86024 | tf_op jit(solution)/shard_map/ppermute | solution.py:31
  160.1 1.8 %collective-permute-done.42.refs_2_ = bf16[8,1792]{1,0:T(8,128)(2,1)S(1)} collective-permute-done((bf16[8,1792]{1,0:T(8,128)(2,1)S(1)}, bf16[8,1792]{1,0:T(8,128)(2,1)S(1)}, u32[]{:S(2)}, u32[]{:S(2)}) %collective-permute-start.42) | collective-permute-done | bytes 28704 | tf_op jit(solution)/shard_map/ppermute | solution.py:31
  161.8 1.7 %collective-permute-done.41.refs_1_ = bf16[8,1792]{1,0:T(8,128)(2,1)S(1)} collective-permute-done((bf16[8,1792]{1,0:T(8,128)(2,1)S(1)}, bf16[8,1792]{1,0:T(8,128)(2,1)S(1)}, u32[]{:S(2)}, u32[]{:S(2)}) %collective-permute-start.41) | collective-permute-done | bytes 28704 | tf_op jit(solution)/shard_map/ppermute | solution.py:31
  164.2 1.6 finish.1
  (140 shorter events, 18.8 us)
Async XLA Ops:
  1.8 5.3 %collective-permute-start = (bf16[8,1920]{1,0:T(8,128)(2,1)}, bf16[8,1920]{1,0:T(8,128)(2,1)S(1)}, u32[]{:S(2)}, u32[]{:S(2)}) collective-permute-start(bf16[8,1920]{1,0:T(8,128)(2,1)} %get-tuple-element.16), channel_id=1, source_target_pairs={{0,3},{1,0},{2,1},{3,2},{4,7},{5,4},{6,5},{7,6},{8,11},{9,8},{10,9... | collective-permute-start | bytes 92168 | tf_op jit(solution)/shard_map/ppermute | solution.py:31
  4.6 5.6 %collective-permute-start.1 = (bf16[8,1920]{1,0:T(8,128)(2,1)}, bf16[8,1920]{1,0:T(8,128)(2,1)S(1)}, u32[]{:S(2)}, u32[]{:S(2)}) collective-permute-start(bf16[8,1920]{1,0:T(8,128)(2,1)} %get-tuple-element.17), channel_id=1, source_target_pairs={{0,2},{1,3},{2,0},{3,1},{4,6},{5,7},{6,4},{7,5},{8,10},{9,11},{10,... | collective-permute-start | bytes 92168 | tf_op jit(solution)/shard_map/ppermute | solution.py:31
  5.4 5.3 %collective-permute-start.2 = (bf16[8,1920]{1,0:T(8,128)(2,1)}, bf16[8,1920]{1,0:T(8,128)(2,1)S(1)}, u32[]{:S(2)}, u32[]{:S(2)}) collective-permute-start(bf16[8,1920]{1,0:T(8,128)(2,1)} %get-tuple-element.18), channel_id=1, source_target_pairs={{0,1},{1,2},{2,3},{3,0},{4,5},{5,6},{6,7},{7,4},{8,9},{9,10},{10,1... | collective-permute-start | bytes 92168 | tf_op jit(solution)/shard_map/ppermute | solution.py:31
  10.7 5.5 %collective-permute-start.3 = (bf16[32,1920]{1,0:T(8,128)(2,1)S(1)}, bf16[32,1920]{1,0:T(8,128)(2,1)S(1)}, u32[]{:S(2)}, u32[]{:S(2)}) collective-permute-start(bf16[32,1920]{1,0:T(8,128)(2,1)S(1)} %get-tuple-element.56), channel_id=1, source_target_pairs={{0,96},{4,28},{8,104},{12,4},{16,112},{20,12},{24,120},{28,20},{32... | collective-permute-start | bytes 368648 | tf_op jit(solution)/shard_map/ppermute | solution.py:32
  13.8 7.5 %collective-permute-start.5 = (bf16[32,1920]{1,0:T(8,128)(2,1)S(1)}, bf16[32,1920]{1,0:T(8,128)(2,1)S(1)}, u32[]{:S(2)}, u32[]{:S(2)}) collective-permute-start(bf16[32,1920]{1,0:T(8,128)(2,1)S(1)} %get-tuple-element.56), channel_id=1, source_target_pairs={{0,32},{4,12},{8,40},{12,20},{16,48},{20,28},{24,56},{28,4},{32,64... | collective-permute-start | bytes 368648 | tf_op jit(solution)/shard_map/ppermute | solution.py:32
  13.9 6.6 %collective-permute-start.4 = (bf16[32,1920]{1,0:T(8,128)(2,1)S(1)}, bf16[32,1920]{1,0:T(8,128)(2,1)S(1)}, u32[]{:S(2)}, u32[]{:S(2)}) collective-permute-start(bf16[32,1920]{1,0:T(8,128)(2,1)S(1)} %get-tuple-element.56), channel_id=1, source_target_pairs={{0,64},{4,20},{8,72},{12,28},{16,80},{20,4},{24,88},{28,12},{32,96... | collective-permute-start | bytes 368648 | tf_op jit(solution)/shard_map/ppermute | solution.py:32
  21.7 4.7 %collective-permute-start.11 = (bf16[64,1920]{1,0:T(8,128)(2,1)S(1)}, bf16[64,1920]{1,0:T(8,128)(2,1)S(1)}, u32[]{:S(2)}, u32[]{:S(2)}) collective-permute-start(bf16[64,1920]{1,0:T(8,128)(2,1)S(1)} %convolution_convert_fusion.4), channel_id=1, source_target_pairs={{0,4},{4,0},{8,12},{12,8},{16,20},{20,16},{24,28},{28,24},{32,36},... | collective-permute-start | bytes 737288 | tf_op jit(solution)/shard_map/ppermute | solution.py:32
  21.8 18.1 %collective-permute-start.7 = (bf16[128,1920]{1,0:T(8,128)(2,1)S(1)}, bf16[128,1920]{1,0:T(8,128)(2,1)S(1)}, u32[]{:S(2)}, u32[]{:S(2)}) collective-permute-start(bf16[128,1920]{1,0:T(8,128)(2,1)S(1)} %constant_dynamic-update-slice_fusion.4), channel_id=1, source_target_pairs={{0,8},{4,36},{8,16},{12,44},{16,24},{20,52},{24,0},{28,60},{32,40}... | collective-permute-start | bytes 1474568 | tf_op jit(solution)/shard_map/ppermute | solution.py:32
  23.8 22.1 %collective-permute-start.6 = (bf16[128,1920]{1,0:T(8,128)(2,1)S(1)}, bf16[128,1920]{1,0:T(8,128)(2,1)S(1)}, u32[]{:S(2)}, u32[]{:S(2)}) collective-permute-start(bf16[128,1920]{1,0:T(8,128)(2,1)S(1)} %constant_dynamic-update-slice_fusion.4), channel_id=1, source_target_pairs={{0,24},{4,100},{8,0},{12,108},{16,8},{20,116},{24,16},{28,124},{32... | collective-permute-start | bytes 1474568 | tf_op jit(solution)/shard_map/ppermute | solution.py:32
  26.6 5.1 %slice-start.5 = ((s8[7340032]{0:T(1024)(128)(4,1)}), s8[3145728]{0:T(1024)(128)(4,1)S(1)}, s32[]{:S(2)}) async-start(s8[7340032]{0:T(1024)(128)(4,1)} %bitcast.58), calls=%async_computation.5 | async-start | bytes 6291456
  33.0 6.9 %collective-permute-start.12 = (bf16[32,2048]{1,0:T(8,128)(2,1)S(1)}, bf16[32,2048]{1,0:T(8,128)(2,1)S(1)}, u32[]{:S(2)}, u32[]{:S(2)}) collective-permute-start(bf16[32,2048]{1,0:T(8,128)(2,1)S(1)} %get-tuple-element.43), channel_id=1, source_target_pairs={{0,1},{1,2},{2,3},{3,0},{4,5},{5,6},{6,7},{7,4},{8,9},{9,10},{10,1... | collective-permute-start | bytes 393224 | tf_op jit(solution)/shard_map/ppermute | solution.py:31
  33.0 21.7 %collective-permute-start.14 = (bf16[32,2048]{1,0:T(8,128)(2,1)S(1)}, bf16[32,2048]{1,0:T(8,128)(2,1)S(1)}, u32[]{:S(2)}, u32[]{:S(2)}) collective-permute-start(bf16[32,2048]{1,0:T(8,128)(2,1)S(1)} %get-tuple-element.44), channel_id=1, source_target_pairs={{0,3},{1,0},{2,1},{3,2},{4,7},{5,4},{6,5},{7,6},{8,11},{9,8},{10,9... | collective-permute-start | bytes 393224 | tf_op jit(solution)/shard_map/ppermute | solution.py:31
  36.3 18.5 %collective-permute-start.15 = (bf16[32,2048]{1,0:T(8,128)(2,1)S(1)}, bf16[32,2048]{1,0:T(8,128)(2,1)S(1)}, u32[]{:S(2)}, u32[]{:S(2)}) collective-permute-start(bf16[32,2048]{1,0:T(8,128)(2,1)S(1)} %get-tuple-element.45), channel_id=1, source_target_pairs={{0,1},{1,2},{2,3},{3,0},{4,5},{5,6},{6,7},{7,4},{8,9},{9,10},{10,1... | collective-permute-start | bytes 393224 | tf_op jit(solution)/shard_map/ppermute | solution.py:31
  39.9 5.0 %collective-permute-start.16 = (bf16[32,2048]{1,0:T(8,128)(2,1)S(1)}, bf16[32,2048]{1,0:T(8,128)(2,1)S(1)}, u32[]{:S(2)}, u32[]{:S(2)}) collective-permute-start(bf16[32,2048]{1,0:T(8,128)(2,1)S(1)} %get-tuple-element.46), channel_id=1, source_target_pairs={{0,3},{1,0},{2,1},{3,2},{4,7},{5,4},{6,5},{7,6},{8,11},{9,8},{10,9... | collective-permute-start | bytes 393224 | tf_op jit(solution)/shard_map/ppermute | solution.py:31
  39.9 14.8 %collective-permute-start.13 = (bf16[32,2048]{1,0:T(8,128)(2,1)S(1)}, bf16[32,2048]{1,0:T(8,128)(2,1)S(1)}, u32[]{:S(2)}, u32[]{:S(2)}) collective-permute-start(bf16[32,2048]{1,0:T(8,128)(2,1)S(1)} %add_convert_fusion.6), channel_id=1, source_target_pairs={{0,1},{1,2},{2,3},{3,0},{4,5},{5,6},{6,7},{7,4},{8,9},{9,10},{10,1... | collective-permute-start | bytes 393224 | tf_op jit(solution)/shard_map/ppermute | solution.py:31
  44.8 7.4 %collective-permute-start.8 = (bf16[64,1920]{1,0:T(8,128)(2,1)S(1)}, bf16[64,1920]{1,0:T(8,128)(2,1)S(1)}, u32[]{:S(2)}, u32[]{:S(2)}) collective-permute-start(bf16[64,1920]{1,0:T(8,128)(2,1)S(1)} %slice.193), channel_id=1, source_target_pairs={{0,8},{4,36},{8,16},{12,44},{16,24},{20,52},{24,0},{28,60},{32,40}... | collective-permute-start | bytes 737288 | tf_op jit(solution)/shard_map/ppermute | solution.py:32
  45.9 7.7 %collective-permute-start.9 = (bf16[64,1920]{1,0:T(8,128)(2,1)S(1)}, bf16[64,1920]{1,0:T(8,128)(2,1)S(1)}, u32[]{:S(2)}, u32[]{:S(2)}) collective-permute-start(bf16[64,1920]{1,0:T(8,128)(2,1)S(1)} %slice.194), channel_id=1, source_target_pairs={{0,24},{4,100},{8,0},{12,108},{16,8},{20,116},{24,16},{28,124},{32... | collective-permute-start | bytes 737288 | tf_op jit(solution)/shard_map/ppermute | solution.py:32
  48.2 13.4 %slice-start.2 = ((s8[7340032]{0:T(1024)(128)(4,1)}), s8[4194304]{0:T(1024)(128)(4,1)S(1)}, s32[]{:S(2)}) async-start(s8[7340032]{0:T(1024)(128)(4,1)} %bitcast.56), calls=%async_computation.2 | async-start | bytes 8388608
  52.2 5.0 %collective-permute-start.17 = (bf16[32,2048]{1,0:T(8,128)(2,1)S(1)}, bf16[32,2048]{1,0:T(8,128)(2,1)S(1)}, u32[]{:S(2)}, u32[]{:S(2)}) collective-permute-start(bf16[32,2048]{1,0:T(8,128)(2,1)S(1)} %add_convert_fusion.5), channel_id=1, source_target_pairs={{0,3},{1,0},{2,1},{3,2},{4,7},{5,4},{6,5},{7,6},{8,11},{9,8},{10,9... | collective-permute-start | bytes 393224 | tf_op jit(solution)/shard_map/ppermute | solution.py:31
  54.7 3.5 %collective-permute-start.10 = (bf16[192,1920]{1,0:T(8,128)(2,1)S(1)}, bf16[192,1920]{1,0:T(8,128)(2,1)S(1)}, u32[]{:S(2)}, u32[]{:S(2)}) collective-permute-start(bf16[192,1920]{1,0:T(8,128)(2,1)S(1)} %convolution_convert_fusion.1), channel_id=1, source_target_pairs={{0,4},{4,0},{8,12},{12,8},{16,20},{20,16},{24,28},{28,24},{32,36},... | collective-permute-start | bytes 2211848 | tf_op jit(solution)/shard_map/ppermute | solution.py:32
  58.4 12.9 %collective-permute-start.21 = (bf16[32,2048]{1,0:T(8,128)(2,1)S(1)}, bf16[32,2048]{1,0:T(8,128)(2,1)S(1)}, u32[]{:S(2)}, u32[]{:S(2)}) collective-permute-start(bf16[32,2048]{1,0:T(8,128)(2,1)S(1)} %multiply_convert_fusion.1), channel_id=1, source_target_pairs={{0,1},{1,2},{2,3},{3,0},{4,5},{5,6},{6,7},{7,4},{8,9},{9,10},{10,1... | collective-permute-start | bytes 393224 | tf_op jit(solution)/shard_map/ppermute | solution.py:31
  58.4 16.1 %collective-permute-start.20 = (bf16[32,2048]{1,0:T(8,128)(2,1)S(1)}, bf16[32,2048]{1,0:T(8,128)(2,1)S(1)}, u32[]{:S(2)}, u32[]{:S(2)}) collective-permute-start(bf16[32,2048]{1,0:T(8,128)(2,1)S(1)} %multiply_convert_fusion.1), channel_id=1, source_target_pairs={{0,3},{1,0},{2,1},{3,2},{4,7},{5,4},{6,5},{7,6},{8,11},{9,8},{10,9... | collective-permute-start | bytes 393224 | tf_op jit(solution)/shard_map/ppermute | solution.py:31
  61.7 41.4 %slice-start = ((s8[7340032]{0:T(1024)(128)(4,1)}), s8[4194304]{0:T(1024)(128)(4,1)S(1)}, s32[]{:S(2)}) async-start(s8[7340032]{0:T(1024)(128)(4,1)} %bitcast.54), calls=%async_computation | async-start | bytes 8388608
  64.7 38.4 %slice-start.1 = ((s8[7340032]{0:T(1024)(128)(4,1)}), s8[3145728]{0:T(1024)(128)(4,1)S(1)}, s32[]{:S(2)}) async-start(s8[7340032]{0:T(1024)(128)(4,1)} %bitcast.54), calls=%async_computation.1 | async-start | bytes 6291456
  67.8 20.5 %collective-permute-start.18 = (bf16[96,2048]{1,0:T(8,128)(2,1)S(1)}, bf16[96,2048]{1,0:T(8,128)(2,1)S(1)}, u32[]{:S(2)}, u32[]{:S(2)}) collective-permute-start(bf16[96,2048]{1,0:T(8,128)(2,1)S(1)} %get-tuple-element.31), channel_id=1, source_target_pairs={{0,1},{1,2},{2,3},{3,0},{4,5},{5,6},{6,7},{7,4},{8,9},{9,10},{10,1... | collective-permute-start | bytes 1179656 | tf_op jit(solution)/shard_map/ppermute | solution.py:31
  67.9 30.3 %collective-permute-start.24 = (bf16[96,2048]{1,0:T(8,128)(2,1)S(1)}, bf16[96,2048]{1,0:T(8,128)(2,1)S(1)}, u32[]{:S(2)}, u32[]{:S(2)}) collective-permute-start(bf16[96,2048]{1,0:T(8,128)(2,1)S(1)} %get-tuple-element.32), channel_id=1, source_target_pairs={{0,3},{1,0},{2,1},{3,2},{4,7},{5,4},{6,5},{7,6},{8,11},{9,8},{10,9... | collective-permute-start | bytes 1179656 | tf_op jit(solution)/shard_map/ppermute | solution.py:31
  71.2 27.0 %collective-permute-start.25 = (bf16[96,2048]{1,0:T(8,128)(2,1)S(1)}, bf16[96,2048]{1,0:T(8,128)(2,1)S(1)}, u32[]{:S(2)}, u32[]{:S(2)}) collective-permute-start(bf16[96,2048]{1,0:T(8,128)(2,1)S(1)} %get-tuple-element.33), channel_id=1, source_target_pairs={{0,1},{1,2},{2,3},{3,0},{4,5},{5,6},{6,7},{7,4},{8,9},{9,10},{10,1... | collective-permute-start | bytes 1179656 | tf_op jit(solution)/shard_map/ppermute | solution.py:31
  71.3 19.2 %collective-permute-start.26 = (bf16[96,2048]{1,0:T(8,128)(2,1)S(1)}, bf16[96,2048]{1,0:T(8,128)(2,1)S(1)}, u32[]{:S(2)}, u32[]{:S(2)}) collective-permute-start(bf16[96,2048]{1,0:T(8,128)(2,1)S(1)} %get-tuple-element.34), channel_id=1, source_target_pairs={{0,3},{1,0},{2,1},{3,2},{4,7},{5,4},{6,5},{7,6},{8,11},{9,8},{10,9... | collective-permute-start | bytes 1179656 | tf_op jit(solution)/shard_map/ppermute | solution.py:31
  74.6 13.7 %collective-permute-start.22 = (bf16[16,2048]{1,0:T(8,128)(2,1)S(1)}, bf16[16,2048]{1,0:T(8,128)(2,1)S(1)}, u32[]{:S(2)}, u32[]{:S(2)}) collective-permute-start(bf16[16,2048]{1,0:T(8,128)(2,1)S(1)} %slice.210), channel_id=1, source_target_pairs={{0,1},{1,2},{2,3},{3,0},{4,5},{5,6},{6,7},{7,4},{8,9},{9,10},{10,1... | collective-permute-start | bytes 196616 | tf_op jit(solution)/shard_map/ppermute | solution.py:31
  88.3 5.0 %collective-permute-start.23 = (bf16[16,2048]{1,0:T(8,128)(2,1)S(1)}, bf16[16,2048]{1,0:T(8,128)(2,1)S(1)}, u32[]{:S(2)}, u32[]{:S(2)}) collective-permute-start(bf16[16,2048]{1,0:T(8,128)(2,1)S(1)} %slice.211), channel_id=1, source_target_pairs={{0,3},{1,0},{2,1},{3,2},{4,7},{5,4},{6,5},{7,6},{8,11},{9,8},{10,9... | collective-permute-start | bytes 196616 | tf_op jit(solution)/shard_map/ppermute | solution.py:31
  88.4 9.8 %collective-permute-start.19 = (bf16[96,2048]{1,0:T(8,128)(2,1)S(1)}, bf16[96,2048]{1,0:T(8,128)(2,1)S(1)}, u32[]{:S(2)}, u32[]{:S(2)}) collective-permute-start(bf16[96,2048]{1,0:T(8,128)(2,1)S(1)} %add_convert_fusion.2), channel_id=1, source_target_pairs={{0,1},{1,2},{2,3},{3,0},{4,5},{5,6},{6,7},{7,4},{8,9},{9,10},{10,1... | collective-permute-start | bytes 1179656 | tf_op jit(solution)/shard_map/ppermute | solution.py:31
  90.6 8.7 %collective-permute-start.27 = (bf16[96,2048]{1,0:T(8,128)(2,1)S(1)}, bf16[96,2048]{1,0:T(8,128)(2,1)S(1)}, u32[]{:S(2)}, u32[]{:S(2)}) collective-permute-start(bf16[96,2048]{1,0:T(8,128)(2,1)S(1)} %add_convert_fusion.1), channel_id=1, source_target_pairs={{0,3},{1,0},{2,1},{3,2},{4,7},{5,4},{6,5},{7,6},{8,11},{9,8},{10,9... | collective-permute-start | bytes 1179656 | tf_op jit(solution)/shard_map/ppermute | solution.py:31
  99.8 9.1 %collective-permute-start.29 = (bf16[96,2048]{1,0:T(8,128)(2,1)S(1)}, bf16[96,2048]{1,0:T(8,128)(2,1)S(1)}, u32[]{:S(2)}, u32[]{:S(2)}) collective-permute-start(bf16[96,2048]{1,0:T(8,128)(2,1)S(1)} %get-tuple-element.30), channel_id=1, source_target_pairs={{0,1},{1,2},{2,3},{3,0},{4,5},{5,6},{6,7},{7,4},{8,9},{9,10},{10,1... | collective-permute-start | bytes 1179656 | tf_op jit(solution)/shard_map/ppermute | solution.py:31
  100.2 8.8 %collective-permute-start.28 = (bf16[96,2048]{1,0:T(8,128)(2,1)S(1)}, bf16[96,2048]{1,0:T(8,128)(2,1)S(1)}, u32[]{:S(2)}, u32[]{:S(2)}) collective-permute-start(bf16[96,2048]{1,0:T(8,128)(2,1)S(1)} %get-tuple-element.30), channel_id=1, source_target_pairs={{0,3},{1,0},{2,1},{3,2},{4,7},{5,4},{6,5},{7,6},{8,11},{9,8},{10,9... | collective-permute-start | bytes 1179656 | tf_op jit(solution)/shard_map/ppermute | solution.py:31
  104.3 1.6 collective-permute-start.32
  108.9 6.9 %collective-permute-start.30 = (bf16[48,2048]{1,0:T(8,128)(2,1)S(1)}, bf16[48,2048]{1,0:T(8,128)(2,1)S(1)}, u32[]{:S(2)}, u32[]{:S(2)}) collective-permute-start(bf16[48,2048]{1,0:T(8,128)(2,1)S(1)} %slice.217), channel_id=1, source_target_pairs={{0,1},{1,2},{2,3},{3,0},{4,5},{5,6},{6,7},{7,4},{8,9},{9,10},{10,1... | collective-permute-start | bytes 589832 | tf_op jit(solution)/shard_map/ppermute | solution.py:31
  109.0 6.9 %collective-permute-start.31 = (bf16[48,2048]{1,0:T(8,128)(2,1)S(1)}, bf16[48,2048]{1,0:T(8,128)(2,1)S(1)}, u32[]{:S(2)}, u32[]{:S(2)}) collective-permute-start(bf16[48,2048]{1,0:T(8,128)(2,1)S(1)} %slice.218), channel_id=1, source_target_pairs={{0,3},{1,0},{2,1},{3,2},{4,7},{5,4},{6,5},{7,6},{8,11},{9,8},{10,9... | collective-permute-start | bytes 589832 | tf_op jit(solution)/shard_map/ppermute | solution.py:31
  119.0 2.2 %collective-permute-start.33 = (bf16[192,1792]{1,0:T(8,128)(2,1)S(1)}, bf16[192,1792]{1,0:T(8,128)(2,1)S(1)}, u32[]{:S(2)}, u32[]{:S(2)}) collective-permute-start(bf16[192,1792]{1,0:T(8,128)(2,1)S(1)} %bitcast.72), channel_id=1, source_target_pairs={{0,4},{4,0},{8,12},{12,8},{16,20},{20,16},{24,28},{28,24},{32,36},... | collective-permute-start | bytes 2064392 | tf_op jit(solution)/shard_map/ppermute | solution.py:32
  122.3 7.3 %collective-permute-start.34 = (bf16[64,1792]{1,0:T(8,128)(2,1)S(1)}, bf16[64,1792]{1,0:T(8,128)(2,1)S(1)}, u32[]{:S(2)}, u32[]{:S(2)}) collective-permute-start(bf16[64,1792]{1,0:T(8,128)(2,1)S(1)} %get-tuple-element.37), channel_id=1, source_target_pairs={{0,8},{4,36},{8,16},{12,44},{16,24},{20,52},{24,0},{28,60},{32,40}... | collective-permute-start | bytes 688136 | tf_op jit(solution)/shard_map/ppermute | solution.py:32
  123.9 6.0 %collective-permute-start.36 = (bf16[64,1792]{1,0:T(8,128)(2,1)S(1)}, bf16[64,1792]{1,0:T(8,128)(2,1)S(1)}, u32[]{:S(2)}, u32[]{:S(2)}) collective-permute-start(bf16[64,1792]{1,0:T(8,128)(2,1)S(1)} %get-tuple-element.38), channel_id=1, source_target_pairs={{0,24},{4,100},{8,0},{12,108},{16,8},{20,116},{24,16},{28,124},{32... | collective-permute-start | bytes 688136 | tf_op jit(solution)/shard_map/ppermute | solution.py:32
  130.1 9.0 %collective-permute-start.37 = (bf16[128,1792]{1,0:T(8,128)(2,1)S(1)}, bf16[128,1792]{1,0:T(8,128)(2,1)S(1)}, u32[]{:S(2)}, u32[]{:S(2)}) collective-permute-start(bf16[128,1792]{1,0:T(8,128)(2,1)S(1)} %pad_maximum_fusion.3), channel_id=1, source_target_pairs={{0,24},{4,100},{8,0},{12,108},{16,8},{20,116},{24,16},{28,124},{32... | collective-permute-start | bytes 1376264 | tf_op jit(solution)/shard_map/ppermute | solution.py:32
  133.2 9.8 %collective-permute-start.35 = (bf16[128,1792]{1,0:T(8,128)(2,1)S(1)}, bf16[128,1792]{1,0:T(8,128)(2,1)S(1)}, u32[]{:S(2)}, u32[]{:S(2)}) collective-permute-start(bf16[128,1792]{1,0:T(8,128)(2,1)S(1)} %pad_maximum_fusion.2), channel_id=1, source_target_pairs={{0,8},{4,36},{8,16},{12,44},{16,24},{20,52},{24,0},{28,60},{32,40}... | collective-permute-start | bytes 1376264 | tf_op jit(solution)/shard_map/ppermute | solution.py:32
  143.2 6.0 %collective-permute-start.38 = (bf16[32,1792]{1,0:T(8,128)(2,1)S(1)}, bf16[32,1792]{1,0:T(8,128)(2,1)S(1)}, u32[]{:S(2)}, u32[]{:S(2)}) collective-permute-start(bf16[32,1792]{1,0:T(8,128)(2,1)S(1)} %get-tuple-element.47), channel_id=1, source_target_pairs={{0,96},{4,28},{8,104},{12,4},{16,112},{20,12},{24,120},{28,20},{32... | collective-permute-start | bytes 344072 | tf_op jit(solution)/shard_map/ppermute | solution.py:32
  146.8 7.2 %collective-permute-start.40 = (bf16[32,1792]{1,0:T(8,128)(2,1)S(1)}, bf16[32,1792]{1,0:T(8,128)(2,1)S(1)}, u32[]{:S(2)}, u32[]{:S(2)}) collective-permute-start(bf16[32,1792]{1,0:T(8,128)(2,1)S(1)} %get-tuple-element.48), channel_id=1, source_target_pairs={{0,32},{4,12},{8,40},{12,20},{16,48},{20,28},{24,56},{28,4},{32,64... | collective-permute-start | bytes 344072 | tf_op jit(solution)/shard_map/ppermute | solution.py:32
  146.8 7.2 %collective-permute-start.39 = (bf16[32,1792]{1,0:T(8,128)(2,1)S(1)}, bf16[32,1792]{1,0:T(8,128)(2,1)S(1)}, u32[]{:S(2)}, u32[]{:S(2)}) collective-permute-start(bf16[32,1792]{1,0:T(8,128)(2,1)S(1)} %get-tuple-element.49), channel_id=1, source_target_pairs={{0,64},{4,20},{8,72},{12,28},{16,80},{20,4},{24,88},{28,12},{32,96... | collective-permute-start | bytes 344072 | tf_op jit(solution)/shard_map/ppermute | solution.py:32
  154.7 5.4 %collective-permute-start.43 = (bf16[8,1792]{1,0:T(8,128)(2,1)S(1)}, bf16[8,1792]{1,0:T(8,128)(2,1)S(1)}, u32[]{:S(2)}, u32[]{:S(2)}) collective-permute-start(bf16[8,1792]{1,0:T(8,128)(2,1)S(1)} %get-tuple-element.52), channel_id=1, source_target_pairs={{0,1},{1,2},{2,3},{3,0},{4,5},{5,6},{6,7},{7,4},{8,9},{9,10},{10,1... | collective-permute-start | bytes 86024 | tf_op jit(solution)/shard_map/ppermute | solution.py:31
  154.7 7.1 %collective-permute-start.42 = (bf16[8,1792]{1,0:T(8,128)(2,1)S(1)}, bf16[8,1792]{1,0:T(8,128)(2,1)S(1)}, u32[]{:S(2)}, u32[]{:S(2)}) collective-permute-start(bf16[8,1792]{1,0:T(8,128)(2,1)S(1)} %get-tuple-element.53), channel_id=1, source_target_pairs={{0,2},{1,3},{2,0},{3,1},{4,6},{5,7},{6,4},{7,5},{8,10},{9,11},{10,... | collective-permute-start | bytes 86024 | tf_op jit(solution)/shard_map/ppermute | solution.py:31
  159.7 3.9 %collective-permute-start.41 = (bf16[8,1792]{1,0:T(8,128)(2,1)S(1)}, bf16[8,1792]{1,0:T(8,128)(2,1)S(1)}, u32[]{:S(2)}, u32[]{:S(2)}) collective-permute-start(bf16[8,1792]{1,0:T(8,128)(2,1)S(1)} %get-tuple-element.54), channel_id=1, source_target_pairs={{0,3},{1,0},{2,1},{3,2},{4,7},{5,4},{6,5},{7,6},{8,11},{9,8},{10,9... | collective-permute-start | bytes 86024 | tf_op jit(solution)/shard_map/ppermute | solution.py:31
  (5 other events, 14.7 us)

commit v5 on v4

--- a/solution.py
+++ b/solution.py
@@ -134,6 +134,12 @@
     ).astype(jnp.bfloat16)
 
 
+def hold(first, then):
+    count = len(first)
+    values = lax.optimization_barrier((*first, *then))
+    return values[:count], values[count:]
+
+
 def shards(hidden, norm_gain, routes, route_scores, capacity, w_gate, w_up, w_down):
     experts = capacity.shape[0]
     expert = lax.axis_index("attn")
@@ -148,57 +154,82 @@
         out_specs=[pl.BlockSpec(memory_space=pltpu.VMEM)] * RING,
         name="prepare",
     )(place, hidden, norm_gain.reshape(1, -1), routes, route_scores, capacity.reshape(1, -1))
+    lane = jnp.arange(PAD)[None, :]
+    mine = (lane == expert + experts) | (lane == expert + 2 * experts)
+
+    def enter(lines, cuts):
+        picks = lines[:, width:].astype(jnp.float32)
+        quarter = lines.shape[0] // 2 // RING
+        theirs = move(pick(choose(picks, other), lines), "core", 1)
+        both = [value.reshape(RING, quarter, width + PAD) for value in (pick(choose(picks, expert), lines), theirs)]
+        slots = [value[:, low:high] for low, high in zip(cuts, cuts[1:] + [quarter]) for value in both]
+        slots = jnp.concatenate(slots, axis=1).reshape(RING * 2 * quarter, width + PAD)
+        scale = jnp.sum(jnp.where(mine, slots[:, width:].astype(jnp.float32), 0.0), axis=1)
+        return slots[:, :width], scale
+
+    def product(slots, weights):
+        part = slots.shape[0] // RING
+        value = jnp.dot(slots, weights[0], preferred_element_type=jnp.float32).astype(jnp.bfloat16)
+        return [value[r * part : (r + 1) * part] for r in range(RING)]
+
+    def activate(gate, gate_low, gate_high, up, up_low, up_high):
+        gate_sum = gate.astype(jnp.float32) + gate_low.astype(jnp.float32) + gate_high.astype(jnp.float32)
+        up_sum = up.astype(jnp.float32) + up_low.astype(jnp.float32) + up_high.astype(jnp.float32)
+        return (jax.nn.silu(gate_sum) * up_sum).astype(jnp.bfloat16)
+
+    def leave(whole, scale, lines):
+        picks = lines[:, width:].astype(jnp.float32)
+        chosen = jnp.concatenate([choose(picks, expert), choose(picks, other)], axis=1)
+        out = jnp.dot(whole, w_down[0], preferred_element_type=jnp.float32)
+        out = (out * scale[:, None]).astype(jnp.bfloat16).reshape(RING, 2, -1, width)
+        theirs = move(out[:, 1].reshape(-1, width), "core", 1)
+        returned = jnp.concatenate([out[:, 0].reshape(-1, width), theirs], axis=0)
+        return jnp.dot(chosen, returned, preferred_element_type=jnp.float32).astype(jnp.bfloat16)
+
     lines = jnp.concatenate(direct(blocks, "x"), axis=0)
     near = jnp.concatenate(direct([lines] * RING, 0), axis=0)
-    far = jnp.concatenate(gather_ring(near, 1)[1:], axis=0)
-    lane = jnp.arange(PAD)[None, :]
-    mine = (lane == expert + experts) | (lane == expert + 2 * experts)
-    spread = []
-    after = None
-    for lines in (near, far):
-        picks = lines[:, width:].astype(jnp.float32)
-        chosen = [choose(picks, expert), choose(picks, other)]
-        quarter = lines.shape[0] // 2 // RING
-        theirs = move(pick(chosen[1], lines), "core", 1)
-        slots = [value.reshape(RING, quarter, width + PAD) for value in (pick(chosen[0], lines), theirs)]
-        slots = jnp.concatenate(slots, axis=1).reshape(RING * 2 * quarter, width + PAD)
-        scale = jnp.sum(jnp.where(mine, slots[:, width:].astype(jnp.float32), 0.0), axis=1)
-        slots = slots[:, :width]
-        if after is not None:
-            slots, after = lax.optimization_barrier((slots, after))
-        part = 2 * quarter
-        gate = jnp.dot(slots, w_gate[0], preferred_element_type=jnp.float32).astype(jnp.bfloat16)
-        gate = [gate[r * part : (r + 1) * part] for r in range(RING)]
-        gate_far = move(gate[2], "x", 1)
-        gate_high = move(gate[3], "x", -1)
-        up = jnp.dot(slots, w_up[0], preferred_element_type=jnp.float32).astype(jnp.bfloat16)
-        up = [up[r * part : (r + 1) * part] for r in range(RING)]
-        up_far = move(up[2], "x", -1)
-        up_low = move(up[1], "x", 1)
-        gate_low = move(add(gate[1], gate_far), "x", 1)
-        up_high = move(add(up[3], up_far), "x", -1)
-        if after is not None:
-            whole = jnp.concatenate(gather_ring(after, "x"), axis=0)
-            gate_low, whole = lax.optimization_barrier((gate_low, whole))
-            near_state[0] = whole
-        gate_sum = gate[0].astype(jnp.float32) + gate_low.astype(jnp.float32) + gate_high.astype(jnp.float32)
-        up_sum = up[0].astype(jnp.float32) + up_low.astype(jnp.float32) + up_high.astype(jnp.float32)
-        activation = (jax.nn.silu(gate_sum) * up_sum).astype(jnp.bfloat16)
-        if after is None:
-            after = activation
-            near_state = [None, scale, jnp.concatenate(chosen, axis=1)]
-    far_state = [jnp.concatenate(gather_ring(activation, "x"), axis=0), scale, jnp.concatenate(chosen, axis=1)]
-    for whole, scale, chosen in (near_state, far_state):
-        if spread:
-            whole, spread[0] = lax.optimization_barrier((whole, spread[0]))
-        expert_out = jnp.dot(whole, w_down[0], preferred_element_type=jnp.float32)
-        expert_out = (expert_out * scale[:, None]).astype(jnp.bfloat16)
-        expert_out = expert_out.reshape(RING, 2, -1, width)
-        theirs = move(expert_out[:, 1].reshape(-1, width), "core", 1)
-        returned = jnp.concatenate([expert_out[:, 0].reshape(-1, width), theirs], axis=0)
-        spread.append(jnp.dot(chosen, returned, preferred_element_type=jnp.float32).astype(jnp.bfloat16))
-    part = spread[0].shape[0]
-    summed = scatter_ring(spread[0], [spread[1][r * part : (r + 1) * part] for r in range(RING - 1)], 1)
+    low, high = move(near, 1, 1), move(near, 1, -1)
+    slots, near_scale = enter(near, [0])
+    gate, up = product(slots, w_gate), product(slots, w_up)
+    (low, high), near_parts = hold((low, high), (*gate, *up))
+    gate, up = near_parts[:RING], near_parts[RING:]
+    half = near.shape[0] // 2
+    first, second = move(low[:half], 1, 1), move(high[half:], 1, -1)
+    gate_far, up_far = move(gate[2], "x", 1), move(up[2], "x", -1)
+    up_low, gate_high = move(up[1], "x", 1), move(gate[3], "x", -1)
+    (first, second), (gate_far, up_far) = hold((first, second), (gate_far, up_far))
+    gate_low, up_high = move(add(gate[1], gate_far), "x", 1), move(add(up[3], up_far), "x", -1)
+    near_act = activate(gate[0], gate_low, gate_high, up[0], up_low, up_high)
+    two = jnp.concatenate([first, second], axis=0)
+    one = jnp.concatenate([high, low], axis=0)
+    far = jnp.concatenate([first, second, high, low], axis=0)
+    cut = near.shape[0] // 2 // RING
+    slots, far_scale = enter(far, [0, cut])
+    gate = product(slots, w_gate)
+    gate_far, gate_high = move(gate[2], "x", 1), move(gate[3], "x", -1)
+    (near_act,), (slots,) = hold((near_act,), (slots,))
+    near_low, near_high = move(near_act, "x", 1), move(near_act, "x", -1)
+    up = product(slots, w_up)
+    (near_low, near_high), up = hold((near_low, near_high), up)
+    up_far, up_low = move(up[2], "x", -1), move(up[1], "x", 1)
+    gate_low, up_high = move(add(gate[1], gate_far), "x", 1), move(add(up[3], up_far), "x", -1)
+    (gate_high, up_low), (near_low, near_high) = hold((gate_high, up_low), (near_low, near_high))
+    half = near_act.shape[0] // 2
+    near_first, near_second = move(near_low[:half], "x", 1), move(near_high[half:], "x", -1)
+    (gate_low, up_high), (near_first, near_second) = hold((gate_low, up_high), (near_first, near_second))
+    near_whole = jnp.concatenate([near_act, near_high, near_first, near_second, near_low], axis=0)
+    far_act = activate(gate[0], gate_low, gate_high, up[0], up_low, up_high)
+    pieces = gather_ring(far_act, "x")
+    near_sum = leave(near_whole, near_scale, near)
+    (near_sum,), pieces = hold((near_sum,), pieces)
+    inner = 2 * cut
+    two_whole = jnp.concatenate([pieces[r][:inner] for r in (0, 1, 2, 4)], axis=0)
+    one_whole = jnp.concatenate([pieces[0][inner:], pieces[1][inner:], pieces[2][inner:], pieces[3], pieces[4][inner:]], axis=0)
+    far_scale = far_scale.reshape(RING, -1)
+    two_sum = leave(two_whole, far_scale[:, :inner].reshape(-1), two)
+    one_sum = leave(one_whole, far_scale[:, inner:].reshape(-1), one)
+    part = near.shape[0]
+    summed = scatter_ring(near_sum, [one_sum[:part], two_sum, one_sum[part:]], 1)
     part = part // RING
     pieces = direct([summed[r * part : (r + 1) * part] for r in range(RING)], 0)
     summed = sum(piece.astype(jnp.float32) for piece in pieces).astype(jnp.bfloat16)

time: 166 us -> 161 us (0.970)
  waiting for transfers between devices: 75.1 us -> 65.1 us
  matrix products: 19.2 us -> 22.5 us
    ppermute x26, waiting for transfers between devices: 43.1 us -> 38 us  [move(): lax.ppermute(value, 'exp', [(i, (i + step) % RING) for i in range(RING)])]
    ppermute x18 -> x19, waiting for transfers between devices: 31.9 us -> 27.1 us  [move(): return lax.ppermute(value, 'attn', attn_pairs(axis, step))]
    dot_general x8 -> x10, matrix products: 17.1 us -> 20.3 us  [the longest x4 11.6 us: product(): jnp.dot(slots, weights[0], preferred_element_type=jnp.float32)]
    ppermute x26, starting transfers between devices: 36.6 us -> 38.6 us  [move(): lax.ppermute(value, 'exp', [(i, (i + step) % RING) for i in range(RING)])]
    ppermute x18 -> x19, starting transfers between devices: 24.8 us -> 23.1 us  [move(): return lax.ppermute(value, 'attn', attn_pairs(axis, step))]
  transfers between devices with their start and end apart: 44 -> 45, of which waited for: 26 -> 23; matrix products, arithmetic and copies ran while one was open for 11% -> 11% of each run, Pallas kernels for 0% -> 0%
where the time goes in v5:
time: 161 us
  waiting for transfers between devices  65.1 us (40%)
  starting transfers between devices  61.6 us (38%)
  matrix products  22.5 us (14%)
  local copies, waits for them, and re-layouts  4.86 us (3%)
  Pallas kernels  3.38 us (2%)
  other arithmetic  2.59 us (2%)
    ppermute x26, starting transfers between devices, move(): lax.ppermute(value, 'exp', [(i, (i + step) % RING) for i in range(RING)])  38.6 us
    ppermute x26, waiting for transfers between devices, move(): lax.ppermute(value, 'exp', [(i, (i + step) % RING) for i in range(RING)])  38 us
    ppermute x19, waiting for transfers between devices, move(): return lax.ppermute(value, 'attn', attn_pairs(axis, step))  27.1 us
    ppermute x19, starting transfers between devices, move(): return lax.ppermute(value, 'attn', attn_pairs(axis, step))  23.1 us
    dot_general x4, matrix products, product(): jnp.dot(slots, weights[0], preferred_element_type=jnp.float32)  11.6 us
    dot_general x3, matrix products, leave(): out = jnp.dot(whole, w_down[0], preferred_element_type=jnp.float32)  7.61 us
  transfers between devices with their start and end apart: 45, of which 23 were waited for; matrix products, arithmetic and copies ran while one was open for 11% of the time, Pallas kernels for 0%

profile of v5, /device:TPU:0, one launch (start us, length us, event | category | flops | bytes accessed | tf_op | source)
XLA Modules:
  0.0 160.9 jit_solution(8438694159365070443)
XLA Ops:
  0.0 1.8 %prepare.1 = (bf16[8,1920]{1,0:T(8,128)(2,1)}, bf16[8,1920]{1,0:T(8,128)(2,1)}, bf16[8,1920]{1,0:T(8,128)(2,1)}, bf16[8,1920]{1,0:T(8,128)(2,1)}) custom-call(s32[1]{0:T(128)} %bitcast.place_ref, bf16[8,7168]{1,0:T(8,128)(2,1)} %hidden_ref.3, f32[1,7168]{1,0:T(1,128)} %bitcast.92, s32[8,8]{1,0:T(8,128)} %routes_ref.1, f32[8,8]{1,0:T(8,128)} %scores_ref.1, ...), custom_call_target="tpu_custom_call" | custom-call | tf_op jit(solution)/shard_map/prepare/pallas_call | solution.py:150
  1.8 2.8 %collective-permute-start = (bf16[8,1920]{1,0:T(8,128)(2,1)}, bf16[8,1920]{1,0:T(8,128)(2,1)S(1)}, u32[]{:S(2)}, u32[]{:S(2)}) collective-permute-start(bf16[8,1920]{1,0:T(8,128)(2,1)} %get-tuple-element.46), channel_id=1, source_target_pairs={{0,3},{1,0},{2,1},{3,2},{4,7},{5,4},{6,5},{7,6},{8,11},{9,8},{10,9... | collective-permute-start | bytes 92168 | tf_op jit(solution)/shard_map/ppermute | solution.py:31
  7.1 3.1 %collective-permute-done.1 = bf16[8,1920]{1,0:T(8,128)(2,1)S(1)} collective-permute-done((bf16[8,1920]{1,0:T(8,128)(2,1)}, bf16[8,1920]{1,0:T(8,128)(2,1)S(1)}, u32[]{:S(2)}, u32[]{:S(2)}) %collective-permute-start.1) | collective-permute-done | bytes 30752 | tf_op jit(solution)/shard_map/ppermute | solution.py:31
  10.7 3.0 %collective-permute-start.3 = (bf16[32,1920]{1,0:T(8,128)(2,1)S(1)}, bf16[32,1920]{1,0:T(8,128)(2,1)S(1)}, u32[]{:S(2)}, u32[]{:S(2)}) collective-permute-start(bf16[32,1920]{1,0:T(8,128)(2,1)S(1)} %get-tuple-element.126), channel_id=1, source_target_pairs={{0,96},{4,28},{8,104},{12,4},{16,112},{20,12},{24,120},{28,20},{32... | collective-permute-start | bytes 368648 | tf_op jit(solution)/shard_map/ppermute | solution.py:32
  13.9 2.2 %collective-permute-start.4 = (bf16[32,1920]{1,0:T(8,128)(2,1)S(1)}, bf16[32,1920]{1,0:T(8,128)(2,1)S(1)}, u32[]{:S(2)}, u32[]{:S(2)}) collective-permute-start(bf16[32,1920]{1,0:T(8,128)(2,1)S(1)} %get-tuple-element.126), channel_id=1, source_target_pairs={{0,64},{4,20},{8,72},{12,28},{16,80},{20,4},{24,88},{28,12},{32,96... | collective-permute-start | bytes 368648 | tf_op jit(solution)/shard_map/ppermute | solution.py:32
  16.2 4.2 %collective-permute-done.4 = bf16[32,1920]{1,0:T(8,128)(2,1)S(1)} collective-permute-done((bf16[32,1920]{1,0:T(8,128)(2,1)S(1)}, bf16[32,1920]{1,0:T(8,128)(2,1)S(1)}, u32[]{:S(2)}, u32[]{:S(2)}) %collective-permute-start.4) | collective-permute-done | bytes 122912 | tf_op jit(solution)/shard_map/ppermute | solution.py:32
  21.8 4.1 %collective-permute-start.7 = (bf16[128,1920]{1,0:T(8,128)(2,1)S(1)}, bf16[128,1920]{1,0:T(8,128)(2,1)S(1)}, u32[]{:S(2)}, u32[]{:S(2)}) collective-permute-start(bf16[128,1920]{1,0:T(8,128)(2,1)S(1)} %constant_dynamic-update-slice_fusion.4), channel_id=1, source_target_pairs={{0,24},{4,100},{8,0},{12,108},{16,8},{20,116},{24,16},{28,124},{32... | collective-permute-start | bytes 1474568 | tf_op jit(solution)/shard_map/ppermute | solution.py:32
  26.4 4.4 %fusion.41 = bf16[128,2048]{1,0:T(8,128)(2,1)S(1)} fusion(bf16[1,1792,2048]{2,1,0:T(8,128)(2,1)} %param.14, bf16[128,1920]{1,0:T(8,128)(2,1)S(1)} %bitcast.71), kind=kOutput, calls=%fused_computation.26 | convolution fusion | flops 939786240 | bytes 8323072 | tf_op jit(solution)/shard_map/dot_general | solution.py:172
  31.6 1.2 fusion.38
  33.0 3.0 %collective-permute-done.6 = bf16[128,1920]{1,0:T(8,128)(2,1)S(1)} collective-permute-done((bf16[128,1920]{1,0:T(8,128)(2,1)S(1)}, bf16[128,1920]{1,0:T(8,128)(2,1)S(1)}, u32[]{:S(2)}, u32[]{:S(2)}) %collective-permute-start.6) | collective-permute-done | bytes 491552 | tf_op jit(solution)/shard_map/ppermute | solution.py:32
  36.4 1.8 %collective-permute-start.9 = (bf16[64,1920]{1,0:T(8,128)(2,1)S(1)}, bf16[64,1920]{1,0:T(8,128)(2,1)S(1)}, u32[]{:S(2)}, u32[]{:S(2)}) collective-permute-start(bf16[64,1920]{1,0:T(8,128)(2,1)S(1)} %slice.209), channel_id=1, source_target_pairs={{0,8},{4,36},{8,16},{12,44},{16,24},{20,52},{24,0},{28,60},{32,40}... | collective-permute-start | bytes 737288 | tf_op jit(solution)/shard_map/ppermute | solution.py:32
  38.4 3.2 %collective-permute-start.12 = (bf16[32,2048]{1,0:T(8,128)(2,1)S(1)}, bf16[32,2048]{1,0:T(8,128)(2,1)S(1)}, u32[]{:S(2)}, u32[]{:S(2)}) collective-permute-start(bf16[32,2048]{1,0:T(8,128)(2,1)S(1)} %get-tuple-element.54), channel_id=1, source_target_pairs={{0,3},{1,0},{2,1},{3,2},{4,7},{5,4},{6,5},{7,6},{8,11},{9,8},{10,9... | collective-permute-start | bytes 393224 | tf_op jit(solution)/shard_map/ppermute | solution.py:31
  41.8 3.1 %collective-permute-done.11 = bf16[32,2048]{1,0:T(8,128)(2,1)S(1)} collective-permute-done((bf16[32,2048]{1,0:T(8,128)(2,1)S(1)}, bf16[32,2048]{1,0:T(8,128)(2,1)S(1)}, u32[]{:S(2)}, u32[]{:S(2)}) %collective-permute-start.11) | collective-permute-done | bytes 131104 | tf_op jit(solution)/shard_map/ppermute | solution.py:31
  45.0 3.3 %collective-permute-start.16 = (bf16[32,2048]{1,0:T(8,128)(2,1)S(1)}, bf16[32,2048]{1,0:T(8,128)(2,1)S(1)}, u32[]{:S(2)}, u32[]{:S(2)}) collective-permute-start(bf16[32,2048]{1,0:T(8,128)(2,1)S(1)} %add_convert_fusion.5), channel_id=1, source_target_pairs={{0,3},{1,0},{2,1},{3,2},{4,7},{5,4},{6,5},{7,6},{8,11},{9,8},{10,9... | collective-permute-start | bytes 393224 | tf_op jit(solution)/shard_map/ppermute | solution.py:31
  51.1 3.5 %collective-permute-done.13 = bf16[32,2048]{1,0:T(8,128)(2,1)S(1)} collective-permute-done((bf16[32,2048]{1,0:T(8,128)(2,1)S(1)}, bf16[32,2048]{1,0:T(8,128)(2,1)S(1)}, u32[]{:S(2)}, u32[]{:S(2)}) %collective-permute-start.13) | collective-permute-done | bytes 131104 | tf_op jit(solution)/shard_map/ppermute | solution.py:31
  55.1 3.0 %fusion.14 = bf16[384,2048]{1,0:T(8,128)(2,1)S(1)} fusion(bf16[1,1792,2048]{2,1,0:T(8,128)(2,1)S(1)} %bitcast.68, bf16[384,1920]{1,0:T(8,128)(2,1)S(1)} %bitcast.75), kind=kOutput, calls=%fused_computation.14 | convolution fusion | flops 2819358720 | bytes 10289152 | tf_op jit(solution)/shard_map/dot_general | solution.py:172
  58.6 1.6 collective-permute-start.19
  60.2 3.0 %fusion.17 = bf16[384,2048]{1,0:T(8,128)(2,1)S(1)} fusion(bf16[384,1792]{1,0:T(8,128)(2,1)S(1)} %slice.278, bf16[1,1792,2048]{2,1,0:T(8,128)(2,1)S(1)} %bitcast.70), kind=kOutput, calls=%fused_computation.15 | convolution fusion | flops 2819358720 | bytes 10289152 | tf_op jit(solution)/shard_map/dot_general | solution.py:172
  63.5 3.3 %collective-permute-start.18 = (bf16[96,2048]{1,0:T(8,128)(2,1)S(1)}, bf16[96,2048]{1,0:T(8,128)(2,1)S(1)}, u32[]{:S(2)}, u32[]{:S(2)}) collective-permute-start(bf16[96,2048]{1,0:T(8,128)(2,1)S(1)} %get-tuple-element.94), channel_id=1, source_target_pairs={{0,3},{1,0},{2,1},{3,2},{4,7},{5,4},{6,5},{7,6},{8,11},{9,8},{10,9... | collective-permute-start | bytes 1179656 | tf_op jit(solution)/shard_map/ppermute | solution.py:31
  66.8 3.2 %collective-permute-start.24 = (bf16[96,2048]{1,0:T(8,128)(2,1)S(1)}, bf16[96,2048]{1,0:T(8,128)(2,1)S(1)}, u32[]{:S(2)}, u32[]{:S(2)}) collective-permute-start(bf16[96,2048]{1,0:T(8,128)(2,1)S(1)} %get-tuple-element.70), channel_id=1, source_target_pairs={{0,3},{1,0},{2,1},{3,2},{4,7},{5,4},{6,5},{7,6},{8,11},{9,8},{10,9... | collective-permute-start | bytes 1179656 | tf_op jit(solution)/shard_map/ppermute | solution.py:31
  70.1 6.6 %collective-permute-done.22 = bf16[96,2048]{1,0:T(8,128)(2,1)S(1)} collective-permute-done((bf16[96,2048]{1,0:T(8,128)(2,1)S(1)}, bf16[96,2048]{1,0:T(8,128)(2,1)S(1)}, u32[]{:S(2)}, u32[]{:S(2)}) %collective-permute-start.22) | collective-permute-done | bytes 393248 | tf_op jit(solution)/shard_map/ppermute | solution.py:31
  76.8 5.0 %collective-permute-done.24 = bf16[96,2048]{1,0:T(8,128)(2,1)S(1)} collective-permute-done((bf16[96,2048]{1,0:T(8,128)(2,1)S(1)}, bf16[96,2048]{1,0:T(8,128)(2,1)S(1)}, u32[]{:S(2)}, u32[]{:S(2)}) %collective-permute-start.24) | collective-permute-done | bytes 393248 | tf_op jit(solution)/shard_map/ppermute | solution.py:31
  81.9 3.8 %collective-permute-start.25 = (bf16[96,2048]{1,0:T(8,128)(2,1)S(1)}, bf16[96,2048]{1,0:T(8,128)(2,1)S(1)}, u32[]{:S(2)}, u32[]{:S(2)}) collective-permute-start(bf16[96,2048]{1,0:T(8,128)(2,1)S(1)} %add_convert_fusion.1), channel_id=1, source_target_pairs={{0,3},{1,0},{2,1},{3,2},{4,7},{5,4},{6,5},{7,6},{8,11},{9,8},{10,9... | collective-permute-start | bytes 1179656 | tf_op jit(solution)/shard_map/ppermute | solution.py:31
  85.8 3.2 %collective-permute-start.27 = (bf16[16,2048]{1,0:T(8,128)(2,1)S(1)}, bf16[16,2048]{1,0:T(8,128)(2,1)S(1)}, u32[]{:S(2)}, u32[]{:S(2)}) collective-permute-start(bf16[16,2048]{1,0:T(8,128)(2,1)S(1)} %slice.225), channel_id=1, source_target_pairs={{0,3},{1,0},{2,1},{3,2},{4,7},{5,4},{6,5},{7,6},{8,11},{9,8},{10,9... | collective-permute-start | bytes 196616 | tf_op jit(solution)/shard_map/ppermute | solution.py:31
  89.0 3.1 %collective-permute-done.26 = bf16[16,2048]{1,0:T(8,128)(2,1)S(1)} collective-permute-done((bf16[16,2048]{1,0:T(8,128)(2,1)S(1)}, bf16[16,2048]{1,0:T(8,128)(2,1)S(1)}, u32[]{:S(2)}, u32[]{:S(2)}) %collective-permute-start.26) | collective-permute-done | bytes 65568 | tf_op jit(solution)/shard_map/ppermute | solution.py:31
  92.1 1.0 collective-permute-done.27
  93.6 1.8 %collective-permute-start.30 = (bf16[96,2048]{1,0:T(8,128)(2,1)S(1)}, bf16[96,2048]{1,0:T(8,128)(2,1)S(1)}, u32[]{:S(2)}, u32[]{:S(2)}) collective-permute-start(bf16[96,2048]{1,0:T(8,128)(2,1)S(1)} %multiply_convert_fusion), channel_id=1, source_target_pairs={{0,1},{1,2},{2,3},{3,0},{4,5},{5,6},{6,7},{7,4},{8,9},{9,10},{10,1... | collective-permute-start | bytes 1179656 | tf_op jit(solution)/shard_map/ppermute | solution.py:31
  95.4 1.5 collective-permute-start.29
  97.0 1.2 fusion.35
  98.7 5.1 %collective-permute-done.30 = bf16[96,2048]{1,0:T(8,128)(2,1)S(1)} collective-permute-done((bf16[96,2048]{1,0:T(8,128)(2,1)S(1)}, bf16[96,2048]{1,0:T(8,128)(2,1)S(1)}, u32[]{:S(2)}, u32[]{:S(2)}) %collective-permute-start.30) | collective-permute-done | bytes 393248 | tf_op jit(solution)/shard_map/ppermute | solution.py:31
  103.8 0.9 collective-permute-start.31
  104.7 2.5 %collective-permute-start.32 = (bf16[48,2048]{1,0:T(8,128)(2,1)S(1)}, bf16[48,2048]{1,0:T(8,128)(2,1)S(1)}, u32[]{:S(2)}, u32[]{:S(2)}) collective-permute-start(bf16[48,2048]{1,0:T(8,128)(2,1)S(1)} %slice.291), channel_id=1, source_target_pairs={{0,3},{1,0},{2,1},{3,2},{4,7},{5,4},{6,5},{7,6},{8,11},{9,8},{10,9... | collective-permute-start | bytes 589832 | tf_op jit(solution)/shard_map/ppermute | solution.py:31
  108.0 2.8 %collective-permute-done.31 = bf16[48,2048]{1,0:T(8,128)(2,1)S(1)} collective-permute-done((bf16[48,2048]{1,0:T(8,128)(2,1)S(1)}, bf16[48,2048]{1,0:T(8,128)(2,1)S(1)}, u32[]{:S(2)}, u32[]{:S(2)}) %collective-permute-start.31) | collective-permute-done | bytes 196640 | tf_op jit(solution)/shard_map/ppermute | solution.py:31
  110.9 4.4 %fusion.32 = bf16[128,1792]{1,0:T(8,128)(2,1)S(1)} fusion(bf16[1,2048,1792]{2,1,0:T(8,128)(2,1)} %param.15, bf16[32,2048]{1,0:T(8,128)(2,1)S(1)} %slice.246, bf16[32,2048]{1,0:T(8,128)(2,1)S(1)} %slice.245, bf16[32,2048]{1,0:T(8,128)(2,1)S(1)} %slice.244, bf16[32,2048]{1,0:T(8,128)(2,1)S(1)} %slice.243, f32[128]{0:T(128)S(1)} %mul.137), kind=kOutput, calls=%fused_computation.23 | convolution fusion | flops 942080000 | bytes 8323584 | tf_op jit(solution)/shard_map/dot_general | solution.py:183
  116.1 2.1 %fusion.23 = bf16[256,1792]{1,0:T(8,128)(2,1)S(1)} fusion(bf16[256,2048]{1,0:T(8,128)(2,1)S(1)} %slice_dynamic-update-slice_fusion, bf16[1,2048,1792]{2,1,0:T(8,128)(2,1)S(1)} %bitcast.66, f32[256]{0:T(256)S(1)} %mul.134), kind=kOutput, calls=%fused_computation.18 | convolution fusion | flops 1879965696 | bytes 9307136 | tf_op jit(solution)/shard_map/dot_general | solution.py:183
  118.9 3.2 %collective-permute-start.37 = (bf16[64,1792]{1,0:T(8,128)(2,1)S(1)}, bf16[64,1792]{1,0:T(8,128)(2,1)S(1)}, u32[]{:S(2)}, u32[]{:S(2)}) collective-permute-start(bf16[64,1792]{1,0:T(8,128)(2,1)S(1)} %get-tuple-element.117), channel_id=1, source_target_pairs={{0,24},{4,100},{8,0},{12,108},{16,8},{20,116},{24,16},{28,124},{32... | collective-permute-start | bytes 688136 | tf_op jit(solution)/shard_map/ppermute | solution.py:32
  122.5 3.5 %collective-permute-done.35 = bf16[64,1792]{1,0:T(8,128)(2,1)S(1)} collective-permute-done((bf16[64,1792]{1,0:T(8,128)(2,1)S(1)}, bf16[64,1792]{1,0:T(8,128)(2,1)S(1)}, u32[]{:S(2)}, u32[]{:S(2)}) %collective-permute-start.35) | collective-permute-done | bytes 229408 | tf_op jit(solution)/shard_map/ppermute | solution.py:32
  126.2 3.3 %collective-permute-start.38 = (bf16[128,1792]{1,0:T(8,128)(2,1)S(1)}, bf16[128,1792]{1,0:T(8,128)(2,1)S(1)}, u32[]{:S(2)}, u32[]{:S(2)}) collective-permute-start(bf16[128,1792]{1,0:T(8,128)(2,1)S(1)} %pad_maximum_fusion.3), channel_id=1, source_target_pairs={{0,24},{4,100},{8,0},{12,108},{16,8},{20,116},{24,16},{28,124},{32... | collective-permute-start | bytes 1376264 | tf_op jit(solution)/shard_map/ppermute | solution.py:32
  129.6 5.9 %collective-permute-done.38 = bf16[128,1792]{1,0:T(8,128)(2,1)S(1)} collective-permute-done((bf16[128,1792]{1,0:T(8,128)(2,1)S(1)}, bf16[128,1792]{1,0:T(8,128)(2,1)S(1)}, u32[]{:S(2)}, u32[]{:S(2)}) %collective-permute-start.38) | collective-permute-done | bytes 458784 | tf_op jit(solution)/shard_map/ppermute | solution.py:32
  135.5 3.8 %collective-permute-done.36 = bf16[128,1792]{1,0:T(8,128)(2,1)S(1)} collective-permute-done((bf16[128,1792]{1,0:T(8,128)(2,1)S(1)}, bf16[128,1792]{1,0:T(8,128)(2,1)S(1)}, u32[]{:S(2)}, u32[]{:S(2)}) %collective-permute-start.36) | collective-permute-done | bytes 458784 | tf_op jit(solution)/shard_map/ppermute | solution.py:32
  139.6 2.6 %collective-permute-start.39 = (bf16[32,1792]{1,0:T(8,128)(2,1)S(1)}, bf16[32,1792]{1,0:T(8,128)(2,1)S(1)}, u32[]{:S(2)}, u32[]{:S(2)}) collective-permute-start(bf16[32,1792]{1,0:T(8,128)(2,1)S(1)} %get-tuple-element.113), channel_id=1, source_target_pairs={{0,96},{4,28},{8,104},{12,4},{16,112},{20,12},{24,120},{28,20},{32... | collective-permute-start | bytes 344072 | tf_op jit(solution)/shard_map/ppermute | solution.py:32
  142.1 1.5 collective-permute-start.40
  144.5 4.9 %collective-permute-done.41 = bf16[32,1792]{1,0:T(8,128)(2,1)S(1)} collective-permute-done((bf16[32,1792]{1,0:T(8,128)(2,1)S(1)}, bf16[32,1792]{1,0:T(8,128)(2,1)S(1)}, u32[]{:S(2)}, u32[]{:S(2)}) %collective-permute-start.41) | collective-permute-done | bytes 114720 | tf_op jit(solution)/shard_map/ppermute | solution.py:32
  150.0 1.2 collective-permute-start.44
  151.2 3.6 %collective-permute-start.43 = (bf16[8,1792]{1,0:T(8,128)(2,1)S(1)}, bf16[8,1792]{1,0:T(8,128)(2,1)S(1)}, u32[]{:S(2)}, u32[]{:S(2)}) collective-permute-start(bf16[8,1792]{1,0:T(8,128)(2,1)S(1)} %get-tuple-element.123), channel_id=1, source_target_pairs={{0,2},{1,3},{2,0},{3,1},{4,6},{5,7},{6,4},{7,5},{8,10},{9,11},{10,... | collective-permute-start | bytes 86024 | tf_op jit(solution)/shard_map/ppermute | solution.py:31
  155.2 1.8 %collective-permute-done.43.refs_2_ = bf16[8,1792]{1,0:T(8,128)(2,1)S(1)} collective-permute-done((bf16[8,1792]{1,0:T(8,128)(2,1)S(1)}, bf16[8,1792]{1,0:T(8,128)(2,1)S(1)}, u32[]{:S(2)}, u32[]{:S(2)}) %collective-permute-start.43) | collective-permute-done | bytes 28704 | tf_op jit(solution)/shard_map/ppermute | solution.py:31
  157.0 1.7 %collective-permute-done.42.refs_1_ = bf16[8,1792]{1,0:T(8,128)(2,1)S(1)} collective-permute-done((bf16[8,1792]{1,0:T(8,128)(2,1)S(1)}, bf16[8,1792]{1,0:T(8,128)(2,1)S(1)}, u32[]{:S(2)}, u32[]{:S(2)}) %collective-permute-start.42) | collective-permute-done | bytes 28704 | tf_op jit(solution)/shard_map/ppermute | solution.py:31
  159.3 1.6 %finish.1 = bf16[8,7168]{1,0:T(8,128)(2,1)} custom-call(s32[1]{0:T(128)} %bitcast.place_ref, bf16[8,7168]{1,0:T(8,128)(2,1)} %hidden_ref.3, bf16[8,1792]{1,0:T(8,128)(2,1)} %get-tuple-element.125.refs_0_, bf16[8,1792]{1,0:T(8,128)(2,1)} %copy-done.2, bf16[8,1792]{1,0:T(8,128)(2,1)} %copy-done.1, bf16[8,1792]{1,0:T(8,128)(2,1)} %copy-done), custom_call_target="tpu_custom_call" | custom-call | tf_op jit(solution)/shard_map/finish/pallas_call | solution.py:237
  (172 shorter events, 17.8 us)
Async XLA Ops:
  1.8 5.4 %collective-permute-start = (bf16[8,1920]{1,0:T(8,128)(2,1)}, bf16[8,1920]{1,0:T(8,128)(2,1)S(1)}, u32[]{:S(2)}, u32[]{:S(2)}) collective-permute-start(bf16[8,1920]{1,0:T(8,128)(2,1)} %get-tuple-element.46), channel_id=1, source_target_pairs={{0,3},{1,0},{2,1},{3,2},{4,7},{5,4},{6,5},{7,6},{8,11},{9,8},{10,9... | collective-permute-start | bytes 92168 | tf_op jit(solution)/shard_map/ppermute | solution.py:31
  4.6 5.6 %collective-permute-start.1 = (bf16[8,1920]{1,0:T(8,128)(2,1)}, bf16[8,1920]{1,0:T(8,128)(2,1)S(1)}, u32[]{:S(2)}, u32[]{:S(2)}) collective-permute-start(bf16[8,1920]{1,0:T(8,128)(2,1)} %get-tuple-element.47), channel_id=1, source_target_pairs={{0,2},{1,3},{2,0},{3,1},{4,6},{5,7},{6,4},{7,5},{8,10},{9,11},{10,... | collective-permute-start | bytes 92168 | tf_op jit(solution)/shard_map/ppermute | solution.py:31
  5.4 5.3 %collective-permute-start.2 = (bf16[8,1920]{1,0:T(8,128)(2,1)}, bf16[8,1920]{1,0:T(8,128)(2,1)S(1)}, u32[]{:S(2)}, u32[]{:S(2)}) collective-permute-start(bf16[8,1920]{1,0:T(8,128)(2,1)} %get-tuple-element.48), channel_id=1, source_target_pairs={{0,1},{1,2},{2,3},{3,0},{4,5},{5,6},{6,7},{7,4},{8,9},{9,10},{10,1... | collective-permute-start | bytes 92168 | tf_op jit(solution)/shard_map/ppermute | solution.py:31
  10.7 5.5 %collective-permute-start.3 = (bf16[32,1920]{1,0:T(8,128)(2,1)S(1)}, bf16[32,1920]{1,0:T(8,128)(2,1)S(1)}, u32[]{:S(2)}, u32[]{:S(2)}) collective-permute-start(bf16[32,1920]{1,0:T(8,128)(2,1)S(1)} %get-tuple-element.126), channel_id=1, source_target_pairs={{0,96},{4,28},{8,104},{12,4},{16,112},{20,12},{24,120},{28,20},{32... | collective-permute-start | bytes 368648 | tf_op jit(solution)/shard_map/ppermute | solution.py:32
  13.8 7.5 %collective-permute-start.5 = (bf16[32,1920]{1,0:T(8,128)(2,1)S(1)}, bf16[32,1920]{1,0:T(8,128)(2,1)S(1)}, u32[]{:S(2)}, u32[]{:S(2)}) collective-permute-start(bf16[32,1920]{1,0:T(8,128)(2,1)S(1)} %get-tuple-element.126), channel_id=1, source_target_pairs={{0,32},{4,12},{8,40},{12,20},{16,48},{20,28},{24,56},{28,4},{32,64... | collective-permute-start | bytes 368648 | tf_op jit(solution)/shard_map/ppermute | solution.py:32
  13.9 6.6 %collective-permute-start.4 = (bf16[32,1920]{1,0:T(8,128)(2,1)S(1)}, bf16[32,1920]{1,0:T(8,128)(2,1)S(1)}, u32[]{:S(2)}, u32[]{:S(2)}) collective-permute-start(bf16[32,1920]{1,0:T(8,128)(2,1)S(1)} %get-tuple-element.126), channel_id=1, source_target_pairs={{0,64},{4,20},{8,72},{12,28},{16,80},{20,4},{24,88},{28,12},{32,96... | collective-permute-start | bytes 368648 | tf_op jit(solution)/shard_map/ppermute | solution.py:32
  21.7 4.6 %collective-permute-start.8 = (bf16[64,1920]{1,0:T(8,128)(2,1)S(1)}, bf16[64,1920]{1,0:T(8,128)(2,1)S(1)}, u32[]{:S(2)}, u32[]{:S(2)}) collective-permute-start(bf16[64,1920]{1,0:T(8,128)(2,1)S(1)} %convolution_convert_fusion.5), channel_id=1, source_target_pairs={{0,4},{4,0},{8,12},{12,8},{16,20},{20,16},{24,28},{28,24},{32,36},... | collective-permute-start | bytes 737288 | tf_op jit(solution)/shard_map/ppermute | solution.py:32
  21.8 11.1 %collective-permute-start.7 = (bf16[128,1920]{1,0:T(8,128)(2,1)S(1)}, bf16[128,1920]{1,0:T(8,128)(2,1)S(1)}, u32[]{:S(2)}, u32[]{:S(2)}) collective-permute-start(bf16[128,1920]{1,0:T(8,128)(2,1)S(1)} %constant_dynamic-update-slice_fusion.4), channel_id=1, source_target_pairs={{0,24},{4,100},{8,0},{12,108},{16,8},{20,116},{24,16},{28,124},{32... | collective-permute-start | bytes 1474568 | tf_op jit(solution)/shard_map/ppermute | solution.py:32
  26.0 10.0 %collective-permute-start.6 = (bf16[128,1920]{1,0:T(8,128)(2,1)S(1)}, bf16[128,1920]{1,0:T(8,128)(2,1)S(1)}, u32[]{:S(2)}, u32[]{:S(2)}) collective-permute-start(bf16[128,1920]{1,0:T(8,128)(2,1)S(1)} %constant_dynamic-update-slice_fusion.4), channel_id=1, source_target_pairs={{0,8},{4,36},{8,16},{12,44},{16,24},{20,52},{24,0},{28,60},{32,40}... | collective-permute-start | bytes 1474568 | tf_op jit(solution)/shard_map/ppermute | solution.py:32
  36.0 8.9 %collective-permute-start.10 = (bf16[64,1920]{1,0:T(8,128)(2,1)S(1)}, bf16[64,1920]{1,0:T(8,128)(2,1)S(1)}, u32[]{:S(2)}, u32[]{:S(2)}) collective-permute-start(bf16[64,1920]{1,0:T(8,128)(2,1)S(1)} %slice.210), channel_id=1, source_target_pairs={{0,24},{4,100},{8,0},{12,108},{16,8},{20,116},{24,16},{28,124},{32... | collective-permute-start | bytes 737288 | tf_op jit(solution)/shard_map/ppermute | solution.py:32
  36.4 8.6 %collective-permute-start.9 = (bf16[64,1920]{1,0:T(8,128)(2,1)S(1)}, bf16[64,1920]{1,0:T(8,128)(2,1)S(1)}, u32[]{:S(2)}, u32[]{:S(2)}) collective-permute-start(bf16[64,1920]{1,0:T(8,128)(2,1)S(1)} %slice.209), channel_id=1, source_target_pairs={{0,8},{4,36},{8,16},{12,44},{16,24},{20,52},{24,0},{28,60},{32,40}... | collective-permute-start | bytes 737288 | tf_op jit(solution)/shard_map/ppermute | solution.py:32
  38.3 6.7 %collective-permute-start.11 = (bf16[32,2048]{1,0:T(8,128)(2,1)S(1)}, bf16[32,2048]{1,0:T(8,128)(2,1)S(1)}, u32[]{:S(2)}, u32[]{:S(2)}) collective-permute-start(bf16[32,2048]{1,0:T(8,128)(2,1)S(1)} %get-tuple-element.53), channel_id=1, source_target_pairs={{0,1},{1,2},{2,3},{3,0},{4,5},{5,6},{6,7},{7,4},{8,9},{9,10},{10,1... | collective-permute-start | bytes 393224 | tf_op jit(solution)/shard_map/ppermute | solution.py:31
  38.4 6.6 %collective-permute-start.12 = (bf16[32,2048]{1,0:T(8,128)(2,1)S(1)}, bf16[32,2048]{1,0:T(8,128)(2,1)S(1)}, u32[]{:S(2)}, u32[]{:S(2)}) collective-permute-start(bf16[32,2048]{1,0:T(8,128)(2,1)S(1)} %get-tuple-element.54), channel_id=1, source_target_pairs={{0,3},{1,0},{2,1},{3,2},{4,7},{5,4},{6,5},{7,6},{8,11},{9,8},{10,9... | collective-permute-start | bytes 393224 | tf_op jit(solution)/shard_map/ppermute | solution.py:31
  41.6 9.1 %collective-permute-start.14 = (bf16[32,2048]{1,0:T(8,128)(2,1)S(1)}, bf16[32,2048]{1,0:T(8,128)(2,1)S(1)}, u32[]{:S(2)}, u32[]{:S(2)}) collective-permute-start(bf16[32,2048]{1,0:T(8,128)(2,1)S(1)} %get-tuple-element.56), channel_id=1, source_target_pairs={{0,3},{1,0},{2,1},{3,2},{4,7},{5,4},{6,5},{7,6},{8,11},{9,8},{10,9... | collective-permute-start | bytes 393224 | tf_op jit(solution)/shard_map/ppermute | solution.py:31
  44.9 6.2 %collective-permute-start.15 = (bf16[32,2048]{1,0:T(8,128)(2,1)S(1)}, bf16[32,2048]{1,0:T(8,128)(2,1)S(1)}, u32[]{:S(2)}, u32[]{:S(2)}) collective-permute-start(bf16[32,2048]{1,0:T(8,128)(2,1)S(1)} %get-tuple-element.58), channel_id=1, source_target_pairs={{0,1},{1,2},{2,3},{3,0},{4,5},{5,6},{6,7},{7,4},{8,9},{9,10},{10,1... | collective-permute-start | bytes 393224 | tf_op jit(solution)/shard_map/ppermute | solution.py:31
  45.0 6.1 %collective-permute-start.16 = (bf16[32,2048]{1,0:T(8,128)(2,1)S(1)}, bf16[32,2048]{1,0:T(8,128)(2,1)S(1)}, u32[]{:S(2)}, u32[]{:S(2)}) collective-permute-start(bf16[32,2048]{1,0:T(8,128)(2,1)S(1)} %add_convert_fusion.5), channel_id=1, source_target_pairs={{0,3},{1,0},{2,1},{3,2},{4,7},{5,4},{6,5},{7,6},{8,11},{9,8},{10,9... | collective-permute-start | bytes 393224 | tf_op jit(solution)/shard_map/ppermute | solution.py:31
  48.3 6.2 %collective-permute-start.13 = (bf16[32,2048]{1,0:T(8,128)(2,1)S(1)}, bf16[32,2048]{1,0:T(8,128)(2,1)S(1)}, u32[]{:S(2)}, u32[]{:S(2)}) collective-permute-start(bf16[32,2048]{1,0:T(8,128)(2,1)S(1)} %add_convert_fusion.6), channel_id=1, source_target_pairs={{0,1},{1,2},{2,3},{3,0},{4,5},{5,6},{6,7},{7,4},{8,9},{9,10},{10,1... | collective-permute-start | bytes 393224 | tf_op jit(solution)/shard_map/ppermute | solution.py:31
  49.5 5.3 %collective-permute-start.17 = (bf16[192,1920]{1,0:T(8,128)(2,1)S(1)}, bf16[192,1920]{1,0:T(8,128)(2,1)S(1)}, u32[]{:S(2)}, u32[]{:S(2)}) collective-permute-start(bf16[192,1920]{1,0:T(8,128)(2,1)S(1)} %convolution_convert_fusion.1), channel_id=1, source_target_pairs={{0,4},{4,0},{8,12},{12,8},{16,20},{20,16},{24,28},{28,24},{32,36},... | collective-permute-start | bytes 2211848 | tf_op jit(solution)/shard_map/ppermute | solution.py:32
  54.9 5.3 %slice-start.6 = ((s8[7340032]{0:T(1024)(128)(4,1)}), s8[4194304]{0:T(1024)(128)(4,1)S(1)}, s32[]{:S(2)}) async-start(s8[7340032]{0:T(1024)(128)(4,1)} %bitcast.69), calls=%async_computation.6 | async-start | bytes 8388608
  55.1 41.9 %slice-start = ((s8[7340032]{0:T(1024)(128)(4,1)}), s8[3145728]{0:T(1024)(128)(4,1)S(1)}, s32[]{:S(2)}) async-start(s8[7340032]{0:T(1024)(128)(4,1)} %bitcast.63), calls=%async_computation | async-start | bytes 6291456
  58.1 38.9 %slice-start.1 = ((s8[7340032]{0:T(1024)(128)(4,1)}), s8[4194304]{0:T(1024)(128)(4,1)S(1)}, s32[]{:S(2)}) async-start(s8[7340032]{0:T(1024)(128)(4,1)} %bitcast.63), calls=%async_computation.1 | async-start | bytes 8388608
  58.1 8.7 %collective-permute-start.20 = (bf16[32,2048]{1,0:T(8,128)(2,1)S(1)}, bf16[32,2048]{1,0:T(8,128)(2,1)S(1)}, u32[]{:S(2)}, u32[]{:S(2)}) collective-permute-start(bf16[32,2048]{1,0:T(8,128)(2,1)S(1)} %multiply_convert_fusion.1), channel_id=1, source_target_pairs={{0,3},{1,0},{2,1},{3,2},{4,7},{5,4},{6,5},{7,6},{8,11},{9,8},{10,9... | collective-permute-start | bytes 393224 | tf_op jit(solution)/shard_map/ppermute | solution.py:31
  58.6 8.2 %collective-permute-start.19 = (bf16[32,2048]{1,0:T(8,128)(2,1)S(1)}, bf16[32,2048]{1,0:T(8,128)(2,1)S(1)}, u32[]{:S(2)}, u32[]{:S(2)}) collective-permute-start(bf16[32,2048]{1,0:T(8,128)(2,1)S(1)} %multiply_convert_fusion.1), channel_id=1, source_target_pairs={{0,1},{1,2},{2,3},{3,0},{4,5},{5,6},{6,7},{7,4},{8,9},{9,10},{10,1... | collective-permute-start | bytes 393224 | tf_op jit(solution)/shard_map/ppermute | solution.py:31
  63.3 13.3 %collective-permute-start.22 = (bf16[96,2048]{1,0:T(8,128)(2,1)S(1)}, bf16[96,2048]{1,0:T(8,128)(2,1)S(1)}, u32[]{:S(2)}, u32[]{:S(2)}) collective-permute-start(bf16[96,2048]{1,0:T(8,128)(2,1)S(1)} %get-tuple-element.93), channel_id=1, source_target_pairs={{0,1},{1,2},{2,3},{3,0},{4,5},{5,6},{6,7},{7,4},{8,9},{9,10},{10,1... | collective-permute-start | bytes 1179656 | tf_op jit(solution)/shard_map/ppermute | solution.py:31
  63.5 22.1 %collective-permute-start.18 = (bf16[96,2048]{1,0:T(8,128)(2,1)S(1)}, bf16[96,2048]{1,0:T(8,128)(2,1)S(1)}, u32[]{:S(2)}, u32[]{:S(2)}) collective-permute-start(bf16[96,2048]{1,0:T(8,128)(2,1)S(1)} %get-tuple-element.94), channel_id=1, source_target_pairs={{0,3},{1,0},{2,1},{3,2},{4,7},{5,4},{6,5},{7,6},{8,11},{9,8},{10,9... | collective-permute-start | bytes 1179656 | tf_op jit(solution)/shard_map/ppermute | solution.py:31
  66.8 18.8 %collective-permute-start.21 = (bf16[96,2048]{1,0:T(8,128)(2,1)S(1)}, bf16[96,2048]{1,0:T(8,128)(2,1)S(1)}, u32[]{:S(2)}, u32[]{:S(2)}) collective-permute-start(bf16[96,2048]{1,0:T(8,128)(2,1)S(1)} %get-tuple-element.65), channel_id=1, source_target_pairs={{0,1},{1,2},{2,3},{3,0},{4,5},{5,6},{6,7},{7,4},{8,9},{9,10},{10,1... | collective-permute-start | bytes 1179656 | tf_op jit(solution)/shard_map/ppermute | solution.py:31
  66.8 14.9 %collective-permute-start.24 = (bf16[96,2048]{1,0:T(8,128)(2,1)S(1)}, bf16[96,2048]{1,0:T(8,128)(2,1)S(1)}, u32[]{:S(2)}, u32[]{:S(2)}) collective-permute-start(bf16[96,2048]{1,0:T(8,128)(2,1)S(1)} %get-tuple-element.70), channel_id=1, source_target_pairs={{0,3},{1,0},{2,1},{3,2},{4,7},{5,4},{6,5},{7,6},{8,11},{9,8},{10,9... | collective-permute-start | bytes 1179656 | tf_op jit(solution)/shard_map/ppermute | solution.py:31
  76.7 16.4 %collective-permute-start.23 = (bf16[96,2048]{1,0:T(8,128)(2,1)S(1)}, bf16[96,2048]{1,0:T(8,128)(2,1)S(1)}, u32[]{:S(2)}, u32[]{:S(2)}) collective-permute-start(bf16[96,2048]{1,0:T(8,128)(2,1)S(1)} %add_convert_fusion.2), channel_id=1, source_target_pairs={{0,1},{1,2},{2,3},{3,0},{4,5},{5,6},{6,7},{7,4},{8,9},{9,10},{10,1... | collective-permute-start | bytes 1179656 | tf_op jit(solution)/shard_map/ppermute | solution.py:31
  81.9 11.3 %collective-permute-start.25 = (bf16[96,2048]{1,0:T(8,128)(2,1)S(1)}, bf16[96,2048]{1,0:T(8,128)(2,1)S(1)}, u32[]{:S(2)}, u32[]{:S(2)}) collective-permute-start(bf16[96,2048]{1,0:T(8,128)(2,1)S(1)} %add_convert_fusion.1), channel_id=1, source_target_pairs={{0,3},{1,0},{2,1},{3,2},{4,7},{5,4},{6,5},{7,6},{8,11},{9,8},{10,9... | collective-permute-start | bytes 1179656 | tf_op jit(solution)/shard_map/ppermute | solution.py:31
  85.7 6.4 %collective-permute-start.26 = (bf16[16,2048]{1,0:T(8,128)(2,1)S(1)}, bf16[16,2048]{1,0:T(8,128)(2,1)S(1)}, u32[]{:S(2)}, u32[]{:S(2)}) collective-permute-start(bf16[16,2048]{1,0:T(8,128)(2,1)S(1)} %slice.224), channel_id=1, source_target_pairs={{0,1},{1,2},{2,3},{3,0},{4,5},{5,6},{6,7},{7,4},{8,9},{9,10},{10,1... | collective-permute-start | bytes 196616 | tf_op jit(solution)/shard_map/ppermute | solution.py:31
  85.8 7.4 %collective-permute-start.27 = (bf16[16,2048]{1,0:T(8,128)(2,1)S(1)}, bf16[16,2048]{1,0:T(8,128)(2,1)S(1)}, u32[]{:S(2)}, u32[]{:S(2)}) collective-permute-start(bf16[16,2048]{1,0:T(8,128)(2,1)S(1)} %slice.225), channel_id=1, source_target_pairs={{0,3},{1,0},{2,1},{3,2},{4,7},{5,4},{6,5},{7,6},{8,11},{9,8},{10,9... | collective-permute-start | bytes 196616 | tf_op jit(solution)/shard_map/ppermute | solution.py:31
  93.6 10.2 %collective-permute-start.30 = (bf16[96,2048]{1,0:T(8,128)(2,1)S(1)}, bf16[96,2048]{1,0:T(8,128)(2,1)S(1)}, u32[]{:S(2)}, u32[]{:S(2)}) collective-permute-start(bf16[96,2048]{1,0:T(8,128)(2,1)S(1)} %multiply_convert_fusion), channel_id=1, source_target_pairs={{0,1},{1,2},{2,3},{3,0},{4,5},{5,6},{6,7},{7,4},{8,9},{9,10},{10,1... | collective-permute-start | bytes 1179656 | tf_op jit(solution)/shard_map/ppermute | solution.py:31
  95.4 9.3 %collective-permute-start.29 = (bf16[96,2048]{1,0:T(8,128)(2,1)S(1)}, bf16[96,2048]{1,0:T(8,128)(2,1)S(1)}, u32[]{:S(2)}, u32[]{:S(2)}) collective-permute-start(bf16[96,2048]{1,0:T(8,128)(2,1)S(1)} %multiply_convert_fusion), channel_id=1, source_target_pairs={{0,3},{1,0},{2,1},{3,2},{4,7},{5,4},{6,5},{7,6},{8,11},{9,8},{10,9... | collective-permute-start | bytes 1179656 | tf_op jit(solution)/shard_map/ppermute | solution.py:31
  98.2 9.4 %collective-permute-start.28 = (bf16[64,1792]{1,0:T(8,128)(2,1)S(1)}, bf16[64,1792]{1,0:T(8,128)(2,1)S(1)}, u32[]{:S(2)}, u32[]{:S(2)}) collective-permute-start(bf16[64,1792]{1,0:T(8,128)(2,1)S(1)} %bitcast.90), channel_id=1, source_target_pairs={{0,4},{4,0},{8,12},{12,8},{16,20},{20,16},{24,28},{28,24},{32,36},... | collective-permute-start | bytes 688136 | tf_op jit(solution)/shard_map/ppermute | solution.py:32
  103.8 6.9 %collective-permute-start.31 = (bf16[48,2048]{1,0:T(8,128)(2,1)S(1)}, bf16[48,2048]{1,0:T(8,128)(2,1)S(1)}, u32[]{:S(2)}, u32[]{:S(2)}) collective-permute-start(bf16[48,2048]{1,0:T(8,128)(2,1)S(1)} %slice.290), channel_id=1, source_target_pairs={{0,1},{1,2},{2,3},{3,0},{4,5},{5,6},{6,7},{7,4},{8,9},{9,10},{10,1... | collective-permute-start | bytes 589832 | tf_op jit(solution)/shard_map/ppermute | solution.py:31
  104.7 6.0 %collective-permute-start.32 = (bf16[48,2048]{1,0:T(8,128)(2,1)S(1)}, bf16[48,2048]{1,0:T(8,128)(2,1)S(1)}, u32[]{:S(2)}, u32[]{:S(2)}) collective-permute-start(bf16[48,2048]{1,0:T(8,128)(2,1)S(1)} %slice.291), channel_id=1, source_target_pairs={{0,3},{1,0},{2,1},{3,2},{4,7},{5,4},{6,5},{7,6},{8,11},{9,8},{10,9... | collective-permute-start | bytes 589832 | tf_op jit(solution)/shard_map/ppermute | solution.py:31
  115.3 3.1 %collective-permute-start.34 = (bf16[64,1792]{1,0:T(8,128)(2,1)S(1)}, bf16[64,1792]{1,0:T(8,128)(2,1)S(1)}, u32[]{:S(2)}, u32[]{:S(2)}) collective-permute-start(bf16[64,1792]{1,0:T(8,128)(2,1)S(1)} %bitcast.91), channel_id=1, source_target_pairs={{0,4},{4,0},{8,12},{12,8},{16,20},{20,16},{24,28},{28,24},{32,36},... | collective-permute-start | bytes 688136 | tf_op jit(solution)/shard_map/ppermute | solution.py:32
  118.3 3.8 %collective-permute-start.33 = (bf16[128,1792]{1,0:T(8,128)(2,1)S(1)}, bf16[128,1792]{1,0:T(8,128)(2,1)S(1)}, u32[]{:S(2)}, u32[]{:S(2)}) collective-permute-start(bf16[128,1792]{1,0:T(8,128)(2,1)S(1)} %bitcast.87), channel_id=1, source_target_pairs={{0,4},{4,0},{8,12},{12,8},{16,20},{20,16},{24,28},{28,24},{32,36},... | collective-permute-start | bytes 1376264 | tf_op jit(solution)/shard_map/ppermute | solution.py:32
  118.8 7.3 %collective-permute-start.35 = (bf16[64,1792]{1,0:T(8,128)(2,1)S(1)}, bf16[64,1792]{1,0:T(8,128)(2,1)S(1)}, u32[]{:S(2)}, u32[]{:S(2)}) collective-permute-start(bf16[64,1792]{1,0:T(8,128)(2,1)S(1)} %get-tuple-element.116), channel_id=1, source_target_pairs={{0,8},{4,36},{8,16},{12,44},{16,24},{20,52},{24,0},{28,60},{32,40}... | collective-permute-start | bytes 688136 | tf_op jit(solution)/shard_map/ppermute | solution.py:32
  118.9 7.2 %collective-permute-start.37 = (bf16[64,1792]{1,0:T(8,128)(2,1)S(1)}, bf16[64,1792]{1,0:T(8,128)(2,1)S(1)}, u32[]{:S(2)}, u32[]{:S(2)}) collective-permute-start(bf16[64,1792]{1,0:T(8,128)(2,1)S(1)} %get-tuple-element.117), channel_id=1, source_target_pairs={{0,24},{4,100},{8,0},{12,108},{16,8},{20,116},{24,16},{28,124},{32... | collective-permute-start | bytes 688136 | tf_op jit(solution)/shard_map/ppermute | solution.py:32
  126.2 9.3 %collective-permute-start.38 = (bf16[128,1792]{1,0:T(8,128)(2,1)S(1)}, bf16[128,1792]{1,0:T(8,128)(2,1)S(1)}, u32[]{:S(2)}, u32[]{:S(2)}) collective-permute-start(bf16[128,1792]{1,0:T(8,128)(2,1)S(1)} %pad_maximum_fusion.3), channel_id=1, source_target_pairs={{0,24},{4,100},{8,0},{12,108},{16,8},{20,116},{24,16},{28,124},{32... | collective-permute-start | bytes 1376264 | tf_op jit(solution)/shard_map/ppermute | solution.py:32
  129.6 9.8 %collective-permute-start.36 = (bf16[128,1792]{1,0:T(8,128)(2,1)S(1)}, bf16[128,1792]{1,0:T(8,128)(2,1)S(1)}, u32[]{:S(2)}, u32[]{:S(2)}) collective-permute-start(bf16[128,1792]{1,0:T(8,128)(2,1)S(1)} %pad_maximum_fusion.2), channel_id=1, source_target_pairs={{0,8},{4,36},{8,16},{12,44},{16,24},{20,52},{24,0},{28,60},{32,40}... | collective-permute-start | bytes 1376264 | tf_op jit(solution)/shard_map/ppermute | solution.py:32
  139.6 4.9 %collective-permute-start.39 = (bf16[32,1792]{1,0:T(8,128)(2,1)S(1)}, bf16[32,1792]{1,0:T(8,128)(2,1)S(1)}, u32[]{:S(2)}, u32[]{:S(2)}) collective-permute-start(bf16[32,1792]{1,0:T(8,128)(2,1)S(1)} %get-tuple-element.113), channel_id=1, source_target_pairs={{0,96},{4,28},{8,104},{12,4},{16,112},{20,12},{24,120},{28,20},{32... | collective-permute-start | bytes 344072 | tf_op jit(solution)/shard_map/ppermute | solution.py:32
  142.1 7.2 %collective-permute-start.41 = (bf16[32,1792]{1,0:T(8,128)(2,1)S(1)}, bf16[32,1792]{1,0:T(8,128)(2,1)S(1)}, u32[]{:S(2)}, u32[]{:S(2)}) collective-permute-start(bf16[32,1792]{1,0:T(8,128)(2,1)S(1)} %get-tuple-element.114), channel_id=1, source_target_pairs={{0,32},{4,12},{8,40},{12,20},{16,48},{20,28},{24,56},{28,4},{32,64... | collective-permute-start | bytes 344072 | tf_op jit(solution)/shard_map/ppermute | solution.py:32
  142.1 7.2 %collective-permute-start.40 = (bf16[32,1792]{1,0:T(8,128)(2,1)S(1)}, bf16[32,1792]{1,0:T(8,128)(2,1)S(1)}, u32[]{:S(2)}, u32[]{:S(2)}) collective-permute-start(bf16[32,1792]{1,0:T(8,128)(2,1)S(1)} %get-tuple-element.115), channel_id=1, source_target_pairs={{0,64},{4,20},{8,72},{12,28},{16,80},{20,4},{24,88},{28,12},{32,96... | collective-permute-start | bytes 344072 | tf_op jit(solution)/shard_map/ppermute | solution.py:32
  150.0 5.2 %collective-permute-start.44 = (bf16[8,1792]{1,0:T(8,128)(2,1)S(1)}, bf16[8,1792]{1,0:T(8,128)(2,1)S(1)}, u32[]{:S(2)}, u32[]{:S(2)}) collective-permute-start(bf16[8,1792]{1,0:T(8,128)(2,1)S(1)} %get-tuple-element.122), channel_id=1, source_target_pairs={{0,1},{1,2},{2,3},{3,0},{4,5},{5,6},{6,7},{7,4},{8,9},{9,10},{10,1... | collective-permute-start | bytes 86024 | tf_op jit(solution)/shard_map/ppermute | solution.py:31
  151.2 5.8 %collective-permute-start.43 = (bf16[8,1792]{1,0:T(8,128)(2,1)S(1)}, bf16[8,1792]{1,0:T(8,128)(2,1)S(1)}, u32[]{:S(2)}, u32[]{:S(2)}) collective-permute-start(bf16[8,1792]{1,0:T(8,128)(2,1)S(1)} %get-tuple-element.123), channel_id=1, source_target_pairs={{0,2},{1,3},{2,0},{3,1},{4,6},{5,7},{6,4},{7,5},{8,10},{9,11},{10,... | collective-permute-start | bytes 86024 | tf_op jit(solution)/shard_map/ppermute | solution.py:31
  154.8 3.9 %collective-permute-start.42 = (bf16[8,1792]{1,0:T(8,128)(2,1)S(1)}, bf16[8,1792]{1,0:T(8,128)(2,1)S(1)}, u32[]{:S(2)}, u32[]{:S(2)}) collective-permute-start(bf16[8,1792]{1,0:T(8,128)(2,1)S(1)} %get-tuple-element.124), channel_id=1, source_target_pairs={{0,3},{1,0},{2,1},{3,2},{4,7},{5,4},{6,5},{7,6},{8,11},{9,8},{10,9... | collective-permute-start | bytes 86024 | tf_op jit(solution)/shard_map/ppermute | solution.py:31
  (8 other events, 30.6 us)

commit v6 on v5

--- a/solution.py
+++ b/solution.py
@@ -135,9 +135,7 @@
 
 
 def hold(first, then):
-    count = len(first)
-    values = lax.optimization_barrier((*first, *then))
-    return values[:count], values[count:]
+    return lax.optimization_barrier((*first, *then))[len(first) :]
 
 
 def shards(hidden, norm_gain, routes, route_scores, capacity, w_gate, w_up, w_down):
@@ -157,11 +155,14 @@
     lane = jnp.arange(PAD)[None, :]
     mine = (lane == expert + experts) | (lane == expert + 2 * experts)
 
-    def enter(lines, cuts):
-        picks = lines[:, width:].astype(jnp.float32)
-        quarter = lines.shape[0] // 2 // RING
-        theirs = move(pick(choose(picks, other), lines), "core", 1)
-        both = [value.reshape(RING, quarter, width + PAD) for value in (pick(choose(picks, expert), lines), theirs)]
+    def picks_of(lines):
+        columns = lines[:, width:].astype(jnp.float32)
+        theirs = move(pick(choose(columns, other), lines), "core", 1)
+        return pick(choose(columns, expert), lines), theirs
+
+    def enter(own, theirs, cuts):
+        quarter = own.shape[0] // RING
+        both = [value.reshape(RING, quarter, width + PAD) for value in (own, theirs)]
         slots = [value[:, low:high] for low, high in zip(cuts, cuts[1:] + [quarter]) for value in both]
         slots = jnp.concatenate(slots, axis=1).reshape(RING * 2 * quarter, width + PAD)
         scale = jnp.sum(jnp.where(mine, slots[:, width:].astype(jnp.float32), 0.0), axis=1)
@@ -172,16 +173,27 @@
         value = jnp.dot(slots, weights[0], preferred_element_type=jnp.float32).astype(jnp.bfloat16)
         return [value[r * part : (r + 1) * part] for r in range(RING)]
 
-    def activate(gate, gate_low, gate_high, up, up_low, up_high):
-        gate_sum = gate.astype(jnp.float32) + gate_low.astype(jnp.float32) + gate_high.astype(jnp.float32)
-        up_sum = up.astype(jnp.float32) + up_low.astype(jnp.float32) + up_high.astype(jnp.float32)
+    def sends(gate, gate_far, up, up_far):
+        return (
+            jnp.concatenate([add(gate[1], gate_far), up[1]], axis=0),
+            jnp.concatenate([add(up[3], up_far), gate[3]], axis=0),
+        )
+
+    def activate(gate, up, low, high):
+        part = gate.shape[0]
+        low, high = low.astype(jnp.float32), high.astype(jnp.float32)
+        gate_sum = gate.astype(jnp.float32) + low[:part] + high[part:]
+        up_sum = up.astype(jnp.float32) + low[part:] + high[:part]
         return (jax.nn.silu(gate_sum) * up_sum).astype(jnp.bfloat16)
 
-    def leave(whole, scale, lines):
-        picks = lines[:, width:].astype(jnp.float32)
-        chosen = jnp.concatenate([choose(picks, expert), choose(picks, other)], axis=1)
+    def last(whole, scale):
         out = jnp.dot(whole, w_down[0], preferred_element_type=jnp.float32)
-        out = (out * scale[:, None]).astype(jnp.bfloat16).reshape(RING, 2, -1, width)
+        return (out * scale[:, None]).astype(jnp.bfloat16).reshape(RING, -1, width)
+
+    def leave(out, lines):
+        columns = lines[:, width:].astype(jnp.float32)
+        chosen = jnp.concatenate([choose(columns, expert), choose(columns, other)], axis=1)
+        out = out.reshape(RING, 2, -1, width)
         theirs = move(out[:, 1].reshape(-1, width), "core", 1)
         returned = jnp.concatenate([out[:, 0].reshape(-1, width), theirs], axis=0)
         return jnp.dot(chosen, returned, preferred_element_type=jnp.float32).astype(jnp.bfloat16)
@@ -189,45 +201,39 @@
     lines = jnp.concatenate(direct(blocks, "x"), axis=0)
     near = jnp.concatenate(direct([lines] * RING, 0), axis=0)
     low, high = move(near, 1, 1), move(near, 1, -1)
-    slots, near_scale = enter(near, [0])
+    slots, near_scale = enter(*picks_of(near), [0])
     gate, up = product(slots, w_gate), product(slots, w_up)
-    (low, high), near_parts = hold((low, high), (*gate, *up))
+    low, high, *near_parts = hold((), (low, high, *gate, *up))
     gate, up = near_parts[:RING], near_parts[RING:]
     half = near.shape[0] // 2
     first, second = move(low[:half], 1, 1), move(high[half:], 1, -1)
     gate_far, up_far = move(gate[2], "x", 1), move(up[2], "x", -1)
-    up_low, gate_high = move(up[1], "x", 1), move(gate[3], "x", -1)
-    (first, second), (gate_far, up_far) = hold((first, second), (gate_far, up_far))
-    gate_low, up_high = move(add(gate[1], gate_far), "x", 1), move(add(up[3], up_far), "x", -1)
-    near_act = activate(gate[0], gate_low, gate_high, up[0], up_low, up_high)
     two = jnp.concatenate([first, second], axis=0)
     one = jnp.concatenate([high, low], axis=0)
     far = jnp.concatenate([first, second, high, low], axis=0)
+    own, theirs = picks_of(far)
+    gate_far, up_far = hold((own,), (gate_far, up_far))
+    to_low, to_high = sends(gate, gate_far, up, up_far)
+    near_act = activate(gate[0], up[0], move(to_low, "x", 1), move(to_high, "x", -1))
     cut = near.shape[0] // 2 // RING
-    slots, far_scale = enter(far, [0, cut])
-    gate = product(slots, w_gate)
-    gate_far, gate_high = move(gate[2], "x", 1), move(gate[3], "x", -1)
-    (near_act,), (slots,) = hold((near_act,), (slots,))
+    slots, far_scale = enter(own, theirs, [0, cut])
+    gate, up = product(slots, w_gate), product(slots, w_up)
+    gate_far, up_far = move(gate[2], "x", 1), move(up[2], "x", -1)
+    (near_act,) = hold(up, (near_act,))
     near_low, near_high = move(near_act, "x", 1), move(near_act, "x", -1)
-    up = product(slots, w_up)
-    (near_low, near_high), up = hold((near_low, near_high), up)
-    up_far, up_low = move(up[2], "x", -1), move(up[1], "x", 1)
-    gate_low, up_high = move(add(gate[1], gate_far), "x", 1), move(add(up[3], up_far), "x", -1)
-    (gate_high, up_low), (near_low, near_high) = hold((gate_high, up_low), (near_low, near_high))
+    to_low, to_high = sends(gate, gate_far, up, up_far)
+    to_low, to_high, near_low, near_high = hold((), (to_low, to_high, near_low, near_high))
+    far_low, far_high = move(to_low, "x", 1), move(to_high, "x", -1)
     half = near_act.shape[0] // 2
     near_first, near_second = move(near_low[:half], "x", 1), move(near_high[half:], "x", -1)
-    (gate_low, up_high), (near_first, near_second) = hold((gate_low, up_high), (near_first, near_second))
+    near_first, near_second = hold((far_low, far_high), (near_first, near_second))
     near_whole = jnp.concatenate([near_act, near_high, near_first, near_second, near_low], axis=0)
-    far_act = activate(gate[0], gate_low, gate_high, up[0], up_low, up_high)
-    pieces = gather_ring(far_act, "x")
-    near_sum = leave(near_whole, near_scale, near)
-    (near_sum,), pieces = hold((near_sum,), pieces)
-    inner = 2 * cut
-    two_whole = jnp.concatenate([pieces[r][:inner] for r in (0, 1, 2, 4)], axis=0)
-    one_whole = jnp.concatenate([pieces[0][inner:], pieces[1][inner:], pieces[2][inner:], pieces[3], pieces[4][inner:]], axis=0)
-    far_scale = far_scale.reshape(RING, -1)
-    two_sum = leave(two_whole, far_scale[:, :inner].reshape(-1), two)
-    one_sum = leave(one_whole, far_scale[:, inner:].reshape(-1), one)
+    pieces = gather_ring(activate(gate[0], up[0], far_low, far_high), "x")
+    near_sum = leave(last(near_whole, near_scale), near)
+    pieces = hold((near_sum,), pieces)
+    out = last(jnp.concatenate(pieces, axis=0), far_scale)
+    two_sum = leave(out[:, : 2 * cut], two)
+    one_sum = leave(out[:, 2 * cut :], one)
     part = near.shape[0]
     summed = scatter_ring(near_sum, [one_sum[:part], two_sum, one_sum[part:]], 1)
     part = part // RING

time: 161 us -> 162 us (level)
  matrix products: 22.5 us -> 18.9 us
  starting transfers between devices: 61.6 us -> 64.2 us
  waiting for transfers between devices: 65.1 us -> 67.2 us
    dot_general x3 -> x2, matrix products: 7.61 us -> 4.19 us  [last(): out = jnp.dot(whole, w_down[0], preferred_element_type=jnp.float32)]
    ppermute x19, starting transfers between devices: 23.1 us -> 25.3 us  [move(): return lax.ppermute(value, 'attn', attn_pairs(axis, step))]
    ppermute x26 -> x22, waiting for transfers between devices: 38 us -> 39 us  [move(): lax.ppermute(value, 'exp', [(i, (i + step) % RING) for i in range(RING)])]
    ppermute x26 -> x22, starting transfers between devices: 38.6 us -> 38.9 us  [move(): lax.ppermute(value, 'exp', [(i, (i + step) % RING) for i in range(RING)])]
  transfers between devices with their start and end apart: 45 -> 41, of which waited for: 23 -> 23; matrix products, arithmetic and copies ran while one was open for 11% -> 9% of each run, Pallas kernels for 0% -> 0%
where the time goes in v6:
time: 162 us
  waiting for transfers between devices  67.2 us (41%)
  starting transfers between devices  64.2 us (40%)
  matrix products  18.9 us (12%)
  local copies, waits for them, and re-layouts  3.97 us (2%)
  other arithmetic  3.57 us (2%)
  Pallas kernels  3.38 us (2%)
    ppermute x22, waiting for transfers between devices, move(): lax.ppermute(value, 'exp', [(i, (i + step) % RING) for i in range(RING)])  39 us
    ppermute x22, starting transfers between devices, move(): lax.ppermute(value, 'exp', [(i, (i + step) % RING) for i in range(RING)])  38.9 us
    ppermute x19, waiting for transfers between devices, move(): return lax.ppermute(value, 'attn', attn_pairs(axis, step))  28.2 us
    ppermute x19, starting transfers between devices, move(): return lax.ppermute(value, 'attn', attn_pairs(axis, step))  25.3 us
    dot_general x4, matrix products, product(): jnp.dot(slots, weights[0], preferred_element_type=jnp.float32)  11.6 us
    dot_general x2, matrix products, last(): out = jnp.dot(whole, w_down[0], preferred_element_type=jnp.float32)  4.19 us
  transfers between devices with their start and end apart: 41, of which 23 were waited for; matrix products, arithmetic and copies ran while one was open for 9% of the time, Pallas kernels for 0%

profile of v6, /device:TPU:0, one launch (start us, length us, event | category | flops | bytes accessed | tf_op | source)
XLA Modules:
  0.0 162.3 jit_solution(1037526649289159054)
XLA Ops:
  0.0 1.8 %prepare.1 = (bf16[8,1920]{1,0:T(8,128)(2,1)}, bf16[8,1920]{1,0:T(8,128)(2,1)}, bf16[8,1920]{1,0:T(8,128)(2,1)}, bf16[8,1920]{1,0:T(8,128)(2,1)}) custom-call(s32[1]{0:T(128)} %bitcast.place_ref, bf16[8,7168]{1,0:T(8,128)(2,1)} %hidden_ref.3, f32[1,7168]{1,0:T(1,128)} %bitcast.87, s32[8,8]{1,0:T(8,128)} %routes_ref.1, f32[8,8]{1,0:T(8,128)} %scores_ref.1, ...), custom_call_target="tpu_custom_call" | custom-call | tf_op jit(solution)/shard_map/prepare/pallas_call | solution.py:148
  1.8 2.8 %collective-permute-start = (bf16[8,1920]{1,0:T(8,128)(2,1)}, bf16[8,1920]{1,0:T(8,128)(2,1)S(1)}, u32[]{:S(2)}, u32[]{:S(2)}) collective-permute-start(bf16[8,1920]{1,0:T(8,128)(2,1)} %get-tuple-element.34), channel_id=1, source_target_pairs={{0,3},{1,0},{2,1},{3,2},{4,7},{5,4},{6,5},{7,6},{8,11},{9,8},{10,9... | collective-permute-start | bytes 92168 | tf_op jit(solution)/shard_map/ppermute | solution.py:31
  5.4 0.9 collective-permute-start.2
  7.1 3.1 %collective-permute-done.1 = bf16[8,1920]{1,0:T(8,128)(2,1)S(1)} collective-permute-done((bf16[8,1920]{1,0:T(8,128)(2,1)}, bf16[8,1920]{1,0:T(8,128)(2,1)S(1)}, u32[]{:S(2)}, u32[]{:S(2)}) %collective-permute-start.1) | collective-permute-done | bytes 30752 | tf_op jit(solution)/shard_map/ppermute | solution.py:31
  10.7 3.0 %collective-permute-start.3 = (bf16[32,1920]{1,0:T(8,128)(2,1)S(1)}, bf16[32,1920]{1,0:T(8,128)(2,1)S(1)}, u32[]{:S(2)}, u32[]{:S(2)}) collective-permute-start(bf16[32,1920]{1,0:T(8,128)(2,1)S(1)} %get-tuple-element.100), channel_id=1, source_target_pairs={{0,96},{4,28},{8,104},{12,4},{16,112},{20,12},{24,120},{28,20},{32... | collective-permute-start | bytes 368648 | tf_op jit(solution)/shard_map/ppermute | solution.py:32
  13.9 2.2 %collective-permute-start.4 = (bf16[32,1920]{1,0:T(8,128)(2,1)S(1)}, bf16[32,1920]{1,0:T(8,128)(2,1)S(1)}, u32[]{:S(2)}, u32[]{:S(2)}) collective-permute-start(bf16[32,1920]{1,0:T(8,128)(2,1)S(1)} %get-tuple-element.100), channel_id=1, source_target_pairs={{0,64},{4,20},{8,72},{12,28},{16,80},{20,4},{24,88},{28,12},{32,96... | collective-permute-start | bytes 368648 | tf_op jit(solution)/shard_map/ppermute | solution.py:32
  16.2 4.2 %collective-permute-done.4 = bf16[32,1920]{1,0:T(8,128)(2,1)S(1)} collective-permute-done((bf16[32,1920]{1,0:T(8,128)(2,1)S(1)}, bf16[32,1920]{1,0:T(8,128)(2,1)S(1)}, u32[]{:S(2)}, u32[]{:S(2)}) %collective-permute-start.4) | collective-permute-done | bytes 122912 | tf_op jit(solution)/shard_map/ppermute | solution.py:32
  21.9 4.1 %collective-permute-start.7 = (bf16[128,1920]{1,0:T(8,128)(2,1)S(1)}, bf16[128,1920]{1,0:T(8,128)(2,1)S(1)}, u32[]{:S(2)}, u32[]{:S(2)}) collective-permute-start(bf16[128,1920]{1,0:T(8,128)(2,1)S(1)} %constant_dynamic-update-slice_fusion.4), channel_id=1, source_target_pairs={{0,24},{4,100},{8,0},{12,108},{16,8},{20,116},{24,16},{28,124},{32... | collective-permute-start | bytes 1474568 | tf_op jit(solution)/shard_map/ppermute | solution.py:32
  26.4 4.4 %fusion.33 = bf16[128,2048]{1,0:T(8,128)(2,1)S(1)} fusion(bf16[1,1792,2048]{2,1,0:T(8,128)(2,1)} %param.14, bf16[128,1920]{1,0:T(8,128)(2,1)S(1)} %bitcast.64), kind=kOutput, calls=%fused_computation.22 | convolution fusion | flops 939786240 | bytes 8323072 | tf_op jit(solution)/shard_map/dot_general | solution.py:173
  30.8 0.8 slice-done.3
  31.6 1.2 fusion.30
  32.9 3.1 %collective-permute-done.6 = bf16[128,1920]{1,0:T(8,128)(2,1)S(1)} collective-permute-done((bf16[128,1920]{1,0:T(8,128)(2,1)S(1)}, bf16[128,1920]{1,0:T(8,128)(2,1)S(1)}, u32[]{:S(2)}, u32[]{:S(2)}) %collective-permute-start.6) | collective-permute-done | bytes 491552 | tf_op jit(solution)/shard_map/ppermute | solution.py:32
  36.2 3.3 %collective-permute-start.10 = (bf16[64,1920]{1,0:T(8,128)(2,1)S(1)}, bf16[64,1920]{1,0:T(8,128)(2,1)S(1)}, u32[]{:S(2)}, u32[]{:S(2)}) collective-permute-start(bf16[64,1920]{1,0:T(8,128)(2,1)S(1)} %slice.210), channel_id=1, source_target_pairs={{0,24},{4,100},{8,0},{12,108},{16,8},{20,116},{24,16},{28,124},{32... | collective-permute-start | bytes 737288 | tf_op jit(solution)/shard_map/ppermute | solution.py:32
  40.0 3.2 %collective-permute-start.13 = (bf16[32,2048]{1,0:T(8,128)(2,1)S(1)}, bf16[32,2048]{1,0:T(8,128)(2,1)S(1)}, u32[]{:S(2)}, u32[]{:S(2)}) collective-permute-start(bf16[32,2048]{1,0:T(8,128)(2,1)S(1)} %get-tuple-element.42), channel_id=1, source_target_pairs={{0,3},{1,0},{2,1},{3,2},{4,7},{5,4},{6,5},{7,6},{8,11},{9,8},{10,9... | collective-permute-start | bytes 393224 | tf_op jit(solution)/shard_map/ppermute | solution.py:31
  45.3 0.8 collective-permute-done.12
  46.3 3.8 %collective-permute-start.15 = (bf16[64,2048]{1,0:T(8,128)(2,1)S(1)}, bf16[64,2048]{1,0:T(8,128)(2,1)S(1)}, u32[]{:S(2)}, u32[]{:S(2)}) collective-permute-start(bf16[64,2048]{1,0:T(8,128)(2,1)S(1)} %pad_maximum_fusion.7), channel_id=1, source_target_pairs={{0,3},{1,0},{2,1},{3,2},{4,7},{5,4},{6,5},{7,6},{8,11},{9,8},{10,9... | collective-permute-start | bytes 786440 | tf_op jit(solution)/shard_map/ppermute | solution.py:31
  50.8 3.1 %collective-permute-done.15 = bf16[64,2048]{1,0:T(8,128)(2,1)S(1)} collective-permute-done((bf16[64,2048]{1,0:T(8,128)(2,1)S(1)}, bf16[64,2048]{1,0:T(8,128)(2,1)S(1)}, u32[]{:S(2)}, u32[]{:S(2)}) %collective-permute-start.15) | collective-permute-done | bytes 262176 | tf_op jit(solution)/shard_map/ppermute | solution.py:31
  53.9 3.8 %collective-permute-done.14 = bf16[64,2048]{1,0:T(8,128)(2,1)S(1)} collective-permute-done((bf16[64,2048]{1,0:T(8,128)(2,1)S(1)}, bf16[64,2048]{1,0:T(8,128)(2,1)S(1)}, u32[]{:S(2)}, u32[]{:S(2)}) %collective-permute-start.14) | collective-permute-done | bytes 262176 | tf_op jit(solution)/shard_map/ppermute | solution.py:31
  58.2 3.0 %fusion.18 = bf16[384,2048]{1,0:T(8,128)(2,1)S(1)} fusion(bf16[1,1792,2048]{2,1,0:T(8,128)(2,1)S(1)} %bitcast.61, bf16[384,1920]{1,0:T(8,128)(2,1)S(1)} %bitcast.72), kind=kOutput, calls=%fused_computation.14 | convolution fusion | flops 2819358720 | bytes 10289152 | tf_op jit(solution)/shard_map/dot_general | solution.py:173
  61.2 3.0 %fusion.21 = bf16[384,2048]{1,0:T(8,128)(2,1)S(1)} fusion(bf16[1,1792,2048]{2,1,0:T(8,128)(2,1)S(1)} %bitcast.63, bf16[384,1920]{1,0:T(8,128)(2,1)S(1)} %bitcast.73), kind=kOutput, calls=%fused_computation.15 | convolution fusion | flops 2819358720 | bytes 10289152 | tf_op jit(solution)/shard_map/dot_general | solution.py:173
  64.4 3.3 %collective-permute-start.19 = (bf16[32,2048]{1,0:T(8,128)(2,1)S(1)}, bf16[32,2048]{1,0:T(8,128)(2,1)S(1)}, u32[]{:S(2)}, u32[]{:S(2)}) collective-permute-start(bf16[32,2048]{1,0:T(8,128)(2,1)S(1)} %fusion.54), channel_id=1, source_target_pairs={{0,3},{1,0},{2,1},{3,2},{4,7},{5,4},{6,5},{7,6},{8,11},{9,8},{10,9... | collective-permute-start | bytes 393224 | tf_op jit(solution)/shard_map/ppermute | solution.py:31
  67.7 3.2 %collective-permute-start.17 = (bf16[96,2048]{1,0:T(8,128)(2,1)S(1)}, bf16[96,2048]{1,0:T(8,128)(2,1)S(1)}, u32[]{:S(2)}, u32[]{:S(2)}) collective-permute-start(bf16[96,2048]{1,0:T(8,128)(2,1)S(1)} %get-tuple-element.71), channel_id=1, source_target_pairs={{0,3},{1,0},{2,1},{3,2},{4,7},{5,4},{6,5},{7,6},{8,11},{9,8},{10,9... | collective-permute-start | bytes 1179656 | tf_op jit(solution)/shard_map/ppermute | solution.py:31
  71.0 2.4 %collective-permute-done.16 = bf16[96,2048]{1,0:T(8,128)(2,1)S(1)} collective-permute-done((bf16[96,2048]{1,0:T(8,128)(2,1)S(1)}, bf16[96,2048]{1,0:T(8,128)(2,1)S(1)}, u32[]{:S(2)}, u32[]{:S(2)}) %collective-permute-start.16) | collective-permute-done | bytes 393248 | tf_op jit(solution)/shard_map/ppermute | solution.py:31
  73.5 4.7 %collective-permute-done.17 = bf16[96,2048]{1,0:T(8,128)(2,1)S(1)} collective-permute-done((bf16[96,2048]{1,0:T(8,128)(2,1)S(1)}, bf16[96,2048]{1,0:T(8,128)(2,1)S(1)}, u32[]{:S(2)}, u32[]{:S(2)}) %collective-permute-start.17) | collective-permute-done | bytes 393248 | tf_op jit(solution)/shard_map/ppermute | solution.py:31
  78.5 3.8 %collective-permute-start.21 = (bf16[192,2048]{1,0:T(8,128)(2,1)S(1)}, bf16[192,2048]{1,0:T(8,128)(2,1)S(1)}, u32[]{:S(2)}, u32[]{:S(2)}) collective-permute-start(bf16[192,2048]{1,0:T(8,128)(2,1)S(1)} %pad_maximum_fusion.2), channel_id=1, source_target_pairs={{0,3},{1,0},{2,1},{3,2},{4,7},{5,4},{6,5},{7,6},{8,11},{9,8},{10,9... | collective-permute-start | bytes 2359304 | tf_op jit(solution)/shard_map/ppermute | solution.py:31
  82.7 3.2 %collective-permute-start.23 = (bf16[16,2048]{1,0:T(8,128)(2,1)S(1)}, bf16[16,2048]{1,0:T(8,128)(2,1)S(1)}, u32[]{:S(2)}, u32[]{:S(2)}) collective-permute-start(bf16[16,2048]{1,0:T(8,128)(2,1)S(1)} %slice.229), channel_id=1, source_target_pairs={{0,3},{1,0},{2,1},{3,2},{4,7},{5,4},{6,5},{7,6},{8,11},{9,8},{10,9... | collective-permute-start | bytes 196616 | tf_op jit(solution)/shard_map/ppermute | solution.py:31
  85.9 10.8 %collective-permute-done.21 = bf16[192,2048]{1,0:T(8,128)(2,1)S(1)} collective-permute-done((bf16[192,2048]{1,0:T(8,128)(2,1)S(1)}, bf16[192,2048]{1,0:T(8,128)(2,1)S(1)}, u32[]{:S(2)}, u32[]{:S(2)}) %collective-permute-start.21) | collective-permute-done | bytes 786464 | tf_op jit(solution)/shard_map/ppermute | solution.py:31
  97.6 3.8 %collective-permute-start.25 = (bf16[96,2048]{1,0:T(8,128)(2,1)S(1)}, bf16[96,2048]{1,0:T(8,128)(2,1)S(1)}, u32[]{:S(2)}, u32[]{:S(2)}) collective-permute-start(bf16[96,2048]{1,0:T(8,128)(2,1)S(1)} %fusion.42), channel_id=1, source_target_pairs={{0,3},{1,0},{2,1},{3,2},{4,7},{5,4},{6,5},{7,6},{8,11},{9,8},{10,9... | collective-permute-start | bytes 1179656 | tf_op jit(solution)/shard_map/ppermute | solution.py:31
  101.4 1.2 fusion.27
  102.9 4.1 %collective-permute-done.26 = bf16[96,2048]{1,0:T(8,128)(2,1)S(1)} collective-permute-done((bf16[96,2048]{1,0:T(8,128)(2,1)S(1)}, bf16[96,2048]{1,0:T(8,128)(2,1)S(1)}, u32[]{:S(2)}, u32[]{:S(2)}) %collective-permute-start.26) | collective-permute-done | bytes 393248 | tf_op jit(solution)/shard_map/ppermute | solution.py:31
  107.2 3.5 %collective-permute-start.28 = (bf16[48,2048]{1,0:T(8,128)(2,1)S(1)}, bf16[48,2048]{1,0:T(8,128)(2,1)S(1)}, u32[]{:S(2)}, u32[]{:S(2)}) collective-permute-start(bf16[48,2048]{1,0:T(8,128)(2,1)S(1)} %slice.299), channel_id=1, source_target_pairs={{0,3},{1,0},{2,1},{3,2},{4,7},{5,4},{6,5},{7,6},{8,11},{9,8},{10,9... | collective-permute-start | bytes 589832 | tf_op jit(solution)/shard_map/ppermute | solution.py:31
  111.1 2.9 %collective-permute-done.27 = bf16[48,2048]{1,0:T(8,128)(2,1)S(1)} collective-permute-done((bf16[48,2048]{1,0:T(8,128)(2,1)S(1)}, bf16[48,2048]{1,0:T(8,128)(2,1)S(1)}, u32[]{:S(2)}, u32[]{:S(2)}) %collective-permute-start.27) | collective-permute-done | bytes 196640 | tf_op jit(solution)/shard_map/ppermute | solution.py:31
  114.2 3.0 %fusion.15 = bf16[384,1792]{1,0:T(8,128)(2,1)S(1)} fusion(bf16[384,2048]{1,0:T(8,128)(2,1)S(1)} %constant_dynamic-update-slice_fusion.20, bf16[1,2048,1792]{2,1,0:T(8,128)(2,1)S(1)} %bitcast.57, f32[384]{0:T(512)S(1)} %select_reduce_fusion), kind=kOutput, calls=%fused_computation.13 | convolution fusion | flops 2819948544 | bytes 10290688 | tf_op jit(solution)/shard_map/dot_general | solution.py:190
  118.1 0.8 collective-permute-done.30
  119.4 3.3 %collective-permute-start.33 = (bf16[64,1792]{1,0:T(8,128)(2,1)S(1)}, bf16[64,1792]{1,0:T(8,128)(2,1)S(1)}, u32[]{:S(2)}, u32[]{:S(2)}) collective-permute-start(bf16[64,1792]{1,0:T(8,128)(2,1)S(1)} %get-tuple-element.91), channel_id=1, source_target_pairs={{0,24},{4,100},{8,0},{12,108},{16,8},{20,116},{24,16},{28,124},{32... | collective-permute-start | bytes 688136 | tf_op jit(solution)/shard_map/ppermute | solution.py:32
  123.1 3.5 %collective-permute-done.31 = bf16[64,1792]{1,0:T(8,128)(2,1)S(1)} collective-permute-done((bf16[64,1792]{1,0:T(8,128)(2,1)S(1)}, bf16[64,1792]{1,0:T(8,128)(2,1)S(1)}, u32[]{:S(2)}, u32[]{:S(2)}) %collective-permute-start.31) | collective-permute-done | bytes 229408 | tf_op jit(solution)/shard_map/ppermute | solution.py:32
  126.7 3.4 %collective-permute-start.34 = (bf16[128,1792]{1,0:T(8,128)(2,1)S(1)}, bf16[128,1792]{1,0:T(8,128)(2,1)S(1)}, u32[]{:S(2)}, u32[]{:S(2)}) collective-permute-start(bf16[128,1792]{1,0:T(8,128)(2,1)S(1)} %pad_maximum_fusion.5), channel_id=1, source_target_pairs={{0,24},{4,100},{8,0},{12,108},{16,8},{20,116},{24,16},{28,124},{32... | collective-permute-start | bytes 1376264 | tf_op jit(solution)/shard_map/ppermute | solution.py:32
  130.2 5.9 %collective-permute-done.34 = bf16[128,1792]{1,0:T(8,128)(2,1)S(1)} collective-permute-done((bf16[128,1792]{1,0:T(8,128)(2,1)S(1)}, bf16[128,1792]{1,0:T(8,128)(2,1)S(1)}, u32[]{:S(2)}, u32[]{:S(2)}) %collective-permute-start.34) | collective-permute-done | bytes 458784 | tf_op jit(solution)/shard_map/ppermute | solution.py:32
  136.1 3.8 %collective-permute-done.32 = bf16[128,1792]{1,0:T(8,128)(2,1)S(1)} collective-permute-done((bf16[128,1792]{1,0:T(8,128)(2,1)S(1)}, bf16[128,1792]{1,0:T(8,128)(2,1)S(1)}, u32[]{:S(2)}, u32[]{:S(2)}) %collective-permute-start.32) | collective-permute-done | bytes 458784 | tf_op jit(solution)/shard_map/ppermute | solution.py:32
  140.1 3.1 %collective-permute-start.35 = (bf16[32,1792]{1,0:T(8,128)(2,1)S(1)}, bf16[32,1792]{1,0:T(8,128)(2,1)S(1)}, u32[]{:S(2)}, u32[]{:S(2)}) collective-permute-start(bf16[32,1792]{1,0:T(8,128)(2,1)S(1)} %get-tuple-element.87), channel_id=1, source_target_pairs={{0,96},{4,28},{8,104},{12,4},{16,112},{20,12},{24,120},{28,20},{32... | collective-permute-start | bytes 344072 | tf_op jit(solution)/shard_map/ppermute | solution.py:32
  143.2 1.5 collective-permute-start.36
  145.6 4.9 %collective-permute-done.37 = bf16[32,1792]{1,0:T(8,128)(2,1)S(1)} collective-permute-done((bf16[32,1792]{1,0:T(8,128)(2,1)S(1)}, bf16[32,1792]{1,0:T(8,128)(2,1)S(1)}, u32[]{:S(2)}, u32[]{:S(2)}) %collective-permute-start.37) | collective-permute-done | bytes 114720 | tf_op jit(solution)/shard_map/ppermute | solution.py:32
  151.2 1.5 collective-permute-start.40
  152.6 3.5 %collective-permute-start.39 = (bf16[8,1792]{1,0:T(8,128)(2,1)S(1)}, bf16[8,1792]{1,0:T(8,128)(2,1)S(1)}, u32[]{:S(2)}, u32[]{:S(2)}) collective-permute-start(bf16[8,1792]{1,0:T(8,128)(2,1)S(1)} %get-tuple-element.97), channel_id=1, source_target_pairs={{0,2},{1,3},{2,0},{3,1},{4,6},{5,7},{6,4},{7,5},{8,10},{9,11},{10,... | collective-permute-start | bytes 86024 | tf_op jit(solution)/shard_map/ppermute | solution.py:31
  156.2 1.2 collective-permute-start.38
  157.3 1.0 collective-permute-done.39.refs_2_
  158.3 1.7 %collective-permute-done.38.refs_1_ = bf16[8,1792]{1,0:T(8,128)(2,1)S(1)} collective-permute-done((bf16[8,1792]{1,0:T(8,128)(2,1)S(1)}, bf16[8,1792]{1,0:T(8,128)(2,1)S(1)}, u32[]{:S(2)}, u32[]{:S(2)}) %collective-permute-start.38) | collective-permute-done | bytes 28704 | tf_op jit(solution)/shard_map/ppermute | solution.py:31
  160.7 1.6 finish.1
  (166 shorter events, 15.2 us)
Async XLA Ops:
  1.8 5.3 %collective-permute-start = (bf16[8,1920]{1,0:T(8,128)(2,1)}, bf16[8,1920]{1,0:T(8,128)(2,1)S(1)}, u32[]{:S(2)}, u32[]{:S(2)}) collective-permute-start(bf16[8,1920]{1,0:T(8,128)(2,1)} %get-tuple-element.34), channel_id=1, source_target_pairs={{0,3},{1,0},{2,1},{3,2},{4,7},{5,4},{6,5},{7,6},{8,11},{9,8},{10,9... | collective-permute-start | bytes 92168 | tf_op jit(solution)/shard_map/ppermute | solution.py:31
  4.6 5.6 %collective-permute-start.1 = (bf16[8,1920]{1,0:T(8,128)(2,1)}, bf16[8,1920]{1,0:T(8,128)(2,1)S(1)}, u32[]{:S(2)}, u32[]{:S(2)}) collective-permute-start(bf16[8,1920]{1,0:T(8,128)(2,1)} %get-tuple-element.35), channel_id=1, source_target_pairs={{0,2},{1,3},{2,0},{3,1},{4,6},{5,7},{6,4},{7,5},{8,10},{9,11},{10,... | collective-permute-start | bytes 92168 | tf_op jit(solution)/shard_map/ppermute | solution.py:31
  5.4 5.3 %collective-permute-start.2 = (bf16[8,1920]{1,0:T(8,128)(2,1)}, bf16[8,1920]{1,0:T(8,128)(2,1)S(1)}, u32[]{:S(2)}, u32[]{:S(2)}) collective-permute-start(bf16[8,1920]{1,0:T(8,128)(2,1)} %get-tuple-element.36), channel_id=1, source_target_pairs={{0,1},{1,2},{2,3},{3,0},{4,5},{5,6},{6,7},{7,4},{8,9},{9,10},{10,1... | collective-permute-start | bytes 92168 | tf_op jit(solution)/shard_map/ppermute | solution.py:31
  10.7 5.5 %collective-permute-start.3 = (bf16[32,1920]{1,0:T(8,128)(2,1)S(1)}, bf16[32,1920]{1,0:T(8,128)(2,1)S(1)}, u32[]{:S(2)}, u32[]{:S(2)}) collective-permute-start(bf16[32,1920]{1,0:T(8,128)(2,1)S(1)} %get-tuple-element.100), channel_id=1, source_target_pairs={{0,96},{4,28},{8,104},{12,4},{16,112},{20,12},{24,120},{28,20},{32... | collective-permute-start | bytes 368648 | tf_op jit(solution)/shard_map/ppermute | solution.py:32
  13.8 7.5 %collective-permute-start.5 = (bf16[32,1920]{1,0:T(8,128)(2,1)S(1)}, bf16[32,1920]{1,0:T(8,128)(2,1)S(1)}, u32[]{:S(2)}, u32[]{:S(2)}) collective-permute-start(bf16[32,1920]{1,0:T(8,128)(2,1)S(1)} %get-tuple-element.100), channel_id=1, source_target_pairs={{0,32},{4,12},{8,40},{12,20},{16,48},{20,28},{24,56},{28,4},{32,64... | collective-permute-start | bytes 368648 | tf_op jit(solution)/shard_map/ppermute | solution.py:32
  13.9 6.6 %collective-permute-start.4 = (bf16[32,1920]{1,0:T(8,128)(2,1)S(1)}, bf16[32,1920]{1,0:T(8,128)(2,1)S(1)}, u32[]{:S(2)}, u32[]{:S(2)}) collective-permute-start(bf16[32,1920]{1,0:T(8,128)(2,1)S(1)} %get-tuple-element.100), channel_id=1, source_target_pairs={{0,64},{4,20},{8,72},{12,28},{16,80},{20,4},{24,88},{28,12},{32,96... | collective-permute-start | bytes 368648 | tf_op jit(solution)/shard_map/ppermute | solution.py:32
  21.8 4.6 %collective-permute-start.8 = (bf16[64,1920]{1,0:T(8,128)(2,1)S(1)}, bf16[64,1920]{1,0:T(8,128)(2,1)S(1)}, u32[]{:S(2)}, u32[]{:S(2)}) collective-permute-start(bf16[64,1920]{1,0:T(8,128)(2,1)S(1)} %convolution_convert_fusion.5), channel_id=1, source_target_pairs={{0,4},{4,0},{8,12},{12,8},{16,20},{20,16},{24,28},{28,24},{32,36},... | collective-permute-start | bytes 737288 | tf_op jit(solution)/shard_map/ppermute | solution.py:32
  21.9 11.0 %collective-permute-start.7 = (bf16[128,1920]{1,0:T(8,128)(2,1)S(1)}, bf16[128,1920]{1,0:T(8,128)(2,1)S(1)}, u32[]{:S(2)}, u32[]{:S(2)}) collective-permute-start(bf16[128,1920]{1,0:T(8,128)(2,1)S(1)} %constant_dynamic-update-slice_fusion.4), channel_id=1, source_target_pairs={{0,24},{4,100},{8,0},{12,108},{16,8},{20,116},{24,16},{28,124},{32... | collective-permute-start | bytes 1474568 | tf_op jit(solution)/shard_map/ppermute | solution.py:32
  26.0 10.0 %collective-permute-start.6 = (bf16[128,1920]{1,0:T(8,128)(2,1)S(1)}, bf16[128,1920]{1,0:T(8,128)(2,1)S(1)}, u32[]{:S(2)}, u32[]{:S(2)}) collective-permute-start(bf16[128,1920]{1,0:T(8,128)(2,1)S(1)} %constant_dynamic-update-slice_fusion.4), channel_id=1, source_target_pairs={{0,8},{4,36},{8,16},{12,44},{16,24},{20,52},{24,0},{28,60},{32,40}... | collective-permute-start | bytes 1474568 | tf_op jit(solution)/shard_map/ppermute | solution.py:32
  26.3 4.4 %slice-start.2 = ((s8[7340032]{0:T(1024)(128)(4,1)}), s8[4194304]{0:T(1024)(128)(4,1)S(1)}, s32[]{:S(2)}) async-start(s8[7340032]{0:T(1024)(128)(4,1)} %bitcast.58), calls=%async_computation.2 | async-start | bytes 8388608
  26.4 5.2 %slice-start.3 = ((s8[7340032]{0:T(1024)(128)(4,1)}), s8[3145728]{0:T(1024)(128)(4,1)S(1)}, s32[]{:S(2)}) async-start(s8[7340032]{0:T(1024)(128)(4,1)} %bitcast.58), calls=%async_computation.3 | async-start | bytes 6291456
  36.0 7.5 %collective-permute-start.9 = (bf16[64,1920]{1,0:T(8,128)(2,1)S(1)}, bf16[64,1920]{1,0:T(8,128)(2,1)S(1)}, u32[]{:S(2)}, u32[]{:S(2)}) collective-permute-start(bf16[64,1920]{1,0:T(8,128)(2,1)S(1)} %slice.209), channel_id=1, source_target_pairs={{0,8},{4,36},{8,16},{12,44},{16,24},{20,52},{24,0},{28,60},{32,40}... | collective-permute-start | bytes 737288 | tf_op jit(solution)/shard_map/ppermute | solution.py:32
  36.2 7.4 %collective-permute-start.10 = (bf16[64,1920]{1,0:T(8,128)(2,1)S(1)}, bf16[64,1920]{1,0:T(8,128)(2,1)S(1)}, u32[]{:S(2)}, u32[]{:S(2)}) collective-permute-start(bf16[64,1920]{1,0:T(8,128)(2,1)S(1)} %slice.210), channel_id=1, source_target_pairs={{0,24},{4,100},{8,0},{12,108},{16,8},{20,116},{24,16},{28,124},{32... | collective-permute-start | bytes 737288 | tf_op jit(solution)/shard_map/ppermute | solution.py:32
  40.0 6.2 %collective-permute-start.12 = (bf16[32,2048]{1,0:T(8,128)(2,1)S(1)}, bf16[32,2048]{1,0:T(8,128)(2,1)S(1)}, u32[]{:S(2)}, u32[]{:S(2)}) collective-permute-start(bf16[32,2048]{1,0:T(8,128)(2,1)S(1)} %get-tuple-element.41), channel_id=1, source_target_pairs={{0,1},{1,2},{2,3},{3,0},{4,5},{5,6},{6,7},{7,4},{8,9},{9,10},{10,1... | collective-permute-start | bytes 393224 | tf_op jit(solution)/shard_map/ppermute | solution.py:31
  40.0 6.2 %collective-permute-start.13 = (bf16[32,2048]{1,0:T(8,128)(2,1)S(1)}, bf16[32,2048]{1,0:T(8,128)(2,1)S(1)}, u32[]{:S(2)}, u32[]{:S(2)}) collective-permute-start(bf16[32,2048]{1,0:T(8,128)(2,1)S(1)} %get-tuple-element.42), channel_id=1, source_target_pairs={{0,3},{1,0},{2,1},{3,2},{4,7},{5,4},{6,5},{7,6},{8,11},{9,8},{10,9... | collective-permute-start | bytes 393224 | tf_op jit(solution)/shard_map/ppermute | solution.py:31
  43.9 14.3 %slice-start.4 = ((s8[7340032]{0:T(1024)(128)(4,1)}), s8[4194304]{0:T(1024)(128)(4,1)S(1)}, s32[]{:S(2)}) async-start(s8[7340032]{0:T(1024)(128)(4,1)} %bitcast.60), calls=%async_computation.4 | async-start | bytes 8388608
  46.3 7.7 %collective-permute-start.15 = (bf16[64,2048]{1,0:T(8,128)(2,1)S(1)}, bf16[64,2048]{1,0:T(8,128)(2,1)S(1)}, u32[]{:S(2)}, u32[]{:S(2)}) collective-permute-start(bf16[64,2048]{1,0:T(8,128)(2,1)S(1)} %pad_maximum_fusion.7), channel_id=1, source_target_pairs={{0,3},{1,0},{2,1},{3,2},{4,7},{5,4},{6,5},{7,6},{8,11},{9,8},{10,9... | collective-permute-start | bytes 786440 | tf_op jit(solution)/shard_map/ppermute | solution.py:31
  50.1 7.7 %collective-permute-start.14 = (bf16[64,2048]{1,0:T(8,128)(2,1)S(1)}, bf16[64,2048]{1,0:T(8,128)(2,1)S(1)}, u32[]{:S(2)}, u32[]{:S(2)}) collective-permute-start(bf16[64,2048]{1,0:T(8,128)(2,1)S(1)} %pad_maximum_fusion.6), channel_id=1, source_target_pairs={{0,1},{1,2},{2,3},{3,0},{4,5},{5,6},{6,7},{7,4},{8,9},{9,10},{10,1... | collective-permute-start | bytes 786440 | tf_op jit(solution)/shard_map/ppermute | solution.py:31
  50.2 7.8 %collective-permute-start.11 = (bf16[192,1920]{1,0:T(8,128)(2,1)S(1)}, bf16[192,1920]{1,0:T(8,128)(2,1)S(1)}, u32[]{:S(2)}, u32[]{:S(2)}) collective-permute-start(bf16[192,1920]{1,0:T(8,128)(2,1)S(1)} %convolution_convert_fusion.1), channel_id=1, source_target_pairs={{0,4},{4,0},{8,12},{12,8},{16,20},{20,16},{24,28},{28,24},{32,36},... | collective-permute-start | bytes 2211848 | tf_op jit(solution)/shard_map/ppermute | solution.py:32
  50.7 7.4 %slice-start.5 = ((s8[7340032]{0:T(1024)(128)(4,1)}), s8[3145728]{0:T(1024)(128)(4,1)S(1)}, s32[]{:S(2)}) async-start(s8[7340032]{0:T(1024)(128)(4,1)} %bitcast.60), calls=%async_computation.5 | async-start | bytes 6291456
  64.3 9.1 %collective-permute-start.16 = (bf16[96,2048]{1,0:T(8,128)(2,1)S(1)}, bf16[96,2048]{1,0:T(8,128)(2,1)S(1)}, u32[]{:S(2)}, u32[]{:S(2)}) collective-permute-start(bf16[96,2048]{1,0:T(8,128)(2,1)S(1)} %get-tuple-element.70), channel_id=1, source_target_pairs={{0,1},{1,2},{2,3},{3,0},{4,5},{5,6},{6,7},{7,4},{8,9},{9,10},{10,1... | collective-permute-start | bytes 1179656 | tf_op jit(solution)/shard_map/ppermute | solution.py:31
  64.4 13.9 %collective-permute-start.19 = (bf16[32,2048]{1,0:T(8,128)(2,1)S(1)}, bf16[32,2048]{1,0:T(8,128)(2,1)S(1)}, u32[]{:S(2)}, u32[]{:S(2)}) collective-permute-start(bf16[32,2048]{1,0:T(8,128)(2,1)S(1)} %fusion.54), channel_id=1, source_target_pairs={{0,3},{1,0},{2,1},{3,2},{4,7},{5,4},{6,5},{7,6},{8,11},{9,8},{10,9... | collective-permute-start | bytes 393224 | tf_op jit(solution)/shard_map/ppermute | solution.py:31
  67.7 10.7 %collective-permute-start.18 = (bf16[32,2048]{1,0:T(8,128)(2,1)S(1)}, bf16[32,2048]{1,0:T(8,128)(2,1)S(1)}, u32[]{:S(2)}, u32[]{:S(2)}) collective-permute-start(bf16[32,2048]{1,0:T(8,128)(2,1)S(1)} %fusion.54), channel_id=1, source_target_pairs={{0,1},{1,2},{2,3},{3,0},{4,5},{5,6},{6,7},{7,4},{8,9},{9,10},{10,1... | collective-permute-start | bytes 393224 | tf_op jit(solution)/shard_map/ppermute | solution.py:31
  67.7 10.5 %collective-permute-start.17 = (bf16[96,2048]{1,0:T(8,128)(2,1)S(1)}, bf16[96,2048]{1,0:T(8,128)(2,1)S(1)}, u32[]{:S(2)}, u32[]{:S(2)}) collective-permute-start(bf16[96,2048]{1,0:T(8,128)(2,1)S(1)} %get-tuple-element.71), channel_id=1, source_target_pairs={{0,3},{1,0},{2,1},{3,2},{4,7},{5,4},{6,5},{7,6},{8,11},{9,8},{10,9... | collective-permute-start | bytes 1179656 | tf_op jit(solution)/shard_map/ppermute | solution.py:31
  73.4 28.0 %slice-start = ((s8[7340032]{0:T(1024)(128)(4,1)}), s8[4194304]{0:T(1024)(128)(4,1)S(1)}, s32[]{:S(2)}) async-start(s8[7340032]{0:T(1024)(128)(4,1)} %bitcast.56), calls=%async_computation | async-start | bytes 8388608
  73.5 8.7 %copy-start.3 = (s32[128]{0:T(128)S(1)}, s32[128]{0:T(128)}, u32[]{:S(2)}) copy-start(s32[128]{0:T(128)} %get-tuple-element.121) | copy-start | bytes 1540
  78.4 18.5 %collective-permute-start.20 = (bf16[192,2048]{1,0:T(8,128)(2,1)S(1)}, bf16[192,2048]{1,0:T(8,128)(2,1)S(1)}, u32[]{:S(2)}, u32[]{:S(2)}) collective-permute-start(bf16[192,2048]{1,0:T(8,128)(2,1)S(1)} %pad_maximum_fusion.1), channel_id=1, source_target_pairs={{0,1},{1,2},{2,3},{3,0},{4,5},{5,6},{6,7},{7,4},{8,9},{9,10},{10,1... | collective-permute-start | bytes 2359304 | tf_op jit(solution)/shard_map/ppermute | solution.py:31
  78.5 18.3 %collective-permute-start.21 = (bf16[192,2048]{1,0:T(8,128)(2,1)S(1)}, bf16[192,2048]{1,0:T(8,128)(2,1)S(1)}, u32[]{:S(2)}, u32[]{:S(2)}) collective-permute-start(bf16[192,2048]{1,0:T(8,128)(2,1)S(1)} %pad_maximum_fusion.2), channel_id=1, source_target_pairs={{0,3},{1,0},{2,1},{3,2},{4,7},{5,4},{6,5},{7,6},{8,11},{9,8},{10,9... | collective-permute-start | bytes 2359304 | tf_op jit(solution)/shard_map/ppermute | solution.py:31
  82.6 18.8 %collective-permute-start.22 = (bf16[16,2048]{1,0:T(8,128)(2,1)S(1)}, bf16[16,2048]{1,0:T(8,128)(2,1)S(1)}, u32[]{:S(2)}, u32[]{:S(2)}) collective-permute-start(bf16[16,2048]{1,0:T(8,128)(2,1)S(1)} %slice.228), channel_id=1, source_target_pairs={{0,1},{1,2},{2,3},{3,0},{4,5},{5,6},{6,7},{7,4},{8,9},{9,10},{10,1... | collective-permute-start | bytes 196616 | tf_op jit(solution)/shard_map/ppermute | solution.py:31
  82.7 18.7 %collective-permute-start.23 = (bf16[16,2048]{1,0:T(8,128)(2,1)S(1)}, bf16[16,2048]{1,0:T(8,128)(2,1)S(1)}, u32[]{:S(2)}, u32[]{:S(2)}) collective-permute-start(bf16[16,2048]{1,0:T(8,128)(2,1)S(1)} %slice.229), channel_id=1, source_target_pairs={{0,3},{1,0},{2,1},{3,2},{4,7},{5,4},{6,5},{7,6},{8,11},{9,8},{10,9... | collective-permute-start | bytes 196616 | tf_op jit(solution)/shard_map/ppermute | solution.py:31
  85.9 15.5 %slice-start.1 = ((s8[7340032]{0:T(1024)(128)(4,1)}), s8[3145728]{0:T(1024)(128)(4,1)S(1)}, s32[]{:S(2)}) async-start(s8[7340032]{0:T(1024)(128)(4,1)} %bitcast.56), calls=%async_computation.1 | async-start | bytes 6291456
  97.5 9.5 %collective-permute-start.26 = (bf16[96,2048]{1,0:T(8,128)(2,1)S(1)}, bf16[96,2048]{1,0:T(8,128)(2,1)S(1)}, u32[]{:S(2)}, u32[]{:S(2)}) collective-permute-start(bf16[96,2048]{1,0:T(8,128)(2,1)S(1)} %fusion.42), channel_id=1, source_target_pairs={{0,1},{1,2},{2,3},{3,0},{4,5},{5,6},{6,7},{7,4},{8,9},{9,10},{10,1... | collective-permute-start | bytes 1179656 | tf_op jit(solution)/shard_map/ppermute | solution.py:31
  97.6 9.5 %collective-permute-start.25 = (bf16[96,2048]{1,0:T(8,128)(2,1)S(1)}, bf16[96,2048]{1,0:T(8,128)(2,1)S(1)}, u32[]{:S(2)}, u32[]{:S(2)}) collective-permute-start(bf16[96,2048]{1,0:T(8,128)(2,1)S(1)} %fusion.42), channel_id=1, source_target_pairs={{0,3},{1,0},{2,1},{3,2},{4,7},{5,4},{6,5},{7,6},{8,11},{9,8},{10,9... | collective-permute-start | bytes 1179656 | tf_op jit(solution)/shard_map/ppermute | solution.py:31
  102.7 8.1 %collective-permute-start.24 = (bf16[64,1792]{1,0:T(8,128)(2,1)S(1)}, bf16[64,1792]{1,0:T(8,128)(2,1)S(1)}, u32[]{:S(2)}, u32[]{:S(2)}) collective-permute-start(bf16[64,1792]{1,0:T(8,128)(2,1)S(1)} %bitcast.85), channel_id=1, source_target_pairs={{0,4},{4,0},{8,12},{12,8},{16,20},{20,16},{24,28},{28,24},{32,36},... | collective-permute-start | bytes 688136 | tf_op jit(solution)/shard_map/ppermute | solution.py:32
  107.1 6.9 %collective-permute-start.27 = (bf16[48,2048]{1,0:T(8,128)(2,1)S(1)}, bf16[48,2048]{1,0:T(8,128)(2,1)S(1)}, u32[]{:S(2)}, u32[]{:S(2)}) collective-permute-start(bf16[48,2048]{1,0:T(8,128)(2,1)S(1)} %slice.298), channel_id=1, source_target_pairs={{0,1},{1,2},{2,3},{3,0},{4,5},{5,6},{6,7},{7,4},{8,9},{9,10},{10,1... | collective-permute-start | bytes 589832 | tf_op jit(solution)/shard_map/ppermute | solution.py:31
  107.2 6.8 %collective-permute-start.28 = (bf16[48,2048]{1,0:T(8,128)(2,1)S(1)}, bf16[48,2048]{1,0:T(8,128)(2,1)S(1)}, u32[]{:S(2)}, u32[]{:S(2)}) collective-permute-start(bf16[48,2048]{1,0:T(8,128)(2,1)S(1)} %slice.299), channel_id=1, source_target_pairs={{0,3},{1,0},{2,1},{3,2},{4,7},{5,4},{6,5},{7,6},{8,11},{9,8},{10,9... | collective-permute-start | bytes 589832 | tf_op jit(solution)/shard_map/ppermute | solution.py:31
  117.3 1.6 collective-permute-start.30
  117.5 5.2 %collective-permute-start.29 = (bf16[128,1792]{1,0:T(8,128)(2,1)S(1)}, bf16[128,1792]{1,0:T(8,128)(2,1)S(1)}, u32[]{:S(2)}, u32[]{:S(2)}) collective-permute-start(bf16[128,1792]{1,0:T(8,128)(2,1)S(1)} %bitcast.83), channel_id=1, source_target_pairs={{0,4},{4,0},{8,12},{12,8},{16,20},{20,16},{24,28},{28,24},{32,36},... | collective-permute-start | bytes 1376264 | tf_op jit(solution)/shard_map/ppermute | solution.py:32
  119.3 7.3 %collective-permute-start.31 = (bf16[64,1792]{1,0:T(8,128)(2,1)S(1)}, bf16[64,1792]{1,0:T(8,128)(2,1)S(1)}, u32[]{:S(2)}, u32[]{:S(2)}) collective-permute-start(bf16[64,1792]{1,0:T(8,128)(2,1)S(1)} %get-tuple-element.90), channel_id=1, source_target_pairs={{0,8},{4,36},{8,16},{12,44},{16,24},{20,52},{24,0},{28,60},{32,40}... | collective-permute-start | bytes 688136 | tf_op jit(solution)/shard_map/ppermute | solution.py:32
  119.4 7.2 %collective-permute-start.33 = (bf16[64,1792]{1,0:T(8,128)(2,1)S(1)}, bf16[64,1792]{1,0:T(8,128)(2,1)S(1)}, u32[]{:S(2)}, u32[]{:S(2)}) collective-permute-start(bf16[64,1792]{1,0:T(8,128)(2,1)S(1)} %get-tuple-element.91), channel_id=1, source_target_pairs={{0,24},{4,100},{8,0},{12,108},{16,8},{20,116},{24,16},{28,124},{32... | collective-permute-start | bytes 688136 | tf_op jit(solution)/shard_map/ppermute | solution.py:32
  126.7 9.4 %collective-permute-start.34 = (bf16[128,1792]{1,0:T(8,128)(2,1)S(1)}, bf16[128,1792]{1,0:T(8,128)(2,1)S(1)}, u32[]{:S(2)}, u32[]{:S(2)}) collective-permute-start(bf16[128,1792]{1,0:T(8,128)(2,1)S(1)} %pad_maximum_fusion.5), channel_id=1, source_target_pairs={{0,24},{4,100},{8,0},{12,108},{16,8},{20,116},{24,16},{28,124},{32... | collective-permute-start | bytes 1376264 | tf_op jit(solution)/shard_map/ppermute | solution.py:32
  130.1 9.8 %collective-permute-start.32 = (bf16[128,1792]{1,0:T(8,128)(2,1)S(1)}, bf16[128,1792]{1,0:T(8,128)(2,1)S(1)}, u32[]{:S(2)}, u32[]{:S(2)}) collective-permute-start(bf16[128,1792]{1,0:T(8,128)(2,1)S(1)} %pad_maximum_fusion.4), channel_id=1, source_target_pairs={{0,8},{4,36},{8,16},{12,44},{16,24},{20,52},{24,0},{28,60},{32,40}... | collective-permute-start | bytes 1376264 | tf_op jit(solution)/shard_map/ppermute | solution.py:32
  140.1 5.5 %collective-permute-start.35 = (bf16[32,1792]{1,0:T(8,128)(2,1)S(1)}, bf16[32,1792]{1,0:T(8,128)(2,1)S(1)}, u32[]{:S(2)}, u32[]{:S(2)}) collective-permute-start(bf16[32,1792]{1,0:T(8,128)(2,1)S(1)} %get-tuple-element.87), channel_id=1, source_target_pairs={{0,96},{4,28},{8,104},{12,4},{16,112},{20,12},{24,120},{28,20},{32... | collective-permute-start | bytes 344072 | tf_op jit(solution)/shard_map/ppermute | solution.py:32
  143.2 7.2 %collective-permute-start.37 = (bf16[32,1792]{1,0:T(8,128)(2,1)S(1)}, bf16[32,1792]{1,0:T(8,128)(2,1)S(1)}, u32[]{:S(2)}, u32[]{:S(2)}) collective-permute-start(bf16[32,1792]{1,0:T(8,128)(2,1)S(1)} %get-tuple-element.88), channel_id=1, source_target_pairs={{0,32},{4,12},{8,40},{12,20},{16,48},{20,28},{24,56},{28,4},{32,64... | collective-permute-start | bytes 344072 | tf_op jit(solution)/shard_map/ppermute | solution.py:32
  143.2 7.2 %collective-permute-start.36 = (bf16[32,1792]{1,0:T(8,128)(2,1)S(1)}, bf16[32,1792]{1,0:T(8,128)(2,1)S(1)}, u32[]{:S(2)}, u32[]{:S(2)}) collective-permute-start(bf16[32,1792]{1,0:T(8,128)(2,1)S(1)} %get-tuple-element.89), channel_id=1, source_target_pairs={{0,64},{4,20},{8,72},{12,28},{16,80},{20,4},{24,88},{28,12},{32,96... | collective-permute-start | bytes 344072 | tf_op jit(solution)/shard_map/ppermute | solution.py:32
  151.2 6.2 %collective-permute-start.40 = (bf16[8,1792]{1,0:T(8,128)(2,1)S(1)}, bf16[8,1792]{1,0:T(8,128)(2,1)S(1)}, u32[]{:S(2)}, u32[]{:S(2)}) collective-permute-start(bf16[8,1792]{1,0:T(8,128)(2,1)S(1)} %get-tuple-element.96), channel_id=1, source_target_pairs={{0,1},{1,2},{2,3},{3,0},{4,5},{5,6},{6,7},{7,4},{8,9},{9,10},{10,1... | collective-permute-start | bytes 86024 | tf_op jit(solution)/shard_map/ppermute | solution.py:31
  152.6 5.7 %collective-permute-start.39 = (bf16[8,1792]{1,0:T(8,128)(2,1)S(1)}, bf16[8,1792]{1,0:T(8,128)(2,1)S(1)}, u32[]{:S(2)}, u32[]{:S(2)}) collective-permute-start(bf16[8,1792]{1,0:T(8,128)(2,1)S(1)} %get-tuple-element.97), channel_id=1, source_target_pairs={{0,2},{1,3},{2,0},{3,1},{4,6},{5,7},{6,4},{7,5},{8,10},{9,11},{10,... | collective-permute-start | bytes 86024 | tf_op jit(solution)/shard_map/ppermute | solution.py:31
  156.2 3.9 %collective-permute-start.38 = (bf16[8,1792]{1,0:T(8,128)(2,1)S(1)}, bf16[8,1792]{1,0:T(8,128)(2,1)S(1)}, u32[]{:S(2)}, u32[]{:S(2)}) collective-permute-start(bf16[8,1792]{1,0:T(8,128)(2,1)S(1)} %get-tuple-element.98), channel_id=1, source_target_pairs={{0,3},{1,0},{2,1},{3,2},{4,7},{5,4},{6,5},{7,6},{8,11},{9,8},{10,9... | collective-permute-start | bytes 86024 | tf_op jit(solution)/shard_map/ppermute | solution.py:31
  (5 other events, 11.3 us)

commit v7 on v6

--- a/solution.py
+++ b/solution.py
@@ -32,8 +32,15 @@
     return lax.ppermute(value, "attn", attn_pairs(axis, step))
 
 
-def direct(chunks, axis):
-    return [chunks[0], move(chunks[3], axis, -1), move(chunks[2], axis, 2), move(chunks[1], axis, 1)]
+def swap(value):
+    groups = []
+    for core in range(2):
+        for line in range(RING):
+            near = [(a * RING + line if core == 0 else line * RING + a) * 2 + core for a in range(RING)]
+            groups.append([attn * RING + x for attn in near for x in range(RING)])
+    return lax.all_to_all(
+        value, ("attn", "exp"), split_axis=0, concat_axis=0, axis_index_groups=groups, tiled=True
+    )
 
 
 def gather_ring(value, axis):
@@ -61,10 +68,9 @@
     return total.astype(jnp.bfloat16)
 
 
-def prepare_kernel(place_ref, hidden_ref, gain_ref, routes_ref, scores_ref, capacity_ref, *out_refs):
+def prepare_kernel(hidden_ref, gain_ref, routes_ref, scores_ref, capacity_ref, out_ref):
     rows, top = routes_ref.shape
     experts = capacity_ref.shape[1]
-    width = out_refs[0].shape[1] - PAD
     hidden = hidden_ref[...].astype(jnp.float32)
     scale = lax.rsqrt(jnp.mean(hidden * hidden, axis=1, keepdims=True) + EPSILON)
     routes = routes_ref[...]
@@ -94,34 +100,33 @@
     group = lane // experts
     value = jnp.where(group == 0, rank + 1.0, jnp.where(group == 1, high, weight - high))
     columns = jnp.where(kept & (group < 3), value, 0.0).astype(jnp.bfloat16)
+    width = out_ref.shape[2] - PAD
     for r in range(RING):
-        start = pl.multiple_of(lax.rem(place_ref[0] + r, RING) * width, PAD)
-        part = hidden_ref[:, pl.ds(start, width)].astype(jnp.float32) * scale * gain_ref[:, pl.ds(start, width)]
-        out_refs[r][:, :width] = part.astype(jnp.bfloat16)
-        out_refs[r][:, width:] = columns
-
-
-def finish_kernel(place_ref, hidden_ref, *refs):
-    out_ref = refs[-1]
-    width = refs[0].shape[1]
+        cut = slice(r * width, (r + 1) * width)
+        part = (hidden_ref[:, cut].astype(jnp.float32) * scale * gain_ref[:, cut]).astype(jnp.bfloat16)
+        for a in range(RING):
+            out_ref[a * RING + r, :, :width] = part
+            out_ref[a * RING + r, :, width:] = columns
+
+
+def finish_kernel(hidden_ref, back_ref, out_ref):
+    width = back_ref.shape[2]
     for r in range(RING):
-        start = pl.multiple_of(lax.rem(place_ref[0] + r, RING) * width, PAD)
-        total = hidden_ref[:, pl.ds(start, width)].astype(jnp.float32) + refs[r][...].astype(jnp.float32)
-        out_ref[:, pl.ds(start, width)] = total.astype(jnp.bfloat16)
-
-
-def specs(count):
-    return [pl.BlockSpec(memory_space=pltpu.SMEM)] + [pl.BlockSpec(memory_space=pltpu.VMEM)] * count
-
-
-def choose(picks, expert):
+        cut = slice(r * width, (r + 1) * width)
+        total = hidden_ref[:, cut].astype(jnp.float32)
+        total += sum(back_ref[a * RING + r].astype(jnp.float32) for a in range(RING))
+        out_ref[:, cut] = total.astype(jnp.bfloat16)
+
+
+def choose(picks, expert, place):
     lanes = jnp.arange(PAD)[None, :]
     code = jnp.sum(jnp.where(lanes == expert, picks, 0.0), axis=1)
     rows = picks.shape[0]
     per = rows // 16
     row = jnp.arange(rows, dtype=jnp.int32)
     slot = jnp.arange(rows // 2, dtype=jnp.int32)
-    block = row % 32 // 8 * per + row // 32 * 2 + row % 8 // 4
+    turned = (row % 32 // 8 + RING - place) % RING
+    block = turned * per + row // 32 * 2 + row % 8 // 4
     chosen = (block[:, None] == slot[None, :] // 2) & (
         code.astype(jnp.int32)[:, None] == (slot % 2 + 1)[None, :]
     )
@@ -142,23 +147,24 @@
     experts = capacity.shape[0]
     expert = lax.axis_index("attn")
     other = expert + 1 - 2 * (expert % 2)
-    place = lax.axis_index("exp").astype(jnp.int32).reshape(1)
+    place = lax.axis_index("exp")
     width = w_gate.shape[1]
     rows = hidden.shape[0]
+    vmem = pl.BlockSpec(memory_space=pltpu.VMEM)
     blocks = pl.pallas_call(
         prepare_kernel,
-        out_shape=[jax.ShapeDtypeStruct((rows, width + PAD), jnp.bfloat16)] * RING,
-        in_specs=specs(5),
-        out_specs=[pl.BlockSpec(memory_space=pltpu.VMEM)] * RING,
+        out_shape=jax.ShapeDtypeStruct((RING * RING, rows, width + PAD), jnp.bfloat16),
+        in_specs=[vmem] * 5,
+        out_specs=vmem,
         name="prepare",
-    )(place, hidden, norm_gain.reshape(1, -1), routes, route_scores, capacity.reshape(1, -1))
+    )(hidden, norm_gain.reshape(1, -1), routes, route_scores, capacity.reshape(1, -1))
     lane = jnp.arange(PAD)[None, :]
     mine = (lane == expert + experts) | (lane == expert + 2 * experts)
 
     def picks_of(lines):
         columns = lines[:, width:].astype(jnp.float32)
-        theirs = move(pick(choose(columns, other), lines), "core", 1)
-        return pick(choose(columns, expert), lines), theirs
+        theirs = move(pick(choose(columns, other, place), lines), "core", 1)
+        return pick(choose(columns, expert, place), lines), theirs
 
     def enter(own, theirs, cuts):
         quarter = own.shape[0] // RING
@@ -192,14 +198,13 @@
 
     def leave(out, lines):
         columns = lines[:, width:].astype(jnp.float32)
-        chosen = jnp.concatenate([choose(columns, expert), choose(columns, other)], axis=1)
+        chosen = jnp.concatenate([choose(columns, expert, place), choose(columns, other, place)], axis=1)
         out = out.reshape(RING, 2, -1, width)
         theirs = move(out[:, 1].reshape(-1, width), "core", 1)
         returned = jnp.concatenate([out[:, 0].reshape(-1, width), theirs], axis=0)
         return jnp.dot(chosen, returned, preferred_element_type=jnp.float32).astype(jnp.bfloat16)
 
-    lines = jnp.concatenate(direct(blocks, "x"), axis=0)
-    near = jnp.concatenate(direct([lines] * RING, 0), axis=0)
+    near = swap(blocks).reshape(RING * RING * rows, width + PAD)
     low, high = move(near, 1, 1), move(near, 1, -1)
     slots, near_scale = enter(*picks_of(near), [0])
     gate, up = product(slots, w_gate), product(slots, w_up)
@@ -236,17 +241,14 @@
     one_sum = leave(out[:, 2 * cut :], one)
     part = near.shape[0]
     summed = scatter_ring(near_sum, [one_sum[:part], two_sum, one_sum[part:]], 1)
-    part = part // RING
-    pieces = direct([summed[r * part : (r + 1) * part] for r in range(RING)], 0)
-    summed = sum(piece.astype(jnp.float32) for piece in pieces).astype(jnp.bfloat16)
-    back = direct([summed[r * rows : (r + 1) * rows] for r in range(RING)], "x")
+    back = swap(summed.reshape(RING * RING, rows, width))
     return pl.pallas_call(
         finish_kernel,
         out_shape=jax.ShapeDtypeStruct(hidden.shape, jnp.bfloat16),
-        in_specs=specs(1 + RING),
-        out_specs=pl.BlockSpec(memory_space=pltpu.VMEM),
+        in_specs=[vmem] * 2,
+        out_specs=vmem,
         name="finish",
-    )(place, hidden, *back)
+    )(hidden, back)
 
 
 def solution(mesh):

time: 162 us -> 157 us (0.969)
  blocking collectives: 0 us -> 15.4 us
  starting transfers between devices: 64.2 us -> 49.2 us
  waiting for transfers between devices: 67.2 us -> 62.5 us
  local copies, waits for them, and re-layouts: 3.97 us -> 1.87 us
    all_to_all x0 -> x1, blocking collectives: none -> 15.4 us  [swap(): lax.all_to_all(value, ('attn', 'exp'), split_axis=0, concat_axis=0, axis_...]
    all_to_all x0 -> x1, waiting for transfers between devices: none -> 12.3 us  [swap(): lax.all_to_all(value, ('attn', 'exp'), split_axis=0, concat_axis=0, axis_...]
    ppermute x19 -> x13, starting transfers between devices: 25.3 us -> 13.9 us  [move(): return lax.ppermute(value, 'attn', attn_pairs(axis, step))]
    ppermute x19 -> x13, waiting for transfers between devices: 28.2 us -> 17.5 us  [move(): return lax.ppermute(value, 'attn', attn_pairs(axis, step))]
    ppermute x22 -> x16, starting transfers between devices: 38.9 us -> 28.2 us  [move(): lax.ppermute(value, 'exp', [(i, (i + step) % RING) for i in range(RING)])]
    all_to_all x0 -> x1, starting transfers between devices: none -> 7.12 us  [swap(): lax.all_to_all(value, ('attn', 'exp'), split_axis=0, concat_axis=0, axis_...]
    ppermute x22 -> x16, waiting for transfers between devices: 39 us -> 32.8 us  [move(): lax.ppermute(value, 'exp', [(i, (i + step) % RING) for i in range(RING)])]
  transfers between devices with their start and end apart: 41 -> 30, of which waited for: 23 -> 16; matrix products, arithmetic and copies ran while one was open for 9% -> 8% of each run, Pallas kernels for 0% -> 0%
where the time goes in v7:
time: 157 us; the launch traced here: 156 us
  waiting for transfers between devices  62.5 us (40%)
  starting transfers between devices  49.2 us (31%)
  matrix products  18.9 us (12%)
  blocking collectives  15.4 us (10%)
  Pallas kernels  3.73 us (2%)
  other arithmetic  3.6 us (2%)
  local copies, waits for them, and re-layouts  1.87 us (1%)
    ppermute x16, waiting for transfers between devices, move(): lax.ppermute(value, 'exp', [(i, (i + step) % RING) for i in range(RING)])  32.8 us
    ppermute x16, starting transfers between devices, move(): lax.ppermute(value, 'exp', [(i, (i + step) % RING) for i in range(RING)])  28.2 us
    ppermute x13, waiting for transfers between devices, move(): return lax.ppermute(value, 'attn', attn_pairs(axis, step))  17.5 us
    all_to_all x1, blocking collectives, swap(): lax.all_to_all(value, ('attn', 'exp'), split_axis=0, concat_axis=0, axis_...  15.4 us
    ppermute x13, starting transfers between devices, move(): return lax.ppermute(value, 'attn', attn_pairs(axis, step))  13.9 us
    all_to_all x1, waiting for transfers between devices, swap(): lax.all_to_all(value, ('attn', 'exp'), split_axis=0, concat_axis=0, axis_...  12.3 us
    dot_general x4, matrix products, product(): jnp.dot(slots, weights[0], preferred_element_type=jnp.float32)  11.5 us
    all_to_all x1, starting transfers between devices, swap(): lax.all_to_all(value, ('attn', 'exp'), split_axis=0, concat_axis=0, axis_...  7.12 us
  transfers between devices with their start and end apart: 30, of which 16 were waited for; matrix products, arithmetic and copies ran while one was open for 8% of the time, Pallas kernels for 0%

profile of v7, /device:TPU:0, one launch (start us, length us, event | category | flops | bytes accessed | tf_op | source)
XLA Modules:
  0.0 156.2 jit_solution(11946580532474005696)
XLA Ops:
  0.0 1.9 %prepare.1 = bf16[16,8,1920]{2,1,0:T(8,128)(2,1)} custom-call(bf16[8,7168]{1,0:T(8,128)(2,1)} %hidden_ref.3, f32[1,7168]{1,0:T(1,128)} %bitcast.94, s32[8,8]{1,0:T(8,128)} %routes_ref.1, f32[8,8]{1,0:T(8,128)} %scores_ref.1, s32[1,32]{1,0:T(1,128)} %bitcast.95), custom_call_target="tpu_custom_call" | custom-call | tf_op jit(solution)/shard_map/prepare/pallas_call | solution.py:154
  1.9 7.1 %all-to-all-start = ((bf16[16,8,1920]{2,1,0:T(8,128)(2,1)}), bf16[16,8,1920]{2,1,0:T(8,128)(2,1)S(1)}, u32[]{:S(2)}, u32[]{:S(2)}) async-start(bf16[16,8,1920]{2,1,0:T(8,128)(2,1)} %prepare.1), calls=%async_computation | async-start | bytes 983040 | tf_op jit(solution)/shard_map/all_to_all | solution.py:41
  9.1 12.3 %all-to-all-done = bf16[16,8,1920]{2,1,0:T(8,128)(2,1)S(1)} async-done(((bf16[16,8,1920]{2,1,0:T(8,128)(2,1)}), bf16[16,8,1920]{2,1,0:T(8,128)(2,1)S(1)}, u32[]{:S(2)}, u32[]{:S(2)}) %all-to-all-start) | async-done | bytes 491552 | tf_op jit(solution)/shard_map/all_to_all | solution.py:41
  21.5 0.4 convolution_convert_fusion.5
  22.0 2.7 %collective-permute-start.1 = (bf16[128,1920]{1,0:T(8,128)(2,1)S(1)}, bf16[128,1920]{1,0:T(8,128)(2,1)S(1)}, u32[]{:S(2)}, u32[]{:S(2)}) collective-permute-start(bf16[128,1920]{1,0:T(8,128)(2,1)S(1)} %bitcast.72), channel_id=1, source_target_pairs={{0,24},{4,100},{8,0},{12,108},{16,8},{20,116},{24,16},{28,124},{32... | collective-permute-start | bytes 1474568 | tf_op jit(solution)/shard_map/ppermute | solution.py:32
  24.8 0.3 convolution_convert_fusion.6
  25.2 4.4 %fusion.33 = bf16[128,2048]{1,0:T(8,128)(2,1)S(1)} fusion(bf16[1,1792,2048]{2,1,0:T(8,128)(2,1)} %param.14, bf16[128,1920]{1,0:T(8,128)(2,1)S(1)} %bitcast.68), kind=kOutput, calls=%fused_computation.22 | convolution fusion | flops 939786240 | bytes 8323072 | tf_op jit(solution)/shard_map/dot_general | solution.py:179
  29.6 0.8 slice-done.3
  30.4 1.2 fusion.30
  31.7 3.1 %collective-permute-done = bf16[128,1920]{1,0:T(8,128)(2,1)S(1)} collective-permute-done((bf16[128,1920]{1,0:T(8,128)(2,1)S(1)}, bf16[128,1920]{1,0:T(8,128)(2,1)S(1)}, u32[]{:S(2)}, u32[]{:S(2)}) %collective-permute-start) | collective-permute-done | bytes 491552 | tf_op jit(solution)/shard_map/ppermute | solution.py:32
  35.0 3.3 %collective-permute-start.4 = (bf16[64,1920]{1,0:T(8,128)(2,1)S(1)}, bf16[64,1920]{1,0:T(8,128)(2,1)S(1)}, u32[]{:S(2)}, u32[]{:S(2)}) collective-permute-start(bf16[64,1920]{1,0:T(8,128)(2,1)S(1)} %slice.186), channel_id=1, source_target_pairs={{0,24},{4,100},{8,0},{12,108},{16,8},{20,116},{24,16},{28,124},{32... | collective-permute-start | bytes 737288 | tf_op jit(solution)/shard_map/ppermute | solution.py:32
  38.3 0.5 and_select_fusion.1
  38.8 0.6 collective-permute-start.6
  39.3 2.7 %collective-permute-start.7 = (bf16[32,2048]{1,0:T(8,128)(2,1)S(1)}, bf16[32,2048]{1,0:T(8,128)(2,1)S(1)}, u32[]{:S(2)}, u32[]{:S(2)}) collective-permute-start(bf16[32,2048]{1,0:T(8,128)(2,1)S(1)} %get-tuple-element.34), channel_id=1, source_target_pairs={{0,3},{1,0},{2,1},{3,2},{4,7},{5,4},{6,5},{7,6},{8,11},{9,8},{10,9... | collective-permute-start | bytes 393224 | tf_op jit(solution)/shard_map/ppermute | solution.py:31
  42.7 0.7 convolution_convert_fusion.2
  43.4 0.7 convolution_convert_fusion.1
  44.1 0.8 collective-permute-done.6
  45.2 3.8 %collective-permute-start.9 = (bf16[64,2048]{1,0:T(8,128)(2,1)S(1)}, bf16[64,2048]{1,0:T(8,128)(2,1)S(1)}, u32[]{:S(2)}, u32[]{:S(2)}) collective-permute-start(bf16[64,2048]{1,0:T(8,128)(2,1)S(1)} %pad_maximum_fusion.7), channel_id=1, source_target_pairs={{0,3},{1,0},{2,1},{3,2},{4,7},{5,4},{6,5},{7,6},{8,11},{9,8},{10,9... | collective-permute-start | bytes 786440 | tf_op jit(solution)/shard_map/ppermute | solution.py:31
  49.8 3.1 %collective-permute-done.9 = bf16[64,2048]{1,0:T(8,128)(2,1)S(1)} collective-permute-done((bf16[64,2048]{1,0:T(8,128)(2,1)S(1)}, bf16[64,2048]{1,0:T(8,128)(2,1)S(1)}, u32[]{:S(2)}, u32[]{:S(2)}) %collective-permute-start.9) | collective-permute-done | bytes 262176 | tf_op jit(solution)/shard_map/ppermute | solution.py:31
  52.9 3.8 %collective-permute-done.8 = bf16[64,2048]{1,0:T(8,128)(2,1)S(1)} collective-permute-done((bf16[64,2048]{1,0:T(8,128)(2,1)S(1)}, bf16[64,2048]{1,0:T(8,128)(2,1)S(1)}, u32[]{:S(2)}, u32[]{:S(2)}) %collective-permute-start.8) | collective-permute-done | bytes 262176 | tf_op jit(solution)/shard_map/ppermute | solution.py:31
  57.1 3.0 %fusion.18 = bf16[384,2048]{1,0:T(8,128)(2,1)S(1)} fusion(bf16[1,1792,2048]{2,1,0:T(8,128)(2,1)S(1)} %bitcast.65, bf16[384,1920]{1,0:T(8,128)(2,1)S(1)} %bitcast.79), kind=kOutput, calls=%fused_computation.14 | convolution fusion | flops 2819358720 | bytes 10289152 | tf_op jit(solution)/shard_map/dot_general | solution.py:179
  60.2 3.0 %fusion.21 = bf16[384,2048]{1,0:T(8,128)(2,1)S(1)} fusion(bf16[1,1792,2048]{2,1,0:T(8,128)(2,1)S(1)} %bitcast.67, bf16[384,1920]{1,0:T(8,128)(2,1)S(1)} %bitcast.80), kind=kOutput, calls=%fused_computation.15 | convolution fusion | flops 2819358720 | bytes 10289152 | tf_op jit(solution)/shard_map/dot_general | solution.py:179
  63.4 3.3 %collective-permute-start.13 = (bf16[32,2048]{1,0:T(8,128)(2,1)S(1)}, bf16[32,2048]{1,0:T(8,128)(2,1)S(1)}, u32[]{:S(2)}, u32[]{:S(2)}) collective-permute-start(bf16[32,2048]{1,0:T(8,128)(2,1)S(1)} %fusion.55), channel_id=1, source_target_pairs={{0,3},{1,0},{2,1},{3,2},{4,7},{5,4},{6,5},{7,6},{8,11},{9,8},{10,9... | collective-permute-start | bytes 393224 | tf_op jit(solution)/shard_map/ppermute | solution.py:31
  66.7 3.2 %collective-permute-start.11 = (bf16[96,2048]{1,0:T(8,128)(2,1)S(1)}, bf16[96,2048]{1,0:T(8,128)(2,1)S(1)}, u32[]{:S(2)}, u32[]{:S(2)}) collective-permute-start(bf16[96,2048]{1,0:T(8,128)(2,1)S(1)} %get-tuple-element.63), channel_id=1, source_target_pairs={{0,3},{1,0},{2,1},{3,2},{4,7},{5,4},{6,5},{7,6},{8,11},{9,8},{10,9... | collective-permute-start | bytes 1179656 | tf_op jit(solution)/shard_map/ppermute | solution.py:31
  69.9 2.4 %collective-permute-done.10 = bf16[96,2048]{1,0:T(8,128)(2,1)S(1)} collective-permute-done((bf16[96,2048]{1,0:T(8,128)(2,1)S(1)}, bf16[96,2048]{1,0:T(8,128)(2,1)S(1)}, u32[]{:S(2)}, u32[]{:S(2)}) %collective-permute-start.10) | collective-permute-done | bytes 393248 | tf_op jit(solution)/shard_map/ppermute | solution.py:31
  72.5 4.7 %collective-permute-done.11 = bf16[96,2048]{1,0:T(8,128)(2,1)S(1)} collective-permute-done((bf16[96,2048]{1,0:T(8,128)(2,1)S(1)}, bf16[96,2048]{1,0:T(8,128)(2,1)S(1)}, u32[]{:S(2)}, u32[]{:S(2)}) %collective-permute-start.11) | collective-permute-done | bytes 393248 | tf_op jit(solution)/shard_map/ppermute | solution.py:31
  77.4 3.8 %collective-permute-start.15 = (bf16[192,2048]{1,0:T(8,128)(2,1)S(1)}, bf16[192,2048]{1,0:T(8,128)(2,1)S(1)}, u32[]{:S(2)}, u32[]{:S(2)}) collective-permute-start(bf16[192,2048]{1,0:T(8,128)(2,1)S(1)} %pad_maximum_fusion.2), channel_id=1, source_target_pairs={{0,3},{1,0},{2,1},{3,2},{4,7},{5,4},{6,5},{7,6},{8,11},{9,8},{10,9... | collective-permute-start | bytes 2359304 | tf_op jit(solution)/shard_map/ppermute | solution.py:31
  81.6 3.2 %collective-permute-start.17 = (bf16[16,2048]{1,0:T(8,128)(2,1)S(1)}, bf16[16,2048]{1,0:T(8,128)(2,1)S(1)}, u32[]{:S(2)}, u32[]{:S(2)}) collective-permute-start(bf16[16,2048]{1,0:T(8,128)(2,1)S(1)} %slice.205), channel_id=1, source_target_pairs={{0,3},{1,0},{2,1},{3,2},{4,7},{5,4},{6,5},{7,6},{8,11},{9,8},{10,9... | collective-permute-start | bytes 196616 | tf_op jit(solution)/shard_map/ppermute | solution.py:31
  84.9 10.8 %collective-permute-done.15 = bf16[192,2048]{1,0:T(8,128)(2,1)S(1)} collective-permute-done((bf16[192,2048]{1,0:T(8,128)(2,1)S(1)}, bf16[192,2048]{1,0:T(8,128)(2,1)S(1)}, u32[]{:S(2)}, u32[]{:S(2)}) %collective-permute-start.15) | collective-permute-done | bytes 786464 | tf_op jit(solution)/shard_map/ppermute | solution.py:31
  96.0 0.4 fusion.42
  96.6 3.8 %collective-permute-start.19 = (bf16[96,2048]{1,0:T(8,128)(2,1)S(1)}, bf16[96,2048]{1,0:T(8,128)(2,1)S(1)}, u32[]{:S(2)}, u32[]{:S(2)}) collective-permute-start(bf16[96,2048]{1,0:T(8,128)(2,1)S(1)} %fusion.42), channel_id=1, source_target_pairs={{0,3},{1,0},{2,1},{3,2},{4,7},{5,4},{6,5},{7,6},{8,11},{9,8},{10,9... | collective-permute-start | bytes 1179656 | tf_op jit(solution)/shard_map/ppermute | solution.py:31
  100.4 1.2 fusion.27
  101.9 4.1 %collective-permute-done.20 = bf16[96,2048]{1,0:T(8,128)(2,1)S(1)} collective-permute-done((bf16[96,2048]{1,0:T(8,128)(2,1)S(1)}, bf16[96,2048]{1,0:T(8,128)(2,1)S(1)}, u32[]{:S(2)}, u32[]{:S(2)}) %collective-permute-start.20) | collective-permute-done | bytes 393248 | tf_op jit(solution)/shard_map/ppermute | solution.py:31
  106.1 3.5 %collective-permute-start.22 = (bf16[48,2048]{1,0:T(8,128)(2,1)S(1)}, bf16[48,2048]{1,0:T(8,128)(2,1)S(1)}, u32[]{:S(2)}, u32[]{:S(2)}) collective-permute-start(bf16[48,2048]{1,0:T(8,128)(2,1)S(1)} %slice.267), channel_id=1, source_target_pairs={{0,3},{1,0},{2,1},{3,2},{4,7},{5,4},{6,5},{7,6},{8,11},{9,8},{10,9... | collective-permute-start | bytes 589832 | tf_op jit(solution)/shard_map/ppermute | solution.py:31
  109.8 0.3 convolution_convert_fusion.4
  110.1 2.9 %collective-permute-done.21 = bf16[48,2048]{1,0:T(8,128)(2,1)S(1)} collective-permute-done((bf16[48,2048]{1,0:T(8,128)(2,1)S(1)}, bf16[48,2048]{1,0:T(8,128)(2,1)S(1)}, u32[]{:S(2)}, u32[]{:S(2)}) %collective-permute-start.21) | collective-permute-done | bytes 196640 | tf_op jit(solution)/shard_map/ppermute | solution.py:31
  113.1 3.0 %fusion.15 = bf16[384,1792]{1,0:T(8,128)(2,1)S(1)} fusion(bf16[384,2048]{1,0:T(8,128)(2,1)S(1)} %constant_dynamic-update-slice_fusion.9, bf16[1,2048,1792]{2,1,0:T(8,128)(2,1)S(1)} %bitcast.61, f32[384]{0:T(512)S(1)} %select_reduce_fusion), kind=kOutput, calls=%fused_computation.13 | convolution fusion | flops 2819948544 | bytes 10290688 | tf_op jit(solution)/shard_map/dot_general | solution.py:196
  116.5 0.6 collective-permute-start.23
  117.0 0.8 collective-permute-done.24
  117.9 0.3 convolution_convert_fusion.3
  118.3 3.2 %collective-permute-start.27 = (bf16[64,1792]{1,0:T(8,128)(2,1)S(1)}, bf16[64,1792]{1,0:T(8,128)(2,1)S(1)}, u32[]{:S(2)}, u32[]{:S(2)}) collective-permute-start(bf16[64,1792]{1,0:T(8,128)(2,1)S(1)} %get-tuple-element.80), channel_id=1, source_target_pairs={{0,24},{4,100},{8,0},{12,108},{16,8},{20,116},{24,16},{28,124},{32... | collective-permute-start | bytes 688136 | tf_op jit(solution)/shard_map/ppermute | solution.py:32
  121.5 0.4 convolution_convert_fusion
  122.0 3.5 %collective-permute-done.25 = bf16[64,1792]{1,0:T(8,128)(2,1)S(1)} collective-permute-done((bf16[64,1792]{1,0:T(8,128)(2,1)S(1)}, bf16[64,1792]{1,0:T(8,128)(2,1)S(1)}, u32[]{:S(2)}, u32[]{:S(2)}) %collective-permute-start.25) | collective-permute-done | bytes 229408 | tf_op jit(solution)/shard_map/ppermute | solution.py:32
  125.7 3.3 %collective-permute-start.28 = (bf16[128,1792]{1,0:T(8,128)(2,1)S(1)}, bf16[128,1792]{1,0:T(8,128)(2,1)S(1)}, u32[]{:S(2)}, u32[]{:S(2)}) collective-permute-start(bf16[128,1792]{1,0:T(8,128)(2,1)S(1)} %pad_maximum_fusion.5), channel_id=1, source_target_pairs={{0,24},{4,100},{8,0},{12,108},{16,8},{20,116},{24,16},{28,124},{32... | collective-permute-start | bytes 1376264 | tf_op jit(solution)/shard_map/ppermute | solution.py:32
  129.1 5.9 %collective-permute-done.28 = bf16[128,1792]{1,0:T(8,128)(2,1)S(1)} collective-permute-done((bf16[128,1792]{1,0:T(8,128)(2,1)S(1)}, bf16[128,1792]{1,0:T(8,128)(2,1)S(1)}, u32[]{:S(2)}, u32[]{:S(2)}) %collective-permute-start.28) | collective-permute-done | bytes 458784 | tf_op jit(solution)/shard_map/ppermute | solution.py:32
  135.0 3.8 %collective-permute-done.26 = bf16[128,1792]{1,0:T(8,128)(2,1)S(1)} collective-permute-done((bf16[128,1792]{1,0:T(8,128)(2,1)S(1)}, bf16[128,1792]{1,0:T(8,128)(2,1)S(1)}, u32[]{:S(2)}, u32[]{:S(2)}) %collective-permute-start.26) | collective-permute-done | bytes 458784 | tf_op jit(solution)/shard_map/ppermute | solution.py:32
  139.0 15.4 %all_to_all.10.back_ref = bf16[16,8,1792]{2,1,0:T(8,128)(2,1)} all-to-all(bf16[16,8,1792]{2,1,0:T(8,128)(2,1)S(1)} %fusion.43), channel_id=1, replica_groups={{0,1,2,3,32,33,34,35,64,65,66,67,96,97,98,99},{8,9,10,11,40,41,42,43,72..., dimensions={0} | all-to-all | bytes 917504 | tf_op jit(solution)/shard_map/all_to_all | solution.py:41
  154.4 1.8 %finish.1 = bf16[8,7168]{1,0:T(8,128)(2,1)} custom-call(bf16[8,7168]{1,0:T(8,128)(2,1)} %hidden_ref.3, bf16[16,8,1792]{2,1,0:T(8,128)(2,1)} %all_to_all.10.back_ref), custom_call_target="tpu_custom_call" | custom-call | tf_op jit(solution)/shard_map/finish/pallas_call | solution.py:245
  (129 shorter events, 5.4 us)
Async XLA Ops:
  1.9 19.5 %all-to-all-start = ((bf16[16,8,1920]{2,1,0:T(8,128)(2,1)}), bf16[16,8,1920]{2,1,0:T(8,128)(2,1)S(1)}, u32[]{:S(2)}, u32[]{:S(2)}) async-start(bf16[16,8,1920]{2,1,0:T(8,128)(2,1)} %prepare.1), calls=%async_computation | async-start | bytes 983040 | tf_op jit(solution)/shard_map/all_to_all | solution.py:41
  21.9 3.2 %collective-permute-start.2 = (bf16[64,1920]{1,0:T(8,128)(2,1)S(1)}, bf16[64,1920]{1,0:T(8,128)(2,1)S(1)}, u32[]{:S(2)}, u32[]{:S(2)}) collective-permute-start(bf16[64,1920]{1,0:T(8,128)(2,1)S(1)} %convolution_convert_fusion.5), channel_id=1, source_target_pairs={{0,4},{4,0},{8,12},{12,8},{16,20},{20,16},{24,28},{28,24},{32,36},... | collective-permute-start | bytes 737288 | tf_op jit(solution)/shard_map/ppermute | solution.py:32
  22.0 9.7 %collective-permute-start.1 = (bf16[128,1920]{1,0:T(8,128)(2,1)S(1)}, bf16[128,1920]{1,0:T(8,128)(2,1)S(1)}, u32[]{:S(2)}, u32[]{:S(2)}) collective-permute-start(bf16[128,1920]{1,0:T(8,128)(2,1)S(1)} %bitcast.72), channel_id=1, source_target_pairs={{0,24},{4,100},{8,0},{12,108},{16,8},{20,116},{24,16},{28,124},{32... | collective-permute-start | bytes 1474568 | tf_op jit(solution)/shard_map/ppermute | solution.py:32
  24.8 10.0 %collective-permute-start = (bf16[128,1920]{1,0:T(8,128)(2,1)S(1)}, bf16[128,1920]{1,0:T(8,128)(2,1)S(1)}, u32[]{:S(2)}, u32[]{:S(2)}) collective-permute-start(bf16[128,1920]{1,0:T(8,128)(2,1)S(1)} %bitcast.73), channel_id=1, source_target_pairs={{0,8},{4,36},{8,16},{12,44},{16,24},{20,52},{24,0},{28,60},{32,40}... | collective-permute-start | bytes 1474568 | tf_op jit(solution)/shard_map/ppermute | solution.py:32
  25.1 4.4 %slice-start.2 = ((s8[7340032]{0:T(1024)(128)(4,1)}), s8[4194304]{0:T(1024)(128)(4,1)S(1)}, s32[]{:S(2)}) async-start(s8[7340032]{0:T(1024)(128)(4,1)} %bitcast.62), calls=%async_computation.4 | async-start | bytes 8388608
  25.2 5.2 %slice-start.3 = ((s8[7340032]{0:T(1024)(128)(4,1)}), s8[3145728]{0:T(1024)(128)(4,1)S(1)}, s32[]{:S(2)}) async-start(s8[7340032]{0:T(1024)(128)(4,1)} %bitcast.62), calls=%async_computation.5 | async-start | bytes 6291456
  34.8 7.5 %collective-permute-start.3 = (bf16[64,1920]{1,0:T(8,128)(2,1)S(1)}, bf16[64,1920]{1,0:T(8,128)(2,1)S(1)}, u32[]{:S(2)}, u32[]{:S(2)}) collective-permute-start(bf16[64,1920]{1,0:T(8,128)(2,1)S(1)} %slice.185), channel_id=1, source_target_pairs={{0,8},{4,36},{8,16},{12,44},{16,24},{20,52},{24,0},{28,60},{32,40}... | collective-permute-start | bytes 737288 | tf_op jit(solution)/shard_map/ppermute | solution.py:32
  35.0 7.4 %collective-permute-start.4 = (bf16[64,1920]{1,0:T(8,128)(2,1)S(1)}, bf16[64,1920]{1,0:T(8,128)(2,1)S(1)}, u32[]{:S(2)}, u32[]{:S(2)}) collective-permute-start(bf16[64,1920]{1,0:T(8,128)(2,1)S(1)} %slice.186), channel_id=1, source_target_pairs={{0,24},{4,100},{8,0},{12,108},{16,8},{20,116},{24,16},{28,124},{32... | collective-permute-start | bytes 737288 | tf_op jit(solution)/shard_map/ppermute | solution.py:32
  38.8 6.2 %collective-permute-start.6 = (bf16[32,2048]{1,0:T(8,128)(2,1)S(1)}, bf16[32,2048]{1,0:T(8,128)(2,1)S(1)}, u32[]{:S(2)}, u32[]{:S(2)}) collective-permute-start(bf16[32,2048]{1,0:T(8,128)(2,1)S(1)} %get-tuple-element.33), channel_id=1, source_target_pairs={{0,1},{1,2},{2,3},{3,0},{4,5},{5,6},{6,7},{7,4},{8,9},{9,10},{10,1... | collective-permute-start | bytes 393224 | tf_op jit(solution)/shard_map/ppermute | solution.py:31
  39.3 5.8 %collective-permute-start.7 = (bf16[32,2048]{1,0:T(8,128)(2,1)S(1)}, bf16[32,2048]{1,0:T(8,128)(2,1)S(1)}, u32[]{:S(2)}, u32[]{:S(2)}) collective-permute-start(bf16[32,2048]{1,0:T(8,128)(2,1)S(1)} %get-tuple-element.34), channel_id=1, source_target_pairs={{0,3},{1,0},{2,1},{3,2},{4,7},{5,4},{6,5},{7,6},{8,11},{9,8},{10,9... | collective-permute-start | bytes 393224 | tf_op jit(solution)/shard_map/ppermute | solution.py:31
  42.6 14.4 %slice-start.4 = ((s8[7340032]{0:T(1024)(128)(4,1)}), s8[4194304]{0:T(1024)(128)(4,1)S(1)}, s32[]{:S(2)}) async-start(s8[7340032]{0:T(1024)(128)(4,1)} %bitcast.64), calls=%async_computation.6 | async-start | bytes 8388608
  45.2 7.7 %collective-permute-start.9 = (bf16[64,2048]{1,0:T(8,128)(2,1)S(1)}, bf16[64,2048]{1,0:T(8,128)(2,1)S(1)}, u32[]{:S(2)}, u32[]{:S(2)}) collective-permute-start(bf16[64,2048]{1,0:T(8,128)(2,1)S(1)} %pad_maximum_fusion.7), channel_id=1, source_target_pairs={{0,3},{1,0},{2,1},{3,2},{4,7},{5,4},{6,5},{7,6},{8,11},{9,8},{10,9... | collective-permute-start | bytes 786440 | tf_op jit(solution)/shard_map/ppermute | solution.py:31
  49.0 7.7 %collective-permute-start.8 = (bf16[64,2048]{1,0:T(8,128)(2,1)S(1)}, bf16[64,2048]{1,0:T(8,128)(2,1)S(1)}, u32[]{:S(2)}, u32[]{:S(2)}) collective-permute-start(bf16[64,2048]{1,0:T(8,128)(2,1)S(1)} %pad_maximum_fusion.6), channel_id=1, source_target_pairs={{0,1},{1,2},{2,3},{3,0},{4,5},{5,6},{6,7},{7,4},{8,9},{9,10},{10,1... | collective-permute-start | bytes 786440 | tf_op jit(solution)/shard_map/ppermute | solution.py:31
  49.1 7.8 %collective-permute-start.5 = (bf16[192,1920]{1,0:T(8,128)(2,1)S(1)}, bf16[192,1920]{1,0:T(8,128)(2,1)S(1)}, u32[]{:S(2)}, u32[]{:S(2)}) collective-permute-start(bf16[192,1920]{1,0:T(8,128)(2,1)S(1)} %convolution_convert_fusion.1), channel_id=1, source_target_pairs={{0,4},{4,0},{8,12},{12,8},{16,20},{20,16},{24,28},{28,24},{32,36},... | collective-permute-start | bytes 2211848 | tf_op jit(solution)/shard_map/ppermute | solution.py:32
  49.7 7.4 %slice-start.5 = ((s8[7340032]{0:T(1024)(128)(4,1)}), s8[3145728]{0:T(1024)(128)(4,1)S(1)}, s32[]{:S(2)}) async-start(s8[7340032]{0:T(1024)(128)(4,1)} %bitcast.64), calls=%async_computation.7 | async-start | bytes 6291456
  56.9 3.2 %slice-start.6 = ((s8[7340032]{0:T(1024)(128)(4,1)}), s8[4194304]{0:T(1024)(128)(4,1)S(1)}, s32[]{:S(2)}) async-start(s8[7340032]{0:T(1024)(128)(4,1)} %bitcast.66), calls=%async_computation.8 | async-start | bytes 8388608
  57.1 3.1 %slice-start.7 = ((s8[7340032]{0:T(1024)(128)(4,1)}), s8[3145728]{0:T(1024)(128)(4,1)S(1)}, s32[]{:S(2)}) async-start(s8[7340032]{0:T(1024)(128)(4,1)} %bitcast.66), calls=%async_computation.9 | async-start | bytes 6291456
  63.2 9.1 %collective-permute-start.10 = (bf16[96,2048]{1,0:T(8,128)(2,1)S(1)}, bf16[96,2048]{1,0:T(8,128)(2,1)S(1)}, u32[]{:S(2)}, u32[]{:S(2)}) collective-permute-start(bf16[96,2048]{1,0:T(8,128)(2,1)S(1)} %get-tuple-element.62), channel_id=1, source_target_pairs={{0,1},{1,2},{2,3},{3,0},{4,5},{5,6},{6,7},{7,4},{8,9},{9,10},{10,1... | collective-permute-start | bytes 1179656 | tf_op jit(solution)/shard_map/ppermute | solution.py:31
  63.4 13.9 %collective-permute-start.13 = (bf16[32,2048]{1,0:T(8,128)(2,1)S(1)}, bf16[32,2048]{1,0:T(8,128)(2,1)S(1)}, u32[]{:S(2)}, u32[]{:S(2)}) collective-permute-start(bf16[32,2048]{1,0:T(8,128)(2,1)S(1)} %fusion.55), channel_id=1, source_target_pairs={{0,3},{1,0},{2,1},{3,2},{4,7},{5,4},{6,5},{7,6},{8,11},{9,8},{10,9... | collective-permute-start | bytes 393224 | tf_op jit(solution)/shard_map/ppermute | solution.py:31
  66.7 10.7 %collective-permute-start.12 = (bf16[32,2048]{1,0:T(8,128)(2,1)S(1)}, bf16[32,2048]{1,0:T(8,128)(2,1)S(1)}, u32[]{:S(2)}, u32[]{:S(2)}) collective-permute-start(bf16[32,2048]{1,0:T(8,128)(2,1)S(1)} %fusion.55), channel_id=1, source_target_pairs={{0,1},{1,2},{2,3},{3,0},{4,5},{5,6},{6,7},{7,4},{8,9},{9,10},{10,1... | collective-permute-start | bytes 393224 | tf_op jit(solution)/shard_map/ppermute | solution.py:31
  66.7 10.5 %collective-permute-start.11 = (bf16[96,2048]{1,0:T(8,128)(2,1)S(1)}, bf16[96,2048]{1,0:T(8,128)(2,1)S(1)}, u32[]{:S(2)}, u32[]{:S(2)}) collective-permute-start(bf16[96,2048]{1,0:T(8,128)(2,1)S(1)} %get-tuple-element.63), channel_id=1, source_target_pairs={{0,3},{1,0},{2,1},{3,2},{4,7},{5,4},{6,5},{7,6},{8,11},{9,8},{10,9... | collective-permute-start | bytes 1179656 | tf_op jit(solution)/shard_map/ppermute | solution.py:31
  72.4 28.0 %slice-start = ((s8[7340032]{0:T(1024)(128)(4,1)}), s8[4194304]{0:T(1024)(128)(4,1)S(1)}, s32[]{:S(2)}) async-start(s8[7340032]{0:T(1024)(128)(4,1)} %bitcast.60), calls=%async_computation.2 | async-start | bytes 8388608
  72.5 8.7 %copy-start = (s32[128]{0:T(128)S(1)}, s32[128]{0:T(128)}, u32[]{:S(2)}) copy-start(s32[128]{0:T(128)} %get-tuple-element.98) | copy-start | bytes 1540
  77.4 18.5 %collective-permute-start.14 = (bf16[192,2048]{1,0:T(8,128)(2,1)S(1)}, bf16[192,2048]{1,0:T(8,128)(2,1)S(1)}, u32[]{:S(2)}, u32[]{:S(2)}) collective-permute-start(bf16[192,2048]{1,0:T(8,128)(2,1)S(1)} %pad_maximum_fusion.1), channel_id=1, source_target_pairs={{0,1},{1,2},{2,3},{3,0},{4,5},{5,6},{6,7},{7,4},{8,9},{9,10},{10,1... | collective-permute-start | bytes 2359304 | tf_op jit(solution)/shard_map/ppermute | solution.py:31
  77.4 18.2 %collective-permute-start.15 = (bf16[192,2048]{1,0:T(8,128)(2,1)S(1)}, bf16[192,2048]{1,0:T(8,128)(2,1)S(1)}, u32[]{:S(2)}, u32[]{:S(2)}) collective-permute-start(bf16[192,2048]{1,0:T(8,128)(2,1)S(1)} %pad_maximum_fusion.2), channel_id=1, source_target_pairs={{0,3},{1,0},{2,1},{3,2},{4,7},{5,4},{6,5},{7,6},{8,11},{9,8},{10,9... | collective-permute-start | bytes 2359304 | tf_op jit(solution)/shard_map/ppermute | solution.py:31
  81.6 18.8 %collective-permute-start.16 = (bf16[16,2048]{1,0:T(8,128)(2,1)S(1)}, bf16[16,2048]{1,0:T(8,128)(2,1)S(1)}, u32[]{:S(2)}, u32[]{:S(2)}) collective-permute-start(bf16[16,2048]{1,0:T(8,128)(2,1)S(1)} %slice.204), channel_id=1, source_target_pairs={{0,1},{1,2},{2,3},{3,0},{4,5},{5,6},{6,7},{7,4},{8,9},{9,10},{10,1... | collective-permute-start | bytes 196616 | tf_op jit(solution)/shard_map/ppermute | solution.py:31
  81.6 18.7 %collective-permute-start.17 = (bf16[16,2048]{1,0:T(8,128)(2,1)S(1)}, bf16[16,2048]{1,0:T(8,128)(2,1)S(1)}, u32[]{:S(2)}, u32[]{:S(2)}) collective-permute-start(bf16[16,2048]{1,0:T(8,128)(2,1)S(1)} %slice.205), channel_id=1, source_target_pairs={{0,3},{1,0},{2,1},{3,2},{4,7},{5,4},{6,5},{7,6},{8,11},{9,8},{10,9... | collective-permute-start | bytes 196616 | tf_op jit(solution)/shard_map/ppermute | solution.py:31
  84.9 15.5 %slice-start.1 = ((s8[7340032]{0:T(1024)(128)(4,1)}), s8[3145728]{0:T(1024)(128)(4,1)S(1)}, s32[]{:S(2)}) async-start(s8[7340032]{0:T(1024)(128)(4,1)} %bitcast.60), calls=%async_computation.3 | async-start | bytes 6291456
  96.5 9.5 %collective-permute-start.20 = (bf16[96,2048]{1,0:T(8,128)(2,1)S(1)}, bf16[96,2048]{1,0:T(8,128)(2,1)S(1)}, u32[]{:S(2)}, u32[]{:S(2)}) collective-permute-start(bf16[96,2048]{1,0:T(8,128)(2,1)S(1)} %fusion.42), channel_id=1, source_target_pairs={{0,1},{1,2},{2,3},{3,0},{4,5},{5,6},{6,7},{7,4},{8,9},{9,10},{10,1... | collective-permute-start | bytes 1179656 | tf_op jit(solution)/shard_map/ppermute | solution.py:31
  96.6 9.5 %collective-permute-start.19 = (bf16[96,2048]{1,0:T(8,128)(2,1)S(1)}, bf16[96,2048]{1,0:T(8,128)(2,1)S(1)}, u32[]{:S(2)}, u32[]{:S(2)}) collective-permute-start(bf16[96,2048]{1,0:T(8,128)(2,1)S(1)} %fusion.42), channel_id=1, source_target_pairs={{0,3},{1,0},{2,1},{3,2},{4,7},{5,4},{6,5},{7,6},{8,11},{9,8},{10,9... | collective-permute-start | bytes 1179656 | tf_op jit(solution)/shard_map/ppermute | solution.py:31
  101.6 8.1 %collective-permute-start.18 = (bf16[64,1792]{1,0:T(8,128)(2,1)S(1)}, bf16[64,1792]{1,0:T(8,128)(2,1)S(1)}, u32[]{:S(2)}, u32[]{:S(2)}) collective-permute-start(bf16[64,1792]{1,0:T(8,128)(2,1)S(1)} %bitcast.92), channel_id=1, source_target_pairs={{0,4},{4,0},{8,12},{12,8},{16,20},{20,16},{24,28},{28,24},{32,36},... | collective-permute-start | bytes 688136 | tf_op jit(solution)/shard_map/ppermute | solution.py:32
  106.0 6.9 %collective-permute-start.21 = (bf16[48,2048]{1,0:T(8,128)(2,1)S(1)}, bf16[48,2048]{1,0:T(8,128)(2,1)S(1)}, u32[]{:S(2)}, u32[]{:S(2)}) collective-permute-start(bf16[48,2048]{1,0:T(8,128)(2,1)S(1)} %slice.266), channel_id=1, source_target_pairs={{0,1},{1,2},{2,3},{3,0},{4,5},{5,6},{6,7},{7,4},{8,9},{9,10},{10,1... | collective-permute-start | bytes 589832 | tf_op jit(solution)/shard_map/ppermute | solution.py:31
  106.1 6.8 %collective-permute-start.22 = (bf16[48,2048]{1,0:T(8,128)(2,1)S(1)}, bf16[48,2048]{1,0:T(8,128)(2,1)S(1)}, u32[]{:S(2)}, u32[]{:S(2)}) collective-permute-start(bf16[48,2048]{1,0:T(8,128)(2,1)S(1)} %slice.267), channel_id=1, source_target_pairs={{0,3},{1,0},{2,1},{3,2},{4,7},{5,4},{6,5},{7,6},{8,11},{9,8},{10,9... | collective-permute-start | bytes 589832 | tf_op jit(solution)/shard_map/ppermute | solution.py:31
  116.3 1.6 %collective-permute-start.24 = (bf16[64,1792]{1,0:T(8,128)(2,1)S(1)}, bf16[64,1792]{1,0:T(8,128)(2,1)S(1)}, u32[]{:S(2)}, u32[]{:S(2)}) collective-permute-start(bf16[64,1792]{1,0:T(8,128)(2,1)S(1)} %bitcast.93), channel_id=1, source_target_pairs={{0,4},{4,0},{8,12},{12,8},{16,20},{20,16},{24,28},{28,24},{32,36},... | collective-permute-start | bytes 688136 | tf_op jit(solution)/shard_map/ppermute | solution.py:32
  116.5 5.1 %collective-permute-start.23 = (bf16[128,1792]{1,0:T(8,128)(2,1)S(1)}, bf16[128,1792]{1,0:T(8,128)(2,1)S(1)}, u32[]{:S(2)}, u32[]{:S(2)}) collective-permute-start(bf16[128,1792]{1,0:T(8,128)(2,1)S(1)} %bitcast.90), channel_id=1, source_target_pairs={{0,4},{4,0},{8,12},{12,8},{16,20},{20,16},{24,28},{28,24},{32,36},... | collective-permute-start | bytes 1376264 | tf_op jit(solution)/shard_map/ppermute | solution.py:32
  118.2 7.3 %collective-permute-start.25 = (bf16[64,1792]{1,0:T(8,128)(2,1)S(1)}, bf16[64,1792]{1,0:T(8,128)(2,1)S(1)}, u32[]{:S(2)}, u32[]{:S(2)}) collective-permute-start(bf16[64,1792]{1,0:T(8,128)(2,1)S(1)} %get-tuple-element.79), channel_id=1, source_target_pairs={{0,8},{4,36},{8,16},{12,44},{16,24},{20,52},{24,0},{28,60},{32,40}... | collective-permute-start | bytes 688136 | tf_op jit(solution)/shard_map/ppermute | solution.py:32
  118.3 7.2 %collective-permute-start.27 = (bf16[64,1792]{1,0:T(8,128)(2,1)S(1)}, bf16[64,1792]{1,0:T(8,128)(2,1)S(1)}, u32[]{:S(2)}, u32[]{:S(2)}) collective-permute-start(bf16[64,1792]{1,0:T(8,128)(2,1)S(1)} %get-tuple-element.80), channel_id=1, source_target_pairs={{0,24},{4,100},{8,0},{12,108},{16,8},{20,116},{24,16},{28,124},{32... | collective-permute-start | bytes 688136 | tf_op jit(solution)/shard_map/ppermute | solution.py:32
  125.7 9.3 %collective-permute-start.28 = (bf16[128,1792]{1,0:T(8,128)(2,1)S(1)}, bf16[128,1792]{1,0:T(8,128)(2,1)S(1)}, u32[]{:S(2)}, u32[]{:S(2)}) collective-permute-start(bf16[128,1792]{1,0:T(8,128)(2,1)S(1)} %pad_maximum_fusion.5), channel_id=1, source_target_pairs={{0,24},{4,100},{8,0},{12,108},{16,8},{20,116},{24,16},{28,124},{32... | collective-permute-start | bytes 1376264 | tf_op jit(solution)/shard_map/ppermute | solution.py:32
  129.0 9.8 %collective-permute-start.26 = (bf16[128,1792]{1,0:T(8,128)(2,1)S(1)}, bf16[128,1792]{1,0:T(8,128)(2,1)S(1)}, u32[]{:S(2)}, u32[]{:S(2)}) collective-permute-start(bf16[128,1792]{1,0:T(8,128)(2,1)S(1)} %pad_maximum_fusion.4), channel_id=1, source_target_pairs={{0,8},{4,36},{8,16},{12,44},{16,24},{20,52},{24,0},{28,60},{32,40}... | collective-permute-start | bytes 1376264 | tf_op jit(solution)/shard_map/ppermute | solution.py:32

commit v8 on v7

--- a/solution.py
+++ b/solution.py
@@ -217,26 +217,30 @@
     one = jnp.concatenate([high, low], axis=0)
     far = jnp.concatenate([first, second, high, low], axis=0)
     own, theirs = picks_of(far)
-    gate_far, up_far = hold((own,), (gate_far, up_far))
-    to_low, to_high = sends(gate, gate_far, up, up_far)
-    near_act = activate(gate[0], up[0], move(to_low, "x", 1), move(to_high, "x", -1))
+    near_gate, near_up, near_fars = gate, up, (gate_far, up_far)
     cut = near.shape[0] // 2 // RING
     slots, far_scale = enter(own, theirs, [0, cut])
     gate, up = product(slots, w_gate), product(slots, w_up)
     gate_far, up_far = move(gate[2], "x", 1), move(up[2], "x", -1)
-    (near_act,) = hold(up, (near_act,))
+    far_sends = sends(gate, gate_far, up, up_far)
+    far_low, far_high = move(far_sends[0], "x", 1), move(far_sends[1], "x", -1)
+    near_fars = hold(far_sends, near_fars)
+    near_sends = sends(near_gate, near_fars[0], near_up, near_fars[1])
+    near_low, near_high = move(near_sends[0], "x", 1), move(near_sends[1], "x", -1)
+    far_act = activate(gate[0], up[0], far_low, far_high)
+    far_low, far_high = move(far_act, "x", 1), move(far_act, "x", -1)
+    near_low, near_high = hold((far_act,), (near_low, near_high))
+    near_act = activate(near_gate[0], near_up[0], near_low, near_high)
     near_low, near_high = move(near_act, "x", 1), move(near_act, "x", -1)
-    to_low, to_high = sends(gate, gate_far, up, up_far)
-    to_low, to_high, near_low, near_high = hold((), (to_low, to_high, near_low, near_high))
-    far_low, far_high = move(to_low, "x", 1), move(to_high, "x", -1)
+    half = far_act.shape[0] // 2
+    far_first, far_second = move(far_low[:half], "x", 1), move(far_high[half:], "x", -1)
+    near_low, near_high = hold((far_low, far_high), (near_low, near_high))
     half = near_act.shape[0] // 2
     near_first, near_second = move(near_low[:half], "x", 1), move(near_high[half:], "x", -1)
-    near_first, near_second = hold((far_low, far_high), (near_first, near_second))
+    out = last(jnp.concatenate([far_act, far_high, far_first, far_second, far_low], axis=0), far_scale)
+    near_first, near_second = hold((out,), (near_first, near_second))
     near_whole = jnp.concatenate([near_act, near_high, near_first, near_second, near_low], axis=0)
-    pieces = gather_ring(activate(gate[0], up[0], far_low, far_high), "x")
     near_sum = leave(last(near_whole, near_scale), near)
-    pieces = hold((near_sum,), pieces)
-    out = last(jnp.concatenate(pieces, axis=0), far_scale)
     two_sum = leave(out[:, : 2 * cut], two)
     one_sum = leave(out[:, 2 * cut :], one)
     part = near.shape[0]

time: 157 us -> 153 us (0.975)
  starting transfers between devices: 49.2 us -> 41.2 us
  waiting for transfers between devices: 62.5 us -> 68.9 us
  blocking collectives: 15.4 us -> 13 us
    ppermute x16, starting transfers between devices: 28.2 us -> 20.2 us  [move(): lax.ppermute(value, 'exp', [(i, (i + step) % RING) for i in range(RING)])]
    ppermute x16, waiting for transfers between devices: 32.8 us -> 36.5 us  [move(): lax.ppermute(value, 'exp', [(i, (i + step) % RING) for i in range(RING)])]
    ppermute x13, waiting for transfers between devices: 17.5 us -> 20.1 us  [move(): return lax.ppermute(value, 'attn', attn_pairs(axis, step))]
    all_to_all x1, blocking collectives: 15.4 us -> 13 us  [swap(): lax.all_to_all(value, ('attn', 'exp'), split_axis=0, concat_axis=0, axis_...]
  transfers between devices with their start and end apart: 30 -> 30, of which waited for: 16 -> 15; matrix products, arithmetic and copies ran while one was open for 8% -> 14% of each run, Pallas kernels for 0% -> 0%
where the time goes in v8:
time: 153 us; the launch traced here: 152 us
  waiting for transfers between devices  68.9 us (45%)
  starting transfers between devices  41.2 us (27%)
  matrix products  19 us (12%)
  blocking collectives  13 us (8%)
  Pallas kernels  3.72 us (2%)
  other arithmetic  2.8 us (2%)
  local copies, waits for them, and re-layouts  2.48 us (2%)
    ppermute x16, waiting for transfers between devices, move(): lax.ppermute(value, 'exp', [(i, (i + step) % RING) for i in range(RING)])  36.5 us
    ppermute x16, starting transfers between devices, move(): lax.ppermute(value, 'exp', [(i, (i + step) % RING) for i in range(RING)])  20.2 us
    ppermute x13, waiting for transfers between devices, move(): return lax.ppermute(value, 'attn', attn_pairs(axis, step))  20.1 us
    ppermute x13, starting transfers between devices, move(): return lax.ppermute(value, 'attn', attn_pairs(axis, step))  13.9 us
    all_to_all x1, blocking collectives, swap(): lax.all_to_all(value, ('attn', 'exp'), split_axis=0, concat_axis=0, axis_...  13 us
    all_to_all x1, waiting for transfers between devices, swap(): lax.all_to_all(value, ('attn', 'exp'), split_axis=0, concat_axis=0, axis_...  12.3 us
    dot_general x4, matrix products, product(): jnp.dot(slots, weights[0], preferred_element_type=jnp.float32)  11.6 us
    all_to_all x1, starting transfers between devices, swap(): lax.all_to_all(value, ('attn', 'exp'), split_axis=0, concat_axis=0, axis_...  7.12 us
  transfers between devices with their start and end apart: 30, of which 15 were waited for; matrix products, arithmetic and copies ran while one was open for 14% of the time, Pallas kernels for 0%

profile of v8, /device:TPU:0, one launch (start us, length us, event | category | flops | bytes accessed | tf_op | source)
XLA Modules:
  0.0 151.9 jit_solution(13890999700168758165)
XLA Ops:
  0.0 1.9 %prepare.1 = bf16[16,8,1920]{2,1,0:T(8,128)(2,1)} custom-call(bf16[8,7168]{1,0:T(8,128)(2,1)} %hidden_ref.3, f32[1,7168]{1,0:T(1,128)} %bitcast.92, s32[8,8]{1,0:T(8,128)} %routes_ref.1, f32[8,8]{1,0:T(8,128)} %scores_ref.1, s32[1,32]{1,0:T(1,128)} %bitcast.93), custom_call_target="tpu_custom_call" | custom-call | tf_op jit(solution)/shard_map/prepare/pallas_call | solution.py:154
  1.9 7.1 %all-to-all-start = ((bf16[16,8,1920]{2,1,0:T(8,128)(2,1)}), bf16[16,8,1920]{2,1,0:T(8,128)(2,1)S(1)}, u32[]{:S(2)}, u32[]{:S(2)}) async-start(bf16[16,8,1920]{2,1,0:T(8,128)(2,1)} %prepare.1), calls=%async_computation | async-start | bytes 983040 | tf_op jit(solution)/shard_map/all_to_all | solution.py:41
  9.2 12.3 %all-to-all-done = bf16[16,8,1920]{2,1,0:T(8,128)(2,1)S(1)} async-done(((bf16[16,8,1920]{2,1,0:T(8,128)(2,1)}), bf16[16,8,1920]{2,1,0:T(8,128)(2,1)S(1)}, u32[]{:S(2)}, u32[]{:S(2)}) %all-to-all-start) | async-done | bytes 491552 | tf_op jit(solution)/shard_map/all_to_all | solution.py:41
  21.5 0.4 convolution_convert_fusion.5
  22.0 2.7 %collective-permute-start.1 = (bf16[128,1920]{1,0:T(8,128)(2,1)S(1)}, bf16[128,1920]{1,0:T(8,128)(2,1)S(1)}, u32[]{:S(2)}, u32[]{:S(2)}) collective-permute-start(bf16[128,1920]{1,0:T(8,128)(2,1)S(1)} %bitcast.70), channel_id=1, source_target_pairs={{0,24},{4,100},{8,0},{12,108},{16,8},{20,116},{24,16},{28,124},{32... | collective-permute-start | bytes 1474568 | tf_op jit(solution)/shard_map/ppermute | solution.py:32
  24.7 0.3 convolution_convert_fusion.6
  25.2 4.4 %fusion.33 = bf16[128,2048]{1,0:T(8,128)(2,1)S(1)} fusion(bf16[1,1792,2048]{2,1,0:T(8,128)(2,1)} %param.14, bf16[128,1920]{1,0:T(8,128)(2,1)S(1)} %bitcast.66), kind=kOutput, calls=%fused_computation.22 | convolution fusion | flops 939786240 | bytes 8323072 | tf_op jit(solution)/shard_map/dot_general | solution.py:179
  29.6 0.8 slice-done.5
  30.4 1.2 fusion.30
  31.7 3.1 %collective-permute-done = bf16[128,1920]{1,0:T(8,128)(2,1)S(1)} collective-permute-done((bf16[128,1920]{1,0:T(8,128)(2,1)S(1)}, bf16[128,1920]{1,0:T(8,128)(2,1)S(1)}, u32[]{:S(2)}, u32[]{:S(2)}) %collective-permute-start) | collective-permute-done | bytes 491552 | tf_op jit(solution)/shard_map/ppermute | solution.py:32
  34.9 3.3 %collective-permute-start.4 = (bf16[64,1920]{1,0:T(8,128)(2,1)S(1)}, bf16[64,1920]{1,0:T(8,128)(2,1)S(1)}, u32[]{:S(2)}, u32[]{:S(2)}) collective-permute-start(bf16[64,1920]{1,0:T(8,128)(2,1)S(1)} %slice.186), channel_id=1, source_target_pairs={{0,24},{4,100},{8,0},{12,108},{16,8},{20,116},{24,16},{28,124},{32... | collective-permute-start | bytes 737288 | tf_op jit(solution)/shard_map/ppermute | solution.py:32
  38.3 4.0 %collective-permute-done.3 = bf16[64,1920]{1,0:T(8,128)(2,1)S(1)} collective-permute-done((bf16[64,1920]{1,0:T(8,128)(2,1)S(1)}, bf16[64,1920]{1,0:T(8,128)(2,1)S(1)}, u32[]{:S(2)}, u32[]{:S(2)}) %collective-permute-start.3) | collective-permute-done | bytes 245792 | tf_op jit(solution)/shard_map/ppermute | solution.py:32
  42.6 0.7 convolution_convert_fusion.1
  43.6 0.6 collective-permute-start.10
  44.2 2.7 %collective-permute-start.11 = (bf16[32,2048]{1,0:T(8,128)(2,1)S(1)}, bf16[32,2048]{1,0:T(8,128)(2,1)S(1)}, u32[]{:S(2)}, u32[]{:S(2)}) collective-permute-start(bf16[32,2048]{1,0:T(8,128)(2,1)S(1)} %get-tuple-element.28), channel_id=1, source_target_pairs={{0,3},{1,0},{2,1},{3,2},{4,7},{5,4},{6,5},{7,6},{8,11},{9,8},{10,9... | collective-permute-start | bytes 393224 | tf_op jit(solution)/shard_map/ppermute | solution.py:31
  47.1 0.7 convolution_convert_fusion.2
  48.2 0.7 slice-done.3
  49.0 3.0 %fusion.21 = bf16[384,2048]{1,0:T(8,128)(2,1)S(1)} fusion(bf16[1,1792,2048]{2,1,0:T(8,128)(2,1)S(1)} %bitcast.63, bf16[384,1920]{1,0:T(8,128)(2,1)S(1)} %bitcast.77), kind=kOutput, calls=%fused_computation.15 | convolution fusion | flops 2819358720 | bytes 10289152 | tf_op jit(solution)/shard_map/dot_general | solution.py:179
  52.0 3.0 %fusion.18 = bf16[384,2048]{1,0:T(8,128)(2,1)S(1)} fusion(bf16[1,1792,2048]{2,1,0:T(8,128)(2,1)S(1)} %bitcast.65, bf16[384,1920]{1,0:T(8,128)(2,1)S(1)} %bitcast.78), kind=kOutput, calls=%fused_computation.14 | convolution fusion | flops 2819358720 | bytes 10289152 | tf_op jit(solution)/shard_map/dot_general | solution.py:179
  55.2 2.1 %collective-permute-start.6 = (bf16[96,2048]{1,0:T(8,128)(2,1)S(1)}, bf16[96,2048]{1,0:T(8,128)(2,1)S(1)}, u32[]{:S(2)}, u32[]{:S(2)}) collective-permute-start(bf16[96,2048]{1,0:T(8,128)(2,1)S(1)} %get-tuple-element.53), channel_id=1, source_target_pairs={{0,1},{1,2},{2,3},{3,0},{4,5},{5,6},{6,7},{7,4},{8,9},{9,10},{10,1... | collective-permute-start | bytes 1179656 | tf_op jit(solution)/shard_map/ppermute | solution.py:31
  57.3 8.8 %collective-permute-done.8 = bf16[96,2048]{1,0:T(8,128)(2,1)S(1)} collective-permute-done((bf16[96,2048]{1,0:T(8,128)(2,1)S(1)}, bf16[96,2048]{1,0:T(8,128)(2,1)S(1)}, u32[]{:S(2)}, u32[]{:S(2)}) %collective-permute-start.8) | collective-permute-done | bytes 393248 | tf_op jit(solution)/shard_map/ppermute | solution.py:31
  66.3 1.6 %collective-permute-start.9 = (bf16[192,2048]{1,0:T(8,128)(2,1)S(1)}, bf16[192,2048]{1,0:T(8,128)(2,1)S(1)}, u32[]{:S(2)}, u32[]{:S(2)}) collective-permute-start(bf16[192,2048]{1,0:T(8,128)(2,1)S(1)} %pad_maximum_fusion.2), channel_id=1, source_target_pairs={{0,3},{1,0},{2,1},{3,2},{4,7},{5,4},{6,5},{7,6},{8,11},{9,8},{10,9... | collective-permute-start | bytes 2359304 | tf_op jit(solution)/shard_map/ppermute | solution.py:31
  68.0 0.6 collective-permute-start.7
  68.7 2.8 %collective-permute-start.13 = (bf16[64,2048]{1,0:T(8,128)(2,1)S(1)}, bf16[64,2048]{1,0:T(8,128)(2,1)S(1)}, u32[]{:S(2)}, u32[]{:S(2)}) collective-permute-start(bf16[64,2048]{1,0:T(8,128)(2,1)S(1)} %pad_maximum_fusion.7), channel_id=1, source_target_pairs={{0,3},{1,0},{2,1},{3,2},{4,7},{5,4},{6,5},{7,6},{8,11},{9,8},{10,9... | collective-permute-start | bytes 786440 | tf_op jit(solution)/shard_map/ppermute | solution.py:31
  71.6 15.2 %collective-permute-done.9 = bf16[192,2048]{1,0:T(8,128)(2,1)S(1)} collective-permute-done((bf16[192,2048]{1,0:T(8,128)(2,1)S(1)}, bf16[192,2048]{1,0:T(8,128)(2,1)S(1)}, u32[]{:S(2)}, u32[]{:S(2)}) %collective-permute-start.9) | collective-permute-done | bytes 786464 | tf_op jit(solution)/shard_map/ppermute | solution.py:31
  87.0 2.8 %collective-permute-done.7 = bf16[192,2048]{1,0:T(8,128)(2,1)S(1)} collective-permute-done((bf16[192,2048]{1,0:T(8,128)(2,1)S(1)}, bf16[192,2048]{1,0:T(8,128)(2,1)S(1)}, u32[]{:S(2)}, u32[]{:S(2)}) %collective-permute-start.7) | collective-permute-done | bytes 786464 | tf_op jit(solution)/shard_map/ppermute | solution.py:31
  90.0 0.4 constant_dynamic-update-slice_fusion.8
  90.4 2.0 %collective-permute-start.14 = (bf16[96,2048]{1,0:T(8,128)(2,1)S(1)}, bf16[96,2048]{1,0:T(8,128)(2,1)S(1)}, u32[]{:S(2)}, u32[]{:S(2)}) collective-permute-start(bf16[96,2048]{1,0:T(8,128)(2,1)S(1)} %get-tuple-element.52), channel_id=1, source_target_pairs={{0,1},{1,2},{2,3},{3,0},{4,5},{5,6},{6,7},{7,4},{8,9},{9,10},{10,1... | collective-permute-start | bytes 1179656 | tf_op jit(solution)/shard_map/ppermute | solution.py:31
  92.5 2.9 %collective-permute-done.12 = bf16[64,2048]{1,0:T(8,128)(2,1)S(1)} collective-permute-done((bf16[64,2048]{1,0:T(8,128)(2,1)S(1)}, bf16[64,2048]{1,0:T(8,128)(2,1)S(1)}, u32[]{:S(2)}, u32[]{:S(2)}) %collective-permute-start.12) | collective-permute-done | bytes 262176 | tf_op jit(solution)/shard_map/ppermute | solution.py:31
  95.7 2.0 %collective-permute-start.16 = (bf16[32,2048]{1,0:T(8,128)(2,1)S(1)}, bf16[32,2048]{1,0:T(8,128)(2,1)S(1)}, u32[]{:S(2)}, u32[]{:S(2)}) collective-permute-start(bf16[32,2048]{1,0:T(8,128)(2,1)S(1)} %get-tuple-element.50), channel_id=1, source_target_pairs={{0,1},{1,2},{2,3},{3,0},{4,5},{5,6},{6,7},{7,4},{8,9},{9,10},{10,1... | collective-permute-start | bytes 393224 | tf_op jit(solution)/shard_map/ppermute | solution.py:31
  98.0 3.3 %collective-permute-done.15 = bf16[96,2048]{1,0:T(8,128)(2,1)S(1)} collective-permute-done((bf16[96,2048]{1,0:T(8,128)(2,1)S(1)}, bf16[96,2048]{1,0:T(8,128)(2,1)S(1)}, u32[]{:S(2)}, u32[]{:S(2)}) %collective-permute-start.15) | collective-permute-done | bytes 393248 | tf_op jit(solution)/shard_map/ppermute | solution.py:31
  101.3 2.1 %collective-permute-start.19 = (bf16[48,2048]{1,0:T(8,128)(2,1)S(1)}, bf16[48,2048]{1,0:T(8,128)(2,1)S(1)}, u32[]{:S(2)}, u32[]{:S(2)}) collective-permute-start(bf16[48,2048]{1,0:T(8,128)(2,1)S(1)} %slice.264), channel_id=1, source_target_pairs={{0,3},{1,0},{2,1},{3,2},{4,7},{5,4},{6,5},{7,6},{8,11},{9,8},{10,9... | collective-permute-start | bytes 589832 | tf_op jit(solution)/shard_map/ppermute | solution.py:31
  103.8 1.5 %collective-permute-done.16 = bf16[32,2048]{1,0:T(8,128)(2,1)S(1)} collective-permute-done((bf16[32,2048]{1,0:T(8,128)(2,1)S(1)}, bf16[32,2048]{1,0:T(8,128)(2,1)S(1)}, u32[]{:S(2)}, u32[]{:S(2)}) %collective-permute-start.16) | collective-permute-done | bytes 131104 | tf_op jit(solution)/shard_map/ppermute | solution.py:31
  105.5 3.2 %collective-permute-start.21 = (bf16[16,2048]{1,0:T(8,128)(2,1)S(1)}, bf16[16,2048]{1,0:T(8,128)(2,1)S(1)}, u32[]{:S(2)}, u32[]{:S(2)}) collective-permute-start(bf16[16,2048]{1,0:T(8,128)(2,1)S(1)} %slice.213), channel_id=1, source_target_pairs={{0,3},{1,0},{2,1},{3,2},{4,7},{5,4},{6,5},{7,6},{8,11},{9,8},{10,9... | collective-permute-start | bytes 196616 | tf_op jit(solution)/shard_map/ppermute | solution.py:31
  108.8 1.7 %collective-permute-done.18 = bf16[48,2048]{1,0:T(8,128)(2,1)S(1)} collective-permute-done((bf16[48,2048]{1,0:T(8,128)(2,1)S(1)}, bf16[48,2048]{1,0:T(8,128)(2,1)S(1)}, u32[]{:S(2)}, u32[]{:S(2)}) %collective-permute-start.18) | collective-permute-done | bytes 196640 | tf_op jit(solution)/shard_map/ppermute | solution.py:31
  110.5 3.0 %fusion.15 = bf16[384,1792]{1,0:T(8,128)(2,1)S(1)} fusion(bf16[384,2048]{1,0:T(8,128)(2,1)S(1)} %constant_dynamic-update-slice_fusion.4, bf16[1,2048,1792]{2,1,0:T(8,128)(2,1)S(1)} %bitcast.61, f32[384]{0:T(512)S(1)} %select_reduce_fusion), kind=kOutput, calls=%fused_computation.13 | convolution fusion | flops 2819948544 | bytes 10290688 | tf_op jit(solution)/shard_map/dot_general | solution.py:196
  113.9 0.6 collective-permute-start.23
  114.5 1.2 fusion.27
  116.1 3.4 %collective-permute-start.27 = (bf16[64,1792]{1,0:T(8,128)(2,1)S(1)}, bf16[64,1792]{1,0:T(8,128)(2,1)S(1)}, u32[]{:S(2)}, u32[]{:S(2)}) collective-permute-start(bf16[64,1792]{1,0:T(8,128)(2,1)S(1)} %get-tuple-element.74), channel_id=1, source_target_pairs={{0,24},{4,100},{8,0},{12,108},{16,8},{20,116},{24,16},{28,124},{32... | collective-permute-start | bytes 688136 | tf_op jit(solution)/shard_map/ppermute | solution.py:32
  119.5 0.4 convolution_convert_fusion
  120.0 3.5 %collective-permute-done.25 = bf16[64,1792]{1,0:T(8,128)(2,1)S(1)} collective-permute-done((bf16[64,1792]{1,0:T(8,128)(2,1)S(1)}, bf16[64,1792]{1,0:T(8,128)(2,1)S(1)}, u32[]{:S(2)}, u32[]{:S(2)}) %collective-permute-start.25) | collective-permute-done | bytes 229408 | tf_op jit(solution)/shard_map/ppermute | solution.py:32
  123.6 3.4 %collective-permute-start.28 = (bf16[128,1792]{1,0:T(8,128)(2,1)S(1)}, bf16[128,1792]{1,0:T(8,128)(2,1)S(1)}, u32[]{:S(2)}, u32[]{:S(2)}) collective-permute-start(bf16[128,1792]{1,0:T(8,128)(2,1)S(1)} %pad_maximum_fusion.5), channel_id=1, source_target_pairs={{0,24},{4,100},{8,0},{12,108},{16,8},{20,116},{24,16},{28,124},{32... | collective-permute-start | bytes 1376264 | tf_op jit(solution)/shard_map/ppermute | solution.py:32
  127.2 1.5 collective-permute-done.22
  128.7 4.3 %collective-permute-done.28 = bf16[128,1792]{1,0:T(8,128)(2,1)S(1)} collective-permute-done((bf16[128,1792]{1,0:T(8,128)(2,1)S(1)}, bf16[128,1792]{1,0:T(8,128)(2,1)S(1)}, u32[]{:S(2)}, u32[]{:S(2)}) %collective-permute-start.28) | collective-permute-done | bytes 458784 | tf_op jit(solution)/shard_map/ppermute | solution.py:32
  133.0 3.8 %collective-permute-done.26 = bf16[128,1792]{1,0:T(8,128)(2,1)S(1)} collective-permute-done((bf16[128,1792]{1,0:T(8,128)(2,1)S(1)}, bf16[128,1792]{1,0:T(8,128)(2,1)S(1)}, u32[]{:S(2)}, u32[]{:S(2)}) %collective-permute-start.26) | collective-permute-done | bytes 458784 | tf_op jit(solution)/shard_map/ppermute | solution.py:32
  136.7 0.4 fusion.40
  137.1 13.0 %all_to_all.10.back_ref = bf16[16,8,1792]{2,1,0:T(8,128)(2,1)} all-to-all(bf16[16,8,1792]{2,1,0:T(8,128)(2,1)S(1)} %fusion.40), channel_id=1, replica_groups={{0,1,2,3,32,33,34,35,64,65,66,67,96,97,98,99},{8,9,10,11,40,41,42,43,72..., dimensions={0} | all-to-all | bytes 917504 | tf_op jit(solution)/shard_map/all_to_all | solution.py:41
  150.1 1.8 %finish.1 = bf16[8,7168]{1,0:T(8,128)(2,1)} custom-call(bf16[8,7168]{1,0:T(8,128)(2,1)} %hidden_ref.3, bf16[16,8,1792]{2,1,0:T(8,128)(2,1)} %all_to_all.10.back_ref), custom_call_target="tpu_custom_call" | custom-call | tf_op jit(solution)/shard_map/finish/pallas_call | solution.py:249
  (119 shorter events, 5.1 us)
Async XLA Ops:
  1.9 19.5 %all-to-all-start = ((bf16[16,8,1920]{2,1,0:T(8,128)(2,1)}), bf16[16,8,1920]{2,1,0:T(8,128)(2,1)S(1)}, u32[]{:S(2)}, u32[]{:S(2)}) async-start(bf16[16,8,1920]{2,1,0:T(8,128)(2,1)} %prepare.1), calls=%async_computation | async-start | bytes 983040 | tf_op jit(solution)/shard_map/all_to_all | solution.py:41
  21.9 3.2 %collective-permute-start.2 = (bf16[64,1920]{1,0:T(8,128)(2,1)S(1)}, bf16[64,1920]{1,0:T(8,128)(2,1)S(1)}, u32[]{:S(2)}, u32[]{:S(2)}) collective-permute-start(bf16[64,1920]{1,0:T(8,128)(2,1)S(1)} %convolution_convert_fusion.5), channel_id=1, source_target_pairs={{0,4},{4,0},{8,12},{12,8},{16,20},{20,16},{24,28},{28,24},{32,36},... | collective-permute-start | bytes 737288 | tf_op jit(solution)/shard_map/ppermute | solution.py:32
  22.0 9.7 %collective-permute-start.1 = (bf16[128,1920]{1,0:T(8,128)(2,1)S(1)}, bf16[128,1920]{1,0:T(8,128)(2,1)S(1)}, u32[]{:S(2)}, u32[]{:S(2)}) collective-permute-start(bf16[128,1920]{1,0:T(8,128)(2,1)S(1)} %bitcast.70), channel_id=1, source_target_pairs={{0,24},{4,100},{8,0},{12,108},{16,8},{20,116},{24,16},{28,124},{32... | collective-permute-start | bytes 1474568 | tf_op jit(solution)/shard_map/ppermute | solution.py:32
  24.7 10.0 %collective-permute-start = (bf16[128,1920]{1,0:T(8,128)(2,1)S(1)}, bf16[128,1920]{1,0:T(8,128)(2,1)S(1)}, u32[]{:S(2)}, u32[]{:S(2)}) collective-permute-start(bf16[128,1920]{1,0:T(8,128)(2,1)S(1)} %bitcast.71), channel_id=1, source_target_pairs={{0,8},{4,36},{8,16},{12,44},{16,24},{20,52},{24,0},{28,60},{32,40}... | collective-permute-start | bytes 1474568 | tf_op jit(solution)/shard_map/ppermute | solution.py:32
  25.1 4.5 %slice-start.4 = ((s8[7340032]{0:T(1024)(128)(4,1)}), s8[4194304]{0:T(1024)(128)(4,1)S(1)}, s32[]{:S(2)}) async-start(s8[7340032]{0:T(1024)(128)(4,1)} %bitcast.64), calls=%async_computation.6 | async-start | bytes 8388608
  25.2 5.2 %slice-start.5 = ((s8[7340032]{0:T(1024)(128)(4,1)}), s8[3145728]{0:T(1024)(128)(4,1)S(1)}, s32[]{:S(2)}) async-start(s8[7340032]{0:T(1024)(128)(4,1)} %bitcast.64), calls=%async_computation.7 | async-start | bytes 6291456
  34.8 7.5 %collective-permute-start.3 = (bf16[64,1920]{1,0:T(8,128)(2,1)S(1)}, bf16[64,1920]{1,0:T(8,128)(2,1)S(1)}, u32[]{:S(2)}, u32[]{:S(2)}) collective-permute-start(bf16[64,1920]{1,0:T(8,128)(2,1)S(1)} %slice.185), channel_id=1, source_target_pairs={{0,8},{4,36},{8,16},{12,44},{16,24},{20,52},{24,0},{28,60},{32,40}... | collective-permute-start | bytes 737288 | tf_op jit(solution)/shard_map/ppermute | solution.py:32
  34.9 7.4 %collective-permute-start.4 = (bf16[64,1920]{1,0:T(8,128)(2,1)S(1)}, bf16[64,1920]{1,0:T(8,128)(2,1)S(1)}, u32[]{:S(2)}, u32[]{:S(2)}) collective-permute-start(bf16[64,1920]{1,0:T(8,128)(2,1)S(1)} %slice.186), channel_id=1, source_target_pairs={{0,24},{4,100},{8,0},{12,108},{16,8},{20,116},{24,16},{28,124},{32... | collective-permute-start | bytes 737288 | tf_op jit(solution)/shard_map/ppermute | solution.py:32
  42.3 5.9 %slice-start.2 = ((s8[7340032]{0:T(1024)(128)(4,1)}), s8[4194304]{0:T(1024)(128)(4,1)S(1)}, s32[]{:S(2)}) async-start(s8[7340032]{0:T(1024)(128)(4,1)} %bitcast.62), calls=%async_computation.4 | async-start | bytes 8388608
  43.4 4.7 %collective-permute-start.5 = (bf16[192,1920]{1,0:T(8,128)(2,1)S(1)}, bf16[192,1920]{1,0:T(8,128)(2,1)S(1)}, u32[]{:S(2)}, u32[]{:S(2)}) collective-permute-start(bf16[192,1920]{1,0:T(8,128)(2,1)S(1)} %convolution_convert_fusion.1), channel_id=1, source_target_pairs={{0,4},{4,0},{8,12},{12,8},{16,20},{20,16},{24,28},{28,24},{32,36},... | collective-permute-start | bytes 2211848 | tf_op jit(solution)/shard_map/ppermute | solution.py:32
  43.6 25.0 %collective-permute-start.10 = (bf16[32,2048]{1,0:T(8,128)(2,1)S(1)}, bf16[32,2048]{1,0:T(8,128)(2,1)S(1)}, u32[]{:S(2)}, u32[]{:S(2)}) collective-permute-start(bf16[32,2048]{1,0:T(8,128)(2,1)S(1)} %get-tuple-element.27), channel_id=1, source_target_pairs={{0,1},{1,2},{2,3},{3,0},{4,5},{5,6},{6,7},{7,4},{8,9},{9,10},{10,1... | collective-permute-start | bytes 393224 | tf_op jit(solution)/shard_map/ppermute | solution.py:31
  44.2 24.4 %collective-permute-start.11 = (bf16[32,2048]{1,0:T(8,128)(2,1)S(1)}, bf16[32,2048]{1,0:T(8,128)(2,1)S(1)}, u32[]{:S(2)}, u32[]{:S(2)}) collective-permute-start(bf16[32,2048]{1,0:T(8,128)(2,1)S(1)} %get-tuple-element.28), channel_id=1, source_target_pairs={{0,3},{1,0},{2,1},{3,2},{4,7},{5,4},{6,5},{7,6},{8,11},{9,8},{10,9... | collective-permute-start | bytes 393224 | tf_op jit(solution)/shard_map/ppermute | solution.py:31
  47.1 1.9 %slice-start.3 = ((s8[7340032]{0:T(1024)(128)(4,1)}), s8[3145728]{0:T(1024)(128)(4,1)S(1)}, s32[]{:S(2)}) async-start(s8[7340032]{0:T(1024)(128)(4,1)} %bitcast.62), calls=%async_computation.5 | async-start | bytes 6291456
  55.1 11.0 %collective-permute-start.8 = (bf16[96,2048]{1,0:T(8,128)(2,1)S(1)}, bf16[96,2048]{1,0:T(8,128)(2,1)S(1)}, u32[]{:S(2)}, u32[]{:S(2)}) collective-permute-start(bf16[96,2048]{1,0:T(8,128)(2,1)S(1)} %get-tuple-element.56), channel_id=1, source_target_pairs={{0,3},{1,0},{2,1},{3,2},{4,7},{5,4},{6,5},{7,6},{8,11},{9,8},{10,9... | collective-permute-start | bytes 1179656 | tf_op jit(solution)/shard_map/ppermute | solution.py:31
  55.2 12.6 %collective-permute-start.6 = (bf16[96,2048]{1,0:T(8,128)(2,1)S(1)}, bf16[96,2048]{1,0:T(8,128)(2,1)S(1)}, u32[]{:S(2)}, u32[]{:S(2)}) collective-permute-start(bf16[96,2048]{1,0:T(8,128)(2,1)S(1)} %get-tuple-element.53), channel_id=1, source_target_pairs={{0,1},{1,2},{2,3},{3,0},{4,5},{5,6},{6,7},{7,4},{8,9},{9,10},{10,1... | collective-permute-start | bytes 1179656 | tf_op jit(solution)/shard_map/ppermute | solution.py:31
  66.3 20.5 %collective-permute-start.9 = (bf16[192,2048]{1,0:T(8,128)(2,1)S(1)}, bf16[192,2048]{1,0:T(8,128)(2,1)S(1)}, u32[]{:S(2)}, u32[]{:S(2)}) collective-permute-start(bf16[192,2048]{1,0:T(8,128)(2,1)S(1)} %pad_maximum_fusion.2), channel_id=1, source_target_pairs={{0,3},{1,0},{2,1},{3,2},{4,7},{5,4},{6,5},{7,6},{8,11},{9,8},{10,9... | collective-permute-start | bytes 2359304 | tf_op jit(solution)/shard_map/ppermute | solution.py:31
  68.0 21.8 %collective-permute-start.7 = (bf16[192,2048]{1,0:T(8,128)(2,1)S(1)}, bf16[192,2048]{1,0:T(8,128)(2,1)S(1)}, u32[]{:S(2)}, u32[]{:S(2)}) collective-permute-start(bf16[192,2048]{1,0:T(8,128)(2,1)S(1)} %pad_maximum_fusion.1), channel_id=1, source_target_pairs={{0,1},{1,2},{2,3},{3,0},{4,5},{5,6},{6,7},{7,4},{8,9},{9,10},{10,1... | collective-permute-start | bytes 2359304 | tf_op jit(solution)/shard_map/ppermute | solution.py:31
  68.7 23.8 %collective-permute-start.13 = (bf16[64,2048]{1,0:T(8,128)(2,1)S(1)}, bf16[64,2048]{1,0:T(8,128)(2,1)S(1)}, u32[]{:S(2)}, u32[]{:S(2)}) collective-permute-start(bf16[64,2048]{1,0:T(8,128)(2,1)S(1)} %pad_maximum_fusion.7), channel_id=1, source_target_pairs={{0,3},{1,0},{2,1},{3,2},{4,7},{5,4},{6,5},{7,6},{8,11},{9,8},{10,9... | collective-permute-start | bytes 786440 | tf_op jit(solution)/shard_map/ppermute | solution.py:31
  71.5 23.9 %collective-permute-start.12 = (bf16[64,2048]{1,0:T(8,128)(2,1)S(1)}, bf16[64,2048]{1,0:T(8,128)(2,1)S(1)}, u32[]{:S(2)}, u32[]{:S(2)}) collective-permute-start(bf16[64,2048]{1,0:T(8,128)(2,1)S(1)} %pad_maximum_fusion.6), channel_id=1, source_target_pairs={{0,1},{1,2},{2,3},{3,0},{4,5},{5,6},{6,7},{7,4},{8,9},{9,10},{10,1... | collective-permute-start | bytes 786440 | tf_op jit(solution)/shard_map/ppermute | solution.py:31
  89.8 20.7 %slice-start = ((s8[7340032]{0:T(1024)(128)(4,1)}), s8[4194304]{0:T(1024)(128)(4,1)S(1)}, s32[]{:S(2)}) async-start(s8[7340032]{0:T(1024)(128)(4,1)} %bitcast.60), calls=%async_computation.2 | async-start | bytes 8388608
  90.0 20.6 %slice-start.1 = ((s8[7340032]{0:T(1024)(128)(4,1)}), s8[3145728]{0:T(1024)(128)(4,1)S(1)}, s32[]{:S(2)}) async-start(s8[7340032]{0:T(1024)(128)(4,1)} %bitcast.60), calls=%async_computation.3 | async-start | bytes 6291456
  90.4 10.9 %collective-permute-start.15 = (bf16[96,2048]{1,0:T(8,128)(2,1)S(1)}, bf16[96,2048]{1,0:T(8,128)(2,1)S(1)}, u32[]{:S(2)}, u32[]{:S(2)}) collective-permute-start(bf16[96,2048]{1,0:T(8,128)(2,1)S(1)} %get-tuple-element.52), channel_id=1, source_target_pairs={{0,3},{1,0},{2,1},{3,2},{4,7},{5,4},{6,5},{7,6},{8,11},{9,8},{10,9... | collective-permute-start | bytes 1179656 | tf_op jit(solution)/shard_map/ppermute | solution.py:31
  90.4 13.0 %collective-permute-start.14 = (bf16[96,2048]{1,0:T(8,128)(2,1)S(1)}, bf16[96,2048]{1,0:T(8,128)(2,1)S(1)}, u32[]{:S(2)}, u32[]{:S(2)}) collective-permute-start(bf16[96,2048]{1,0:T(8,128)(2,1)S(1)} %get-tuple-element.52), channel_id=1, source_target_pairs={{0,1},{1,2},{2,3},{3,0},{4,5},{5,6},{6,7},{7,4},{8,9},{9,10},{10,1... | collective-permute-start | bytes 1179656 | tf_op jit(solution)/shard_map/ppermute | solution.py:31
  95.6 8.2 %collective-permute-start.17 = (bf16[32,2048]{1,0:T(8,128)(2,1)S(1)}, bf16[32,2048]{1,0:T(8,128)(2,1)S(1)}, u32[]{:S(2)}, u32[]{:S(2)}) collective-permute-start(bf16[32,2048]{1,0:T(8,128)(2,1)S(1)} %get-tuple-element.50), channel_id=1, source_target_pairs={{0,3},{1,0},{2,1},{3,2},{4,7},{5,4},{6,5},{7,6},{8,11},{9,8},{10,9... | collective-permute-start | bytes 393224 | tf_op jit(solution)/shard_map/ppermute | solution.py:31
  95.7 9.7 %collective-permute-start.16 = (bf16[32,2048]{1,0:T(8,128)(2,1)S(1)}, bf16[32,2048]{1,0:T(8,128)(2,1)S(1)}, u32[]{:S(2)}, u32[]{:S(2)}) collective-permute-start(bf16[32,2048]{1,0:T(8,128)(2,1)S(1)} %get-tuple-element.50), channel_id=1, source_target_pairs={{0,1},{1,2},{2,3},{3,0},{4,5},{5,6},{6,7},{7,4},{8,9},{9,10},{10,1... | collective-permute-start | bytes 393224 | tf_op jit(solution)/shard_map/ppermute | solution.py:31
  101.3 9.1 %collective-permute-start.19 = (bf16[48,2048]{1,0:T(8,128)(2,1)S(1)}, bf16[48,2048]{1,0:T(8,128)(2,1)S(1)}, u32[]{:S(2)}, u32[]{:S(2)}) collective-permute-start(bf16[48,2048]{1,0:T(8,128)(2,1)S(1)} %slice.264), channel_id=1, source_target_pairs={{0,3},{1,0},{2,1},{3,2},{4,7},{5,4},{6,5},{7,6},{8,11},{9,8},{10,9... | collective-permute-start | bytes 589832 | tf_op jit(solution)/shard_map/ppermute | solution.py:31
  103.5 6.9 %collective-permute-start.18 = (bf16[48,2048]{1,0:T(8,128)(2,1)S(1)}, bf16[48,2048]{1,0:T(8,128)(2,1)S(1)}, u32[]{:S(2)}, u32[]{:S(2)}) collective-permute-start(bf16[48,2048]{1,0:T(8,128)(2,1)S(1)} %slice.263), channel_id=1, source_target_pairs={{0,1},{1,2},{2,3},{3,0},{4,5},{5,6},{6,7},{7,4},{8,9},{9,10},{10,1... | collective-permute-start | bytes 589832 | tf_op jit(solution)/shard_map/ppermute | solution.py:31
  105.4 8.4 %collective-permute-start.20 = (bf16[16,2048]{1,0:T(8,128)(2,1)S(1)}, bf16[16,2048]{1,0:T(8,128)(2,1)S(1)}, u32[]{:S(2)}, u32[]{:S(2)}) collective-permute-start(bf16[16,2048]{1,0:T(8,128)(2,1)S(1)} %slice.212), channel_id=1, source_target_pairs={{0,1},{1,2},{2,3},{3,0},{4,5},{5,6},{6,7},{7,4},{8,9},{9,10},{10,1... | collective-permute-start | bytes 196616 | tf_op jit(solution)/shard_map/ppermute | solution.py:31
  105.5 8.3 %collective-permute-start.21 = (bf16[16,2048]{1,0:T(8,128)(2,1)S(1)}, bf16[16,2048]{1,0:T(8,128)(2,1)S(1)}, u32[]{:S(2)}, u32[]{:S(2)}) collective-permute-start(bf16[16,2048]{1,0:T(8,128)(2,1)S(1)} %slice.213), channel_id=1, source_target_pairs={{0,3},{1,0},{2,1},{3,2},{4,7},{5,4},{6,5},{7,6},{8,11},{9,8},{10,9... | collective-permute-start | bytes 196616 | tf_op jit(solution)/shard_map/ppermute | solution.py:31
  113.7 2.0 %collective-permute-start.24 = (bf16[64,1792]{1,0:T(8,128)(2,1)S(1)}, bf16[64,1792]{1,0:T(8,128)(2,1)S(1)}, u32[]{:S(2)}, u32[]{:S(2)}) collective-permute-start(bf16[64,1792]{1,0:T(8,128)(2,1)S(1)} %bitcast.90), channel_id=1, source_target_pairs={{0,4},{4,0},{8,12},{12,8},{16,20},{20,16},{24,28},{28,24},{32,36},... | collective-permute-start | bytes 688136 | tf_op jit(solution)/shard_map/ppermute | solution.py:32
  113.9 5.6 %collective-permute-start.23 = (bf16[128,1792]{1,0:T(8,128)(2,1)S(1)}, bf16[128,1792]{1,0:T(8,128)(2,1)S(1)}, u32[]{:S(2)}, u32[]{:S(2)}) collective-permute-start(bf16[128,1792]{1,0:T(8,128)(2,1)S(1)} %bitcast.88), channel_id=1, source_target_pairs={{0,4},{4,0},{8,12},{12,8},{16,20},{20,16},{24,28},{28,24},{32,36},... | collective-permute-start | bytes 1376264 | tf_op jit(solution)/shard_map/ppermute | solution.py:32
  116.1 7.4 %collective-permute-start.25 = (bf16[64,1792]{1,0:T(8,128)(2,1)S(1)}, bf16[64,1792]{1,0:T(8,128)(2,1)S(1)}, u32[]{:S(2)}, u32[]{:S(2)}) collective-permute-start(bf16[64,1792]{1,0:T(8,128)(2,1)S(1)} %get-tuple-element.73), channel_id=1, source_target_pairs={{0,8},{4,36},{8,16},{12,44},{16,24},{20,52},{24,0},{28,60},{32,40}... | collective-permute-start | bytes 688136 | tf_op jit(solution)/shard_map/ppermute | solution.py:32
  116.1 7.3 %collective-permute-start.27 = (bf16[64,1792]{1,0:T(8,128)(2,1)S(1)}, bf16[64,1792]{1,0:T(8,128)(2,1)S(1)}, u32[]{:S(2)}, u32[]{:S(2)}) collective-permute-start(bf16[64,1792]{1,0:T(8,128)(2,1)S(1)} %get-tuple-element.74), channel_id=1, source_target_pairs={{0,24},{4,100},{8,0},{12,108},{16,8},{20,116},{24,16},{28,124},{32... | collective-permute-start | bytes 688136 | tf_op jit(solution)/shard_map/ppermute | solution.py:32
  123.6 9.4 %collective-permute-start.28 = (bf16[128,1792]{1,0:T(8,128)(2,1)S(1)}, bf16[128,1792]{1,0:T(8,128)(2,1)S(1)}, u32[]{:S(2)}, u32[]{:S(2)}) collective-permute-start(bf16[128,1792]{1,0:T(8,128)(2,1)S(1)} %pad_maximum_fusion.5), channel_id=1, source_target_pairs={{0,24},{4,100},{8,0},{12,108},{16,8},{20,116},{24,16},{28,124},{32... | collective-permute-start | bytes 1376264 | tf_op jit(solution)/shard_map/ppermute | solution.py:32
  127.0 9.8 %collective-permute-start.26 = (bf16[128,1792]{1,0:T(8,128)(2,1)S(1)}, bf16[128,1792]{1,0:T(8,128)(2,1)S(1)}, u32[]{:S(2)}, u32[]{:S(2)}) collective-permute-start(bf16[128,1792]{1,0:T(8,128)(2,1)S(1)} %pad_maximum_fusion.4), channel_id=1, source_target_pairs={{0,8},{4,36},{8,16},{12,44},{16,24},{20,52},{24,0},{28,60},{32,40}... | collective-permute-start | bytes 1376264 | tf_op jit(solution)/shard_map/ppermute | solution.py:32
  127.1 1.6 %collective-permute-start.22 = (bf16[64,1792]{1,0:T(8,128)(2,1)S(1)}, bf16[64,1792]{1,0:T(8,128)(2,1)S(1)}, u32[]{:S(2)}, u32[]{:S(2)}) collective-permute-start(bf16[64,1792]{1,0:T(8,128)(2,1)S(1)} %bitcast.91), channel_id=1, source_target_pairs={{0,4},{4,0},{8,12},{12,8},{16,20},{20,16},{24,28},{28,24},{32,36},... | collective-permute-start | bytes 688136 | tf_op jit(solution)/shard_map/ppermute | solution.py:32
